TPU v7x, 32 devices: a whole 2x2x4 slice. The times are simulated.
32 devices in a mesh: dp: 4 (over y, core), expert: 8 (over z, x).
Axes of the slice: x: 2, y: 2, z: 4, core: 2. Of those that a mesh axis runs over, the one named last changes fastest.
Arguments:
- tokens: bfloat16 [2048, 1024], P(('dp', 'expert')), may hold values from -6 to 6
- cotangent: bfloat16 [2048, 1024], P(('dp', 'expert')), may hold values from -1.5 to 1.5
- routes: int32 [2048, 2], P(('dp', 'expert')), may hold values from 0 to 7, all different within a row
- gates: bfloat16 [2048, 2], P(('dp', 'expert')), may hold values from 0.099609375 to 0.8984375
- proj_in: bfloat16 [8, 1024, 2048], P('expert'), may hold values from -0.1875 to 0.1875
- proj_out: bfloat16 [8, 2048, 1024], P('expert'), may hold values from -0.125 to 0.125
Outputs:
- token_grads: bfloat16 [2048, 1024], P(('dp', 'expert'))
- gate_grads: bfloat16 [2048, 2], P(('dp', 'expert'))
- grad_in: bfloat16 [8, 1024, 2048], P('expert', 'dp')
- grad_out: bfloat16 [8, 2048, 1024], P('expert', 'dp')
All inputs are finite; a program needn't handle non-finite values.
Results may differ from a plain program's by a relative error of at most 0.018.
Values may be sent and summed in bfloat16 or wider, within the bound.
No kernel may reach another device: no remote copies, remote signals or barrier semaphores. Data moves between devices by JAX's collectives and lax.ppermute only.
A program may use at most 64 MiB of HBM per device.

v0:
```python
import jax
import jax.numpy as jnp
from jax import lax
from jax.sharding import PartitionSpec as P


def slope_of(pre_act):
    gauss_cdf = 0.5 * (1.0 + jax.scipy.special.erf(pre_act * 0.7071067811865476))
    gauss_pdf = jnp.exp(-0.5 * pre_act * pre_act) * 0.3989422804014327
    return gauss_cdf + pre_act * gauss_pdf


def reduce_in(recv_x, d_pre):
    return lax.psum_scatter(
        lax.dot_general(
            recv_x, d_pre, (((0,), (0,)), ((), ())), preferred_element_type=jnp.float32
        ).astype(jnp.bfloat16),
        "dp",
        scatter_dimension=0,
        tiled=True,
    )


def reduce_out(hidden, scaled):
    return lax.psum_scatter(
        lax.dot_general(
            hidden, scaled, (((0,), (0,)), ((), ())), preferred_element_type=jnp.float32
        ).astype(jnp.bfloat16),
        "dp",
        scatter_dimension=0,
        tiled=True,
    )


def local(tokens, cotangent, routes, gates, proj_in, proj_out):
    tok_count = tokens.shape[0]
    feat_width = tokens.shape[1]
    experts = lax.axis_size("expert")
    capacity = 2 * tok_count // experts
    slots_all = experts * capacity
    chosen = jnp.concatenate([routes[:, 0], routes[:, 1]])
    one_hot = (chosen[:, None] == jnp.arange(experts, dtype=jnp.int32)[None, :]).astype(jnp.int32)
    earlier = jnp.cumsum(one_hot, axis=0) - one_hot
    slot_pos = jnp.sum(earlier * one_hot, axis=1)
    kept_mask = slot_pos < capacity
    target = jnp.where(kept_mask, chosen * capacity + slot_pos, slots_all)
    both_x = jnp.concatenate([tokens, tokens], axis=0)
    both_dy = jnp.concatenate([cotangent, cotangent], axis=0)
    both_gate = jnp.concatenate([gates[:, 0], gates[:, 1]])[:, None]
    placing = (jnp.arange(slots_all, dtype=jnp.int32)[:, None] == target[None, :]).astype(
        jnp.bfloat16
    )
    send_x = jnp.dot(placing, both_x, preferred_element_type=jnp.float32).astype(jnp.bfloat16)
    send_dy = jnp.dot(placing, both_dy, preferred_element_type=jnp.float32).astype(jnp.bfloat16)
    send_gate = jnp.dot(placing, both_gate, preferred_element_type=jnp.float32).astype(jnp.bfloat16)
    recv_x, recv_dy, recv_gate = (
        lax.all_to_all(
            send_x.reshape(experts, capacity, feat_width),
            "expert",
            split_axis=0,
            concat_axis=0,
            tiled=True,
        ),
        lax.all_to_all(
            send_dy.reshape(experts, capacity, feat_width),
            "expert",
            split_axis=0,
            concat_axis=0,
            tiled=True,
        ),
        lax.all_to_all(
            send_gate.reshape(experts, capacity), "expert", split_axis=0, concat_axis=0, tiled=True
        ),
    )
    recv_x = recv_x.reshape(slots_all, feat_width)
    recv_dy = recv_dy.reshape(slots_all, feat_width)
    recv_gate = recv_gate.reshape(slots_all, 1)
    weight_in = proj_in[0]
    weight_out = proj_out[0]
    pre_act = jnp.dot(recv_x, weight_in, preferred_element_type=jnp.float32)
    hidden = jax.nn.gelu(pre_act, approximate=False).astype(jnp.bfloat16)
    out_rows = jnp.dot(hidden, weight_out, preferred_element_type=jnp.float32)
    dgate_rows = jnp.sum(recv_dy.astype(jnp.float32) * out_rows, axis=1).astype(jnp.bfloat16)
    scaled = (recv_gate.astype(jnp.float32) * recv_dy.astype(jnp.float32)).astype(jnp.bfloat16)
    d_hidden = lax.dot_general(
        scaled, weight_out, (((1,), (1,)), ((), ())), preferred_element_type=jnp.float32
    )
    d_pre = (d_hidden * slope_of(pre_act)).astype(jnp.bfloat16)
    dx_rows = lax.dot_general(
        d_pre, weight_in, (((1,), (1,)), ((), ())), preferred_element_type=jnp.float32
    ).astype(jnp.bfloat16)
    back_x, back_gate = (
        lax.all_to_all(
            dx_rows.reshape(experts, capacity, feat_width),
            "expert",
            split_axis=0,
            concat_axis=0,
            tiled=True,
        ),
        lax.all_to_all(
            dgate_rows.reshape(experts, capacity), "expert", split_axis=0, concat_axis=0, tiled=True
        ),
    )
    grad_out = reduce_out(hidden, scaled)
    grad_in = reduce_in(recv_x, d_pre)
    back_x = back_x.reshape(slots_all, feat_width)
    back_gate = back_gate.reshape(slots_all, 1)
    taken_x = lax.dot_general(
        placing, back_x, (((0,), (0,)), ((), ())), preferred_element_type=jnp.float32
    )
    taken_gate = lax.dot_general(
        placing, back_gate, (((0,), (0,)), ((), ())), preferred_element_type=jnp.float32
    )
    token_grads = (taken_x[:tok_count] + taken_x[tok_count:]).astype(jnp.bfloat16)
    gate_grads = jnp.concatenate([taken_gate[:tok_count], taken_gate[tok_count:]], axis=1).astype(
        jnp.bfloat16
    )
    return (token_grads, gate_grads, grad_in[None], grad_out[None])


def solution(mesh):
    placed = (
        P(("dp", "expert"), None),
        P(("dp", "expert"), None),
        P(("dp", "expert"), None),
        P(("dp", "expert"), None),
        P("expert", None, None),
        P("expert", None, None),
    )
    return jax.shard_map(
        local,
        mesh=mesh,
        in_specs=placed,
        out_specs=(
            P(("dp", "expert"), None),
            P(("dp", "expert"), None),
            P("expert", "dp", None),
            P("expert", "dp", None),
        ),
        check_vma=False,
    )
```

profile of v0, /device:TPU:0, one launch (start us, length us, event | category | flops | bytes accessed | tf_op | source)
XLA Modules:
  0.0 151.7 jit_solution(4402720555833903457)
XLA Ops:
  7.2 0.8 slice_bitcast_fusion.5
  7.9 0.7 slice_bitcast_fusion.3
  8.7 0.1 pad_add_fusion
  8.7 0.1 fusion.47
  8.8 0.2 reduce_window_sum.11
  9.0 0.2 select_reduce_fusion
  9.2 0.1 compare_select_fusion
  9.3 0.2 fusion.23
  9.4 0.7 all_to_all.25
  10.1 7.3 %all-to-all-start = ((bf16[8,1,16]{2,1,0:T(2,128)(2,1)}), bf16[8,1,16]{2,1,0:T(2,128)(2,1)S(1)}, u32[]{:S(2)}, u32[]{:S(2)}) async-start(bf16[8,1,16]{2,1,0:T(2,128)(2,1)} %all_to_all.25), calls=%async_computation | async-start | bytes 8192 | tf_op jit(solution)/shard_map/all_to_all | solution.py:71
  17.4 1.9 %convolution_convert_fusion.2 = bf16[128,1024]{1,0:T(8,128)(2,1)} fusion(bf16[64,1024]{1,0:T(8,128)(2,1)} %param.6, s32[128]{0:T(128)S(1)} %compare_select_fusion), kind=kOutput, calls=%fused_computation.15 | convolution fusion | flops 34226176 | bytes 393728 | tf_op jit(solution)/shard_map/dot_general | solution.py:53
  19.3 4.5 %all-to-all-done = bf16[8,1,16]{2,1,0:T(2,128)(2,1)S(1)} async-done(((bf16[8,1,16]{2,1,0:T(2,128)(2,1)}), bf16[8,1,16]{2,1,0:T(2,128)(2,1)S(1)}, u32[]{:S(2)}, u32[]{:S(2)}) %all-to-all-start) | async-done | bytes 288 | tf_op jit(solution)/shard_map/all_to_all | solution.py:71
  23.8 3.4 %all-to-all-start.2 = ((bf16[8,16,1024]{2,1,0:T(8,128)(2,1)}), bf16[8,16,1024]{2,1,0:T(8,128)(2,1)S(1)}, u32[]{:S(2)}, u32[]{:S(2)}) async-start(bf16[8,16,1024]{2,1,0:T(8,128)(2,1)} %bitcast.10), calls=%async_computation.2 | async-start | bytes 524288 | tf_op jit(solution)/shard_map/all_to_all | solution.py:57
  27.2 1.9 %convolution_convert_fusion.3 = bf16[128,1024]{1,0:T(8,128)(2,1)} fusion(bf16[64,1024]{1,0:T(8,128)(2,1)} %param.7, s32[128]{0:T(128)S(1)} %compare_select_fusion), kind=kOutput, calls=%fused_computation.16 | convolution fusion | flops 34226176 | bytes 393728 | tf_op jit(solution)/shard_map/dot_general | solution.py:54
  29.1 6.3 %all-to-all-done.2 = bf16[8,16,1024]{2,1,0:T(8,128)(2,1)S(1)} async-done(((bf16[8,16,1024]{2,1,0:T(8,128)(2,1)}), bf16[8,16,1024]{2,1,0:T(8,128)(2,1)S(1)}, u32[]{:S(2)}, u32[]{:S(2)}) %all-to-all-start.2) | async-done | bytes 262176 | tf_op jit(solution)/shard_map/all_to_all | solution.py:57
  35.4 3.4 %all-to-all-start.1 = ((bf16[8,16,1024]{2,1,0:T(8,128)(2,1)}), bf16[8,16,1024]{2,1,0:T(8,128)(2,1)S(1)}, u32[]{:S(2)}, u32[]{:S(2)}) async-start(bf16[8,16,1024]{2,1,0:T(8,128)(2,1)} %bitcast.7), calls=%async_computation.1 | async-start | bytes 524288 | tf_op jit(solution)/shard_map/all_to_all | solution.py:64
  38.8 0.0 reduce-scatter.3.cloned.1.call-start
  38.8 4.4 %fusion.31 = (bf16[128,2048]{1,0:T(8,128)(2,1)S(1)}, f32[128,2048]{1,0:T(8,128)S(1)}) fusion(bf16[128,1024]{1,0:T(8,128)(2,1)S(1)} %bitcast.73, bf16[1,1024,2048]{2,1,0:T(8,128)(2,1)} %param.10), kind=kOutput, calls=%fused_computation.29 | convolution fusion | flops 553910272 | bytes 6029312 | tf_op jit(solution)/shard_map/dot_general | solution.py:80
  43.3 3.7 %all-to-all-done.1 = bf16[8,16,1024]{2,1,0:T(8,128)(2,1)S(1)} async-done(((bf16[8,16,1024]{2,1,0:T(8,128)(2,1)}), bf16[8,16,1024]{2,1,0:T(8,128)(2,1)S(1)}, u32[]{:S(2)}, u32[]{:S(2)}) %all-to-all-start.1) | async-done | bytes 262176 | tf_op jit(solution)/shard_map/all_to_all | solution.py:64
  46.9 0.1 multiply_convert_fusion
  47.1 3.8 %fusion.11 = bf16[128,2048]{1,0:T(8,128)(2,1)S(1)} fusion(bf16[128,1024]{1,0:T(8,128)(2,1)S(1)} %bitcast.76, bf16[1,2048,1024]{2,1,0:T(8,128)(2,1)} %param.11, f32[128,2048]{1,0:T(8,128)S(1)} %get-tuple-element.13), kind=kOutput, calls=%fused_computation.11 | convolution fusion | flops 539492352 | bytes 6029312 | tf_op jit(solution)/shard_map/dot_general | solution.py:85
  50.9 3.2 %convolution_convert_fusion.1 = bf16[1024,2048]{1,0:T(8,128)(2,1)} fusion(bf16[128,1024]{1,0:T(8,128)(2,1)S(1)} %bitcast.74, bf16[128,2048]{1,0:T(8,128)(2,1)S(1)} %fusion.11), kind=kOutput, calls=%fused_computation.9 | convolution fusion | flops 538968064 | bytes 4980736 | tf_op jit(solution)/shard_map/dot_general | solution.py:15
  54.1 0.0 reduce-scatter.3.cloned.1.call-update
  54.1 0.0 reduce-scatter.5.cloned.1.call-start
  54.2 0.1 reshape.112
  54.3 0.1 fusion.39
  54.4 3.3 %convolution_convert_fusion = bf16[2048,1024]{1,0:T(8,128)(2,1)} fusion(bf16[128,2048]{1,0:T(8,128)(2,1)S(1)} %get-tuple-element.12, bf16[128,1024]{1,0:T(8,128)(2,1)S(1)} %fusion.39), kind=kOutput, calls=%fused_computation.8 | convolution fusion | flops 538968064 | bytes 4980736 | tf_op jit(solution)/shard_map/dot_general | solution.py:26
  57.6 0.0 reduce-scatter.5.cloned.1.call-update
  57.7 3.1 %fusion.20 = bf16[128]{0:T(256)(128)(2,1)S(1)} fusion(bf16[128,2048]{1,0:T(8,128)(2,1)S(1)} %get-tuple-element.12, bf16[1,2048,1024]{2,1,0:T(8,128)(2,1)} %param.11, bf16[128,1024]{1,0:T(8,128)(2,1)S(1)} %bitcast.72), kind=kOutput, calls=%fused_computation.18 | convolution fusion | flops 537264000 | bytes 4980992 | tf_op jit(solution)/shard_map/dot_general | solution.py:82
  60.8 0.7 convert_element_type.107
  61.5 3.3 %all-to-all-start.4 = ((bf16[8,1,16]{2,1,0:T(2,128)(2,1)}), bf16[8,1,16]{2,1,0:T(2,128)(2,1)S(1)}, u32[]{:S(2)}, u32[]{:S(2)}) async-start(bf16[8,1,16]{2,1,0:T(2,128)(2,1)} %convert_element_type.107), calls=%async_computation.4 | async-start | bytes 8192 | tf_op jit(solution)/shard_map/all_to_all | solution.py:100
  64.8 4.4 %fusion.17 = bf16[128,1024]{1,0:T(8,128)(2,1)} fusion(bf16[128,2048]{1,0:T(8,128)(2,1)S(1)} %fusion.11, bf16[1,1024,2048]{2,1,0:T(8,128)(2,1)} %param.10), kind=kOutput, calls=%fused_computation.17 | convolution fusion | flops 537001984 | bytes 4980736 | tf_op jit(solution)/shard_map/dot_general | solution.py:89
  69.2 1.9 %all-to-all-done.4 = bf16[8,1,16]{2,1,0:T(2,128)(2,1)S(1)} async-done(((bf16[8,1,16]{2,1,0:T(2,128)(2,1)}), bf16[8,1,16]{2,1,0:T(2,128)(2,1)S(1)}, u32[]{:S(2)}, u32[]{:S(2)}) %all-to-all-start.4) | async-done | bytes 288 | tf_op jit(solution)/shard_map/all_to_all | solution.py:100
  71.1 4.0 %all-to-all-start.3 = ((bf16[8,16,1024]{2,1,0:T(8,128)(2,1)}), bf16[8,16,1024]{2,1,0:T(8,128)(2,1)S(1)}, u32[]{:S(2)}, u32[]{:S(2)}) async-start(bf16[8,16,1024]{2,1,0:T(8,128)(2,1)} %bitcast.13), calls=%async_computation.3 | async-start | bytes 524288 | tf_op jit(solution)/shard_map/all_to_all | solution.py:93
  75.2 0.1 reshape.115
  75.3 0.1 fusion.24
  75.4 0.1 slice_bitcast_fusion.1
  75.5 0.5 pad_maximum_fusion
  76.0 7.4 %all-to-all-done.3 = bf16[8,16,1024]{2,1,0:T(8,128)(2,1)S(1)} async-done(((bf16[8,16,1024]{2,1,0:T(8,128)(2,1)}), bf16[8,16,1024]{2,1,0:T(8,128)(2,1)S(1)}, u32[]{:S(2)}, u32[]{:S(2)}) %all-to-all-start.3) | async-done | bytes 262176 | tf_op jit(solution)/shard_map/all_to_all | solution.py:93
  83.4 0.3 fusion.48
  83.7 0.7 fusion.40
  84.3 12.8 %reduce-scatter.3.cloned.1.call-done = bf16[256,2048]{1,0:T(8,128)(2,1)} async-done(((bf16[1024,2048]{1,0:T(8,128)(2,1)}), bf16[256,2048]{1,0:T(8,128)(2,1)}) %reduce-scatter.3.cloned.1.call-update) | async-done | bytes 1048592 | tf_op jit(solution)/shard_map/reduce_scatter | solution.py:14
  97.1 47.8 %reduce-scatter.5.cloned.1.call-done = bf16[512,1024]{1,0:T(8,128)(2,1)} async-done(((bf16[2048,1024]{1,0:T(8,128)(2,1)}), bf16[512,1024]{1,0:T(8,128)(2,1)}) %reduce-scatter.5.cloned.1.call-update) | async-done | bytes 1048592 | tf_op jit(solution)/shard_map/reduce_scatter | solution.py:25
  (2 shorter events, 0.0 us)
Async XLA Ops:
  10.1 13.6 %all-to-all-start = ((bf16[8,1,16]{2,1,0:T(2,128)(2,1)}), bf16[8,1,16]{2,1,0:T(2,128)(2,1)S(1)}, u32[]{:S(2)}, u32[]{:S(2)}) async-start(bf16[8,1,16]{2,1,0:T(2,128)(2,1)} %all_to_all.25), calls=%async_computation | async-start | bytes 8192 | tf_op jit(solution)/shard_map/all_to_all | solution.py:71
  23.8 11.6 %all-to-all-start.2 = ((bf16[8,16,1024]{2,1,0:T(8,128)(2,1)}), bf16[8,16,1024]{2,1,0:T(8,128)(2,1)S(1)}, u32[]{:S(2)}, u32[]{:S(2)}) async-start(bf16[8,16,1024]{2,1,0:T(8,128)(2,1)} %bitcast.10), calls=%async_computation.2 | async-start | bytes 524288 | tf_op jit(solution)/shard_map/all_to_all | solution.py:57
  35.4 11.6 %all-to-all-start.1 = ((bf16[8,16,1024]{2,1,0:T(8,128)(2,1)}), bf16[8,16,1024]{2,1,0:T(8,128)(2,1)S(1)}, u32[]{:S(2)}, u32[]{:S(2)}) async-start(bf16[8,16,1024]{2,1,0:T(8,128)(2,1)} %bitcast.7), calls=%async_computation.1 | async-start | bytes 524288 | tf_op jit(solution)/shard_map/all_to_all | solution.py:64
  38.8 58.3 %reduce-scatter.3.cloned.1.call-start = ((), (), s32[]{:S(2)}) async-start(), calls=%async_computation.7 | async-start | bytes 5242880 | tf_op jit(solution)/shard_map/reduce_scatter | solution.py:14
  54.1 90.8 %reduce-scatter.5.cloned.1.call-start = ((), (), s32[]{:S(2)}) async-start(), calls=%async_computation.8 | async-start | bytes 5242880 | tf_op jit(solution)/shard_map/reduce_scatter | solution.py:25
  61.5 9.6 %all-to-all-start.4 = ((bf16[8,1,16]{2,1,0:T(2,128)(2,1)}), bf16[8,1,16]{2,1,0:T(2,128)(2,1)S(1)}, u32[]{:S(2)}, u32[]{:S(2)}) async-start(bf16[8,1,16]{2,1,0:T(2,128)(2,1)} %convert_element_type.107), calls=%async_computation.4 | async-start | bytes 8192 | tf_op jit(solution)/shard_map/all_to_all | solution.py:100
  71.1 12.3 %all-to-all-start.3 = ((bf16[8,16,1024]{2,1,0:T(8,128)(2,1)}), bf16[8,16,1024]{2,1,0:T(8,128)(2,1)S(1)}, u32[]{:S(2)}, u32[]{:S(2)}) async-start(bf16[8,16,1024]{2,1,0:T(8,128)(2,1)} %bitcast.13), calls=%async_computation.3 | async-start | bytes 524288 | tf_op jit(solution)/shard_map/all_to_all | solution.py:93
Sparse Core Ops, SparseCore 0:
  54.2 42.8 reduce-scatter.2
  100.4 44.4 reduce-scatter.4
where the time goes:
time: 152 us
  waiting for transfers between devices  84.2 us (55%)
  matrix products  26.7 us (18%)
  starting transfers between devices  21.5 us (14%)
  between operations  14.1 us (9%)
  local copies, waits for them, and re-layouts  3.14 us (2%)
  other arithmetic  2.04 us (1%)
    reduce_scatter x1, waiting for transfers between devices, reduce_out(): lax.psum_scatter(lax.dot_general(hidden, scaled, (((0,), (0,)), ((), ()))...  47.8 us
    reduce_scatter x1, waiting for transfers between devices, reduce_in(): lax.psum_scatter(lax.dot_general(recv_x, d_pre, (((0,), (0,)), ((), ())),...  12.8 us
    all_to_all x1, waiting for transfers between devices, local(): lax.all_to_all(dx_rows.reshape(experts, capacity, feat_width), 'expert',...  7.37 us
    all_to_all x1, starting transfers between devices, local(): lax.all_to_all(send_gate.reshape(experts, capacity), 'expert', split_axis...  7.25 us
    all_to_all x1, waiting for transfers between devices, local(): lax.all_to_all(send_x.reshape(experts, capacity, feat_width), 'expert', s...  6.25 us
    all_to_all x1, waiting for transfers between devices, local(): lax.all_to_all(send_gate.reshape(experts, capacity), 'expert', split_axis...  4.48 us
    dot_general x1, matrix products, local(): pre_act = jnp.dot(recv_x, weight_in, preferred_element_type=jnp.float32)  4.44 us
    dot_general x1, matrix products, local(): lax.dot_general(d_pre, weight_in, (((1,), (1,)), ((), ())), preferred_ele...  4.43 us
  transfers between devices with their start and end apart: 7, of which 7 were waited for; matrix products, arithmetic and copies ran while one was open for 14% of the time, Pallas kernels for 0%

commit v1 on v0

v1 whole, which is shorter than its diff:
```python
import jax
import jax.numpy as jnp
from jax import lax
from jax.sharding import PartitionSpec as P


def slope_of(pre_act):
    gauss_cdf = 0.5 * (1.0 + jax.scipy.special.erf(pre_act * 0.7071067811865476))
    gauss_pdf = jnp.exp(-0.5 * pre_act * pre_act) * 0.3989422804014327
    return gauss_cdf + pre_act * gauss_pdf


def gather_groups(rows):
    groups = lax.axis_size("dp")
    swap = [(i, i ^ 1) for i in range(groups)]
    mine = [rows, lax.ppermute(rows, "dp", swap)]
    for k in range(1, groups // 2):
        other = lax.ppermute(rows, "dp", [(i, (i + 2 * k) % groups) for i in range(groups)])
        mine += [other, lax.ppermute(other, "dp", swap)]
    return mine


def local(tokens, cotangent, routes, gates, proj_in, proj_out):
    tok_count = tokens.shape[0]
    feat_width = tokens.shape[1]
    experts = lax.axis_size("expert")
    groups = lax.axis_size("dp")
    me = lax.axis_index("dp")
    capacity = 2 * tok_count // experts
    slots_all = experts * capacity
    weight_in = proj_in[0]
    weight_out = proj_out[0]
    ffw = weight_in.shape[1]
    chosen = jnp.concatenate([routes[:, 0], routes[:, 1]])
    one_hot = (chosen[:, None] == jnp.arange(experts, dtype=jnp.int32)[None, :]).astype(jnp.int32)
    earlier = jnp.cumsum(one_hot, axis=0) - one_hot
    slot_pos = jnp.sum(earlier * one_hot, axis=1)
    kept_mask = slot_pos < capacity
    target = jnp.where(kept_mask, chosen * capacity + slot_pos, slots_all)
    placing = (jnp.arange(slots_all, dtype=jnp.int32)[:, None] == target[None, :]).astype(
        jnp.bfloat16
    )
    either = placing[:, :tok_count] + placing[:, tok_count:]
    send_x = jnp.dot(either, tokens, preferred_element_type=jnp.float32).astype(jnp.bfloat16)
    scaled_tok = jnp.concatenate(
        [
            (gates[:, k : k + 1].astype(jnp.float32) * cotangent.astype(jnp.float32)).astype(
                jnp.bfloat16
            )
            for k in range(2)
        ],
        axis=0,
    )
    send_s = jnp.dot(placing, scaled_tok, preferred_element_type=jnp.float32).astype(jnp.bfloat16)

    def exchange(rows):
        return lax.all_to_all(
            rows.reshape(experts, capacity, rows.shape[1]),
            "expert",
            split_axis=0,
            concat_axis=0,
            tiled=True,
        ).reshape(slots_all, rows.shape[1])

    x_parts = gather_groups(exchange(send_x))
    s_parts = gather_groups(exchange(send_s))

    def forward(x, s):
        pre_act = jnp.dot(x, weight_in, preferred_element_type=jnp.float32)
        hidden = jax.nn.gelu(pre_act, approximate=False).astype(jnp.bfloat16)
        d_hidden = lax.dot_general(
            s, weight_out, (((1,), (1,)), ((), ())), preferred_element_type=jnp.float32
        )
        d_pre = (d_hidden * slope_of(pre_act)).astype(jnp.bfloat16)
        return hidden, d_hidden, d_pre

    hidden0, d_hidden0, d_pre0 = forward(x_parts[0], s_parts[0])
    dgate = jnp.sum(hidden0.astype(jnp.float32) * d_hidden0, axis=1, keepdims=True)
    dx_rows = lax.dot_general(
        d_pre0, weight_in, (((1,), (1,)), ((), ())), preferred_element_type=jnp.float32
    )
    back = exchange(
        jnp.concatenate([dx_rows, jnp.broadcast_to(dgate, (slots_all, 128))], axis=1).astype(
            jnp.bfloat16
        )
    )
    hidden1, _, d_pre1 = forward(
        jnp.concatenate(x_parts[1:], axis=0), jnp.concatenate(s_parts[1:], axis=0)
    )
    x_all = jnp.concatenate(x_parts, axis=0)
    s_all = jnp.concatenate(s_parts, axis=0)
    hidden = jnp.concatenate([hidden0, hidden1], axis=0)
    d_pre = jnp.concatenate([d_pre0, d_pre1], axis=0)
    x_cut = lax.dynamic_slice_in_dim(x_all, me * (feat_width // groups), feat_width // groups, 1)
    h_cut = lax.dynamic_slice_in_dim(hidden, me * (ffw // groups), ffw // groups, 1)
    grad_in = lax.dot_general(
        x_cut, d_pre, (((0,), (0,)), ((), ())), preferred_element_type=jnp.float32
    ).astype(jnp.bfloat16)
    grad_out = lax.dot_general(
        h_cut, s_all, (((0,), (0,)), ((), ())), preferred_element_type=jnp.float32
    ).astype(jnp.bfloat16)
    token_grads = lax.dot_general(
        either, back[:, :feat_width], (((0,), (0,)), ((), ())), preferred_element_type=jnp.float32
    ).astype(jnp.bfloat16)
    taken_gate = lax.dot_general(
        placing,
        back[:, feat_width : feat_width + 1],
        (((0,), (0,)), ((), ())),
        preferred_element_type=jnp.float32,
    )
    gate_grads = (
        jnp.concatenate([taken_gate[:tok_count], taken_gate[tok_count:]], axis=1)
        / gates.astype(jnp.float32)
    ).astype(jnp.bfloat16)
    return (token_grads, gate_grads, grad_in[None], grad_out[None])


def solution(mesh):
    placed = (
        P(("dp", "expert"), None),
        P(("dp", "expert"), None),
        P(("dp", "expert"), None),
        P(("dp", "expert"), None),
        P("expert", None, None),
        P("expert", None, None),
    )
    return jax.shard_map(
        local,
        mesh=mesh,
        in_specs=placed,
        out_specs=(
            P(("dp", "expert"), None),
            P(("dp", "expert"), None),
            P("expert", "dp", None),
            P("expert", "dp", None),
        ),
        check_vma=False,
    )
```

time: 152 us -> 77.2 us (0.51)
  waiting for transfers between devices: 84.2 us -> 22.2 us
  between operations: 14.1 us -> 0.78 us
  matrix products: 26.7 us -> 32 us
  starting transfers between devices: 21.5 us -> 17.1 us
  local copies, waits for them, and re-layouts: 3.14 us -> 1.03 us
  other arithmetic: 2.04 us -> 3.62 us
    reduce_scatter x2 -> x0, waiting for transfers between devices: 60.6 us -> none  [the longest x1 47.8 us: reduce_out(): lax.psum_scatter(lax.dot_general(hidden, scaled, (((0,), (0,)), ((), ()))...]
    all_to_all x5 -> x3, waiting for transfers between devices: 23.7 us -> 11.9 us  [exchange(): lax.all_to_all(rows.reshape(experts, capacity, rows.shape[1]), 'expert',...]
    ppermute x0 -> x6, waiting for transfers between devices: none -> 10.3 us  [the longest x2 10.3 us: gather_groups(): lax.ppermute(rows, 'dp', [(i, (i + 2 * k) % groups) for i in range(groups)])]
    all_to_all x5 -> x3, starting transfers between devices: 21.4 us -> 14.4 us  [exchange(): lax.all_to_all(rows.reshape(experts, capacity, rows.shape[1]), 'expert',...]
    dot_general x11, matrix products: 26.7 us -> 32 us  [the longest x2 12.8 us: forward(): pre_act = jnp.dot(x, weight_in, preferred_element_type=jnp.float32)]
    ppermute x0 -> x6, starting transfers between devices: none -> 2.61 us  [the longest x2 2.09 us: gather_groups(): lax.ppermute(rows, 'dp', [(i, (i + 2 * k) % groups) for i in range(groups)])]
  transfers between devices with their start and end apart: 7 -> 9, of which waited for: 7 -> 4; matrix products, arithmetic and copies ran while one was open for 14% -> 22% of each run, Pallas kernels for 0% -> 0%
where the time goes in v1:
time: 77.2 us; the launch traced here: 76.7 us
  matrix products  32 us (41%)
  waiting for transfers between devices  22.2 us (29%)
  starting transfers between devices  17.1 us (22%)
  other arithmetic  3.62 us (5%)
  local copies, waits for them, and re-layouts  1.03 us (1%)
  between operations  0.78 us (1%)
    all_to_all x3, starting transfers between devices, exchange(): lax.all_to_all(rows.reshape(experts, capacity, rows.shape[1]), 'expert',...  14.4 us
    dot_general x2, matrix products, forward(): pre_act = jnp.dot(x, weight_in, preferred_element_type=jnp.float32)  12.8 us
    all_to_all x3, waiting for transfers between devices, exchange(): lax.all_to_all(rows.reshape(experts, capacity, rows.shape[1]), 'expert',...  11.9 us
    dot_general x2, matrix products, forward(): lax.dot_general(s, weight_out, (((1,), (1,)), ((), ())), preferred_elemen...  11.1 us
    ppermute x2, waiting for transfers between devices, gather_groups(): lax.ppermute(rows, 'dp', [(i, (i + 2 * k) % groups) for i in range(groups)])  10.3 us
    ppermute x2, starting transfers between devices, gather_groups(): lax.ppermute(rows, 'dp', [(i, (i + 2 * k) % groups) for i in range(groups)])  2.09 us
    dot_general x1, matrix products, local(): lax.dot_general(h_cut, s_all, (((0,), (0,)), ((), ())), preferred_element...  1.74 us
    dot_general x1, matrix products, local(): lax.dot_general(x_cut, d_pre, (((0,), (0,)), ((), ())), preferred_element...  1.72 us
  transfers between devices with their start and end apart: 9, of which 4 were waited for; matrix products, arithmetic and copies ran while one was open for 22% of the time, Pallas kernels for 0%

profile of v1, /device:TPU:0, one launch (start us, length us, event | category | flops | bytes accessed | tf_op | source)
XLA Modules:
  0.0 76.7 jit_solution(5336712348700965546)
XLA Ops:
  0.6 0.0 copy-start
  0.6 0.8 slice_bitcast_fusion.3
  1.4 0.1 pad_add_fusion
  1.5 0.1 fusion.81
  1.6 0.2 reduce_window_sum.11
  1.7 0.2 select_reduce_fusion
  1.9 0.1 compare_select_fusion
  2.0 0.0 copy-done
  2.0 1.0 %convolution_convert_fusion.2 = bf16[128,1024]{1,0:T(8,128)(2,1)} fusion(bf16[64,1024]{1,0:T(8,128)(2,1)S(1)} %copy-done, bf16[128,128]{1,0:T(8,128)(2,1)S(1)} %fusion.82), kind=kOutput, calls=%fused_computation.47 | convolution fusion | flops 16916480 | bytes 458752 | tf_op jit(solution)/shard_map/dot_general | solution.py:44
  3.0 7.3 %all-to-all-start.1 = ((bf16[8,16,1024]{2,1,0:T(8,128)(2,1)}), bf16[8,16,1024]{2,1,0:T(8,128)(2,1)S(1)}, u32[]{:S(2)}, u32[]{:S(2)}) async-start(bf16[8,16,1024]{2,1,0:T(8,128)(2,1)} %bitcast.7), calls=%async_computation.1 | async-start | bytes 524288 | tf_op jit(solution)/shard_map/all_to_all | solution.py:57
  10.3 0.7 bitcast_convert_fusion.1
  11.0 1.0 %fusion.71 = (bf16[64,1024]{1,0:T(8,128)(2,1)S(1)}, bf16[64,1024]{1,0:T(8,128)(2,1)S(1)}) fusion(bf16[64,1024]{1,0:T(8,128)(2,1)} %param.7, f32[64]{0:T(128)S(1)} %get-tuple-element.13, f32[64]{0:T(128)S(1)} %get-tuple-element.14), kind=kLoop, calls=%fused_computation.102 | loop fusion | flops 327680 | bytes 393728 | tf_op jit(solution)/shard_map/convert_element_type | solution.py:47
  12.0 0.9 %convolution_convert_fusion.3 = bf16[128,1024]{1,0:T(8,128)(2,1)} fusion(bf16[64,1024]{1,0:T(8,128)(2,1)S(1)} %get-tuple-element.8, bf16[64,1024]{1,0:T(8,128)(2,1)S(1)} %get-tuple-element.7, s32[128]{0:T(128)S(1)} %compare_select_fusion), kind=kOutput, calls=%fused_computation.48 | convolution fusion | flops 34226176 | bytes 524800 | tf_op jit(solution)/shard_map/dot_general | solution.py:54
  12.9 6.2 %all-to-all-done.1 = bf16[8,16,1024]{2,1,0:T(8,128)(2,1)S(1)} async-done(((bf16[8,16,1024]{2,1,0:T(8,128)(2,1)}), bf16[8,16,1024]{2,1,0:T(8,128)(2,1)S(1)}, u32[]{:S(2)}, u32[]{:S(2)}) %all-to-all-start.1) | async-done | bytes 262176 | tf_op jit(solution)/shard_map/all_to_all | solution.py:57
  19.2 3.6 %all-to-all-start = ((bf16[8,16,1024]{2,1,0:T(8,128)(2,1)}), bf16[8,16,1024]{2,1,0:T(8,128)(2,1)S(1)}, u32[]{:S(2)}, u32[]{:S(2)}) async-start(bf16[8,16,1024]{2,1,0:T(8,128)(2,1)} %bitcast.4), calls=%async_computation | async-start | bytes 524288 | tf_op jit(solution)/shard_map/all_to_all | solution.py:57
  22.8 2.9 %fusion.4 = f32[128,2048]{1,0:T(8,128)S(1)} fusion(bf16[128,1024]{1,0:T(8,128)(2,1)S(1)} %bitcast.54, bf16[1,1024,2048]{2,1,0:T(8,128)(2,1)} %param.10), kind=kOutput, calls=%fused_computation.6 | convolution fusion | flops 536870912 | bytes 5505024 | tf_op jit(solution)/shard_map/dot_general | solution.py:69
  25.7 5.7 %all-to-all-done = bf16[8,16,1024]{2,1,0:T(8,128)(2,1)S(1)} async-done(((bf16[8,16,1024]{2,1,0:T(8,128)(2,1)}), bf16[8,16,1024]{2,1,0:T(8,128)(2,1)S(1)}, u32[]{:S(2)}, u32[]{:S(2)}) %all-to-all-start) | async-done | bytes 262176 | tf_op jit(solution)/shard_map/all_to_all | solution.py:57
  31.3 0.0 copy-start.1
  31.3 7.0 %multiply_reduce_fusion = (bf16[128]{0:T(256)(128)(2,1)S(1)}, bf16[128,2048]{1,0:T(8,128)(2,1)}, bf16[128,2048]{1,0:T(8,128)(2,1)S(1)}) fusion(f32[128,2048]{1,0:T(8,128)S(1)} %fusion.4, bf16[128,1024]{1,0:T(8,128)(2,1)S(1)} %bitcast.59, bf16[1,2048,1024]{2,1,0:T(8,128)(2,1)} %param.11), kind=kOutput, calls=%fused_computation.72 | convolution fusion | flops 557318016 | bytes 6553856 | tf_op jit(solution)/shard_map/dot_general | solution.py:71
  38.3 0.0 copy-done.1
  38.3 0.0 copy-start.2
  38.3 1.5 %fusion.33 = bf16[8,16,1024]{2,1,0:T(8,128)(2,1)S(1)} fusion(bf16[8,16,2048]{2,1,0:T(8,128)(2,1)S(1)} %bitcast.58, bf16[1,1024,2048]{2,1,0:T(8,128)(2,1)S(1)} %copy-done.1), kind=kOutput, calls=%fused_computation.49 | convolution fusion | flops 537001984 | bytes 4980736 | tf_op jit(solution)/shard_map/dot_general | solution.py:79
  39.9 0.1 reshape.70
  40.0 0.1 broadcast_in_dim.24
  40.1 0.7 pad_maximum_fusion
  40.8 3.6 %all-to-all-start.2 = ((bf16[8,16,1152]{2,1,0:T(8,128)(2,1)}), bf16[8,16,1152]{2,1,0:T(8,128)(2,1)S(1)}, u32[]{:S(2)}, u32[]{:S(2)}) async-start(bf16[8,16,1152]{2,1,0:T(8,128)(2,1)} %pad_maximum_fusion), calls=%async_computation.2 | async-start | bytes 589824 | tf_op jit(solution)/shard_map/all_to_all | solution.py:57
  44.4 1.6 %collective-permute-start.1 = (bf16[128,1024]{1,0:T(8,128)(2,1)S(1)}, bf16[128,1024]{1,0:T(8,128)(2,1)S(1)}, u32[]{:S(2)}, u32[]{:S(2)}) collective-permute-start(bf16[128,1024]{1,0:T(8,128)(2,1)S(1)} %bitcast.55), channel_id=1, source_target_pairs={{0,16},{8,24},{16,0},{24,8},{1,17},{9,25},{17,1},{25,9},{2,18},{10... | collective-permute-start | bytes 786440 | tf_op jit(solution)/shard_map/ppermute | solution.py:18
  46.0 0.5 collective-permute-start.4
  46.5 0.0 collective-permute-start
  46.5 0.5 collective-permute-start.3
  47.0 6.7 %collective-permute-done.1 = bf16[128,1024]{1,0:T(8,128)(2,1)S(1)} collective-permute-done((bf16[128,1024]{1,0:T(8,128)(2,1)S(1)}, bf16[128,1024]{1,0:T(8,128)(2,1)S(1)}, u32[]{:S(2)}, u32[]{:S(2)}) %collective-permute-start.1) | collective-permute-done | bytes 262176 | tf_op jit(solution)/shard_map/ppermute | solution.py:18
  53.7 0.0 collective-permute-start.2
  53.7 3.6 %collective-permute-done.4 = bf16[128,1024]{1,0:T(8,128)(2,1)S(1)} collective-permute-done((bf16[128,1024]{1,0:T(8,128)(2,1)S(1)}, bf16[128,1024]{1,0:T(8,128)(2,1)S(1)}, u32[]{:S(2)}, u32[]{:S(2)}) %collective-permute-start.4) | collective-permute-done | bytes 262176 | tf_op jit(solution)/shard_map/ppermute | solution.py:18
  57.3 0.0 collective-permute-start.5
  57.3 0.0 all-to-all-done.2
  57.3 0.2 convolution_bitcast_fusion
  57.5 0.1 slice_bitcast_fusion.1
  57.6 0.0 copy-done.2
  57.6 0.5 fusion.88
  58.1 0.9 %convolution_convert_fusion.4 = bf16[64,1024]{1,0:T(8,128)(2,1)} fusion(bf16[128,1152]{1,0:T(8,128)(2,1)S(1)} %bitcast.53, bf16[128,128]{1,0:T(8,128)(2,1)S(1)} %fusion.82), kind=kOutput, calls=%fused_computation.50 | convolution fusion | flops 16850944 | bytes 458752 | tf_op jit(solution)/shard_map/dot_general | solution.py:102
  59.0 0.0 copy-start.3
  59.0 0.0 collective-permute-done
  59.0 0.0 collective-permute-done.2
  59.0 9.9 %fusion.18 = (bf16[384,2048]{1,0:T(8,128)(2,1)S(1)}, f32[384,2048]{1,0:T(8,128)S(1)}) fusion(bf16[1,1024,2048]{2,1,0:T(8,128)(2,1)} %param.10, bf16[128,1024]{1,0:T(8,128)(2,1)S(1)} %collective-permute-done.2, bf16[128,1024]{1,0:T(8,128)(2,1)S(1)} %collective-permute-done.1, bf16[128,1024]{1,0:T(8,128)(2,1)S(1)} %collective-permute-done), kind=kOutput, calls=%fused_computation.20 | convolution fusion | flops 1664090112 | bytes 9699328 | tf_op jit(solution)/shard_map/dot_general | solution.py:69
  69.0 0.0 collective-permute-done.3
  69.0 0.0 collective-permute-done.5
  69.0 0.0 copy-done.3
  69.0 4.2 %fusion.15 = bf16[384,2048]{1,0:T(8,128)(2,1)S(1)} fusion(f32[384,2048]{1,0:T(8,128)S(1)} %get-tuple-element.16, bf16[1,2048,1024]{2,1,0:T(8,128)(2,1)S(1)} %copy-done.3, bf16[128,1024]{1,0:T(8,128)(2,1)S(1)} %collective-permute-done.5, bf16[128,1024]{1,0:T(8,128)(2,1)S(1)} %collective-permute-done.4, bf16[128,1024]{1,0:T(8,128)(2,1)S(1)} %collective-permute-done.3), kind=kOutput, calls=%fused_computation.17 | convolution fusion | flops 1620836352 | bytes 9699328 | tf_op jit(solution)/shard_map/dot_general | solution.py:71
  73.2 0.0 copy-start.4
  73.2 1.7 %fusion.28 = bf16[1,256,2048]{2,1,0:T(8,128)(2,1)} fusion(bf16[384,2048]{1,0:T(8,128)(2,1)S(1)} %fusion.15, bf16[128,2048]{1,0:T(8,128)(2,1)S(1)} %get-tuple-element.6, s32[]{:T(128)S(6)} %select_n.15, bf16[128,1024]{1,0:T(8,128)(2,1)S(1)} %bitcast.57, bf16[128,1024]{1,0:T(8,128)(2,1)S(1)} %collective-permute-done, ...), kind=kOutput, calls=%fused_computation.37 | convolution fusion | flops 542638080 | bytes 4194308 | tf_op jit(solution)/shard_map/dot_general | solution.py:96
  74.9 0.0 copy-done.4
  74.9 1.7 %fusion.32 = bf16[1,512,1024]{2,1,0:T(8,128)(2,1)} fusion(bf16[128,1024]{1,0:T(8,128)(2,1)S(1)} %collective-permute-done.5, bf16[128,1024]{1,0:T(8,128)(2,1)S(1)} %collective-permute-done.4, bf16[128,1024]{1,0:T(8,128)(2,1)S(1)} %collective-permute-done.3, bf16[128,1024]{1,0:T(8,128)(2,1)S(1)} %bitcast.62, s32[]{:T(128)S(6)} %select_n.16, ...), kind=kOutput, calls=%fused_computation.46 | convolution fusion | flops 542638080 | bytes 4194308 | tf_op jit(solution)/shard_map/dot_general | solution.py:99
  (1 shorter events, 0.0 us)
Async XLA Ops:
  0.6 1.4 %copy-start = (bf16[64,1024]{1,0:T(8,128)(2,1)S(1)}, bf16[64,1024]{1,0:T(8,128)(2,1)}, u32[]{:S(2)}) copy-start(bf16[64,1024]{1,0:T(8,128)(2,1)} %param.6) | copy-start | bytes 393220
  3.0 16.2 %all-to-all-start.1 = ((bf16[8,16,1024]{2,1,0:T(8,128)(2,1)}), bf16[8,16,1024]{2,1,0:T(8,128)(2,1)S(1)}, u32[]{:S(2)}, u32[]{:S(2)}) async-start(bf16[8,16,1024]{2,1,0:T(8,128)(2,1)} %bitcast.7), calls=%async_computation.1 | async-start | bytes 524288 | tf_op jit(solution)/shard_map/all_to_all | solution.py:57
  19.2 12.2 %all-to-all-start = ((bf16[8,16,1024]{2,1,0:T(8,128)(2,1)}), bf16[8,16,1024]{2,1,0:T(8,128)(2,1)S(1)}, u32[]{:S(2)}, u32[]{:S(2)}) async-start(bf16[8,16,1024]{2,1,0:T(8,128)(2,1)} %bitcast.4), calls=%async_computation | async-start | bytes 524288 | tf_op jit(solution)/shard_map/all_to_all | solution.py:57
  31.3 7.0 %copy-start.1 = (bf16[1,1024,2048]{2,1,0:T(8,128)(2,1)S(1)}, bf16[1,1024,2048]{2,1,0:T(8,128)(2,1)}, u32[]{:S(2)}) copy-start(bf16[1,1024,2048]{2,1,0:T(8,128)(2,1)} %param.10) | copy-start | bytes 12582916
  38.3 19.2 %copy-start.2 = (bf16[64,2]{0,1:T(2,128)(2,1)S(1)}, bf16[64,2]{0,1:T(2,128)(2,1)}, u32[]{:S(2)}) copy-start(bf16[64,2]{0,1:T(2,128)(2,1)} %param.9) | copy-start | bytes 772
  40.8 16.5 %all-to-all-start.2 = ((bf16[8,16,1152]{2,1,0:T(8,128)(2,1)}), bf16[8,16,1152]{2,1,0:T(8,128)(2,1)S(1)}, u32[]{:S(2)}, u32[]{:S(2)}) async-start(bf16[8,16,1152]{2,1,0:T(8,128)(2,1)} %pad_maximum_fusion), calls=%async_computation.2 | async-start | bytes 589824 | tf_op jit(solution)/shard_map/all_to_all | solution.py:57
  44.4 9.3 %collective-permute-start.1 = (bf16[128,1024]{1,0:T(8,128)(2,1)S(1)}, bf16[128,1024]{1,0:T(8,128)(2,1)S(1)}, u32[]{:S(2)}, u32[]{:S(2)}) collective-permute-start(bf16[128,1024]{1,0:T(8,128)(2,1)S(1)} %bitcast.55), channel_id=1, source_target_pairs={{0,16},{8,24},{16,0},{24,8},{1,17},{9,25},{17,1},{25,9},{2,18},{10... | collective-permute-start | bytes 786440 | tf_op jit(solution)/shard_map/ppermute | solution.py:18
  46.0 11.3 %collective-permute-start.4 = (bf16[128,1024]{1,0:T(8,128)(2,1)S(1)}, bf16[128,1024]{1,0:T(8,128)(2,1)S(1)}, u32[]{:S(2)}, u32[]{:S(2)}) collective-permute-start(bf16[128,1024]{1,0:T(8,128)(2,1)S(1)} %bitcast.60), channel_id=1, source_target_pairs={{0,16},{8,24},{16,0},{24,8},{1,17},{9,25},{17,1},{25,9},{2,18},{10... | collective-permute-start | bytes 786440 | tf_op jit(solution)/shard_map/ppermute | solution.py:18
  46.5 12.5 %collective-permute-start = (bf16[128,1024]{1,0:T(8,128)(2,1)S(1)}, bf16[128,1024]{1,0:T(8,128)(2,1)S(1)}, u32[]{:S(2)}, u32[]{:S(2)}) collective-permute-start(bf16[128,1024]{1,0:T(8,128)(2,1)S(1)} %bitcast.56), channel_id=1, source_target_pairs={{0,8},{8,0},{16,24},{24,16},{1,9},{9,1},{17,25},{25,17},{2,10},{10... | collective-permute-start | bytes 786440 | tf_op jit(solution)/shard_map/ppermute | solution.py:16
  46.5 22.5 %collective-permute-start.3 = (bf16[128,1024]{1,0:T(8,128)(2,1)S(1)}, bf16[128,1024]{1,0:T(8,128)(2,1)S(1)}, u32[]{:S(2)}, u32[]{:S(2)}) collective-permute-start(bf16[128,1024]{1,0:T(8,128)(2,1)S(1)} %bitcast.61), channel_id=1, source_target_pairs={{0,8},{8,0},{16,24},{24,16},{1,9},{9,1},{17,25},{25,17},{2,10},{10... | collective-permute-start | bytes 786440 | tf_op jit(solution)/shard_map/ppermute | solution.py:16
  53.7 5.3 %collective-permute-start.2 = (bf16[128,1024]{1,0:T(8,128)(2,1)S(1)}, bf16[128,1024]{1,0:T(8,128)(2,1)S(1)}, u32[]{:S(2)}, u32[]{:S(2)}) collective-permute-start(bf16[128,1024]{1,0:T(8,128)(2,1)S(1)} %collective-permute-done.1), channel_id=1, source_target_pairs={{0,8},{8,0},{16,24},{24,16},{1,9},{9,1},{17,25},{25,17},{2,10},{10... | collective-permute-start | bytes 786440 | tf_op jit(solution)/shard_map/ppermute | solution.py:19
  57.3 11.7 %collective-permute-start.5 = (bf16[128,1024]{1,0:T(8,128)(2,1)S(1)}, bf16[128,1024]{1,0:T(8,128)(2,1)S(1)}, u32[]{:S(2)}, u32[]{:S(2)}) collective-permute-start(bf16[128,1024]{1,0:T(8,128)(2,1)S(1)} %collective-permute-done.4), channel_id=1, source_target_pairs={{0,8},{8,0},{16,24},{24,16},{1,9},{9,1},{17,25},{25,17},{2,10},{10... | collective-permute-start | bytes 786440 | tf_op jit(solution)/shard_map/ppermute | solution.py:19
  59.0 10.0 %copy-start.3 = (bf16[1,2048,1024]{2,1,0:T(8,128)(2,1)S(1)}, bf16[1,2048,1024]{2,1,0:T(8,128)(2,1)}, u32[]{:S(2)}) copy-start(bf16[1,2048,1024]{2,1,0:T(8,128)(2,1)} %param.11) | copy-start | bytes 12582916
  73.2 1.7 %copy-start.4 = (bf16[128,2048]{1,0:T(8,128)(2,1)S(1)}, bf16[128,2048]{1,0:T(8,128)(2,1)}, u32[]{:S(2)}) copy-start(bf16[128,2048]{1,0:T(8,128)(2,1)} %get-tuple-element.5) | copy-start | bytes 1572868

commit v2 on v1

v2 whole, which is shorter than its diff:
```python
import functools

import jax
import jax.numpy as jnp
from jax import lax
from jax.experimental import pallas as pl
from jax.experimental.pallas import tpu as pltpu
from jax.sharding import PartitionSpec as P

BF16 = jnp.bfloat16
F32 = jnp.float32
LANES = 128
MIB = 1 << 20


def dot(a, b, over=(1, 0)):
    return lax.dot_general(
        a, b, (((over[0],), (over[1],)), ((), ())), preferred_element_type=F32
    )


def gelu_and_slope(pre_act):
    cdf = 0.5 * (1.0 + lax.erf(pre_act * 0.7071067811865476))
    pdf = jnp.exp(-0.5 * pre_act * pre_act) * 0.3989422804014327
    return (pre_act * cdf).astype(BF16), cdf + pre_act * pdf


def call(kernel, out_shape, args, flops=0, limit=24, scratch=()):
    moved = sum(a.size * a.dtype.itemsize for a in args)
    return pl.pallas_call(
        kernel,
        out_shape=out_shape,
        in_specs=[pl.BlockSpec(memory_space=pltpu.VMEM)] * len(args),
        out_specs=jax.tree.map(lambda _: pl.BlockSpec(memory_space=pltpu.VMEM), out_shape),
        scratch_shapes=list(scratch),
        compiler_params=pltpu.CompilerParams(vmem_limit_bytes=limit * MIB),
        cost_estimate=pl.CostEstimate(flops=flops, bytes_accessed=moved, transcendentals=0),
    )(*args)


def shape(dims, dtype=BF16):
    return jax.ShapeDtypeStruct(dims, dtype)


def route_kernel(experts, capacity, routes, gates, tokens, cotangent, *outs):
    blocks_x, blocks_s = outs[:experts], outs[experts : 2 * experts]
    place_refs = outs[2 * experts :]
    tok_count = tokens.shape[0]
    slots_all = experts * capacity
    me = lax.axis_index("expert")
    rows = max(experts, 16)
    before = (
        lax.broadcasted_iota(jnp.int32, (tok_count, tok_count), 0)
        < lax.broadcasted_iota(jnp.int32, (tok_count, tok_count), 1)
    ).astype(F32).astype(BF16)
    expert_id = lax.broadcasted_iota(jnp.int32, (rows, tok_count), 0)
    slot_id = lax.broadcasted_iota(jnp.int32, (slots_all, tok_count), 0)
    taken = jnp.zeros((rows, 1), F32)
    places, gated = [], jnp.zeros((slots_all, tok_count), F32)
    for choice in range(2):
        chosen = routes[choice : choice + 1, :]
        one_hot = (expert_id == chosen).astype(F32)
        earlier = dot(one_hot.astype(BF16), before) + taken
        taken = taken + jnp.sum(one_hot, axis=1, keepdims=True)
        slot_pos = jnp.sum(earlier * one_hot, axis=0, keepdims=True).astype(jnp.int32)
        target = jnp.where(
            slot_pos < capacity, jnp.bitwise_xor(chosen, me) * capacity + slot_pos, slots_all
        )
        place = (slot_id == target).astype(F32)
        place_refs[choice][...] = place.astype(BF16)
        places.append(place)
        gated = gated + place * gates[choice : choice + 1, :].astype(F32)
    x = dot((places[0] + places[1]).astype(BF16), tokens[...]).astype(BF16)
    s = dot(gated.astype(BF16), cotangent[...]).astype(BF16)
    for k in range(experts):
        blocks_x[k][...] = x[k * capacity : (k + 1) * capacity]
        blocks_s[k][...] = s[k * capacity : (k + 1) * capacity]


def combine_kernel(experts, capacity, place0, place1, gates, *refs):
    blocks, (token_grads, gate_grads, rows) = refs[:experts], refs[experts:]
    tok_count, feat_width = token_grads.shape
    for k in range(experts):
        rows[k * capacity : (k + 1) * capacity, :] = blocks[k][...]
    either = (place0[...].astype(F32) + place1[...].astype(F32)).astype(BF16)
    token_grads[...] = dot(either, rows[:, :feat_width], (0, 0)).astype(BF16)
    dgate = rows[:, feat_width : feat_width + tok_count].astype(F32)
    for choice, place in ((0, place0), (1, place1)):
        row = jnp.sum(place[...].astype(F32) * dgate, axis=0, keepdims=True)
        gate_grads[choice : choice + 1, :] = row / gates[choice : choice + 1, :].astype(F32)


def up_kernel(tile, *refs):
    *x_refs, weight_in, hidden, slope = refs
    for at in range(0, weight_in.shape[1], tile):
        cols = slice(at, at + tile)
        weight = weight_in[:, cols]
        for g, x in enumerate(x_refs):
            rows = slice(g * x.shape[0], (g + 1) * x.shape[0])
            hidden[rows, cols], slope[rows, cols] = gelu_and_slope(dot(x[...], weight))


def own_kernel(tile, experts, s, hidden, slope, weight_in, weight_out, d_pre, *blocks):
    slots_all, feat_width = s.shape
    capacity = slots_all // experts
    dgate = jnp.zeros((slots_all, LANES), F32)
    dx = jnp.zeros((slots_all, feat_width), F32)
    for at in range(0, weight_in.shape[1], tile):
        cols = slice(at, at + tile)
        d_hidden = dot(s[...], weight_out[cols, :], (1, 1))
        part = (d_hidden * slope[:, cols]).astype(BF16)
        d_pre[:, cols] = part
        product = d_hidden * hidden[:, cols].astype(F32)
        for lane in range(0, tile, LANES):
            dgate = dgate + product[:, lane : lane + LANES]
        dx = dx + dot(part, weight_in[:, cols], (1, 1))
    dgate = jnp.broadcast_to(jnp.sum(dgate, axis=1, keepdims=True), (slots_all, LANES))
    for k in range(experts):
        rows = slice(k * capacity, (k + 1) * capacity)
        blocks[k][:, :feat_width] = dx[rows].astype(BF16)
        blocks[k][:, feat_width:] = dgate[rows].astype(BF16)


def grads_kernel(tile, groups, *refs):
    x_refs, s_refs, refs = refs[:groups], refs[groups : 2 * groups], refs[2 * groups :]
    hidden0, d_pre0, hidden1, slope1, weight_out, grad_in, grad_out = refs[:7]
    x_cut, s_all, d_pre = refs[7:]
    me = lax.axis_index("dp")
    slots_all = s_refs[0].shape[0]
    cut = x_cut.shape[1]
    ffw = weight_out.shape[0]
    for g in range(groups):
        rows = slice(g * slots_all, (g + 1) * slots_all)
        x_cut[rows, :] = x_refs[g][:, pl.ds(pl.multiple_of(me * cut, cut), cut)]
        s_all[rows, :] = s_refs[g][...]
    d_pre[:slots_all, :] = d_pre0[...]
    for at in range(0, ffw, tile):
        cols = slice(at, at + tile)
        d_hidden = dot(s_all[slots_all:, :], weight_out[cols, :], (1, 1))
        d_pre[slots_all:, cols] = (d_hidden * slope1[:, cols]).astype(BF16)
        grad_in[:, cols] = dot(x_cut[...], d_pre[:, cols], (0, 0)).astype(BF16)
    mine = pl.ds(pl.multiple_of(me * (ffw // groups), ffw // groups), ffw // groups)
    h_cut = jnp.concatenate([hidden0[:, mine], hidden1[:, mine]], axis=0)
    grad_out[...] = dot(h_cut, s_all[...], (0, 0)).astype(BF16)


def exchange(blocks):
    experts = len(blocks)
    return [blocks[0]] + [
        lax.ppermute(blocks[k], "expert", [(i, i ^ k) for i in range(experts)])
        for k in range(1, experts)
    ]


def gather_groups(rows):
    groups = lax.axis_size("dp")
    swap = [(i, i ^ 1) for i in range(groups)]
    others = [lax.ppermute(rows, "dp", swap)]
    for k in range(1, groups // 2):
        other = lax.ppermute(rows, "dp", [(i, (i + 2 * k) % groups) for i in range(groups)])
        others += [other, lax.ppermute(other, "dp", swap)]
    return others


def local(tokens, cotangent, routes, gates, proj_in, proj_out):
    tok_count, feat_width = tokens.shape
    experts = lax.axis_size("expert")
    groups = lax.axis_size("dp")
    capacity = 2 * tok_count // experts
    slots_all = experts * capacity
    weight_in = pltpu.with_memory_space_constraint(proj_in[0], pltpu.VMEM)
    weight_out = pltpu.with_memory_space_constraint(proj_out[0], pltpu.VMEM)
    ffw = weight_in.shape[1]
    tile = ffw // groups
    product = 2 * slots_all * feat_width * ffw
    block = shape((capacity, feat_width))
    place = shape((slots_all, tok_count))

    routed = call(
        functools.partial(route_kernel, experts, capacity),
        [block] * (2 * experts) + [place] * 2,
        [routes.T, gates.T, tokens, cotangent],
    )
    places = routed[2 * experts :]
    got_x = exchange(routed[:experts])
    got_s = exchange(routed[experts : 2 * experts])
    x = jnp.concatenate(got_x, axis=0)
    x_others = gather_groups(x)
    s = jnp.concatenate(got_s, axis=0)
    s_others = gather_groups(s)
    hidden0, slope0 = call(
        functools.partial(up_kernel, tile),
        [shape((slots_all, ffw)), shape((slots_all, ffw), F32)],
        [x, weight_in],
        product,
    )
    d_pre0, *back = call(
        functools.partial(own_kernel, tile, experts),
        [shape((slots_all, ffw))] + [shape((capacity, feat_width + LANES))] * experts,
        [s, hidden0, slope0, weight_in, weight_out],
        2 * product,
    )
    back = exchange(back)
    others = groups - 1
    hidden1, slope1 = call(
        functools.partial(up_kernel, tile),
        [shape((others * slots_all, ffw)), shape((others * slots_all, ffw), F32)],
        [*x_others, weight_in],
        others * product,
    )
    grad_in, grad_out = call(
        functools.partial(grads_kernel, tile, groups),
        [shape((feat_width // groups, ffw)), shape((ffw // groups, feat_width))],
        [x, *x_others, s, *s_others, hidden0, d_pre0, hidden1, slope1, weight_out],
        (others + 2) * product,
        scratch=[
            pltpu.VMEM((groups * slots_all, feat_width // groups), BF16),
            pltpu.VMEM((groups * slots_all, feat_width), BF16),
            pltpu.VMEM((groups * slots_all, ffw), BF16),
        ],
    )
    token_grads, gate_grads = call(
        functools.partial(combine_kernel, experts, capacity),
        [shape((tok_count, feat_width)), shape((2, tok_count), F32)],
        [*places, gates.T, *back],
        scratch=[pltpu.VMEM((slots_all, feat_width + LANES), BF16)],
    )
    return (token_grads, gate_grads.T.astype(BF16), grad_in[None], grad_out[None])


def local_small_blocks(tokens, cotangent, routes, gates, proj_in, proj_out):
    tok_count, feat_width = tokens.shape
    experts = lax.axis_size("expert")
    groups = lax.axis_size("dp")
    me = lax.axis_index("dp")
    capacity = 2 * tok_count // experts
    slots_all = experts * capacity
    weight_in, weight_out = proj_in[0], proj_out[0]
    ffw = weight_in.shape[1]
    chosen = jnp.concatenate([routes[:, 0], routes[:, 1]])
    one_hot = (chosen[:, None] == jnp.arange(experts, dtype=jnp.int32)[None, :]).astype(jnp.int32)
    slot_pos = jnp.sum((jnp.cumsum(one_hot, axis=0) - one_hot) * one_hot, axis=1)
    target = jnp.where(slot_pos < capacity, chosen * capacity + slot_pos, slots_all)
    placing = (jnp.arange(slots_all, dtype=jnp.int32)[:, None] == target[None, :]).astype(BF16)
    either = placing[:, :tok_count] + placing[:, tok_count:]
    scaled = [
        (gates[:, k : k + 1].astype(F32) * cotangent.astype(F32)).astype(BF16) for k in range(2)
    ]

    def swap_blocks(rows):
        return lax.all_to_all(
            rows.astype(BF16).reshape(experts, capacity, rows.shape[1]), "expert", 0, 0, tiled=True
        ).reshape(slots_all, rows.shape[1])

    x = swap_blocks(dot(either, tokens))
    s = swap_blocks(dot(placing, jnp.concatenate(scaled, axis=0)))
    hidden0, slope0 = gelu_and_slope(dot(x, weight_in))
    d_hidden0 = dot(s, weight_out, (1, 1))
    d_pre0 = (d_hidden0 * slope0).astype(BF16)
    dgate = jnp.sum(hidden0.astype(F32) * d_hidden0, axis=1, keepdims=True)
    dx = dot(d_pre0, weight_in, (1, 1))
    back = swap_blocks(
        jnp.concatenate([dx, jnp.broadcast_to(dgate, (slots_all, LANES))], axis=1)
    )
    x_all = jnp.concatenate([x, *gather_groups(x)], axis=0)
    s_all = jnp.concatenate([s, *gather_groups(s)], axis=0)
    hidden1, slope1 = gelu_and_slope(dot(x_all[slots_all:], weight_in))
    d_pre1 = (dot(s_all[slots_all:], weight_out, (1, 1)) * slope1).astype(BF16)
    hidden = jnp.concatenate([hidden0, hidden1], axis=0)
    d_pre = jnp.concatenate([d_pre0, d_pre1], axis=0)
    x_cut = lax.dynamic_slice_in_dim(x_all, me * (feat_width // groups), feat_width // groups, 1)
    h_cut = lax.dynamic_slice_in_dim(hidden, me * (ffw // groups), ffw // groups, 1)
    grad_in = dot(x_cut, d_pre, (0, 0)).astype(BF16)
    grad_out = dot(h_cut, s_all, (0, 0)).astype(BF16)
    token_grads = dot(either, back[:, :feat_width], (0, 0)).astype(BF16)
    taken = dot(placing, back[:, feat_width : feat_width + 1], (0, 0))
    gate_grads = jnp.concatenate([taken[:tok_count], taken[tok_count:]], axis=1)
    gate_grads = (gate_grads / gates.astype(F32)).astype(BF16)
    return (token_grads, gate_grads, grad_in[None], grad_out[None])


def solution(mesh):
    rows = P(("dp", "expert"), None)
    weights = P("expert", None, None)

    def whole(tokens, *others):
        experts = mesh.shape["expert"]
        capacity = 2 * tokens.shape[0] // (mesh.shape["dp"] * experts) // experts
        tiles = capacity % 16 == 0 and experts & (experts - 1) == 0
        return jax.shard_map(
            local if tiles else local_small_blocks,
            mesh=mesh,
            in_specs=(rows, rows, rows, rows, weights, weights),
            out_specs=(rows, rows, P("expert", "dp", None), P("expert", "dp", None)),
            check_vma=False,
        )(tokens, *others)

    return whole
```

time: 77.2 us -> 95.3 us (1.23)
  matrix products: 32 us -> 0 us
  waiting for transfers between devices: 22.2 us -> 45.5 us
  Pallas kernels: 0 us -> 12.3 us
  starting transfers between devices: 17.1 us -> 28 us
  local copies, waits for them, and re-layouts: 1.03 us -> 7.98 us
  other arithmetic: 3.62 us -> 0.51 us
    ppermute x4 -> x25, waiting for transfers between devices: 0.01 us -> 45.4 us  [the longest x21 45.4 us: exchange(): lax.ppermute(blocks[k], 'expert', [(i, i ^ k) for i in range(experts)])]
    dot_general x11 -> x0, matrix products: 32 us -> none  [the longest x2 12.8 us: forward(): pre_act = jnp.dot(x, weight_in, preferred_element_type=jnp.float32)]
    ppermute x4 -> x25, starting transfers between devices: 0.52 us -> 25 us  [the longest x21 24.5 us: exchange(): lax.ppermute(blocks[k], 'expert', [(i, i ^ k) for i in range(experts)])]
    all_to_all x3 -> x0, starting transfers between devices: 14.4 us -> none  [exchange(): lax.all_to_all(rows.reshape(experts, capacity, rows.shape[1]), 'expert',...]
    pallas_call x0 -> x6, Pallas kernels: none -> 12.3 us  [call(): pl.pallas_call(kernel, out_shape=out_shape, in_specs=[pl.BlockSpec(memory...]
    all_to_all x3 -> x0, waiting for transfers between devices: 11.9 us -> none  [exchange(): lax.all_to_all(rows.reshape(experts, capacity, rows.shape[1]), 'expert',...]
    ppermute x2, waiting for transfers between devices: 10.3 us -> 0.01 us  [gather_groups(): lax.ppermute(rows, 'dp', [(i, (i + 2 * k) % groups) for i in range(groups)])]
    unnamed x10 -> x32, local copies, waits for them, and re-layouts: 0.03 us -> 7.97 us
  transfers between devices with their start and end apart: 9 -> 27, of which waited for: 4 -> 14; matrix products, arithmetic and copies ran while one was open for 22% -> 1% of each run, Pallas kernels for 0% -> 8%
where the time goes in v2:
time: 95.3 us; the launch traced here: 95.1 us
  waiting for transfers between devices  45.5 us (48%)
  starting transfers between devices  28 us (29%)
  Pallas kernels  12.3 us (13%)
  local copies, waits for them, and re-layouts  7.98 us (8%)
    ppermute x21, waiting for transfers between devices, exchange(): lax.ppermute(blocks[k], 'expert', [(i, i ^ k) for i in range(experts)])  45.4 us
    ppermute x21, starting transfers between devices, exchange(): lax.ppermute(blocks[k], 'expert', [(i, i ^ k) for i in range(experts)])  24.5 us
    pallas_call x6, Pallas kernels, call(): pl.pallas_call(kernel, out_shape=out_shape, in_specs=[pl.BlockSpec(memory...  12.3 us
    unnamed x32, local copies, waits for them, and re-layouts  7.97 us
    ppermute x2, starting transfers between devices, gather_groups(): lax.ppermute(rows, 'dp', [(i, (i + 2 * k) % groups) for i in range(groups)])  3.04 us
  transfers between devices with their start and end apart: 27, of which 14 were waited for; matrix products, arithmetic and copies ran while one was open for 1% of the time, Pallas kernels for 8%

profile of v2, /device:TPU:0, one launch (start us, length us, event | category | flops | bytes accessed | tf_op | source)
XLA Modules:
  0.0 95.1 jit_solution(14482391933739822051)
XLA Ops:
  0.7 1.0 %copy-done.4 = bf16[64,1024]{1,0:T(8,128)(2,1)S(1)} copy-done((bf16[64,1024]{1,0:T(8,128)(2,1)S(1)}, bf16[64,1024]{1,0:T(8,128)(2,1)}, u32[]{:S(2)}) %copy-start.4) | copy-done | bytes 131096
  1.7 1.2 %copy-done.5 = bf16[64,1024]{1,0:T(8,128)(2,1)S(1)} copy-done((bf16[64,1024]{1,0:T(8,128)(2,1)S(1)}, bf16[64,1024]{1,0:T(8,128)(2,1)}, u32[]{:S(2)}) %copy-start.5) | copy-done | bytes 131096
  2.9 0.7 copy-done.6
  3.5 0.7 copy-done.8
  4.2 0.4 shard_map.93
  4.6 3.0 %collective-permute-start = (bf16[16,1024]{1,0:T(8,128)(2,1)S(1)}, bf16[16,1024]{1,0:T(8,128)(2,1)S(1)}, u32[]{:S(2)}, u32[]{:S(2)}) collective-permute-start(bf16[16,1024]{1,0:T(8,128)(2,1)S(1)} %get-tuple-element.42), channel_id=1, source_target_pairs={{0,1},{1,0},{2,3},{3,2},{4,5},{5,4},{6,7},{7,6},{8,9},{9,8},{10,11... | collective-permute-start | bytes 98312 | tf_op jit(solution)/shard_map/ppermute | solution.py:150
  7.6 1.6 %collective-permute-start.1 = (bf16[16,1024]{1,0:T(8,128)(2,1)S(1)}, bf16[16,1024]{1,0:T(8,128)(2,1)S(1)}, u32[]{:S(2)}, u32[]{:S(2)}) collective-permute-start(bf16[16,1024]{1,0:T(8,128)(2,1)S(1)} %get-tuple-element.43), channel_id=1, source_target_pairs={{0,2},{1,3},{2,0},{3,1},{4,6},{5,7},{6,4},{7,5},{8,10},{9,11},{10,... | collective-permute-start | bytes 98312 | tf_op jit(solution)/shard_map/ppermute | solution.py:150
  9.2 0.0 collective-permute-start.2
  9.2 3.0 %collective-permute-start.3 = (bf16[16,1024]{1,0:T(8,128)(2,1)S(1)}, bf16[16,1024]{1,0:T(8,128)(2,1)S(1)}, u32[]{:S(2)}, u32[]{:S(2)}) collective-permute-start(bf16[16,1024]{1,0:T(8,128)(2,1)S(1)} %get-tuple-element.45), channel_id=1, source_target_pairs={{0,4},{1,5},{2,6},{3,7},{4,0},{5,1},{6,2},{7,3},{8,12},{9,13},{10,... | collective-permute-start | bytes 98312 | tf_op jit(solution)/shard_map/ppermute | solution.py:150
  12.2 1.3 %collective-permute-start.4 = (bf16[16,1024]{1,0:T(8,128)(2,1)S(1)}, bf16[16,1024]{1,0:T(8,128)(2,1)S(1)}, u32[]{:S(2)}, u32[]{:S(2)}) collective-permute-start(bf16[16,1024]{1,0:T(8,128)(2,1)S(1)} %get-tuple-element.46), channel_id=1, source_target_pairs={{0,5},{1,4},{2,7},{3,6},{4,1},{5,0},{6,3},{7,2},{8,13},{9,12},{10,... | collective-permute-start | bytes 98312 | tf_op jit(solution)/shard_map/ppermute | solution.py:150
  13.5 0.0 collective-permute-done
  13.5 3.7 %collective-permute-start.5 = (bf16[16,1024]{1,0:T(8,128)(2,1)S(1)}, bf16[16,1024]{1,0:T(8,128)(2,1)S(1)}, u32[]{:S(2)}, u32[]{:S(2)}) collective-permute-start(bf16[16,1024]{1,0:T(8,128)(2,1)S(1)} %get-tuple-element.47), channel_id=1, source_target_pairs={{0,6},{1,7},{2,4},{3,5},{4,2},{5,3},{6,0},{7,1},{8,14},{9,15},{10,... | collective-permute-start | bytes 98312 | tf_op jit(solution)/shard_map/ppermute | solution.py:150
  17.1 0.0 collective-permute-done.1
  17.1 0.5 collective-permute-start.7
  17.7 3.4 %collective-permute-done.7 = bf16[16,1024]{1,0:T(8,128)(2,1)S(1)} collective-permute-done((bf16[16,1024]{1,0:T(8,128)(2,1)S(1)}, bf16[16,1024]{1,0:T(8,128)(2,1)S(1)}, u32[]{:S(2)}, u32[]{:S(2)}) %collective-permute-start.7) | collective-permute-done | bytes 32800 | tf_op jit(solution)/shard_map/ppermute | solution.py:150
  21.1 0.0 collective-permute-start.8
  21.1 3.9 %collective-permute-done.8 = bf16[16,1024]{1,0:T(8,128)(2,1)S(1)} collective-permute-done((bf16[16,1024]{1,0:T(8,128)(2,1)S(1)}, bf16[16,1024]{1,0:T(8,128)(2,1)S(1)}, u32[]{:S(2)}, u32[]{:S(2)}) %collective-permute-start.8) | collective-permute-done | bytes 32800 | tf_op jit(solution)/shard_map/ppermute | solution.py:150
  25.0 0.2 collective-permute-start.9
  25.2 4.6 %collective-permute-done.9 = bf16[16,1024]{1,0:T(8,128)(2,1)S(1)} collective-permute-done((bf16[16,1024]{1,0:T(8,128)(2,1)S(1)}, bf16[16,1024]{1,0:T(8,128)(2,1)S(1)}, u32[]{:S(2)}, u32[]{:S(2)}) %collective-permute-start.9) | collective-permute-done | bytes 32800 | tf_op jit(solution)/shard_map/ppermute | solution.py:150
  29.8 0.0 collective-permute-start.10
  29.8 4.8 %collective-permute-done.10 = bf16[16,1024]{1,0:T(8,128)(2,1)S(1)} collective-permute-done((bf16[16,1024]{1,0:T(8,128)(2,1)S(1)}, bf16[16,1024]{1,0:T(8,128)(2,1)S(1)}, u32[]{:S(2)}, u32[]{:S(2)}) %collective-permute-start.10) | collective-permute-done | bytes 32800 | tf_op jit(solution)/shard_map/ppermute | solution.py:150
  34.6 0.4 collective-permute-start.11
  35.0 5.3 %collective-permute-done.11 = bf16[16,1024]{1,0:T(8,128)(2,1)S(1)} collective-permute-done((bf16[16,1024]{1,0:T(8,128)(2,1)S(1)}, bf16[16,1024]{1,0:T(8,128)(2,1)S(1)}, u32[]{:S(2)}, u32[]{:S(2)}) %collective-permute-start.11) | collective-permute-done | bytes 32800 | tf_op jit(solution)/shard_map/ppermute | solution.py:150
  40.3 0.2 collective-permute-start.12
  40.6 5.5 %collective-permute-done.12 = bf16[16,1024]{1,0:T(8,128)(2,1)S(1)} collective-permute-done((bf16[16,1024]{1,0:T(8,128)(2,1)S(1)}, bf16[16,1024]{1,0:T(8,128)(2,1)S(1)}, u32[]{:S(2)}, u32[]{:S(2)}) %collective-permute-start.12) | collective-permute-done | bytes 32800 | tf_op jit(solution)/shard_map/ppermute | solution.py:150
  46.0 1.0 %collective-permute-start.13 = (bf16[16,1024]{1,0:T(8,128)(2,1)S(1)}, bf16[16,1024]{1,0:T(8,128)(2,1)S(1)}, u32[]{:S(2)}, u32[]{:S(2)}) collective-permute-start(bf16[16,1024]{1,0:T(8,128)(2,1)S(1)} %get-tuple-element.56), channel_id=1, source_target_pairs={{0,7},{1,6},{2,5},{3,4},{4,3},{5,2},{6,1},{7,0},{8,15},{9,14},{10,... | collective-permute-start | bytes 98312 | tf_op jit(solution)/shard_map/ppermute | solution.py:150
  47.1 5.6 %collective-permute-done.13 = bf16[16,1024]{1,0:T(8,128)(2,1)S(1)} collective-permute-done((bf16[16,1024]{1,0:T(8,128)(2,1)S(1)}, bf16[16,1024]{1,0:T(8,128)(2,1)S(1)}, u32[]{:S(2)}, u32[]{:S(2)}) %collective-permute-start.13) | collective-permute-done | bytes 32800 | tf_op jit(solution)/shard_map/ppermute | solution.py:150
  52.6 1.0 %collective-permute-start.6 = (bf16[16,1024]{1,0:T(8,128)(2,1)S(1)}, bf16[16,1024]{1,0:T(8,128)(2,1)S(1)}, u32[]{:S(2)}, u32[]{:S(2)}) collective-permute-start(bf16[16,1024]{1,0:T(8,128)(2,1)S(1)} %get-tuple-element.48), channel_id=1, source_target_pairs={{0,7},{1,6},{2,5},{3,4},{4,3},{5,2},{6,1},{7,0},{8,15},{9,14},{10,... | collective-permute-start | bytes 98312 | tf_op jit(solution)/shard_map/ppermute | solution.py:150
  53.7 0.0 collective-permute-done.2
  53.7 1.5 %collective-permute-start.22 = (bf16[128,1024]{1,0:T(8,128)(2,1)S(1)}, bf16[128,1024]{1,0:T(8,128)(2,1)S(1)}, u32[]{:S(2)}, u32[]{:S(2)}) collective-permute-start(bf16[128,1024]{1,0:T(8,128)(2,1)S(1)} %constant_dynamic-update-slice_fusion.8.refs_0_), channel_id=1, source_target_pairs={{0,16},{8,24},{16,0},{24,8},{1,17},{9,25},{17,1},{25,9},{2,18},{10... | collective-permute-start | bytes 786440 | tf_op jit(solution)/shard_map/ppermute | solution.py:160
  55.2 0.0 collective-permute-done.3
  55.2 0.0 collective-permute-done.4
  55.2 0.0 collective-permute-done.5
  55.3 4.0 %collective-permute-done.6 = bf16[16,1024]{1,0:T(8,128)(2,1)S(1)} collective-permute-done((bf16[16,1024]{1,0:T(8,128)(2,1)S(1)}, bf16[16,1024]{1,0:T(8,128)(2,1)S(1)}, u32[]{:S(2)}, u32[]{:S(2)}) %collective-permute-start.6) | collective-permute-done | bytes 32800 | tf_op jit(solution)/shard_map/ppermute | solution.py:150
  59.3 1.5 %collective-permute-start.25 = (bf16[128,1024]{1,0:T(8,128)(2,1)S(1)}, bf16[128,1024]{1,0:T(8,128)(2,1)S(1)}, u32[]{:S(2)}, u32[]{:S(2)}) collective-permute-start(bf16[128,1024]{1,0:T(8,128)(2,1)S(1)} %constant_dynamic-update-slice_fusion.s.refs_4_), channel_id=1, source_target_pairs={{0,16},{8,24},{16,0},{24,8},{1,17},{9,25},{17,1},{25,9},{2,18},{10... | collective-permute-start | bytes 786440 | tf_op jit(solution)/shard_map/ppermute | solution.py:160
  60.8 2.2 %copy-done.1 = bf16[1,1024,2048]{2,1,0:T(8,128)(2,1)S(1)} copy-done((bf16[1,1024,2048]{2,1,0:T(8,128)(2,1)S(1)}, bf16[1,1024,2048]{2,1,0:T(8,128)(2,1)}, u32[]{:S(2)}) %copy-start.1) | copy-done | bytes 4194328
  63.0 1.0 %shard_map.94 = (bf16[128,2048]{1,0:T(8,128)(2,1)S(1)}, f32[128,2048]{1,0:T(8,128)S(1)}) custom-call(bf16[128,1024]{1,0:T(8,128)(2,1)S(1)} %constant_dynamic-update-slice_fusion.8.refs_0_, bf16[1024,2048]{1,0:T(8,128)(2,1)S(1)} %bitcast.10), custom_call_target="tpu_custom_call" | custom-call | flops 536870912 | bytes 4456448 | tf_op jit(solution)/shard_map/pallas_call | solution.py:30
  64.0 0.0 copy-start.2
  64.0 2.2 %copy-done.2 = bf16[1,1024,2048]{2,1,0:T(8,128)(2,1)S(1)} copy-done((bf16[1,1024,2048]{2,1,0:T(8,128)(2,1)S(1)}, bf16[1,1024,2048]{2,1,0:T(8,128)(2,1)}, u32[]{:S(2)}) %copy-start.2) | copy-done | bytes 4194328
  66.2 3.0 %shard_map.95 = (bf16[128,2048]{1,0:T(8,128)(2,1)S(1)}, bf16[16,1152]{1,0:T(8,128)(2,1)S(1)}, bf16[16,1152]{1,0:T(8,128)(2,1)S(1)}, bf16[16,1152]{1,0:T(8,128)(2...) custom-call(bf16[128,1024]{1,0:T(8,128)(2,1)S(1)} %constant_dynamic-, ...), custom_call_target="tpu_custom_call" | custom-call | flops 1073741824 | bytes 10223616 | tf_op jit(solution)/shard_map/pallas_call | solution.py:30
  69.3 1.0 %collective-permute-start.14 = (bf16[16,1152]{1,0:T(8,128)(2,1)S(1)}, bf16[16,1152]{1,0:T(8,128)(2,1)S(1)}, u32[]{:S(2)}, u32[]{:S(2)}) collective-permute-start(bf16[16,1152]{1,0:T(8,128)(2,1)S(1)} %get-tuple-element.60), channel_id=1, source_target_pairs={{0,1},{1,0},{2,3},{3,2},{4,5},{5,4},{6,7},{7,6},{8,9},{9,8},{10,11... | collective-permute-start | bytes 110600 | tf_op jit(solution)/shard_map/ppermute | solution.py:150
  70.3 0.0 collective-permute-start.15
  70.3 2.5 %collective-permute-start.16 = (bf16[16,1152]{1,0:T(8,128)(2,1)S(1)}, bf16[16,1152]{1,0:T(8,128)(2,1)S(1)}, u32[]{:S(2)}, u32[]{:S(2)}) collective-permute-start(bf16[16,1152]{1,0:T(8,128)(2,1)S(1)} %get-tuple-element.62), channel_id=1, source_target_pairs={{0,3},{1,2},{2,1},{3,0},{4,7},{5,6},{6,5},{7,4},{8,11},{9,10},{10,... | collective-permute-start | bytes 110600 | tf_op jit(solution)/shard_map/ppermute | solution.py:150
  72.8 0.5 collective-permute-done.14.refs_1_
  73.3 0.0 collective-permute-start.17
  73.3 1.0 %collective-permute-done.15.refs_2_ = bf16[16,1152]{1,0:T(8,128)(2,1)S(1)} collective-permute-done((bf16[16,1152]{1,0:T(8,128)(2,1)S(1)}, bf16[16,1152]{1,0:T(8,128)(2,1)S(1)}, u32[]{:S(2)}, u32[]{:S(2)}) %collective-permute-start.15) | collective-permute-done | bytes 36896 | tf_op jit(solution)/shard_map/ppermute | solution.py:150
  74.3 2.4 %collective-permute-start.18 = (bf16[16,1152]{1,0:T(8,128)(2,1)S(1)}, bf16[16,1152]{1,0:T(8,128)(2,1)S(1)}, u32[]{:S(2)}, u32[]{:S(2)}) collective-permute-start(bf16[16,1152]{1,0:T(8,128)(2,1)S(1)} %get-tuple-element.64), channel_id=1, source_target_pairs={{0,5},{1,4},{2,7},{3,6},{4,1},{5,0},{6,3},{7,2},{8,13},{9,12},{10,... | collective-permute-start | bytes 110600 | tf_op jit(solution)/shard_map/ppermute | solution.py:150
  76.6 0.0 collective-permute-done.16.refs_3_
  76.6 0.0 collective-permute-start.21
  76.6 0.0 collective-permute-done.22.refs_1_.refs_2_
  76.6 0.5 collective-permute-start.23
  77.2 1.0 %collective-permute-done.17.refs_4_ = bf16[16,1152]{1,0:T(8,128)(2,1)S(1)} collective-permute-done((bf16[16,1152]{1,0:T(8,128)(2,1)S(1)}, bf16[16,1152]{1,0:T(8,128)(2,1)S(1)}, u32[]{:S(2)}, u32[]{:S(2)}) %collective-permute-start.17) | collective-permute-done | bytes 36896 | tf_op jit(solution)/shard_map/ppermute | solution.py:150
  78.1 0.2 collective-permute-start.19
  78.4 1.7 %collective-permute-done.18.refs_5_ = bf16[16,1152]{1,0:T(8,128)(2,1)S(1)} collective-permute-done((bf16[16,1152]{1,0:T(8,128)(2,1)S(1)}, bf16[16,1152]{1,0:T(8,128)(2,1)S(1)}, u32[]{:S(2)}, u32[]{:S(2)}) %collective-permute-start.18) | collective-permute-done | bytes 36896 | tf_op jit(solution)/shard_map/ppermute | solution.py:150
  80.0 2.4 %collective-permute-start.20 = (bf16[16,1152]{1,0:T(8,128)(2,1)S(1)}, bf16[16,1152]{1,0:T(8,128)(2,1)S(1)}, u32[]{:S(2)}, u32[]{:S(2)}) collective-permute-start(bf16[16,1152]{1,0:T(8,128)(2,1)S(1)} %get-tuple-element.66), channel_id=1, source_target_pairs={{0,7},{1,6},{2,5},{3,4},{4,3},{5,2},{6,1},{7,0},{8,15},{9,14},{10,... | collective-permute-start | bytes 110600 | tf_op jit(solution)/shard_map/ppermute | solution.py:150
  82.4 1.5 %collective-permute-done.19.refs_6_ = bf16[16,1152]{1,0:T(8,128)(2,1)S(1)} collective-permute-done((bf16[16,1152]{1,0:T(8,128)(2,1)S(1)}, bf16[16,1152]{1,0:T(8,128)(2,1)S(1)}, u32[]{:S(2)}, u32[]{:S(2)}) %collective-permute-start.19) | collective-permute-done | bytes 36896 | tf_op jit(solution)/shard_map/ppermute | solution.py:150
  83.9 2.8 %collective-permute-done.20.refs_7_ = bf16[16,1152]{1,0:T(8,128)(2,1)S(1)} collective-permute-done((bf16[16,1152]{1,0:T(8,128)(2,1)S(1)}, bf16[16,1152]{1,0:T(8,128)(2,1)S(1)}, u32[]{:S(2)}, u32[]{:S(2)}) %collective-permute-start.20) | collective-permute-done | bytes 36896 | tf_op jit(solution)/shard_map/ppermute | solution.py:150
  86.7 0.9 shard_map.96
  87.6 0.0 collective-permute-start.26
  87.6 0.5 convert_bitcast_fusion
  88.1 2.8 %shard_map.97 = (bf16[384,2048]{1,0:T(8,128)(2,1)S(1)}, f32[384,2048]{1,0:T(8,128)S(1)}) custom-call(bf16[128,1024]{1,0:T(8,128)(2,1)S(1)} %collective-permute-done.21.refs_0_.refs_1_, bf16[128,1024]{1,0:T(8,128)(2,1)S(1)} %collective-permute-done.22.refs_1_.refs_2_, bf16[128,1024]{1,0:T(8,128)(2,1)S(1)} %collective-permute-done.23.refs_2_.refs_3_, ...), custom_call_target="tpu_custom_call" | custom-call | flops 1610612736 | bytes 4980736 | tf_op jit(solution)/shard_map/pallas_call | solution.py:30
  90.9 0.0 collective-permute-done.24.refs_5_
  90.9 0.0 collective-permute-done.26.refs_7_
  90.9 4.2 %shard_map.98 = (bf16[256,2048]{1,0:T(8,128)(2,1)}, bf16[512,1024]{1,0:T(8,128)(2,1)}) custom-call(bf16[128,1024]{1,0:T(8,128)(2,1)S(1)} %constant_dynamic-update-slice_fusion.8.refs_0_, bf16[128,1024]{1,0:T(8,128)(2,1)S(1)} %collective-permute-done.21.refs_0_.refs_1_, bf16[128,1024]{1,0:T(8,128)(2,1)S(1)} %collective-permute-done.22.refs_1_.refs_2_, ...), custom_call_target="tpu_custom_call" | custom-call | flops 2684354560 | bytes 12058624 | tf_op jit(solution)/shard_map/pallas_call | solution.py:30
  (31 shorter events, 0.1 us)
Async XLA Ops:
  0.6 63.4 %copy-start = (bf16[1,2048,1024]{2,1,0:T(8,128)(2,1)S(1)}, bf16[1,2048,1024]{2,1,0:T(8,128)(2,1)}, u32[]{:S(2)}) copy-start(bf16[1,2048,1024]{2,1,0:T(8,128)(2,1)} %param.11) | copy-start | bytes 12582916
  0.6 1.1 %copy-start.4 = (bf16[64,1024]{1,0:T(8,128)(2,1)S(1)}, bf16[64,1024]{1,0:T(8,128)(2,1)}, u32[]{:S(2)}) copy-start(bf16[64,1024]{1,0:T(8,128)(2,1)} %tokens.1) | copy-start | bytes 393220
  1.7 1.2 %copy-start.5 = (bf16[64,1024]{1,0:T(8,128)(2,1)S(1)}, bf16[64,1024]{1,0:T(8,128)(2,1)}, u32[]{:S(2)}) copy-start(bf16[64,1024]{1,0:T(8,128)(2,1)} %cotangent.1) | copy-start | bytes 393220
  2.9 0.7 copy-start.6
  3.5 0.7 copy-start.8
  4.6 8.9 %collective-permute-start = (bf16[16,1024]{1,0:T(8,128)(2,1)S(1)}, bf16[16,1024]{1,0:T(8,128)(2,1)S(1)}, u32[]{:S(2)}, u32[]{:S(2)}) collective-permute-start(bf16[16,1024]{1,0:T(8,128)(2,1)S(1)} %get-tuple-element.42), channel_id=1, source_target_pairs={{0,1},{1,0},{2,3},{3,2},{4,5},{5,4},{6,7},{7,6},{8,9},{9,8},{10,11... | collective-permute-start | bytes 98312 | tf_op jit(solution)/shard_map/ppermute | solution.py:150
  7.6 9.5 %collective-permute-start.1 = (bf16[16,1024]{1,0:T(8,128)(2,1)S(1)}, bf16[16,1024]{1,0:T(8,128)(2,1)S(1)}, u32[]{:S(2)}, u32[]{:S(2)}) collective-permute-start(bf16[16,1024]{1,0:T(8,128)(2,1)S(1)} %get-tuple-element.43), channel_id=1, source_target_pairs={{0,2},{1,3},{2,0},{3,1},{4,6},{5,7},{6,4},{7,5},{8,10},{9,11},{10,... | collective-permute-start | bytes 98312 | tf_op jit(solution)/shard_map/ppermute | solution.py:150
  9.2 44.5 %collective-permute-start.2 = (bf16[16,1024]{1,0:T(8,128)(2,1)S(1)}, bf16[16,1024]{1,0:T(8,128)(2,1)S(1)}, u32[]{:S(2)}, u32[]{:S(2)}) collective-permute-start(bf16[16,1024]{1,0:T(8,128)(2,1)S(1)} %get-tuple-element.44), channel_id=1, source_target_pairs={{0,3},{1,2},{2,1},{3,0},{4,7},{5,6},{6,5},{7,4},{8,11},{9,10},{10,... | collective-permute-start | bytes 98312 | tf_op jit(solution)/shard_map/ppermute | solution.py:150
  9.2 46.0 %collective-permute-start.3 = (bf16[16,1024]{1,0:T(8,128)(2,1)S(1)}, bf16[16,1024]{1,0:T(8,128)(2,1)S(1)}, u32[]{:S(2)}, u32[]{:S(2)}) collective-permute-start(bf16[16,1024]{1,0:T(8,128)(2,1)S(1)} %get-tuple-element.45), channel_id=1, source_target_pairs={{0,4},{1,5},{2,6},{3,7},{4,0},{5,1},{6,2},{7,3},{8,12},{9,13},{10,... | collective-permute-start | bytes 98312 | tf_op jit(solution)/shard_map/ppermute | solution.py:150
  12.2 43.0 %collective-permute-start.4 = (bf16[16,1024]{1,0:T(8,128)(2,1)S(1)}, bf16[16,1024]{1,0:T(8,128)(2,1)S(1)}, u32[]{:S(2)}, u32[]{:S(2)}) collective-permute-start(bf16[16,1024]{1,0:T(8,128)(2,1)S(1)} %get-tuple-element.46), channel_id=1, source_target_pairs={{0,5},{1,4},{2,7},{3,6},{4,1},{5,0},{6,3},{7,2},{8,13},{9,12},{10,... | collective-permute-start | bytes 98312 | tf_op jit(solution)/shard_map/ppermute | solution.py:150
  13.5 41.8 %collective-permute-start.5 = (bf16[16,1024]{1,0:T(8,128)(2,1)S(1)}, bf16[16,1024]{1,0:T(8,128)(2,1)S(1)}, u32[]{:S(2)}, u32[]{:S(2)}) collective-permute-start(bf16[16,1024]{1,0:T(8,128)(2,1)S(1)} %get-tuple-element.47), channel_id=1, source_target_pairs={{0,6},{1,7},{2,4},{3,5},{4,2},{5,3},{6,0},{7,1},{8,14},{9,15},{10,... | collective-permute-start | bytes 98312 | tf_op jit(solution)/shard_map/ppermute | solution.py:150
  17.1 3.9 %collective-permute-start.7 = (bf16[16,1024]{1,0:T(8,128)(2,1)S(1)}, bf16[16,1024]{1,0:T(8,128)(2,1)S(1)}, u32[]{:S(2)}, u32[]{:S(2)}) collective-permute-start(bf16[16,1024]{1,0:T(8,128)(2,1)S(1)} %get-tuple-element.50), channel_id=1, source_target_pairs={{0,1},{1,0},{2,3},{3,2},{4,5},{5,4},{6,7},{7,6},{8,9},{9,8},{10,11... | collective-permute-start | bytes 98312 | tf_op jit(solution)/shard_map/ppermute | solution.py:150
  21.1 3.9 %collective-permute-start.8 = (bf16[16,1024]{1,0:T(8,128)(2,1)S(1)}, bf16[16,1024]{1,0:T(8,128)(2,1)S(1)}, u32[]{:S(2)}, u32[]{:S(2)}) collective-permute-start(bf16[16,1024]{1,0:T(8,128)(2,1)S(1)} %get-tuple-element.51), channel_id=1, source_target_pairs={{0,2},{1,3},{2,0},{3,1},{4,6},{5,7},{6,4},{7,5},{8,10},{9,11},{10,... | collective-permute-start | bytes 98312 | tf_op jit(solution)/shard_map/ppermute | solution.py:150
  25.0 4.8 %collective-permute-start.9 = (bf16[16,1024]{1,0:T(8,128)(2,1)S(1)}, bf16[16,1024]{1,0:T(8,128)(2,1)S(1)}, u32[]{:S(2)}, u32[]{:S(2)}) collective-permute-start(bf16[16,1024]{1,0:T(8,128)(2,1)S(1)} %get-tuple-element.52), channel_id=1, source_target_pairs={{0,3},{1,2},{2,1},{3,0},{4,7},{5,6},{6,5},{7,4},{8,11},{9,10},{10,... | collective-permute-start | bytes 98312 | tf_op jit(solution)/shard_map/ppermute | solution.py:150
  29.8 4.8 %collective-permute-start.10 = (bf16[16,1024]{1,0:T(8,128)(2,1)S(1)}, bf16[16,1024]{1,0:T(8,128)(2,1)S(1)}, u32[]{:S(2)}, u32[]{:S(2)}) collective-permute-start(bf16[16,1024]{1,0:T(8,128)(2,1)S(1)} %get-tuple-element.53), channel_id=1, source_target_pairs={{0,4},{1,5},{2,6},{3,7},{4,0},{5,1},{6,2},{7,3},{8,12},{9,13},{10,... | collective-permute-start | bytes 98312 | tf_op jit(solution)/shard_map/ppermute | solution.py:150
  34.6 5.7 %collective-permute-start.11 = (bf16[16,1024]{1,0:T(8,128)(2,1)S(1)}, bf16[16,1024]{1,0:T(8,128)(2,1)S(1)}, u32[]{:S(2)}, u32[]{:S(2)}) collective-permute-start(bf16[16,1024]{1,0:T(8,128)(2,1)S(1)} %get-tuple-element.54), channel_id=1, source_target_pairs={{0,5},{1,4},{2,7},{3,6},{4,1},{5,0},{6,3},{7,2},{8,13},{9,12},{10,... | collective-permute-start | bytes 98312 | tf_op jit(solution)/shard_map/ppermute | solution.py:150
  40.3 5.7 %collective-permute-start.12 = (bf16[16,1024]{1,0:T(8,128)(2,1)S(1)}, bf16[16,1024]{1,0:T(8,128)(2,1)S(1)}, u32[]{:S(2)}, u32[]{:S(2)}) collective-permute-start(bf16[16,1024]{1,0:T(8,128)(2,1)S(1)} %get-tuple-element.55), channel_id=1, source_target_pairs={{0,6},{1,7},{2,4},{3,5},{4,2},{5,3},{6,0},{7,1},{8,14},{9,15},{10,... | collective-permute-start | bytes 98312 | tf_op jit(solution)/shard_map/ppermute | solution.py:150
  46.0 6.6 %collective-permute-start.13 = (bf16[16,1024]{1,0:T(8,128)(2,1)S(1)}, bf16[16,1024]{1,0:T(8,128)(2,1)S(1)}, u32[]{:S(2)}, u32[]{:S(2)}) collective-permute-start(bf16[16,1024]{1,0:T(8,128)(2,1)S(1)} %get-tuple-element.56), channel_id=1, source_target_pairs={{0,7},{1,6},{2,5},{3,4},{4,3},{5,2},{6,1},{7,0},{8,15},{9,14},{10,... | collective-permute-start | bytes 98312 | tf_op jit(solution)/shard_map/ppermute | solution.py:150
  52.6 6.6 %collective-permute-start.6 = (bf16[16,1024]{1,0:T(8,128)(2,1)S(1)}, bf16[16,1024]{1,0:T(8,128)(2,1)S(1)}, u32[]{:S(2)}, u32[]{:S(2)}) collective-permute-start(bf16[16,1024]{1,0:T(8,128)(2,1)S(1)} %get-tuple-element.48), channel_id=1, source_target_pairs={{0,7},{1,6},{2,5},{3,4},{4,3},{5,2},{6,1},{7,0},{8,15},{9,14},{10,... | collective-permute-start | bytes 98312 | tf_op jit(solution)/shard_map/ppermute | solution.py:150
  53.7 23.0 %collective-permute-start.22 = (bf16[128,1024]{1,0:T(8,128)(2,1)S(1)}, bf16[128,1024]{1,0:T(8,128)(2,1)S(1)}, u32[]{:S(2)}, u32[]{:S(2)}) collective-permute-start(bf16[128,1024]{1,0:T(8,128)(2,1)S(1)} %constant_dynamic-update-slice_fusion.8.refs_0_), channel_id=1, source_target_pairs={{0,16},{8,24},{16,0},{24,8},{1,17},{9,25},{17,1},{25,9},{2,18},{10... | collective-permute-start | bytes 786440 | tf_op jit(solution)/shard_map/ppermute | solution.py:160
  59.3 28.3 %collective-permute-start.25 = (bf16[128,1024]{1,0:T(8,128)(2,1)S(1)}, bf16[128,1024]{1,0:T(8,128)(2,1)S(1)}, u32[]{:S(2)}, u32[]{:S(2)}) collective-permute-start(bf16[128,1024]{1,0:T(8,128)(2,1)S(1)} %constant_dynamic-update-slice_fusion.s.refs_4_), channel_id=1, source_target_pairs={{0,16},{8,24},{16,0},{24,8},{1,17},{9,25},{17,1},{25,9},{2,18},{10... | collective-permute-start | bytes 786440 | tf_op jit(solution)/shard_map/ppermute | solution.py:160
  60.8 2.2 %copy-start.1 = (bf16[1,1024,2048]{2,1,0:T(8,128)(2,1)S(1)}, bf16[1,1024,2048]{2,1,0:T(8,128)(2,1)}, u32[]{:S(2)}) copy-start(bf16[1,1024,2048]{2,1,0:T(8,128)(2,1)} %param.10) | copy-start | bytes 12582916
  64.0 2.2 %copy-start.2 = (bf16[1,1024,2048]{2,1,0:T(8,128)(2,1)S(1)}, bf16[1,1024,2048]{2,1,0:T(8,128)(2,1)}, u32[]{:S(2)}) copy-start(bf16[1,1024,2048]{2,1,0:T(8,128)(2,1)} %param.10) | copy-start | bytes 12582916
  66.2 20.5 %copy-start.7 = (bf16[64,2]{0,1:T(2,128)(2,1)S(1)}, bf16[64,2]{0,1:T(2,128)(2,1)}, u32[]{:S(2)}) copy-start(bf16[64,2]{0,1:T(2,128)(2,1)} %param.9) | copy-start | bytes 772
  66.2 21.9 %copy-start.3 = (bf16[1,1024,2048]{2,1,0:T(8,128)(2,1)S(1)}, bf16[1,1024,2048]{2,1,0:T(8,128)(2,1)}, u32[]{:S(2)}) copy-start(bf16[1,1024,2048]{2,1,0:T(8,128)(2,1)} %param.10) | copy-start | bytes 12582916
  69.3 4.0 %collective-permute-start.14 = (bf16[16,1152]{1,0:T(8,128)(2,1)S(1)}, bf16[16,1152]{1,0:T(8,128)(2,1)S(1)}, u32[]{:S(2)}, u32[]{:S(2)}) collective-permute-start(bf16[16,1152]{1,0:T(8,128)(2,1)S(1)} %get-tuple-element.60), channel_id=1, source_target_pairs={{0,1},{1,0},{2,3},{3,2},{4,5},{5,4},{6,7},{7,6},{8,9},{9,8},{10,11... | collective-permute-start | bytes 110600 | tf_op jit(solution)/shard_map/ppermute | solution.py:150
  70.3 4.0 %collective-permute-start.15 = (bf16[16,1152]{1,0:T(8,128)(2,1)S(1)}, bf16[16,1152]{1,0:T(8,128)(2,1)S(1)}, u32[]{:S(2)}, u32[]{:S(2)}) collective-permute-start(bf16[16,1152]{1,0:T(8,128)(2,1)S(1)} %get-tuple-element.61), channel_id=1, source_target_pairs={{0,2},{1,3},{2,0},{3,1},{4,6},{5,7},{6,4},{7,5},{8,10},{9,11},{10,... | collective-permute-start | bytes 110600 | tf_op jit(solution)/shard_map/ppermute | solution.py:150
  70.3 6.3 %collective-permute-start.16 = (bf16[16,1152]{1,0:T(8,128)(2,1)S(1)}, bf16[16,1152]{1,0:T(8,128)(2,1)S(1)}, u32[]{:S(2)}, u32[]{:S(2)}) collective-permute-start(bf16[16,1152]{1,0:T(8,128)(2,1)S(1)} %get-tuple-element.62), channel_id=1, source_target_pairs={{0,3},{1,2},{2,1},{3,0},{4,7},{5,6},{6,5},{7,4},{8,11},{9,10},{10,... | collective-permute-start | bytes 110600 | tf_op jit(solution)/shard_map/ppermute | solution.py:150
  73.3 4.9 %collective-permute-start.17 = (bf16[16,1152]{1,0:T(8,128)(2,1)S(1)}, bf16[16,1152]{1,0:T(8,128)(2,1)S(1)}, u32[]{:S(2)}, u32[]{:S(2)}) collective-permute-start(bf16[16,1152]{1,0:T(8,128)(2,1)S(1)} %get-tuple-element.63), channel_id=1, source_target_pairs={{0,4},{1,5},{2,6},{3,7},{4,0},{5,1},{6,2},{7,3},{8,12},{9,13},{10,... | collective-permute-start | bytes 110600 | tf_op jit(solution)/shard_map/ppermute | solution.py:150
  74.3 5.8 %collective-permute-start.18 = (bf16[16,1152]{1,0:T(8,128)(2,1)S(1)}, bf16[16,1152]{1,0:T(8,128)(2,1)S(1)}, u32[]{:S(2)}, u32[]{:S(2)}) collective-permute-start(bf16[16,1152]{1,0:T(8,128)(2,1)S(1)} %get-tuple-element.64), channel_id=1, source_target_pairs={{0,5},{1,4},{2,7},{3,6},{4,1},{5,0},{6,3},{7,2},{8,13},{9,12},{10,... | collective-permute-start | bytes 110600 | tf_op jit(solution)/shard_map/ppermute | solution.py:150
  76.6 11.5 %collective-permute-start.21 = (bf16[128,1024]{1,0:T(8,128)(2,1)S(1)}, bf16[128,1024]{1,0:T(8,128)(2,1)S(1)}, u32[]{:S(2)}, u32[]{:S(2)}) collective-permute-start(bf16[128,1024]{1,0:T(8,128)(2,1)S(1)} %constant_dynamic-update-slice_fusion.8.refs_0_), channel_id=1, source_target_pairs={{0,8},{8,0},{16,24},{24,16},{1,9},{9,1},{17,25},{25,17},{2,10},{10... | collective-permute-start | bytes 786440 | tf_op jit(solution)/shard_map/ppermute | solution.py:158
  76.6 11.4 %collective-permute-start.23 = (bf16[128,1024]{1,0:T(8,128)(2,1)S(1)}, bf16[128,1024]{1,0:T(8,128)(2,1)S(1)}, u32[]{:S(2)}, u32[]{:S(2)}) collective-permute-start(bf16[128,1024]{1,0:T(8,128)(2,1)S(1)} %collective-permute-done.22.refs_1_.refs_2_), channel_id=1, source_target_pairs={{0,8},{8,0},{16,24},{24,16},{1,9},{9,1},{17,25},{25,17},{2,10},{10... | collective-permute-start | bytes 786440 | tf_op jit(solution)/shard_map/ppermute | solution.py:161
  78.1 5.8 %collective-permute-start.19 = (bf16[16,1152]{1,0:T(8,128)(2,1)S(1)}, bf16[16,1152]{1,0:T(8,128)(2,1)S(1)}, u32[]{:S(2)}, u32[]{:S(2)}) collective-permute-start(bf16[16,1152]{1,0:T(8,128)(2,1)S(1)} %get-tuple-element.65), channel_id=1, source_target_pairs={{0,6},{1,7},{2,4},{3,5},{4,2},{5,3},{6,0},{7,1},{8,14},{9,15},{10,... | collective-permute-start | bytes 110600 | tf_op jit(solution)/shard_map/ppermute | solution.py:150
  80.0 6.7 %collective-permute-start.20 = (bf16[16,1152]{1,0:T(8,128)(2,1)S(1)}, bf16[16,1152]{1,0:T(8,128)(2,1)S(1)}, u32[]{:S(2)}, u32[]{:S(2)}) collective-permute-start(bf16[16,1152]{1,0:T(8,128)(2,1)S(1)} %get-tuple-element.66), channel_id=1, source_target_pairs={{0,7},{1,6},{2,5},{3,4},{4,3},{5,2},{6,1},{7,0},{8,15},{9,14},{10,... | collective-permute-start | bytes 110600 | tf_op jit(solution)/shard_map/ppermute | solution.py:150
  83.9 7.0 %collective-permute-start.24 = (bf16[128,1024]{1,0:T(8,128)(2,1)S(1)}, bf16[128,1024]{1,0:T(8,128)(2,1)S(1)}, u32[]{:S(2)}, u32[]{:S(2)}) collective-permute-start(bf16[128,1024]{1,0:T(8,128)(2,1)S(1)} %constant_dynamic-update-slice_fusion.s.refs_4_), channel_id=1, source_target_pairs={{0,8},{8,0},{16,24},{24,16},{1,9},{9,1},{17,25},{25,17},{2,10},{10... | collective-permute-start | bytes 786440 | tf_op jit(solution)/shard_map/ppermute | solution.py:158
  87.6 3.3 %collective-permute-start.26 = (bf16[128,1024]{1,0:T(8,128)(2,1)S(1)}, bf16[128,1024]{1,0:T(8,128)(2,1)S(1)}, u32[]{:S(2)}, u32[]{:S(2)}) collective-permute-start(bf16[128,1024]{1,0:T(8,128)(2,1)S(1)} %collective-permute-done.25.refs_6_), channel_id=1, source_target_pairs={{0,8},{8,0},{16,24},{24,16},{1,9},{9,1},{17,25},{25,17},{2,10},{10... | collective-permute-start | bytes 786440 | tf_op jit(solution)/shard_map/ppermute | solution.py:161

commit v3 on v2

--- a/solution.py
+++ b/solution.py
@@ -25,12 +25,14 @@
     return (pre_act * cdf).astype(BF16), cdf + pre_act * pdf
 
 
-def call(kernel, out_shape, args, flops=0, limit=24, scratch=()):
+def call(kernel, out_shape, args, flops=0, limit=24, scratch=(), in_space=pltpu.VMEM):
     moved = sum(a.size * a.dtype.itemsize for a in args)
+    if in_space == pltpu.HBM:
+        args = [pltpu.with_memory_space_constraint(a, pltpu.HBM) for a in args]
     return pl.pallas_call(
         kernel,
         out_shape=out_shape,
-        in_specs=[pl.BlockSpec(memory_space=pltpu.VMEM)] * len(args),
+        in_specs=[pl.BlockSpec(memory_space=in_space)] * len(args),
         out_specs=jax.tree.map(lambda _: pl.BlockSpec(memory_space=pltpu.VMEM), out_shape),
         scratch_shapes=list(scratch),
         compiler_params=pltpu.CompilerParams(vmem_limit_bytes=limit * MIB),
@@ -42,10 +44,23 @@
     return jax.ShapeDtypeStruct(dims, dtype)
 
 
-def route_kernel(experts, capacity, routes, gates, tokens, cotangent, *outs):
-    blocks_x, blocks_s = outs[:experts], outs[experts : 2 * experts]
-    place_refs = outs[2 * experts :]
-    tok_count = tokens.shape[0]
+def route_kernel(experts, capacity, routes_hbm, gates_hbm, tokens_hbm, cotangent_hbm, *refs):
+    blocks, place_refs, scratch = refs[:experts], refs[experts : experts + 2], refs[experts + 2 :]
+    routes, gates, tokens, cotangent, sems = scratch
+    copies = [
+        pltpu.make_async_copy(source, target, sems.at[i])
+        for i, (source, target) in enumerate(
+            (
+                (routes_hbm, routes),
+                (gates_hbm, gates),
+                (tokens_hbm, tokens),
+                (cotangent_hbm, cotangent),
+            )
+        )
+    ]
+    for copy in copies:
+        copy.start()
+    tok_count, feat_width = tokens.shape
     slots_all = experts * capacity
     me = lax.axis_index("expert")
     rows = max(experts, 16)
@@ -57,6 +72,8 @@
     slot_id = lax.broadcasted_iota(jnp.int32, (slots_all, tok_count), 0)
     taken = jnp.zeros((rows, 1), F32)
     places, gated = [], jnp.zeros((slots_all, tok_count), F32)
+    copies[0].wait()
+    copies[1].wait()
     for choice in range(2):
         chosen = routes[choice : choice + 1, :]
         one_hot = (expert_id == chosen).astype(F32)
@@ -70,11 +87,24 @@
         place_refs[choice][...] = place.astype(BF16)
         places.append(place)
         gated = gated + place * gates[choice : choice + 1, :].astype(F32)
+    copies[2].wait()
     x = dot((places[0] + places[1]).astype(BF16), tokens[...]).astype(BF16)
+    copies[3].wait()
     s = dot(gated.astype(BF16), cotangent[...]).astype(BF16)
     for k in range(experts):
-        blocks_x[k][...] = x[k * capacity : (k + 1) * capacity]
-        blocks_s[k][...] = s[k * capacity : (k + 1) * capacity]
+        blocks[k][:, :feat_width] = x[k * capacity : (k + 1) * capacity]
+        blocks[k][:, feat_width:] = s[k * capacity : (k + 1) * capacity]
+
+
+def load_kernel(in_hbm, out_hbm, weight_in, weight_out, sems):
+    copies = [
+        pltpu.make_async_copy(source, target, sems.at[i])
+        for i, (source, target) in enumerate(((in_hbm, weight_in), (out_hbm, weight_out)))
+    ]
+    for copy in copies:
+        copy.start()
+    for copy in copies:
+        copy.wait()
 
 
 def combine_kernel(experts, capacity, place0, place1, gates, *refs):
@@ -90,30 +120,38 @@
         gate_grads[choice : choice + 1, :] = row / gates[choice : choice + 1, :].astype(F32)
 
 
-def up_kernel(tile, *refs):
-    *x_refs, weight_in, hidden, slope = refs
-    for at in range(0, weight_in.shape[1], tile):
-        cols = slice(at, at + tile)
-        weight = weight_in[:, cols]
-        for g, x in enumerate(x_refs):
-            rows = slice(g * x.shape[0], (g + 1) * x.shape[0])
-            hidden[rows, cols], slope[rows, cols] = gelu_and_slope(dot(x[...], weight))
-
-
-def own_kernel(tile, experts, s, hidden, slope, weight_in, weight_out, d_pre, *blocks):
-    slots_all, feat_width = s.shape
+def stack(refs, part, width):
+    return jnp.concatenate([ref[:, part * width : (part + 1) * width] for ref in refs], axis=0)
+
+
+def my_part(ref):
+    width = ref.shape[1] // lax.axis_size("dp")
+    return ref[:, pl.ds(pl.multiple_of(lax.axis_index("dp") * width, width), width)]
+
+
+def own_kernel(tile, pieces, experts, *refs):
+    row_refs, (weight_in, weight_out, d_pre, h_cut, *blocks, hidden) = (
+        refs[:pieces],
+        refs[pieces:],
+    )
+    feat_width, ffw = weight_in.shape
+    x, s = stack(row_refs, 0, feat_width), stack(row_refs, 1, feat_width)
+    slots_all = x.shape[0]
     capacity = slots_all // experts
     dgate = jnp.zeros((slots_all, LANES), F32)
     dx = jnp.zeros((slots_all, feat_width), F32)
-    for at in range(0, weight_in.shape[1], tile):
+    for at in range(0, ffw, tile):
         cols = slice(at, at + tile)
-        d_hidden = dot(s[...], weight_out[cols, :], (1, 1))
-        part = (d_hidden * slope[:, cols]).astype(BF16)
+        act, slope = gelu_and_slope(dot(x, weight_in[:, cols]))
+        hidden[:, cols] = act
+        d_hidden = dot(s, weight_out[cols, :], (1, 1))
+        part = (d_hidden * slope).astype(BF16)
         d_pre[:, cols] = part
-        product = d_hidden * hidden[:, cols].astype(F32)
+        product = d_hidden * act.astype(F32)
         for lane in range(0, tile, LANES):
             dgate = dgate + product[:, lane : lane + LANES]
         dx = dx + dot(part, weight_in[:, cols], (1, 1))
+    h_cut[...] = my_part(hidden)
     dgate = jnp.broadcast_to(jnp.sum(dgate, axis=1, keepdims=True), (slots_all, LANES))
     for k in range(experts):
         rows = slice(k * capacity, (k + 1) * capacity)
@@ -121,44 +159,65 @@
         blocks[k][:, feat_width:] = dgate[rows].astype(BF16)
 
 
-def grads_kernel(tile, groups, *refs):
-    x_refs, s_refs, refs = refs[:groups], refs[groups : 2 * groups], refs[2 * groups :]
-    hidden0, d_pre0, hidden1, slope1, weight_out, grad_in, grad_out = refs[:7]
-    x_cut, s_all, d_pre = refs[7:]
-    me = lax.axis_index("dp")
-    slots_all = s_refs[0].shape[0]
-    cut = x_cut.shape[1]
-    ffw = weight_out.shape[0]
-    for g in range(groups):
-        rows = slice(g * slots_all, (g + 1) * slots_all)
-        x_cut[rows, :] = x_refs[g][:, pl.ds(pl.multiple_of(me * cut, cut), cut)]
-        s_all[rows, :] = s_refs[g][...]
-    d_pre[:slots_all, :] = d_pre0[...]
+def backward_tiles(tile, x, s, weight_in, weight_out, hidden, d_pre, rows):
+    for at in range(0, weight_in.shape[1], tile):
+        cols = slice(at, at + tile)
+        act, slope = gelu_and_slope(dot(x, weight_in[:, cols]))
+        hidden[:, cols] = act
+        d_pre[rows, cols] = (dot(s, weight_out[cols, :], (1, 1)) * slope).astype(BF16)
+
+
+def early_kernel(tile, pieces, *refs):
+    row_refs, (weight_in, weight_out, d_pre, h_cut, hidden) = refs[:pieces], refs[pieces:]
+    width = weight_in.shape[0]
+    x, s = stack(row_refs, 0, width), stack(row_refs, 1, width)
+    backward_tiles(tile, x, s, weight_in, weight_out, hidden, d_pre, slice(None))
+    h_cut[...] = my_part(hidden)
+
+
+def grads_kernel(tile, own, early, late, *refs):
+    pieces = own + early + late
+    row_refs, refs = refs[:pieces], refs[pieces:]
+    d_pre0, h_cut0, d_pre1, h_cut1, weight_in, weight_out, grad_in, grad_out = refs[:8]
+    hidden, d_pre = refs[8:]
+    width, ffw = weight_in.shape
+    x, s = stack(row_refs[-late:], 0, width), stack(row_refs[-late:], 1, width)
+    first, second = d_pre0.shape[0], d_pre0.shape[0] + d_pre1.shape[0]
+    d_pre[:first, :] = d_pre0[...]
+    d_pre[first:second, :] = d_pre1[...]
+    cut = grad_in.shape[0]
+    mine = pl.ds(pl.multiple_of(lax.axis_index("dp") * cut, cut), cut)
+    x_cut = jnp.concatenate([ref[:, mine] for ref in row_refs], axis=0)
+    backward_tiles(tile, x, s, weight_in, weight_out, hidden, d_pre, slice(second, None))
     for at in range(0, ffw, tile):
         cols = slice(at, at + tile)
-        d_hidden = dot(s_all[slots_all:, :], weight_out[cols, :], (1, 1))
-        d_pre[slots_all:, cols] = (d_hidden * slope1[:, cols]).astype(BF16)
-        grad_in[:, cols] = dot(x_cut[...], d_pre[:, cols], (0, 0)).astype(BF16)
-    mine = pl.ds(pl.multiple_of(me * (ffw // groups), ffw // groups), ffw // groups)
-    h_cut = jnp.concatenate([hidden0[:, mine], hidden1[:, mine]], axis=0)
-    grad_out[...] = dot(h_cut, s_all[...], (0, 0)).astype(BF16)
-
-
-def exchange(blocks):
-    experts = len(blocks)
-    return [blocks[0]] + [
-        lax.ppermute(blocks[k], "expert", [(i, i ^ k) for i in range(experts)])
-        for k in range(1, experts)
-    ]
+        grad_in[:, cols] = dot(x_cut, d_pre[:, cols], (0, 0)).astype(BF16)
+    h_cut = jnp.concatenate([h_cut0[...], h_cut1[...], my_part(hidden)], axis=0)
+    grad_out[...] = dot(h_cut, stack(row_refs, 1, width), (0, 0)).astype(BF16)
+
+
+def after(value, *first):
+    return lax.optimization_barrier((value, *first))[0]
+
+
+def permute(block, k):
+    return lax.ppermute(block, "expert", [(i, i ^ k) for i in range(lax.axis_size("expert"))])
+
+
+def swap_cores(rows):
+    return lax.ppermute(rows, "dp", [(i, i ^ 1) for i in range(lax.axis_size("dp"))])
+
+
+def shift_chips(rows, k):
+    groups = lax.axis_size("dp")
+    return lax.ppermute(rows, "dp", [(i, (i + 2 * k) % groups) for i in range(groups)])
 
 
 def gather_groups(rows):
-    groups = lax.axis_size("dp")
-    swap = [(i, i ^ 1) for i in range(groups)]
-    others = [lax.ppermute(rows, "dp", swap)]
-    for k in range(1, groups // 2):
-        other = lax.ppermute(rows, "dp", [(i, (i + 2 * k) % groups) for i in range(groups)])
-        others += [other, lax.ppermute(other, "dp", swap)]
+    others = [swap_cores(rows)]
+    for k in range(1, lax.axis_size("dp") // 2):
+        other = shift_chips(rows, k)
+        others += [other, swap_cores(other)]
     return others
 
 
@@ -168,54 +227,86 @@
     groups = lax.axis_size("dp")
     capacity = 2 * tok_count // experts
     slots_all = experts * capacity
-    weight_in = pltpu.with_memory_space_constraint(proj_in[0], pltpu.VMEM)
-    weight_out = pltpu.with_memory_space_constraint(proj_out[0], pltpu.VMEM)
-    ffw = weight_in.shape[1]
+    half = experts // 2
+    ffw = proj_in.shape[2]
     tile = ffw // groups
     product = 2 * slots_all * feat_width * ffw
-    block = shape((capacity, feat_width))
     place = shape((slots_all, tok_count))
 
     routed = call(
         functools.partial(route_kernel, experts, capacity),
-        [block] * (2 * experts) + [place] * 2,
+        [shape((capacity, 2 * feat_width))] * experts + [place] * 2,
         [routes.T, gates.T, tokens, cotangent],
-    )
-    places = routed[2 * experts :]
-    got_x = exchange(routed[:experts])
-    got_s = exchange(routed[experts : 2 * experts])
-    x = jnp.concatenate(got_x, axis=0)
-    x_others = gather_groups(x)
-    s = jnp.concatenate(got_s, axis=0)
-    s_others = gather_groups(s)
-    hidden0, slope0 = call(
-        functools.partial(up_kernel, tile),
-        [shape((slots_all, ffw)), shape((slots_all, ffw), F32)],
-        [x, weight_in],
-        product,
-    )
-    d_pre0, *back = call(
-        functools.partial(own_kernel, tile, experts),
-        [shape((slots_all, ffw))] + [shape((capacity, feat_width + LANES))] * experts,
-        [s, hidden0, slope0, weight_in, weight_out],
-        2 * product,
-    )
-    back = exchange(back)
-    others = groups - 1
-    hidden1, slope1 = call(
-        functools.partial(up_kernel, tile),
-        [shape((others * slots_all, ffw)), shape((others * slots_all, ffw), F32)],
-        [*x_others, weight_in],
-        others * product,
-    )
+        in_space=pltpu.HBM,
+        scratch=[
+            pltpu.VMEM((2, tok_count), jnp.int32),
+            pltpu.VMEM((2, tok_count), BF16),
+            pltpu.VMEM((tok_count, feat_width), BF16),
+            pltpu.VMEM((tok_count, feat_width), BF16),
+            pltpu.SemaphoreType.DMA((4,)),
+        ],
+    )
+    blocks, places = routed[:experts], routed[experts:]
+    weight_in, weight_out = call(
+        load_kernel,
+        [pltpu.VMEM((feat_width, ffw), BF16), pltpu.VMEM((ffw, feat_width), BF16)],
+        [after(proj_in[0], places[0]), after(proj_out[0], places[0])],
+        in_space=pltpu.HBM,
+        scratch=[pltpu.SemaphoreType.DMA((2,))],
+    )
+    weights = [
+        pltpu.with_memory_space_constraint(w, pltpu.VMEM) for w in (weight_in, weight_out)
+    ]
+    got = {0: blocks[0]}
+    near = list(range(1, half))
+    far = list(range(half, experts))
+    first, second = far[len(far) // 2 :], far[: len(far) // 2]
+    for k in near + first:
+        got[k] = permute(blocks[k], k)
+    for k in second:
+        got[k] = permute(after(blocks[k], *[got[j] for j in near]), k)
+    rows_a = jnp.concatenate([got[k] for k in range(half)], axis=0)
+    rows_b = jnp.concatenate([got[k] for k in range(half, experts)], axis=0)
+    core_a = swap_cores(rows_a)
+    chips_a = [shift_chips(rows_a, k) for k in range(1, groups // 2)]
+    rows_b = after(rows_b, core_a)
+    chips_b = [shift_chips(rows_b, k) for k in range(1, groups // 2)]
+    d_pre0, h_cut0, *back = call(
+        functools.partial(own_kernel, tile, 2, experts),
+        [shape((slots_all, ffw)), shape((slots_all, tile))]
+        + [shape((capacity, feat_width + LANES))] * experts,
+        [rows_a, rows_b, *weights],
+        3 * product,
+        scratch=[pltpu.VMEM((slots_all, ffw), BF16)],
+    )
+    relayed_a = [swap_cores(after(rows, d_pre0)) for rows in chips_a]
+    core_b = swap_cores(after(rows_b, d_pre0))
+    early = [core_a, core_b, *chips_a, *relayed_a]
+    early_rows = sum(piece.shape[0] for piece in early)
+    d_pre1, h_cut1 = call(
+        functools.partial(early_kernel, tile, len(early)),
+        [shape((early_rows, ffw)), shape((early_rows, tile))],
+        [*early, *weights],
+        2 * product * early_rows // slots_all,
+        scratch=[pltpu.VMEM((early_rows, ffw), BF16)],
+    )
+    returned = {0: back[0]}
+    for k in first:
+        returned[k] = permute(back[k], k)
+    for k in second:
+        returned[k] = permute(after(back[k], core_b, *relayed_a), k)
+    for k in near:
+        returned[k] = permute(after(back[k], d_pre1), k)
+    back = [returned[k] for k in range(experts)]
+    chips_b += [swap_cores(rows) for rows in chips_b]
+    late_rows = sum(piece.shape[0] for piece in chips_b)
     grad_in, grad_out = call(
-        functools.partial(grads_kernel, tile, groups),
+        functools.partial(grads_kernel, tile, 2, len(early), len(chips_b)),
         [shape((feat_width // groups, ffw)), shape((ffw // groups, feat_width))],
-        [x, *x_others, s, *s_others, hidden0, d_pre0, hidden1, slope1, weight_out],
-        (others + 2) * product,
+        [rows_a, rows_b, *early, *chips_b, d_pre0, h_cut0, d_pre1, h_cut1, *weights],
+        4 * product,
         scratch=[
-            pltpu.VMEM((groups * slots_all, feat_width // groups), BF16),
-            pltpu.VMEM((groups * slots_all, feat_width), BF16),
+            pltpu.VMEM((late_rows, ffw), BF16),
             pltpu.VMEM((groups * slots_all, ffw), BF16),
         ],
     )

time: 95.3 us -> 53.9 us (0.57)
  waiting for transfers between devices: 45.5 us -> 8.55 us
  local copies, waits for them, and re-layouts: 7.98 us -> 0.03 us
  Pallas kernels: 12.3 us -> 16.4 us
    ppermute x27 -> x20, waiting for transfers between devices: 45.5 us -> 8.55 us  [the longest x14 7.53 us: permute(): lax.ppermute(block, 'expert', [(i, i ^ k) for i in range(lax.axis_size('e...]
    unnamed x32 -> x5, local copies, waits for them, and re-layouts: 7.97 us -> 0.02 us
    pallas_call x6, Pallas kernels: 12.3 us -> 16.4 us  [call(): pl.pallas_call(kernel, out_shape=out_shape, in_specs=[pl.BlockSpec(memory...]
    ppermute x27 -> x20, starting transfers between devices: 28 us -> 27.5 us  [the longest x14 24.2 us: permute(): lax.ppermute(block, 'expert', [(i, i ^ k) for i in range(lax.axis_size('e...]
  transfers between devices with their start and end apart: 27 -> 20, of which waited for: 14 -> 5; matrix products, arithmetic and copies ran while one was open for 1% -> 1% of each run, Pallas kernels for 8% -> 20%
where the time goes in v3:
time: 53.9 us; the launch traced here: 53.7 us
  starting transfers between devices  27.5 us (51%)
  Pallas kernels  16.4 us (30%)
  waiting for transfers between devices  8.55 us (16%)
  between operations  0.76 us (1%)
    ppermute x14, starting transfers between devices, permute(): lax.ppermute(block, 'expert', [(i, i ^ k) for i in range(lax.axis_size('e...  24.2 us
    pallas_call x6, Pallas kernels, call(): pl.pallas_call(kernel, out_shape=out_shape, in_specs=[pl.BlockSpec(memory...  16.4 us
    ppermute x14, waiting for transfers between devices, permute(): lax.ppermute(block, 'expert', [(i, i ^ k) for i in range(lax.axis_size('e...  7.53 us
    ppermute x2, starting transfers between devices, shift_chips(): lax.ppermute(rows, 'dp', [(i, (i + 2 * k) % groups) for i in range(groups)])  3.17 us
  transfers between devices with their start and end apart: 20, of which 5 were waited for; matrix products, arithmetic and copies ran while one was open for 1% of the time, Pallas kernels for 20%

profile of v3, /device:TPU:0, one launch (start us, length us, event | category | flops | bytes accessed | tf_op | source)
XLA Modules:
  0.0 53.7 jit_solution(7910662674833079041)
XLA Ops:
  0.6 1.4 %shard_map.93 = (bf16[16,2048]{1,0:T(8,128)(2,1)S(1)}, bf16[16,2048]{1,0:T(8,128)(2,1)S(1)}, bf16[16,2048]{1,0:T(8,128)(2,1)S(1)}, bf16[16,2048]{1,0:T(8,128)(2,...) custom-call(s32[2,64]{1,0:T(2,128)} %bitcast.12, ...), custom_call_target="tpu_custom_call" | custom-call | bytes 262912 | tf_op jit(solution)/shard_map/pallas_call | solution.py:32
  2.0 3.0 %collective-permute-start = (bf16[16,2048]{1,0:T(8,128)(2,1)S(1)}, bf16[16,2048]{1,0:T(8,128)(2,1)S(1)}, u32[]{:S(2)}, u32[]{:S(2)}) collective-permute-start(bf16[16,2048]{1,0:T(8,128)(2,1)S(1)} %get-tuple-element.47), channel_id=1, source_target_pairs={{0,1},{1,0},{2,3},{3,2},{4,5},{5,4},{6,7},{7,6},{8,9},{9,8},{10,11... | collective-permute-start | bytes 196616 | tf_op jit(solution)/shard_map/ppermute | solution.py:204
  5.0 1.6 %collective-permute-start.1 = (bf16[16,2048]{1,0:T(8,128)(2,1)S(1)}, bf16[16,2048]{1,0:T(8,128)(2,1)S(1)}, u32[]{:S(2)}, u32[]{:S(2)}) collective-permute-start(bf16[16,2048]{1,0:T(8,128)(2,1)S(1)} %get-tuple-element.48), channel_id=1, source_target_pairs={{0,2},{1,3},{2,0},{3,1},{4,6},{5,7},{6,4},{7,5},{8,10},{9,11},{10,... | collective-permute-start | bytes 196616 | tf_op jit(solution)/shard_map/ppermute | solution.py:204
  6.6 0.0 collective-permute-start.2
  6.6 4.9 %collective-permute-start.6 = (bf16[16,2048]{1,0:T(8,128)(2,1)S(1)}, bf16[16,2048]{1,0:T(8,128)(2,1)S(1)}, u32[]{:S(2)}, u32[]{:S(2)}) collective-permute-start(bf16[16,2048]{1,0:T(8,128)(2,1)S(1)} %get-tuple-element.55), channel_id=1, source_target_pairs={{0,7},{1,6},{2,5},{3,4},{4,3},{5,2},{6,1},{7,0},{8,15},{9,14},{10,... | collective-permute-start | bytes 196616 | tf_op jit(solution)/shard_map/ppermute | solution.py:204
  11.6 0.2 collective-permute-start.5
  11.8 0.0 collective-permute-done
  11.8 0.0 collective-permute-done.1
  11.8 0.0 collective-permute-done.2
  11.8 2.9 %collective-permute-start.4 = (bf16[16,2048]{1,0:T(8,128)(2,1)S(1)}, bf16[16,2048]{1,0:T(8,128)(2,1)S(1)}, u32[]{:S(2)}, u32[]{:S(2)}) collective-permute-start(bf16[16,2048]{1,0:T(8,128)(2,1)S(1)} %get-tuple-element.53), channel_id=1, source_target_pairs={{0,5},{1,4},{2,7},{3,6},{4,1},{5,0},{6,3},{7,2},{8,13},{9,12},{10,... | collective-permute-start | bytes 196616 | tf_op jit(solution)/shard_map/ppermute | solution.py:204
  14.8 0.0 collective-permute-start.3
  14.8 0.1 collective-permute-start.7
  14.9 3.5 %shard_map.94 = (bf16[1024,2048]{1,0:T(8,128)(2,1)S(1)}, bf16[2048,1024]{1,0:T(8,128)(2,1)S(1)}) custom-call(bf16[1024,2048]{1,0:T(8,128)(2,1)} %bitcast.10, bf16[2048,1024]{1,0:T(8,128)(2,1)} %bitcast.11), custom_call_target="tpu_custom_call" | custom-call | bytes 8388608 | tf_op jit(solution)/shard_map/pallas_call | solution.py:32
  18.4 0.0 collective-permute-done.6
  18.4 1.6 %collective-permute-start.9 = (bf16[64,2048]{1,0:T(8,128)(2,1)S(1)}, bf16[64,2048]{1,0:T(8,128)(2,1)S(1)}, u32[]{:S(2)}, u32[]{:S(2)}) collective-permute-start(bf16[64,2048]{1,0:T(8,128)(2,1)S(1)} %constant_dynamic-update-slice_fusion.refs_0_), channel_id=1, source_target_pairs={{0,16},{8,24},{16,0},{24,8},{1,17},{9,25},{17,1},{25,9},{2,18},{10... | collective-permute-start | bytes 786440 | tf_op jit(solution)/shard_map/ppermute | solution.py:213
  20.0 0.0 collective-permute-done.5
  20.0 0.9 %collective-permute-done.4 = bf16[16,2048]{1,0:T(8,128)(2,1)S(1)} collective-permute-done((bf16[16,2048]{1,0:T(8,128)(2,1)S(1)}, bf16[16,2048]{1,0:T(8,128)(2,1)S(1)}, u32[]{:S(2)}, u32[]{:S(2)}) %collective-permute-start.4) | collective-permute-done | bytes 65568 | tf_op jit(solution)/shard_map/ppermute | solution.py:204
  20.9 1.4 %collective-permute-done.3 = bf16[16,2048]{1,0:T(8,128)(2,1)S(1)} collective-permute-done((bf16[16,2048]{1,0:T(8,128)(2,1)S(1)}, bf16[16,2048]{1,0:T(8,128)(2,1)S(1)}, u32[]{:S(2)}, u32[]{:S(2)}) %collective-permute-start.3) | collective-permute-done | bytes 65568 | tf_op jit(solution)/shard_map/ppermute | solution.py:204
  22.4 0.0 collective-permute-done.7.refs_0_.refs_2_
  22.4 3.7 %shard_map.95 = (bf16[128,2048]{1,0:T(8,128)(2,1)S(1)}, bf16[128,512]{1,0:T(8,128)(2,1)S(1)}, bf16[16,1152]{1,0:T(8,128)(2,1)S(1)}, bf16[16,1152]{1,0:T(8,128)(2...) custom-call(bf16[64,2048]{1,0:T(8,128)(2,1)S(1)} %constant_dynamic-u, ...), custom_call_target="tpu_custom_call" | custom-call | flops 1610612736 | bytes 8912896 | tf_op jit(solution)/shard_map/pallas_call | solution.py:32
  26.1 0.1 collective-permute-start.8
  26.1 1.0 %collective-permute-done.9.refs_2_.refs_4_ = bf16[64,2048]{1,0:T(8,128)(2,1)S(1)} collective-permute-done((bf16[64,2048]{1,0:T(8,128)(2,1)S(1)}, bf16[64,2048]{1,0:T(8,128)(2,1)S(1)}, u32[]{:S(2)}, u32[]{:S(2)}) %collective-permute-start.9) | collective-permute-done | bytes 262176 | tf_op jit(solution)/shard_map/ppermute | solution.py:213
  27.1 0.0 collective-permute-start.10
  27.1 1.6 %collective-permute-start.18 = (bf16[64,2048]{1,0:T(8,128)(2,1)S(1)}, bf16[64,2048]{1,0:T(8,128)(2,1)S(1)}, u32[]{:S(2)}, u32[]{:S(2)}) collective-permute-start(bf16[64,2048]{1,0:T(8,128)(2,1)S(1)} %pad_maximum_fusion.refs_1_), channel_id=1, source_target_pairs={{0,16},{8,24},{16,0},{24,8},{1,17},{9,25},{17,1},{25,9},{2,18},{10... | collective-permute-start | bytes 786440 | tf_op jit(solution)/shard_map/ppermute | solution.py:213
  28.7 3.6 %collective-permute-start.16 = (bf16[16,1152]{1,0:T(8,128)(2,1)S(1)}, bf16[16,1152]{1,0:T(8,128)(2,1)S(1)}, u32[]{:S(2)}, u32[]{:S(2)}) collective-permute-start(bf16[16,1152]{1,0:T(8,128)(2,1)S(1)} %get-tuple-element.76), channel_id=1, source_target_pairs={{0,6},{1,7},{2,4},{3,5},{4,2},{5,3},{6,0},{7,1},{8,14},{9,15},{10,... | collective-permute-start | bytes 110600 | tf_op jit(solution)/shard_map/ppermute | solution.py:204
  32.3 0.0 copy-start
  32.3 1.1 %collective-permute-start.17 = (bf16[16,1152]{1,0:T(8,128)(2,1)S(1)}, bf16[16,1152]{1,0:T(8,128)(2,1)S(1)}, u32[]{:S(2)}, u32[]{:S(2)}) collective-permute-start(bf16[16,1152]{1,0:T(8,128)(2,1)S(1)} %get-tuple-element.77), channel_id=1, source_target_pairs={{0,7},{1,6},{2,5},{3,4},{4,3},{5,2},{6,1},{7,0},{8,15},{9,14},{10,... | collective-permute-start | bytes 110600 | tf_op jit(solution)/shard_map/ppermute | solution.py:204
  33.4 0.0 collective-permute-done.8.refs_1_.refs_3_
  33.4 0.0 collective-permute-done.10.refs_3_.refs_5_
  33.5 2.6 %shard_map.96 = (bf16[256,2048]{1,0:T(8,128)(2,1)S(1)}, bf16[256,512]{1,0:T(8,128)(2,1)S(1)}) custom-call(bf16[64,2048]{1,0:T(8,128)(2,1)S(1)} %collective-permute-done.7.refs_0_.refs_2_, bf16[64,2048]{1,0:T(8,128)(2,1)S(1)} %collective-permute-done.8.refs_1_.refs_3_, bf16[64,2048]{1,0:T(8,128)(2,1)S(1)} %collective-permute-done.9.refs_2_.refs_4_, ...), custom_call_target="tpu_custom_call" | custom-call | flops 2147483648 | bytes 9437184 | tf_op jit(solution)/shard_map/pallas_call | solution.py:32
  36.1 0.6 %collective-permute-start.11 = (bf16[16,1152]{1,0:T(8,128)(2,1)S(1)}, bf16[16,1152]{1,0:T(8,128)(2,1)S(1)}, u32[]{:S(2)}, u32[]{:S(2)}) collective-permute-start(bf16[16,1152]{1,0:T(8,128)(2,1)S(1)} %get-tuple-element.67), channel_id=1, source_target_pairs={{0,1},{1,0},{2,3},{3,2},{4,5},{5,4},{6,7},{7,6},{8,9},{9,8},{10,11... | collective-permute-start | bytes 110600 | tf_op jit(solution)/shard_map/ppermute | solution.py:204
  36.7 0.0 collective-permute-done.18.refs_6_
  36.7 0.0 collective-permute-start.19
  36.7 0.6 %collective-permute-start.12 = (bf16[16,1152]{1,0:T(8,128)(2,1)S(1)}, bf16[16,1152]{1,0:T(8,128)(2,1)S(1)}, u32[]{:S(2)}, u32[]{:S(2)}) collective-permute-start(bf16[16,1152]{1,0:T(8,128)(2,1)S(1)} %get-tuple-element.69), channel_id=1, source_target_pairs={{0,2},{1,3},{2,0},{3,1},{4,6},{5,7},{6,4},{7,5},{8,10},{9,11},{10,... | collective-permute-start | bytes 110600 | tf_op jit(solution)/shard_map/ppermute | solution.py:204
  37.2 0.0 collective-permute-done.16.refs_6_
  37.2 2.4 %collective-permute-start.13 = (bf16[16,1152]{1,0:T(8,128)(2,1)S(1)}, bf16[16,1152]{1,0:T(8,128)(2,1)S(1)}, u32[]{:S(2)}, u32[]{:S(2)}) collective-permute-start(bf16[16,1152]{1,0:T(8,128)(2,1)S(1)} %get-tuple-element.71), channel_id=1, source_target_pairs={{0,3},{1,2},{2,1},{3,0},{4,7},{5,6},{6,5},{7,4},{8,11},{9,10},{10,... | collective-permute-start | bytes 110600 | tf_op jit(solution)/shard_map/ppermute | solution.py:204
  39.6 0.0 collective-permute-done.17.refs_7_
  39.6 2.2 %collective-permute-start.14 = (bf16[16,1152]{1,0:T(8,128)(2,1)S(1)}, bf16[16,1152]{1,0:T(8,128)(2,1)S(1)}, u32[]{:S(2)}, u32[]{:S(2)}) collective-permute-start(bf16[16,1152]{1,0:T(8,128)(2,1)S(1)} %get-tuple-element.73), channel_id=1, source_target_pairs={{0,4},{1,5},{2,6},{3,7},{4,0},{5,1},{6,2},{7,3},{8,12},{9,13},{10,... | collective-permute-start | bytes 110600 | tf_op jit(solution)/shard_map/ppermute | solution.py:204
  41.9 0.0 collective-permute-done.11.refs_1_
  41.9 1.0 %collective-permute-start.15 = (bf16[16,1152]{1,0:T(8,128)(2,1)S(1)}, bf16[16,1152]{1,0:T(8,128)(2,1)S(1)}, u32[]{:S(2)}, u32[]{:S(2)}) collective-permute-start(bf16[16,1152]{1,0:T(8,128)(2,1)S(1)} %get-tuple-element.75), channel_id=1, source_target_pairs={{0,5},{1,4},{2,7},{3,6},{4,1},{5,0},{6,3},{7,2},{8,13},{9,12},{10,... | collective-permute-start | bytes 110600 | tf_op jit(solution)/shard_map/ppermute | solution.py:204
  42.8 0.0 collective-permute-done.12.refs_2_
  42.8 0.0 collective-permute-done.13.refs_3_
  42.8 1.7 %collective-permute-done.14.refs_4_ = bf16[16,1152]{1,0:T(8,128)(2,1)S(1)} collective-permute-done((bf16[16,1152]{1,0:T(8,128)(2,1)S(1)}, bf16[16,1152]{1,0:T(8,128)(2,1)S(1)}, u32[]{:S(2)}, u32[]{:S(2)}) %collective-permute-start.14) | collective-permute-done | bytes 36896 | tf_op jit(solution)/shard_map/ppermute | solution.py:204
  44.5 3.5 %collective-permute-done.15.refs_5_ = bf16[16,1152]{1,0:T(8,128)(2,1)S(1)} collective-permute-done((bf16[16,1152]{1,0:T(8,128)(2,1)S(1)}, bf16[16,1152]{1,0:T(8,128)(2,1)S(1)}, u32[]{:S(2)}, u32[]{:S(2)}) %collective-permute-start.15) | collective-permute-done | bytes 36896 | tf_op jit(solution)/shard_map/ppermute | solution.py:204
  48.0 0.0 copy-done
  48.0 0.9 %shard_map.97 = (bf16[64,1024]{1,0:T(8,128)(2,1)}, f32[2,64]{1,0:T(2,128)S(1)}) custom-call(bf16[128,64]{1,0:T(8,128)(2,1)S(1)} %get-tuple-element.44.place0, bf16[128,64]{1,0:T(8,128)(2,1)S(1)} %get-tuple-element.45.place1, bf16[2,64]{1,0:T(2,128)(2,1)S(1)} %bitcast.9, bf16[16,1152]{1,0:T(8,128)(2,1)S(1)} %get-tuple-element.61.refs_0_, ...), custom_call_target="tpu_custom_call" | custom-call | bytes 327936 | tf_op jit(solution)/shard_map/pallas_call | solution.py:32
  48.9 0.5 convert_bitcast_fusion
  49.4 0.0 collective-permute-done.19.refs_7_
  49.4 4.3 %shard_map.98 = (bf16[256,2048]{1,0:T(8,128)(2,1)}, bf16[512,1024]{1,0:T(8,128)(2,1)}) custom-call(bf16[64,2048]{1,0:T(8,128)(2,1)S(1)} %constant_dynamic-update-slice_fusion.refs_0_, bf16[64,2048]{1,0:T(8,128)(2,1)S(1)} %pad_maximum_fusion.refs_1_, bf16[64,2048]{1,0:T(8,128)(2,1)S(1)} %collective-permute-done.7.refs_0_.refs_2_, ...), custom_call_target="tpu_custom_call" | custom-call | flops 2147483648 | bytes 12451840 | tf_op jit(solution)/shard_map/pallas_call | solution.py:32
  (5 shorter events, 0.0 us)
Async XLA Ops:
  2.0 9.8 %collective-permute-start = (bf16[16,2048]{1,0:T(8,128)(2,1)S(1)}, bf16[16,2048]{1,0:T(8,128)(2,1)S(1)}, u32[]{:S(2)}, u32[]{:S(2)}) collective-permute-start(bf16[16,2048]{1,0:T(8,128)(2,1)S(1)} %get-tuple-element.47), channel_id=1, source_target_pairs={{0,1},{1,0},{2,3},{3,2},{4,5},{5,4},{6,7},{7,6},{8,9},{9,8},{10,11... | collective-permute-start | bytes 196616 | tf_op jit(solution)/shard_map/ppermute | solution.py:204
  5.0 6.8 %collective-permute-start.1 = (bf16[16,2048]{1,0:T(8,128)(2,1)S(1)}, bf16[16,2048]{1,0:T(8,128)(2,1)S(1)}, u32[]{:S(2)}, u32[]{:S(2)}) collective-permute-start(bf16[16,2048]{1,0:T(8,128)(2,1)S(1)} %get-tuple-element.48), channel_id=1, source_target_pairs={{0,2},{1,3},{2,0},{3,1},{4,6},{5,7},{6,4},{7,5},{8,10},{9,11},{10,... | collective-permute-start | bytes 196616 | tf_op jit(solution)/shard_map/ppermute | solution.py:204
  6.6 5.2 %collective-permute-start.2 = (bf16[16,2048]{1,0:T(8,128)(2,1)S(1)}, bf16[16,2048]{1,0:T(8,128)(2,1)S(1)}, u32[]{:S(2)}, u32[]{:S(2)}) collective-permute-start(bf16[16,2048]{1,0:T(8,128)(2,1)S(1)} %get-tuple-element.49), channel_id=1, source_target_pairs={{0,3},{1,2},{2,1},{3,0},{4,7},{5,6},{6,5},{7,4},{8,11},{9,10},{10,... | collective-permute-start | bytes 196616 | tf_op jit(solution)/shard_map/ppermute | solution.py:204
  6.6 11.7 %collective-permute-start.6 = (bf16[16,2048]{1,0:T(8,128)(2,1)S(1)}, bf16[16,2048]{1,0:T(8,128)(2,1)S(1)}, u32[]{:S(2)}, u32[]{:S(2)}) collective-permute-start(bf16[16,2048]{1,0:T(8,128)(2,1)S(1)} %get-tuple-element.55), channel_id=1, source_target_pairs={{0,7},{1,6},{2,5},{3,4},{4,3},{5,2},{6,1},{7,0},{8,15},{9,14},{10,... | collective-permute-start | bytes 196616 | tf_op jit(solution)/shard_map/ppermute | solution.py:204
  11.6 8.4 %collective-permute-start.5 = (bf16[16,2048]{1,0:T(8,128)(2,1)S(1)}, bf16[16,2048]{1,0:T(8,128)(2,1)S(1)}, u32[]{:S(2)}, u32[]{:S(2)}) collective-permute-start(bf16[16,2048]{1,0:T(8,128)(2,1)S(1)} %get-tuple-element.54), channel_id=1, source_target_pairs={{0,6},{1,7},{2,4},{3,5},{4,2},{5,3},{6,0},{7,1},{8,14},{9,15},{10,... | collective-permute-start | bytes 196616 | tf_op jit(solution)/shard_map/ppermute | solution.py:204
  11.8 9.1 %collective-permute-start.4 = (bf16[16,2048]{1,0:T(8,128)(2,1)S(1)}, bf16[16,2048]{1,0:T(8,128)(2,1)S(1)}, u32[]{:S(2)}, u32[]{:S(2)}) collective-permute-start(bf16[16,2048]{1,0:T(8,128)(2,1)S(1)} %get-tuple-element.53), channel_id=1, source_target_pairs={{0,5},{1,4},{2,7},{3,6},{4,1},{5,0},{6,3},{7,2},{8,13},{9,12},{10,... | collective-permute-start | bytes 196616 | tf_op jit(solution)/shard_map/ppermute | solution.py:204
  14.8 7.6 %collective-permute-start.3 = (bf16[16,2048]{1,0:T(8,128)(2,1)S(1)}, bf16[16,2048]{1,0:T(8,128)(2,1)S(1)}, u32[]{:S(2)}, u32[]{:S(2)}) collective-permute-start(bf16[16,2048]{1,0:T(8,128)(2,1)S(1)} %get-tuple-element.51), channel_id=1, source_target_pairs={{0,4},{1,5},{2,6},{3,7},{4,0},{5,1},{6,2},{7,3},{8,12},{9,13},{10,... | collective-permute-start | bytes 196616 | tf_op jit(solution)/shard_map/ppermute | solution.py:204
  14.8 7.6 %collective-permute-start.7 = (bf16[64,2048]{1,0:T(8,128)(2,1)S(1)}, bf16[64,2048]{1,0:T(8,128)(2,1)S(1)}, u32[]{:S(2)}, u32[]{:S(2)}) collective-permute-start(bf16[64,2048]{1,0:T(8,128)(2,1)S(1)} %constant_dynamic-update-slice_fusion.refs_0_), channel_id=1, source_target_pairs={{0,8},{8,0},{16,24},{24,16},{1,9},{9,1},{17,25},{25,17},{2,10},{10... | collective-permute-start | bytes 786440 | tf_op jit(solution)/shard_map/ppermute | solution.py:208
  18.4 8.8 %collective-permute-start.9 = (bf16[64,2048]{1,0:T(8,128)(2,1)S(1)}, bf16[64,2048]{1,0:T(8,128)(2,1)S(1)}, u32[]{:S(2)}, u32[]{:S(2)}) collective-permute-start(bf16[64,2048]{1,0:T(8,128)(2,1)S(1)} %constant_dynamic-update-slice_fusion.refs_0_), channel_id=1, source_target_pairs={{0,16},{8,24},{16,0},{24,8},{1,17},{9,25},{17,1},{25,9},{2,18},{10... | collective-permute-start | bytes 786440 | tf_op jit(solution)/shard_map/ppermute | solution.py:213
  26.1 7.4 %collective-permute-start.8 = (bf16[64,2048]{1,0:T(8,128)(2,1)S(1)}, bf16[64,2048]{1,0:T(8,128)(2,1)S(1)}, u32[]{:S(2)}, u32[]{:S(2)}) collective-permute-start(bf16[64,2048]{1,0:T(8,128)(2,1)S(1)} %pad_maximum_fusion.refs_1_), channel_id=1, source_target_pairs={{0,8},{8,0},{16,24},{24,16},{1,9},{9,1},{17,25},{25,17},{2,10},{10... | collective-permute-start | bytes 786440 | tf_op jit(solution)/shard_map/ppermute | solution.py:208
  27.1 6.3 %collective-permute-start.10 = (bf16[64,2048]{1,0:T(8,128)(2,1)S(1)}, bf16[64,2048]{1,0:T(8,128)(2,1)S(1)}, u32[]{:S(2)}, u32[]{:S(2)}) collective-permute-start(bf16[64,2048]{1,0:T(8,128)(2,1)S(1)} %collective-permute-done.9.refs_2_.refs_4_), channel_id=1, source_target_pairs={{0,8},{8,0},{16,24},{24,16},{1,9},{9,1},{17,25},{25,17},{2,10},{10... | collective-permute-start | bytes 786440 | tf_op jit(solution)/shard_map/ppermute | solution.py:208
  27.1 9.5 %collective-permute-start.18 = (bf16[64,2048]{1,0:T(8,128)(2,1)S(1)}, bf16[64,2048]{1,0:T(8,128)(2,1)S(1)}, u32[]{:S(2)}, u32[]{:S(2)}) collective-permute-start(bf16[64,2048]{1,0:T(8,128)(2,1)S(1)} %pad_maximum_fusion.refs_1_), channel_id=1, source_target_pairs={{0,16},{8,24},{16,0},{24,8},{1,17},{9,25},{17,1},{25,9},{2,18},{10... | collective-permute-start | bytes 786440 | tf_op jit(solution)/shard_map/ppermute | solution.py:213
  28.7 8.5 %collective-permute-start.16 = (bf16[16,1152]{1,0:T(8,128)(2,1)S(1)}, bf16[16,1152]{1,0:T(8,128)(2,1)S(1)}, u32[]{:S(2)}, u32[]{:S(2)}) collective-permute-start(bf16[16,1152]{1,0:T(8,128)(2,1)S(1)} %get-tuple-element.76), channel_id=1, source_target_pairs={{0,6},{1,7},{2,4},{3,5},{4,2},{5,3},{6,0},{7,1},{8,14},{9,15},{10,... | collective-permute-start | bytes 110600 | tf_op jit(solution)/shard_map/ppermute | solution.py:204
  32.3 15.7 %copy-start = (bf16[64,2]{0,1:T(2,128)(2,1)S(1)}, bf16[64,2]{0,1:T(2,128)(2,1)}, u32[]{:S(2)}) copy-start(bf16[64,2]{0,1:T(2,128)(2,1)} %param.9) | copy-start | bytes 772
  32.3 7.3 %collective-permute-start.17 = (bf16[16,1152]{1,0:T(8,128)(2,1)S(1)}, bf16[16,1152]{1,0:T(8,128)(2,1)S(1)}, u32[]{:S(2)}, u32[]{:S(2)}) collective-permute-start(bf16[16,1152]{1,0:T(8,128)(2,1)S(1)} %get-tuple-element.77), channel_id=1, source_target_pairs={{0,7},{1,6},{2,5},{3,4},{4,3},{5,2},{6,1},{7,0},{8,15},{9,14},{10,... | collective-permute-start | bytes 110600 | tf_op jit(solution)/shard_map/ppermute | solution.py:204
  36.1 5.8 %collective-permute-start.11 = (bf16[16,1152]{1,0:T(8,128)(2,1)S(1)}, bf16[16,1152]{1,0:T(8,128)(2,1)S(1)}, u32[]{:S(2)}, u32[]{:S(2)}) collective-permute-start(bf16[16,1152]{1,0:T(8,128)(2,1)S(1)} %get-tuple-element.67), channel_id=1, source_target_pairs={{0,1},{1,0},{2,3},{3,2},{4,5},{5,4},{6,7},{7,6},{8,9},{9,8},{10,11... | collective-permute-start | bytes 110600 | tf_op jit(solution)/shard_map/ppermute | solution.py:204
  36.7 12.7 %collective-permute-start.19 = (bf16[64,2048]{1,0:T(8,128)(2,1)S(1)}, bf16[64,2048]{1,0:T(8,128)(2,1)S(1)}, u32[]{:S(2)}, u32[]{:S(2)}) collective-permute-start(bf16[64,2048]{1,0:T(8,128)(2,1)S(1)} %collective-permute-done.18.refs_6_), channel_id=1, source_target_pairs={{0,8},{8,0},{16,24},{24,16},{1,9},{9,1},{17,25},{25,17},{2,10},{10... | collective-permute-start | bytes 786440 | tf_op jit(solution)/shard_map/ppermute | solution.py:208
  36.7 6.2 %collective-permute-start.12 = (bf16[16,1152]{1,0:T(8,128)(2,1)S(1)}, bf16[16,1152]{1,0:T(8,128)(2,1)S(1)}, u32[]{:S(2)}, u32[]{:S(2)}) collective-permute-start(bf16[16,1152]{1,0:T(8,128)(2,1)S(1)} %get-tuple-element.69), channel_id=1, source_target_pairs={{0,2},{1,3},{2,0},{3,1},{4,6},{5,7},{6,4},{7,5},{8,10},{9,11},{10,... | collective-permute-start | bytes 110600 | tf_op jit(solution)/shard_map/ppermute | solution.py:204
  37.2 5.6 %collective-permute-start.13 = (bf16[16,1152]{1,0:T(8,128)(2,1)S(1)}, bf16[16,1152]{1,0:T(8,128)(2,1)S(1)}, u32[]{:S(2)}, u32[]{:S(2)}) collective-permute-start(bf16[16,1152]{1,0:T(8,128)(2,1)S(1)} %get-tuple-element.71), channel_id=1, source_target_pairs={{0,3},{1,2},{2,1},{3,0},{4,7},{5,6},{6,5},{7,4},{8,11},{9,10},{10,... | collective-permute-start | bytes 110600 | tf_op jit(solution)/shard_map/ppermute | solution.py:204
  39.6 4.9 %collective-permute-start.14 = (bf16[16,1152]{1,0:T(8,128)(2,1)S(1)}, bf16[16,1152]{1,0:T(8,128)(2,1)S(1)}, u32[]{:S(2)}, u32[]{:S(2)}) collective-permute-start(bf16[16,1152]{1,0:T(8,128)(2,1)S(1)} %get-tuple-element.73), channel_id=1, source_target_pairs={{0,4},{1,5},{2,6},{3,7},{4,0},{5,1},{6,2},{7,3},{8,12},{9,13},{10,... | collective-permute-start | bytes 110600 | tf_op jit(solution)/shard_map/ppermute | solution.py:204
  41.9 6.2 %collective-permute-start.15 = (bf16[16,1152]{1,0:T(8,128)(2,1)S(1)}, bf16[16,1152]{1,0:T(8,128)(2,1)S(1)}, u32[]{:S(2)}, u32[]{:S(2)}) collective-permute-start(bf16[16,1152]{1,0:T(8,128)(2,1)S(1)} %get-tuple-element.75), channel_id=1, source_target_pairs={{0,5},{1,4},{2,7},{3,6},{4,1},{5,0},{6,3},{7,2},{8,13},{9,12},{10,... | collective-permute-start | bytes 110600 | tf_op jit(solution)/shard_map/ppermute | solution.py:204

commit v4 on v3

--- a/solution.py
+++ b/solution.py
@@ -96,6 +96,10 @@
         blocks[k][:, feat_width:] = s[k * capacity : (k + 1) * capacity]
 
 
+def block_rows(me, k, capacity):
+    return pl.ds(pl.multiple_of(jnp.bitwise_xor(me, k) * capacity, capacity), capacity)
+
+
 def load_kernel(in_hbm, out_hbm, weight_in, weight_out, sems):
     copies = [
         pltpu.make_async_copy(source, target, sems.at[i])
@@ -107,17 +111,18 @@
         copy.wait()
 
 
-def combine_kernel(experts, capacity, place0, place1, gates, *refs):
-    blocks, (token_grads, gate_grads, rows) = refs[:experts], refs[experts:]
+def combine_kernel(experts, capacity, place0, place1, gates, back, token_grads, gate_grads, rows):
     tok_count, feat_width = token_grads.shape
+    me = lax.axis_index("expert")
     for k in range(experts):
-        rows[k * capacity : (k + 1) * capacity, :] = blocks[k][...]
+        rows[k * capacity : (k + 1) * capacity, :] = back[block_rows(me, k, capacity), :]
     either = (place0[...].astype(F32) + place1[...].astype(F32)).astype(BF16)
     token_grads[...] = dot(either, rows[:, :feat_width], (0, 0)).astype(BF16)
     dgate = rows[:, feat_width : feat_width + tok_count].astype(F32)
-    for choice, place in ((0, place0), (1, place1)):
-        row = jnp.sum(place[...].astype(F32) * dgate, axis=0, keepdims=True)
-        gate_grads[choice : choice + 1, :] = row / gates[choice : choice + 1, :].astype(F32)
+    taken = [
+        jnp.sum(place[...].astype(F32) * dgate, axis=0, keepdims=True) for place in (place0, place1)
+    ]
+    gate_grads[...] = (jnp.concatenate(taken, axis=0) / gates[...].astype(F32)).astype(BF16)
 
 
 def stack(refs, part, width):
@@ -129,15 +134,13 @@
     return ref[:, pl.ds(pl.multiple_of(lax.axis_index("dp") * width, width), width)]
 
 
-def own_kernel(tile, pieces, experts, *refs):
-    row_refs, (weight_in, weight_out, d_pre, h_cut, *blocks, hidden) = (
-        refs[:pieces],
-        refs[pieces:],
-    )
+def own_kernel(tile, order, *refs):
+    row_refs, (weight_in, weight_out, d_pre, h_cut, back, hidden) = refs[:2], refs[2:]
+    me = lax.axis_index("expert")
     feat_width, ffw = weight_in.shape
     x, s = stack(row_refs, 0, feat_width), stack(row_refs, 1, feat_width)
     slots_all = x.shape[0]
-    capacity = slots_all // experts
+    capacity = slots_all // len(order)
     dgate = jnp.zeros((slots_all, LANES), F32)
     dx = jnp.zeros((slots_all, feat_width), F32)
     for at in range(0, ffw, tile):
@@ -153,10 +156,10 @@
         dx = dx + dot(part, weight_in[:, cols], (1, 1))
     h_cut[...] = my_part(hidden)
     dgate = jnp.broadcast_to(jnp.sum(dgate, axis=1, keepdims=True), (slots_all, LANES))
-    for k in range(experts):
-        rows = slice(k * capacity, (k + 1) * capacity)
-        blocks[k][:, :feat_width] = dx[rows].astype(BF16)
-        blocks[k][:, feat_width:] = dgate[rows].astype(BF16)
+    for i, k in enumerate(order):
+        rows, target = slice(i * capacity, (i + 1) * capacity), block_rows(me, k, capacity)
+        back[target, :feat_width] = dx[rows].astype(BF16)
+        back[target, feat_width:] = dgate[rows].astype(BF16)
 
 
 def backward_tiles(tile, x, s, weight_in, weight_out, hidden, d_pre, rows):
@@ -257,47 +260,44 @@
     weights = [
         pltpu.with_memory_space_constraint(w, pltpu.VMEM) for w in (weight_in, weight_out)
     ]
-    got = {0: blocks[0]}
-    near = list(range(1, half))
-    far = list(range(half, experts))
-    first, second = far[len(far) // 2 :], far[: len(far) // 2]
-    for k in near + first:
-        got[k] = permute(blocks[k], k)
-    for k in second:
-        got[k] = permute(after(blocks[k], *[got[j] for j in near]), k)
-    rows_a = jnp.concatenate([got[k] for k in range(half)], axis=0)
-    rows_b = jnp.concatenate([got[k] for k in range(half, experts)], axis=0)
-    core_a = swap_cores(rows_a)
+    rest = list(range(experts - 1, 1, -1))
+    order = [0, *rest[:2], 1, *rest[2:]]
+    order_a, order_b = order[:half], order[half:]
+    got_a = [blocks[0]] + [permute(blocks[k], k) for k in order_a[1:]]
+    got_b = [
+        permute(blocks[k] if i < 2 else after(blocks[k], *got_a[1:]), k)
+        for i, k in enumerate(order_b)
+    ]
+    rows_a = jnp.concatenate(got_a, axis=0)
     chips_a = [shift_chips(rows_a, k) for k in range(1, groups // 2)]
-    rows_b = after(rows_b, core_a)
+    core_a = swap_cores(after(rows_a, got_b[0]))
+    rows_b = jnp.concatenate(got_b, axis=0)
     chips_b = [shift_chips(rows_b, k) for k in range(1, groups // 2)]
-    d_pre0, h_cut0, *back = call(
-        functools.partial(own_kernel, tile, 2, experts),
-        [shape((slots_all, ffw)), shape((slots_all, tile))]
-        + [shape((capacity, feat_width + LANES))] * experts,
+    core_b = swap_cores(rows_b)
+    d_pre0, h_cut0, back = call(
+        functools.partial(own_kernel, tile, order),
+        [
+            shape((slots_all, ffw)),
+            shape((slots_all, tile)),
+            shape((slots_all, feat_width + LANES)),
+        ],
         [rows_a, rows_b, *weights],
-        3 * product,
+        20 * product,
         scratch=[pltpu.VMEM((slots_all, ffw), BF16)],
     )
+    back = lax.all_to_all(
+        back.reshape(experts, capacity, feat_width + LANES), "expert", 0, 0, tiled=True
+    ).reshape(slots_all, feat_width + LANES)
     relayed_a = [swap_cores(after(rows, d_pre0)) for rows in chips_a]
-    core_b = swap_cores(after(rows_b, d_pre0))
     early = [core_a, core_b, *chips_a, *relayed_a]
     early_rows = sum(piece.shape[0] for piece in early)
     d_pre1, h_cut1 = call(
         functools.partial(early_kernel, tile, len(early)),
         [shape((early_rows, ffw)), shape((early_rows, tile))],
         [*early, *weights],
-        2 * product * early_rows // slots_all,
+        product,
         scratch=[pltpu.VMEM((early_rows, ffw), BF16)],
     )
-    returned = {0: back[0]}
-    for k in first:
-        returned[k] = permute(back[k], k)
-    for k in second:
-        returned[k] = permute(after(back[k], core_b, *relayed_a), k)
-    for k in near:
-        returned[k] = permute(after(back[k], d_pre1), k)
-    back = [returned[k] for k in range(experts)]
     chips_b += [swap_cores(rows) for rows in chips_b]
     late_rows = sum(piece.shape[0] for piece in chips_b)
     grad_in, grad_out = call(
@@ -312,11 +312,11 @@
     )
     token_grads, gate_grads = call(
         functools.partial(combine_kernel, experts, capacity),
-        [shape((tok_count, feat_width)), shape((2, tok_count), F32)],
-        [*places, gates.T, *back],
+        [shape((tok_count, feat_width)), shape((2, tok_count))],
+        [*places, gates.T, back],
         scratch=[pltpu.VMEM((slots_all, feat_width + LANES), BF16)],
     )
-    return (token_grads, gate_grads.T.astype(BF16), grad_in[None], grad_out[None])
+    return (token_grads, gate_grads.T, grad_in[None], grad_out[None])
 
 
 def local_small_blocks(tokens, cotangent, routes, gates, proj_in, proj_out):

time: 53.9 us -> 56.8 us (1.054)
  local copies, waits for them, and re-layouts: 0.03 us -> 12 us
  starting transfers between devices: 27.5 us -> 22.1 us
  waiting for transfers between devices: 8.55 us -> 3.5 us
  Pallas kernels: 16.4 us -> 18 us
    unnamed x5 -> x28, local copies, waits for them, and re-layouts: 0.02 us -> 12 us
    ppermute x14 -> x7, starting transfers between devices: 24.2 us -> 12.6 us  [permute(): lax.ppermute(block, 'expert', [(i, i ^ k) for i in range(lax.axis_size('e...]
    ppermute x14 -> x7, waiting for transfers between devices: 7.53 us -> 1.86 us  [permute(): lax.ppermute(block, 'expert', [(i, i ^ k) for i in range(lax.axis_size('e...]
    all_to_all x0 -> x1, starting transfers between devices: none -> 5.24 us  [local(): lax.all_to_all(back.reshape(experts, capacity, feat_width + LANES), 'expe...]
    pallas_call x6, Pallas kernels: 16.4 us -> 18 us  [call(): pl.pallas_call(kernel, out_shape=out_shape, in_specs=[pl.BlockSpec(memory...]
    ppermute x4, waiting for transfers between devices: 0.01 us -> 1.63 us  [swap_cores(): lax.ppermute(rows, 'dp', [(i, i ^ 1) for i in range(lax.axis_size('dp'))])]
    ppermute x2, waiting for transfers between devices: 1.01 us -> 0.01 us  [shift_chips(): lax.ppermute(rows, 'dp', [(i, (i + 2 * k) % groups) for i in range(groups)])]
    ppermute x4, starting transfers between devices: 0.15 us -> 1.02 us  [swap_cores(): lax.ppermute(rows, 'dp', [(i, i ^ 1) for i in range(lax.axis_size('dp'))])]
  transfers between devices with their start and end apart: 20 -> 14, of which waited for: 5 -> 5; matrix products, arithmetic and copies ran while one was open for 1% -> 0% of each run, Pallas kernels for 20% -> 20%
where the time goes in v4:
time: 56.8 us; the launch traced here: 56.4 us
  starting transfers between devices  22.1 us (39%)
  Pallas kernels  18 us (32%)
  local copies, waits for them, and re-layouts  12 us (21%)
  waiting for transfers between devices  3.5 us (6%)
  between operations  0.76 us (1%)
    pallas_call x6, Pallas kernels, call(): pl.pallas_call(kernel, out_shape=out_shape, in_specs=[pl.BlockSpec(memory...  18 us
    ppermute x7, starting transfers between devices, permute(): lax.ppermute(block, 'expert', [(i, i ^ k) for i in range(lax.axis_size('e...  12.6 us
    unnamed x28, local copies, waits for them, and re-layouts  12 us
    all_to_all x1, starting transfers between devices, local(): lax.all_to_all(back.reshape(experts, capacity, feat_width + LANES), 'expe...  5.24 us
    ppermute x2, starting transfers between devices, shift_chips(): lax.ppermute(rows, 'dp', [(i, (i + 2 * k) % groups) for i in range(groups)])  3.23 us
    ppermute x7, waiting for transfers between devices, permute(): lax.ppermute(block, 'expert', [(i, i ^ k) for i in range(lax.axis_size('e...  1.86 us
    ppermute x4, waiting for transfers between devices, swap_cores(): lax.ppermute(rows, 'dp', [(i, i ^ 1) for i in range(lax.axis_size('dp'))])  1.63 us
  transfers between devices with their start and end apart: 14, of which 5 were waited for; matrix products, arithmetic and copies ran while one was open for 0% of the time, Pallas kernels for 20%

profile of v4, /device:TPU:0, one launch (start us, length us, event | category | flops | bytes accessed | tf_op | source)
XLA Modules:
  0.0 56.4 jit_solution(8029516939907385225)
XLA Ops:
  0.6 1.4 %shard_map.93 = (bf16[16,2048]{1,0:T(8,128)(2,1)S(1)}, bf16[16,2048]{1,0:T(8,128)(2,1)S(1)}, bf16[16,2048]{1,0:T(8,128)(2,1)S(1)}, bf16[16,2048]{1,0:T(8,128)(2,...) custom-call(s32[2,64]{1,0:T(2,128)} %bitcast.14, ...), custom_call_target="tpu_custom_call" | custom-call | bytes 262912 | tf_op jit(solution)/shard_map/pallas_call | solution.py:32
  2.0 6.0 %collective-permute-start = (bf16[16,2048]{1,0:T(8,128)(2,1)S(1)}, bf16[16,2048]{1,0:T(8,128)(2,1)S(1)}, u32[]{:S(2)}, u32[]{:S(2)}) collective-permute-start(bf16[16,2048]{1,0:T(8,128)(2,1)S(1)} %get-tuple-element.34), channel_id=1, source_target_pairs={{0,7},{1,6},{2,5},{3,4},{4,3},{5,2},{6,1},{7,0},{8,15},{9,14},{10,... | collective-permute-start | bytes 196616 | tf_op jit(solution)/shard_map/ppermute | solution.py:207
  8.1 0.2 collective-permute-start.1
  8.3 0.4 collective-permute-start.2
  8.7 1.8 %collective-permute-start.3 = (bf16[16,2048]{1,0:T(8,128)(2,1)S(1)}, bf16[16,2048]{1,0:T(8,128)(2,1)S(1)}, u32[]{:S(2)}, u32[]{:S(2)}) collective-permute-start(bf16[16,2048]{1,0:T(8,128)(2,1)S(1)} %get-tuple-element.37), channel_id=1, source_target_pairs={{0,5},{1,4},{2,7},{3,6},{4,1},{5,0},{6,3},{7,2},{8,13},{9,12},{10,... | collective-permute-start | bytes 196616 | tf_op jit(solution)/shard_map/ppermute | solution.py:207
  10.6 2.1 %collective-permute-start.4 = (bf16[16,2048]{1,0:T(8,128)(2,1)S(1)}, bf16[16,2048]{1,0:T(8,128)(2,1)S(1)}, u32[]{:S(2)}, u32[]{:S(2)}) collective-permute-start(bf16[16,2048]{1,0:T(8,128)(2,1)S(1)} %get-tuple-element.38), channel_id=1, source_target_pairs={{0,4},{1,5},{2,6},{3,7},{4,0},{5,1},{6,2},{7,3},{8,12},{9,13},{10,... | collective-permute-start | bytes 196616 | tf_op jit(solution)/shard_map/ppermute | solution.py:207
  12.7 3.5 %shard_map.94 = (bf16[1024,2048]{1,0:T(8,128)(2,1)S(1)}, bf16[2048,1024]{1,0:T(8,128)(2,1)S(1)}) custom-call(bf16[1024,2048]{1,0:T(8,128)(2,1)} %bitcast.12, bf16[2048,1024]{1,0:T(8,128)(2,1)} %bitcast.13), custom_call_target="tpu_custom_call" | custom-call | bytes 8388608 | tf_op jit(solution)/shard_map/pallas_call | solution.py:32
  16.2 0.0 copy-start
  16.2 0.0 copy-start.3
  16.2 0.0 collective-permute-done
  16.2 0.0 collective-permute-done.1
  16.2 0.0 collective-permute-done.2
  16.2 1.3 %collective-permute-start.5 = (bf16[16,2048]{1,0:T(8,128)(2,1)S(1)}, bf16[16,2048]{1,0:T(8,128)(2,1)S(1)}, u32[]{:S(2)}, u32[]{:S(2)}) collective-permute-start(bf16[16,2048]{1,0:T(8,128)(2,1)S(1)} %get-tuple-element.40), channel_id=1, source_target_pairs={{0,3},{1,2},{2,1},{3,0},{4,7},{5,6},{6,5},{7,4},{8,11},{9,10},{10,... | collective-permute-start | bytes 196616 | tf_op jit(solution)/shard_map/ppermute | solution.py:207
  17.6 0.6 %collective-permute-start.6 = (bf16[16,2048]{1,0:T(8,128)(2,1)S(1)}, bf16[16,2048]{1,0:T(8,128)(2,1)S(1)}, u32[]{:S(2)}, u32[]{:S(2)}) collective-permute-start(bf16[16,2048]{1,0:T(8,128)(2,1)S(1)} %get-tuple-element.42), channel_id=1, source_target_pairs={{0,2},{1,3},{2,0},{3,1},{4,6},{5,7},{6,4},{7,5},{8,10},{9,11},{10,... | collective-permute-start | bytes 196616 | tf_op jit(solution)/shard_map/ppermute | solution.py:207
  18.2 1.7 %collective-permute-start.9 = (bf16[64,2048]{1,0:T(8,128)(2,1)S(1)}, bf16[64,2048]{1,0:T(8,128)(2,1)S(1)}, u32[]{:S(2)}, u32[]{:S(2)}) collective-permute-start(bf16[64,2048]{1,0:T(8,128)(2,1)S(1)} %constant_dynamic-update-slice_fusion.refs_0_), channel_id=1, source_target_pairs={{0,16},{8,24},{16,0},{24,8},{1,17},{9,25},{17,1},{25,9},{2,18},{10... | collective-permute-start | bytes 786440 | tf_op jit(solution)/shard_map/ppermute | solution.py:216
  19.9 0.0 collective-permute-done.3
  19.9 0.0 collective-permute-done.4
  20.0 1.5 %collective-permute-done.5 = bf16[16,2048]{1,0:T(8,128)(2,1)S(1)} collective-permute-done((bf16[16,2048]{1,0:T(8,128)(2,1)S(1)}, bf16[16,2048]{1,0:T(8,128)(2,1)S(1)}, u32[]{:S(2)}, u32[]{:S(2)}) %collective-permute-start.5) | collective-permute-done | bytes 65568 | tf_op jit(solution)/shard_map/ppermute | solution.py:207
  21.5 0.3 collective-permute-done.6
  21.8 1.5 %collective-permute-start.11 = (bf16[64,2048]{1,0:T(8,128)(2,1)S(1)}, bf16[64,2048]{1,0:T(8,128)(2,1)}, u32[]{:S(2)}, u32[]{:S(2)}) collective-permute-start(bf16[64,2048]{1,0:T(8,128)(2,1)S(1)} %constant_dynamic-update-slice_fusion.4.refs_1_), channel_id=1, source_target_pairs={{0,16},{8,24},{16,0},{24,8},{1,17},{9,25},{17,1},{25,9},{2,18},{10... | collective-permute-start | bytes 786440 | tf_op jit(solution)/shard_map/ppermute | solution.py:216
  23.3 4.4 %shard_map.95 = (bf16[128,2048]{1,0:T(8,128)(2,1)S(1)}, bf16[128,512]{1,0:T(8,128)(2,1)S(1)}, bf16[128,1152]{1,0:T(8,128)(2,1)}) custom-call(bf16[64,2048]{1,0:T(8,128)(2,1)S(1)} %constant_dynamic-update-slice_fusion.refs_0_, bf16[64,2048]{1,0:T(8,128)(2,1)S(1)} %constant_dynamic-update-slice_fusion.4.refs_1_, ...), custom_call_target="tpu_custom_call" | custom-call | flops 10737418240 | bytes 8912896 | tf_op jit(solution)/shard_map/pallas_call | solution.py:32
  27.7 0.0 copy-done
  27.8 0.0 copy-done.3
  27.8 0.0 copy-start.8
  27.8 0.6 %copy-done.8 = bf16[128,512]{1,0:T(8,128)(2,1)} copy-done((bf16[128,512]{1,0:T(8,128)(2,1)}, bf16[128,512]{1,0:T(8,128)(2,1)S(1)}, u32[]{:S(2)}) %copy-start.8) | copy-done | bytes 131096
  28.4 5.2 %all-to-all-start = ((bf16[8,16,1152]{2,1,0:T(8,128)(2,1)}), bf16[8,16,1152]{2,1,0:T(8,128)(2,1)S(1)}, u32[]{:S(2)}, u32[]{:S(2)}) async-start(bf16[8,16,1152]{2,1,0:T(8,128)(2,1)} %bitcast.4), calls=%async_computation | async-start | bytes 589824 | tf_op jit(solution)/shard_map/all_to_all | solution.py:288
  33.6 0.0 collective-permute-start.7
  33.7 0.5 collective-permute-start.8
  34.2 0.0 collective-permute-done.9.refs_2_.refs_4_
  34.2 0.0 copy-start.10
  34.2 0.1 collective-permute-start.10
  34.2 0.0 collective-permute-done.11.refs_6_
  34.2 0.4 collective-permute-start.12
  34.7 0.5 collective-permute-done.7.refs_0_.refs_2_
  35.2 0.4 collective-permute-done.8.refs_1_.refs_3_
  35.6 0.7 %collective-permute-done.10.refs_3_.refs_5_ = bf16[64,2048]{1,0:T(8,128)(2,1)S(1)} collective-permute-done((bf16[64,2048]{1,0:T(8,128)(2,1)S(1)}, bf16[64,2048]{1,0:T(8,128)(2,1)S(1)}, u32[]{:S(2)}, u32[]{:S(2)}) %collective-permute-start.10) | collective-permute-done | bytes 262176 | tf_op jit(solution)/shard_map/ppermute | solution.py:211
  36.3 0.0 copy-start.1
  36.3 2.2 %copy-done.1 = bf16[1024,2048]{1,0:T(8,128)(2,1)S(1)} copy-done((bf16[1024,2048]{1,0:T(8,128)(2,1)S(1)}, bf16[1024,2048]{1,0:T(8,128)(2,1)}, u32[]{:S(2)}) %copy-start.1) | copy-done | bytes 4194328
  38.5 0.0 copy-start.4
  38.5 2.2 %copy-done.4 = bf16[2048,1024]{1,0:T(8,128)(2,1)S(1)} copy-done((bf16[2048,1024]{1,0:T(8,128)(2,1)S(1)}, bf16[2048,1024]{1,0:T(8,128)(2,1)}, u32[]{:S(2)}) %copy-start.4) | copy-done | bytes 4194328
  40.7 2.6 %shard_map.97 = (bf16[256,2048]{1,0:T(8,128)(2,1)S(1)}, bf16[256,512]{1,0:T(8,128)(2,1)S(1)}) custom-call(bf16[64,2048]{1,0:T(8,128)(2,1)S(1)} %collective-permute-done.7.refs_0_.refs_2_, bf16[64,2048]{1,0:T(8,128)(2,1)S(1)} %collective-permute-done.8.refs_1_.refs_3_, bf16[64,2048]{1,0:T(8,128)(2,1)S(1)} %collective-permute-done.9.refs_2_.refs_4_, ...), custom_call_target="tpu_custom_call" | custom-call | flops 536870912 | bytes 9437184 | tf_op jit(solution)/shard_map/pallas_call | solution.py:32
  43.3 0.0 copy-start.6
  43.3 0.7 %copy-done.6 = bf16[256,512]{1,0:T(8,128)(2,1)} copy-done((bf16[256,512]{1,0:T(8,128)(2,1)}, bf16[256,512]{1,0:T(8,128)(2,1)S(1)}, u32[]{:S(2)}) %copy-start.6) | copy-done | bytes 262168
  44.0 0.0 all-to-all-done
  44.0 0.0 copy-done.10
  44.0 0.9 %shard_map.96 = (bf16[64,1024]{1,0:T(8,128)(2,1)}, bf16[2,64]{1,0:T(2,128)(2,1)}) custom-call(bf16[128,64]{1,0:T(8,128)(2,1)S(1)} %get-tuple-element.31.place0, bf16[128,64]{1,0:T(8,128)(2,1)S(1)} %get-tuple-element.32.place1, bf16[2,64]{1,0:T(2,128)(2,1)S(1)} %bitcast.11, bf16[128,1152]{1,0:T(8,128)(2,1)S(1)} %bitcast.9), custom_call_target="tpu_custom_call" | custom-call | bytes 327936 | tf_op jit(solution)/shard_map/pallas_call | solution.py:32
  44.9 0.0 collective-permute-done.12.refs_7_
  44.9 0.0 copy-start.2
  44.9 2.2 %copy-done.2 = bf16[1024,2048]{1,0:T(8,128)(2,1)S(1)} copy-done((bf16[1024,2048]{1,0:T(8,128)(2,1)S(1)}, bf16[1024,2048]{1,0:T(8,128)(2,1)}, u32[]{:S(2)}) %copy-start.2) | copy-done | bytes 4194328
  47.1 0.0 copy-start.5
  47.1 2.2 %copy-done.5 = bf16[2048,1024]{1,0:T(8,128)(2,1)S(1)} copy-done((bf16[2048,1024]{1,0:T(8,128)(2,1)S(1)}, bf16[2048,1024]{1,0:T(8,128)(2,1)}, u32[]{:S(2)}) %copy-start.5) | copy-done | bytes 4194328
  49.3 0.0 copy-start.7
  49.3 0.9 %copy-done.7 = bf16[256,512]{1,0:T(8,128)(2,1)S(1)} copy-done((bf16[256,512]{1,0:T(8,128)(2,1)S(1)}, bf16[256,512]{1,0:T(8,128)(2,1)}, u32[]{:S(2)}) %copy-start.7) | copy-done | bytes 262168
  50.2 0.0 copy-start.9
  50.2 0.9 %copy-done.9 = bf16[128,512]{1,0:T(8,128)(2,1)S(1)} copy-done((bf16[128,512]{1,0:T(8,128)(2,1)S(1)}, bf16[128,512]{1,0:T(8,128)(2,1)}, u32[]{:S(2)}) %copy-start.9) | copy-done | bytes 131096
  51.1 5.3 %shard_map.98 = (bf16[256,2048]{1,0:T(8,128)(2,1)}, bf16[512,1024]{1,0:T(8,128)(2,1)}) custom-call(bf16[64,2048]{1,0:T(8,128)(2,1)S(1)} %constant_dynamic-update-slice_fusion.refs_0_, bf16[64,2048]{1,0:T(8,128)(2,1)S(1)} %constant_dynamic-update-slice_fusion.4.refs_1_, bf16[64,2048]{1,0:T(8,128)(2,1)S(1)} %collective-permute-done.7.refs_0_.refs_2_, ...), custom_call_target="tpu_custom_call" | custom-call | flops 2147483648 | bytes 12451840 | tf_op jit(solution)/shard_map/pallas_call | solution.py:32
  (8 shorter events, 0.0 us)
Async XLA Ops:
  2.0 14.2 %collective-permute-start = (bf16[16,2048]{1,0:T(8,128)(2,1)S(1)}, bf16[16,2048]{1,0:T(8,128)(2,1)S(1)}, u32[]{:S(2)}, u32[]{:S(2)}) collective-permute-start(bf16[16,2048]{1,0:T(8,128)(2,1)S(1)} %get-tuple-element.34), channel_id=1, source_target_pairs={{0,7},{1,6},{2,5},{3,4},{4,3},{5,2},{6,1},{7,0},{8,15},{9,14},{10,... | collective-permute-start | bytes 196616 | tf_op jit(solution)/shard_map/ppermute | solution.py:207
  8.1 8.1 %collective-permute-start.1 = (bf16[16,2048]{1,0:T(8,128)(2,1)S(1)}, bf16[16,2048]{1,0:T(8,128)(2,1)S(1)}, u32[]{:S(2)}, u32[]{:S(2)}) collective-permute-start(bf16[16,2048]{1,0:T(8,128)(2,1)S(1)} %get-tuple-element.35), channel_id=1, source_target_pairs={{0,6},{1,7},{2,4},{3,5},{4,2},{5,3},{6,0},{7,1},{8,14},{9,15},{10,... | collective-permute-start | bytes 196616 | tf_op jit(solution)/shard_map/ppermute | solution.py:207
  8.3 7.9 %collective-permute-start.2 = (bf16[16,2048]{1,0:T(8,128)(2,1)S(1)}, bf16[16,2048]{1,0:T(8,128)(2,1)S(1)}, u32[]{:S(2)}, u32[]{:S(2)}) collective-permute-start(bf16[16,2048]{1,0:T(8,128)(2,1)S(1)} %get-tuple-element.36), channel_id=1, source_target_pairs={{0,1},{1,0},{2,3},{3,2},{4,5},{5,4},{6,7},{7,6},{8,9},{9,8},{10,11... | collective-permute-start | bytes 196616 | tf_op jit(solution)/shard_map/ppermute | solution.py:207
  8.7 11.2 %collective-permute-start.3 = (bf16[16,2048]{1,0:T(8,128)(2,1)S(1)}, bf16[16,2048]{1,0:T(8,128)(2,1)S(1)}, u32[]{:S(2)}, u32[]{:S(2)}) collective-permute-start(bf16[16,2048]{1,0:T(8,128)(2,1)S(1)} %get-tuple-element.37), channel_id=1, source_target_pairs={{0,5},{1,4},{2,7},{3,6},{4,1},{5,0},{6,3},{7,2},{8,13},{9,12},{10,... | collective-permute-start | bytes 196616 | tf_op jit(solution)/shard_map/ppermute | solution.py:207
  10.6 9.4 %collective-permute-start.4 = (bf16[16,2048]{1,0:T(8,128)(2,1)S(1)}, bf16[16,2048]{1,0:T(8,128)(2,1)S(1)}, u32[]{:S(2)}, u32[]{:S(2)}) collective-permute-start(bf16[16,2048]{1,0:T(8,128)(2,1)S(1)} %get-tuple-element.38), channel_id=1, source_target_pairs={{0,4},{1,5},{2,6},{3,7},{4,0},{5,1},{6,2},{7,3},{8,12},{9,13},{10,... | collective-permute-start | bytes 196616 | tf_op jit(solution)/shard_map/ppermute | solution.py:207
  16.2 11.6 %copy-start = (bf16[1024,2048]{1,0:T(8,128)(2,1)}, bf16[1024,2048]{1,0:T(8,128)(2,1)S(1)}, u32[]{:S(2)}) copy-start(bf16[1024,2048]{1,0:T(8,128)(2,1)S(1)} %get-tuple-element.45.refs_2_.refs_4_.refs_12_) | copy-start | bytes 12582916
  16.2 11.6 %copy-start.3 = (bf16[2048,1024]{1,0:T(8,128)(2,1)}, bf16[2048,1024]{1,0:T(8,128)(2,1)S(1)}, u32[]{:S(2)}) copy-start(bf16[2048,1024]{1,0:T(8,128)(2,1)S(1)} %get-tuple-element.46.refs_3_.refs_5_.refs_13_) | copy-start | bytes 12582916
  16.2 5.2 %collective-permute-start.5 = (bf16[16,2048]{1,0:T(8,128)(2,1)S(1)}, bf16[16,2048]{1,0:T(8,128)(2,1)S(1)}, u32[]{:S(2)}, u32[]{:S(2)}) collective-permute-start(bf16[16,2048]{1,0:T(8,128)(2,1)S(1)} %get-tuple-element.40), channel_id=1, source_target_pairs={{0,3},{1,2},{2,1},{3,0},{4,7},{5,6},{6,5},{7,4},{8,11},{9,10},{10,... | collective-permute-start | bytes 196616 | tf_op jit(solution)/shard_map/ppermute | solution.py:207
  17.6 4.3 %collective-permute-start.6 = (bf16[16,2048]{1,0:T(8,128)(2,1)S(1)}, bf16[16,2048]{1,0:T(8,128)(2,1)S(1)}, u32[]{:S(2)}, u32[]{:S(2)}) collective-permute-start(bf16[16,2048]{1,0:T(8,128)(2,1)S(1)} %get-tuple-element.42), channel_id=1, source_target_pairs={{0,2},{1,3},{2,0},{3,1},{4,6},{5,7},{6,4},{7,5},{8,10},{9,11},{10,... | collective-permute-start | bytes 196616 | tf_op jit(solution)/shard_map/ppermute | solution.py:207
  18.2 15.9 %collective-permute-start.9 = (bf16[64,2048]{1,0:T(8,128)(2,1)S(1)}, bf16[64,2048]{1,0:T(8,128)(2,1)S(1)}, u32[]{:S(2)}, u32[]{:S(2)}) collective-permute-start(bf16[64,2048]{1,0:T(8,128)(2,1)S(1)} %constant_dynamic-update-slice_fusion.refs_0_), channel_id=1, source_target_pairs={{0,16},{8,24},{16,0},{24,8},{1,17},{9,25},{17,1},{25,9},{2,18},{10... | collective-permute-start | bytes 786440 | tf_op jit(solution)/shard_map/ppermute | solution.py:216
  21.8 12.4 %collective-permute-start.11 = (bf16[64,2048]{1,0:T(8,128)(2,1)S(1)}, bf16[64,2048]{1,0:T(8,128)(2,1)}, u32[]{:S(2)}, u32[]{:S(2)}) collective-permute-start(bf16[64,2048]{1,0:T(8,128)(2,1)S(1)} %constant_dynamic-update-slice_fusion.4.refs_1_), channel_id=1, source_target_pairs={{0,16},{8,24},{16,0},{24,8},{1,17},{9,25},{17,1},{25,9},{2,18},{10... | collective-permute-start | bytes 786440 | tf_op jit(solution)/shard_map/ppermute | solution.py:216
  27.8 0.7 %copy-start.8 = (bf16[128,512]{1,0:T(8,128)(2,1)}, bf16[128,512]{1,0:T(8,128)(2,1)S(1)}, u32[]{:S(2)}) copy-start(bf16[128,512]{1,0:T(8,128)(2,1)S(1)} %get-tuple-element.53.refs_9_) | copy-start | bytes 393220
  28.4 15.6 %all-to-all-start = ((bf16[8,16,1152]{2,1,0:T(8,128)(2,1)}), bf16[8,16,1152]{2,1,0:T(8,128)(2,1)S(1)}, u32[]{:S(2)}, u32[]{:S(2)}) async-start(bf16[8,16,1152]{2,1,0:T(8,128)(2,1)} %bitcast.4), calls=%async_computation | async-start | bytes 589824 | tf_op jit(solution)/shard_map/all_to_all | solution.py:288
  33.6 1.5 %collective-permute-start.7 = (bf16[64,2048]{1,0:T(8,128)(2,1)S(1)}, bf16[64,2048]{1,0:T(8,128)(2,1)S(1)}, u32[]{:S(2)}, u32[]{:S(2)}) collective-permute-start(bf16[64,2048]{1,0:T(8,128)(2,1)S(1)} %constant_dynamic-update-slice_fusion.refs_0_), channel_id=1, source_target_pairs={{0,8},{8,0},{16,24},{24,16},{1,9},{9,1},{17,25},{25,17},{2,10},{10... | collective-permute-start | bytes 786440 | tf_op jit(solution)/shard_map/ppermute | solution.py:211
  33.7 1.9 %collective-permute-start.8 = (bf16[64,2048]{1,0:T(8,128)(2,1)S(1)}, bf16[64,2048]{1,0:T(8,128)(2,1)S(1)}, u32[]{:S(2)}, u32[]{:S(2)}) collective-permute-start(bf16[64,2048]{1,0:T(8,128)(2,1)S(1)} %constant_dynamic-update-slice_fusion.4.refs_1_), channel_id=1, source_target_pairs={{0,8},{8,0},{16,24},{24,16},{1,9},{9,1},{17,25},{25,17},{2,10},{10... | collective-permute-start | bytes 786440 | tf_op jit(solution)/shard_map/ppermute | solution.py:211
  34.2 9.8 %copy-start.10 = (bf16[64,2]{0,1:T(2,128)(2,1)S(1)}, bf16[64,2]{0,1:T(2,128)(2,1)}, u32[]{:S(2)}) copy-start(bf16[64,2]{0,1:T(2,128)(2,1)} %param.9) | copy-start | bytes 772
  34.2 2.1 %collective-permute-start.10 = (bf16[64,2048]{1,0:T(8,128)(2,1)S(1)}, bf16[64,2048]{1,0:T(8,128)(2,1)S(1)}, u32[]{:S(2)}, u32[]{:S(2)}) collective-permute-start(bf16[64,2048]{1,0:T(8,128)(2,1)S(1)} %collective-permute-done.9.refs_2_.refs_4_), channel_id=1, source_target_pairs={{0,8},{8,0},{16,24},{24,16},{1,9},{9,1},{17,25},{25,17},{2,10},{10... | collective-permute-start | bytes 786440 | tf_op jit(solution)/shard_map/ppermute | solution.py:211
  34.2 10.7 %collective-permute-start.12 = (bf16[64,2048]{1,0:T(8,128)(2,1)}, bf16[64,2048]{1,0:T(8,128)(2,1)}, u32[]{:S(2)}, u32[]{:S(2)}) collective-permute-start(bf16[64,2048]{1,0:T(8,128)(2,1)} %collective-permute-done.11.refs_6_), channel_id=1, source_target_pairs={{0,8},{8,0},{16,24},{24,16},{1,9},{9,1},{17,25},{25,17},{2,10},{10... | collective-permute-start | bytes 786440 | tf_op jit(solution)/shard_map/ppermute | solution.py:211
  36.3 2.2 %copy-start.1 = (bf16[1024,2048]{1,0:T(8,128)(2,1)S(1)}, bf16[1024,2048]{1,0:T(8,128)(2,1)}, u32[]{:S(2)}) copy-start(bf16[1024,2048]{1,0:T(8,128)(2,1)} %copy-done) | copy-start | bytes 12582916
  38.5 2.2 %copy-start.4 = (bf16[2048,1024]{1,0:T(8,128)(2,1)S(1)}, bf16[2048,1024]{1,0:T(8,128)(2,1)}, u32[]{:S(2)}) copy-start(bf16[2048,1024]{1,0:T(8,128)(2,1)} %copy-done.3) | copy-start | bytes 12582916
  43.3 0.7 %copy-start.6 = (bf16[256,512]{1,0:T(8,128)(2,1)}, bf16[256,512]{1,0:T(8,128)(2,1)S(1)}, u32[]{:S(2)}) copy-start(bf16[256,512]{1,0:T(8,128)(2,1)S(1)} %get-tuple-element.55.refs_11_) | copy-start | bytes 786436
  44.9 2.2 %copy-start.2 = (bf16[1024,2048]{1,0:T(8,128)(2,1)S(1)}, bf16[1024,2048]{1,0:T(8,128)(2,1)}, u32[]{:S(2)}) copy-start(bf16[1024,2048]{1,0:T(8,128)(2,1)} %copy-done) | copy-start | bytes 12582916
  47.1 2.2 %copy-start.5 = (bf16[2048,1024]{1,0:T(8,128)(2,1)S(1)}, bf16[2048,1024]{1,0:T(8,128)(2,1)}, u32[]{:S(2)}) copy-start(bf16[2048,1024]{1,0:T(8,128)(2,1)} %copy-done.3) | copy-start | bytes 12582916
  49.3 0.9 %copy-start.7 = (bf16[256,512]{1,0:T(8,128)(2,1)S(1)}, bf16[256,512]{1,0:T(8,128)(2,1)}, u32[]{:S(2)}) copy-start(bf16[256,512]{1,0:T(8,128)(2,1)} %copy-done.6) | copy-start | bytes 786436
  50.2 0.9 %copy-start.9 = (bf16[128,512]{1,0:T(8,128)(2,1)S(1)}, bf16[128,512]{1,0:T(8,128)(2,1)}, u32[]{:S(2)}) copy-start(bf16[128,512]{1,0:T(8,128)(2,1)} %copy-done.8) | copy-start | bytes 393220

commit v5 on v4

--- a/solution.py
+++ b/solution.py
@@ -25,15 +25,21 @@
     return (pre_act * cdf).astype(BF16), cdf + pre_act * pdf
 
 
-def call(kernel, out_shape, args, flops=0, limit=24, scratch=(), in_space=pltpu.VMEM):
+def call(kernel, out_shape, args, flops=0, limit=24, scratch=(), spaces=None):
+    spaces = spaces or [pltpu.VMEM] * len(args)
     moved = sum(a.size * a.dtype.itemsize for a in args)
-    if in_space == pltpu.HBM:
-        args = [pltpu.with_memory_space_constraint(a, pltpu.HBM) for a in args]
+    args = [
+        pltpu.with_memory_space_constraint(a, space) if space == pltpu.HBM else a
+        for a, space in zip(args, spaces)
+    ]
     return pl.pallas_call(
         kernel,
         out_shape=out_shape,
-        in_specs=[pl.BlockSpec(memory_space=in_space)] * len(args),
-        out_specs=jax.tree.map(lambda _: pl.BlockSpec(memory_space=pltpu.VMEM), out_shape),
+        in_specs=[pl.BlockSpec(memory_space=space) for space in spaces],
+        out_specs=[
+            pl.BlockSpec(memory_space=getattr(out, "memory_space", pltpu.VMEM))
+            for out in out_shape
+        ],
         scratch_shapes=list(scratch),
         compiler_params=pltpu.CompilerParams(vmem_limit_bytes=limit * MIB),
         cost_estimate=pl.CostEstimate(flops=flops, bytes_accessed=moved, transcendentals=0),
@@ -135,7 +141,8 @@
 
 
 def own_kernel(tile, order, *refs):
-    row_refs, (weight_in, weight_out, d_pre, h_cut, back, hidden) = refs[:2], refs[2:]
+    row_refs, (weight_in, weight_out, d_pre_hbm, h_cut, back_hbm, *scratch) = refs[:2], refs[2:]
+    hidden, d_pre, back, sems = scratch
     me = lax.axis_index("expert")
     feat_width, ffw = weight_in.shape
     x, s = stack(row_refs, 0, feat_width), stack(row_refs, 1, feat_width)
@@ -154,49 +161,79 @@
         for lane in range(0, tile, LANES):
             dgate = dgate + product[:, lane : lane + LANES]
         dx = dx + dot(part, weight_in[:, cols], (1, 1))
-    h_cut[...] = my_part(hidden)
+    d_pre_out = pltpu.make_async_copy(d_pre, d_pre_hbm, sems.at[0])
+    d_pre_out.start()
     dgate = jnp.broadcast_to(jnp.sum(dgate, axis=1, keepdims=True), (slots_all, LANES))
     for i, k in enumerate(order):
         rows, target = slice(i * capacity, (i + 1) * capacity), block_rows(me, k, capacity)
         back[target, :feat_width] = dx[rows].astype(BF16)
         back[target, feat_width:] = dgate[rows].astype(BF16)
-
-
-def backward_tiles(tile, x, s, weight_in, weight_out, hidden, d_pre, rows):
-    for at in range(0, weight_in.shape[1], tile):
-        cols = slice(at, at + tile)
+    back_out = pltpu.make_async_copy(back, back_hbm, sems.at[1])
+    back_out.start()
+    h_cut[...] = my_part(hidden)
+    d_pre_out.wait()
+    back_out.wait()
+
+
+def grads_kernel(tile, pieces, *refs):
+    row_refs, refs = refs[:pieces], refs[pieces:]
+    d_pre0, h_cut0, in_hbm, out_hbm, grad_in_hbm, grad_out_hbm = refs[:6]
+    rows, weight_in, weight_out, hidden, h_cut, d_pre, grad_in, grad_out, sems, out_sems = refs[6:]
+    width, ffw = weight_in.shape
+    tiles = [slice(at, at + tile) for at in range(0, ffw, tile)]
+    own = d_pre0.shape[0]
+    piece = row_refs[0].shape[0]
+    todo = []
+
+    def fetch(source, target):
+        todo.append(pltpu.make_async_copy(source, target, sems.at[len(todo)]))
+        todo[-1].start()
+        return todo[-1]
+
+    first = [
+        fetch(ref, rows.at[pl.ds(i * piece, piece)])
+        for i, ref in enumerate(row_refs)
+        if i * piece >= own
+    ]
+    weights = [
+        fetch(*pair)
+        for cols in tiles
+        for pair in (
+            (in_hbm.at[:, cols], weight_in.at[:, cols]),
+            (out_hbm.at[cols, :], weight_out.at[cols, :]),
+        )
+    ]
+    rest = [
+        fetch(ref, rows.at[pl.ds(i * piece, piece)])
+        for i, ref in enumerate(row_refs)
+        if i * piece < own
+    ]
+    rest += [fetch(d_pre0, d_pre.at[:own, :]), fetch(h_cut0, h_cut.at[:own, :])]
+    for copy in first + weights[:2]:
+        copy.wait()
+    x, s = rows[own:, :width], rows[own:, width:]
+    cut = grad_in.shape[0]
+    mine = pl.ds(pl.multiple_of(lax.axis_index("dp") * cut, cut), cut)
+    outs = []
+    for t, cols in enumerate(tiles):
+        if t == 1:
+            for copy in weights[2:] + rest:
+                copy.wait()
         act, slope = gelu_and_slope(dot(x, weight_in[:, cols]))
         hidden[:, cols] = act
-        d_pre[rows, cols] = (dot(s, weight_out[cols, :], (1, 1)) * slope).astype(BF16)
-
-
-def early_kernel(tile, pieces, *refs):
-    row_refs, (weight_in, weight_out, d_pre, h_cut, hidden) = refs[:pieces], refs[pieces:]
-    width = weight_in.shape[0]
-    x, s = stack(row_refs, 0, width), stack(row_refs, 1, width)
-    backward_tiles(tile, x, s, weight_in, weight_out, hidden, d_pre, slice(None))
-    h_cut[...] = my_part(hidden)
-
-
-def grads_kernel(tile, own, early, late, *refs):
-    pieces = own + early + late
-    row_refs, refs = refs[:pieces], refs[pieces:]
-    d_pre0, h_cut0, d_pre1, h_cut1, weight_in, weight_out, grad_in, grad_out = refs[:8]
-    hidden, d_pre = refs[8:]
-    width, ffw = weight_in.shape
-    x, s = stack(row_refs[-late:], 0, width), stack(row_refs[-late:], 1, width)
-    first, second = d_pre0.shape[0], d_pre0.shape[0] + d_pre1.shape[0]
-    d_pre[:first, :] = d_pre0[...]
-    d_pre[first:second, :] = d_pre1[...]
-    cut = grad_in.shape[0]
-    mine = pl.ds(pl.multiple_of(lax.axis_index("dp") * cut, cut), cut)
-    x_cut = jnp.concatenate([ref[:, mine] for ref in row_refs], axis=0)
-    backward_tiles(tile, x, s, weight_in, weight_out, hidden, d_pre, slice(second, None))
-    for at in range(0, ffw, tile):
-        cols = slice(at, at + tile)
-        grad_in[:, cols] = dot(x_cut, d_pre[:, cols], (0, 0)).astype(BF16)
-    h_cut = jnp.concatenate([h_cut0[...], h_cut1[...], my_part(hidden)], axis=0)
-    grad_out[...] = dot(h_cut, stack(row_refs, 1, width), (0, 0)).astype(BF16)
+        d_pre[own:, cols] = (dot(s, weight_out[cols, :], (1, 1)) * slope).astype(BF16)
+    for t, cols in enumerate(tiles):
+        grad_in[:, cols] = dot(rows[:, mine], d_pre[:, cols], (0, 0)).astype(BF16)
+        outs.append(
+            pltpu.make_async_copy(grad_in.at[:, cols], grad_in_hbm.at[:, cols], out_sems.at[t])
+        )
+        outs[-1].start()
+    h_cut[own:, :] = my_part(hidden)
+    grad_out[...] = dot(h_cut[...], rows[:, width:], (0, 0)).astype(BF16)
+    outs.append(pltpu.make_async_copy(grad_out, grad_out_hbm, out_sems.at[len(tiles)]))
+    outs[-1].start()
+    for copy in outs:
+        copy.wait()
 
 
 def after(value, *first):
@@ -240,7 +277,7 @@
         functools.partial(route_kernel, experts, capacity),
         [shape((capacity, 2 * feat_width))] * experts + [place] * 2,
         [routes.T, gates.T, tokens, cotangent],
-        in_space=pltpu.HBM,
+        spaces=[pltpu.HBM] * 4,
         scratch=[
             pltpu.VMEM((2, tok_count), jnp.int32),
             pltpu.VMEM((2, tok_count), BF16),
@@ -250,23 +287,23 @@
         ],
     )
     blocks, places = routed[:experts], routed[experts:]
-    weight_in, weight_out = call(
-        load_kernel,
-        [pltpu.VMEM((feat_width, ffw), BF16), pltpu.VMEM((ffw, feat_width), BF16)],
-        [after(proj_in[0], places[0]), after(proj_out[0], places[0])],
-        in_space=pltpu.HBM,
-        scratch=[pltpu.SemaphoreType.DMA((2,))],
-    )
-    weights = [
-        pltpu.with_memory_space_constraint(w, pltpu.VMEM) for w in (weight_in, weight_out)
-    ]
     rest = list(range(experts - 1, 1, -1))
     order = [0, *rest[:2], 1, *rest[2:]]
     order_a, order_b = order[:half], order[half:]
     got_a = [blocks[0]] + [permute(blocks[k], k) for k in order_a[1:]]
     got_b = [
-        permute(blocks[k] if i < 2 else after(blocks[k], *got_a[1:]), k)
+        permute(blocks[k] if i < 2 else after(blocks[k], got_a[1 - i]), k)
         for i, k in enumerate(order_b)
+    ]
+    weight_in, weight_out = call(
+        load_kernel,
+        [pltpu.VMEM((feat_width, ffw), BF16), pltpu.VMEM((ffw, feat_width), BF16)],
+        [after(proj_in[0], got_b[0]), after(proj_out[0], got_b[0])],
+        spaces=[pltpu.HBM] * 2,
+        scratch=[pltpu.SemaphoreType.DMA((2,))],
+    )
+    weights = [
+        pltpu.with_memory_space_constraint(w, pltpu.VMEM) for w in (weight_in, weight_out)
     ]
     rows_a = jnp.concatenate(got_a, axis=0)
     chips_a = [shift_chips(rows_a, k) for k in range(1, groups // 2)]
@@ -277,38 +314,48 @@
     d_pre0, h_cut0, back = call(
         functools.partial(own_kernel, tile, order),
         [
-            shape((slots_all, ffw)),
+            pltpu.HBM((slots_all, ffw), BF16),
             shape((slots_all, tile)),
-            shape((slots_all, feat_width + LANES)),
+            pltpu.HBM((slots_all, feat_width + LANES), BF16),
         ],
         [rows_a, rows_b, *weights],
         20 * product,
-        scratch=[pltpu.VMEM((slots_all, ffw), BF16)],
+        scratch=[
+            pltpu.VMEM((slots_all, ffw), BF16),
+            pltpu.VMEM((slots_all, ffw), BF16),
+            pltpu.VMEM((slots_all, feat_width + LANES), BF16),
+            pltpu.SemaphoreType.DMA((2,)),
+        ],
     )
     back = lax.all_to_all(
         back.reshape(experts, capacity, feat_width + LANES), "expert", 0, 0, tiled=True
     ).reshape(slots_all, feat_width + LANES)
     relayed_a = [swap_cores(after(rows, d_pre0)) for rows in chips_a]
-    early = [core_a, core_b, *chips_a, *relayed_a]
-    early_rows = sum(piece.shape[0] for piece in early)
-    d_pre1, h_cut1 = call(
-        functools.partial(early_kernel, tile, len(early)),
-        [shape((early_rows, ffw)), shape((early_rows, tile))],
-        [*early, *weights],
-        product,
-        scratch=[pltpu.VMEM((early_rows, ffw), BF16)],
-    )
-    chips_b += [swap_cores(rows) for rows in chips_b]
-    late_rows = sum(piece.shape[0] for piece in chips_b)
+    relayed_b = [swap_cores(rows) for rows in chips_b]
+    pieces = [rows_a, rows_b, core_a, core_b, *chips_a, *relayed_a, *chips_b, *relayed_b]
+    rows_all = groups * slots_all
     grad_in, grad_out = call(
-        functools.partial(grads_kernel, tile, 2, len(early), len(chips_b)),
-        [shape((feat_width // groups, ffw)), shape((ffw // groups, feat_width))],
-        [rows_a, rows_b, *early, *chips_b, d_pre0, h_cut0, d_pre1, h_cut1, *weights],
+        functools.partial(grads_kernel, tile, len(pieces)),
+        [
+            pltpu.HBM((feat_width // groups, ffw), BF16),
+            pltpu.HBM((ffw // groups, feat_width), BF16),
+        ],
+        [*pieces, d_pre0, h_cut0, proj_in[0], proj_out[0]],
         4 * product,
+        limit=32,
         scratch=[
-            pltpu.VMEM((late_rows, ffw), BF16),
-            pltpu.VMEM((groups * slots_all, ffw), BF16),
-        ],
+            pltpu.VMEM((rows_all, 2 * feat_width), BF16),
+            pltpu.VMEM((feat_width, ffw), BF16),
+            pltpu.VMEM((ffw, feat_width), BF16),
+            pltpu.VMEM((rows_all - slots_all, ffw), BF16),
+            pltpu.VMEM((rows_all, tile), BF16),
+            pltpu.VMEM((rows_all, ffw), BF16),
+            pltpu.VMEM((feat_width // groups, ffw), BF16),
+            pltpu.VMEM((ffw // groups, feat_width), BF16),
+            pltpu.SemaphoreType.DMA((len(pieces) + 2 * groups + 2,)),
+            pltpu.SemaphoreType.DMA((groups + 1,)),
+        ],
+        spaces=[pl.ANY] * len(pieces) + [pltpu.HBM, pl.ANY] + [pltpu.HBM] * 2,
     )
     token_grads, gate_grads = call(
         functools.partial(combine_kernel, experts, capacity),

time: 56.8 us -> 51.9 us (0.914)
  local copies, waits for them, and re-layouts: 12 us -> 0.05 us
  waiting for transfers between devices: 3.5 us -> 9.87 us
  Pallas kernels: 18 us -> 18.9 us
    unnamed x28 -> x8, local copies, waits for them, and re-layouts: 12 us -> 0.04 us
    all_to_all x1, waiting for transfers between devices: 0.01 us -> 8.19 us  [local(): lax.all_to_all(back.reshape(experts, capacity, feat_width + LANES), 'expe...]
    ppermute x4, waiting for transfers between devices: 1.63 us -> 0.01 us  [swap_cores(): lax.ppermute(rows, 'dp', [(i, i ^ 1) for i in range(lax.axis_size('dp'))])]
    ppermute x7, starting transfers between devices: 12.6 us -> 14 us  [permute(): lax.ppermute(block, 'expert', [(i, i ^ k) for i in range(lax.axis_size('e...]
    all_to_all x1, starting transfers between devices: 5.24 us -> 3.92 us  [local(): lax.all_to_all(back.reshape(experts, capacity, feat_width + LANES), 'expe...]
    pallas_call x6 -> x5, Pallas kernels: 18 us -> 18.9 us  [call(): pl.pallas_call(kernel, out_shape=out_shape, in_specs=[pl.BlockSpec(memory...]
  transfers between devices with their start and end apart: 14 -> 14, of which waited for: 5 -> 3; matrix products, arithmetic and copies ran while one was open for 0% -> 0% of each run, Pallas kernels for 20% -> 17%
where the time goes in v5:
time: 51.9 us; the launch traced here: 51.7 us
  starting transfers between devices  22.1 us (43%)
  Pallas kernels  18.9 us (36%)
  waiting for transfers between devices  9.87 us (19%)
  between operations  0.74 us (1%)
    pallas_call x5, Pallas kernels, call(): pl.pallas_call(kernel, out_shape=out_shape, in_specs=[pl.BlockSpec(memory...  18.9 us
    ppermute x7, starting transfers between devices, permute(): lax.ppermute(block, 'expert', [(i, i ^ k) for i in range(lax.axis_size('e...  14 us
    all_to_all x1, waiting for transfers between devices, local(): lax.all_to_all(back.reshape(experts, capacity, feat_width + LANES), 'expe...  8.19 us
    all_to_all x1, starting transfers between devices, local(): lax.all_to_all(back.reshape(experts, capacity, feat_width + LANES), 'expe...  3.92 us
    ppermute x2, starting transfers between devices, shift_chips(): lax.ppermute(rows, 'dp', [(i, (i + 2 * k) % groups) for i in range(groups)])  3.16 us
    ppermute x7, waiting for transfers between devices, permute(): lax.ppermute(block, 'expert', [(i, i ^ k) for i in range(lax.axis_size('e...  1.66 us
  transfers between devices with their start and end apart: 14, of which 3 were waited for; matrix products, arithmetic and copies ran while one was open for 0% of the time, Pallas kernels for 17%

profile of v5, /device:TPU:0, one launch (start us, length us, event | category | flops | bytes accessed | tf_op | source)
XLA Modules:
  0.0 51.7 jit_solution(16366548227723922820)
XLA Ops:
  0.6 1.4 %shard_map.93 = (bf16[16,2048]{1,0:T(8,128)(2,1)S(1)}, bf16[16,2048]{1,0:T(8,128)(2,1)S(1)}, bf16[16,2048]{1,0:T(8,128)(2,1)S(1)}, bf16[16,2048]{1,0:T(8,128)(2,...) custom-call(s32[2,64]{1,0:T(2,128)} %bitcast.17, ...), custom_call_target="tpu_custom_call" | custom-call | bytes 262912 | tf_op jit(solution)/shard_map/pallas_call | solution.py:35
  2.0 6.0 %collective-permute-start = (bf16[16,2048]{1,0:T(8,128)(2,1)S(1)}, bf16[16,2048]{1,0:T(8,128)(2,1)S(1)}, u32[]{:S(2)}, u32[]{:S(2)}) collective-permute-start(bf16[16,2048]{1,0:T(8,128)(2,1)S(1)} %get-tuple-element.32), channel_id=1, source_target_pairs={{0,7},{1,6},{2,5},{3,4},{4,3},{5,2},{6,1},{7,0},{8,15},{9,14},{10,... | collective-permute-start | bytes 196616 | tf_op jit(solution)/shard_map/ppermute | solution.py:244
  8.1 0.2 collective-permute-start.1
  8.3 0.4 collective-permute-start.2
  8.7 1.8 %collective-permute-start.3 = (bf16[16,2048]{1,0:T(8,128)(2,1)S(1)}, bf16[16,2048]{1,0:T(8,128)(2,1)S(1)}, u32[]{:S(2)}, u32[]{:S(2)}) collective-permute-start(bf16[16,2048]{1,0:T(8,128)(2,1)S(1)} %get-tuple-element.35), channel_id=1, source_target_pairs={{0,5},{1,4},{2,7},{3,6},{4,1},{5,0},{6,3},{7,2},{8,13},{9,12},{10,... | collective-permute-start | bytes 196616 | tf_op jit(solution)/shard_map/ppermute | solution.py:244
  10.6 2.1 %collective-permute-start.4 = (bf16[16,2048]{1,0:T(8,128)(2,1)S(1)}, bf16[16,2048]{1,0:T(8,128)(2,1)S(1)}, u32[]{:S(2)}, u32[]{:S(2)}) collective-permute-start(bf16[16,2048]{1,0:T(8,128)(2,1)S(1)} %get-tuple-element.36), channel_id=1, source_target_pairs={{0,4},{1,5},{2,6},{3,7},{4,0},{5,1},{6,2},{7,3},{8,12},{9,13},{10,... | collective-permute-start | bytes 196616 | tf_op jit(solution)/shard_map/ppermute | solution.py:244
  12.7 0.0 collective-permute-done.2
  12.7 1.3 %collective-permute-start.5 = (bf16[16,2048]{1,0:T(8,128)(2,1)S(1)}, bf16[16,2048]{1,0:T(8,128)(2,1)S(1)}, u32[]{:S(2)}, u32[]{:S(2)}) collective-permute-start(bf16[16,2048]{1,0:T(8,128)(2,1)S(1)} %get-tuple-element.38), channel_id=1, source_target_pairs={{0,3},{1,2},{2,1},{3,0},{4,7},{5,6},{6,5},{7,4},{8,11},{9,10},{10,... | collective-permute-start | bytes 196616 | tf_op jit(solution)/shard_map/ppermute | solution.py:244
  14.0 0.2 collective-permute-done.1
  14.2 2.0 %collective-permute-start.6 = (bf16[16,2048]{1,0:T(8,128)(2,1)S(1)}, bf16[16,2048]{1,0:T(8,128)(2,1)S(1)}, u32[]{:S(2)}, u32[]{:S(2)}) collective-permute-start(bf16[16,2048]{1,0:T(8,128)(2,1)S(1)} %get-tuple-element.40), channel_id=1, source_target_pairs={{0,2},{1,3},{2,0},{3,1},{4,6},{5,7},{6,4},{7,5},{8,10},{9,11},{10,... | collective-permute-start | bytes 196616 | tf_op jit(solution)/shard_map/ppermute | solution.py:244
  16.3 0.0 collective-permute-done
  16.3 1.6 %collective-permute-start.9 = (bf16[64,2048]{1,0:T(8,128)(2,1)S(1)}, bf16[64,2048]{1,0:T(8,128)(2,1)S(1)}, u32[]{:S(2)}, u32[]{:S(2)}) collective-permute-start(bf16[64,2048]{1,0:T(8,128)(2,1)S(1)} %constant_dynamic-update-slice_fusion.refs_0_), channel_id=1, source_target_pairs={{0,16},{8,24},{16,0},{24,8},{1,17},{9,25},{17,1},{25,9},{2,18},{10... | collective-permute-start | bytes 786440 | tf_op jit(solution)/shard_map/ppermute | solution.py:253
  17.9 0.0 collective-permute-done.3
  17.9 1.4 %collective-permute-done.4 = bf16[16,2048]{1,0:T(8,128)(2,1)S(1)} collective-permute-done((bf16[16,2048]{1,0:T(8,128)(2,1)S(1)}, bf16[16,2048]{1,0:T(8,128)(2,1)S(1)}, u32[]{:S(2)}, u32[]{:S(2)}) %collective-permute-start.4) | collective-permute-done | bytes 65568 | tf_op jit(solution)/shard_map/ppermute | solution.py:244
  19.3 3.5 %shard_map.94 = (bf16[1024,2048]{1,0:T(8,128)(2,1)S(1)}, bf16[2048,1024]{1,0:T(8,128)(2,1)S(1)}) custom-call(bf16[1024,2048]{1,0:T(8,128)(2,1)} %bitcast.12, bf16[2048,1024]{1,0:T(8,128)(2,1)} %bitcast.14), custom_call_target="tpu_custom_call" | custom-call | bytes 8388608 | tf_op jit(solution)/shard_map/pallas_call | solution.py:35
  22.8 0.0 collective-permute-done.5
  22.9 0.0 collective-permute-done.6
  22.9 1.6 %collective-permute-start.11 = (bf16[64,2048]{1,0:T(8,128)(2,1)S(1)}, bf16[64,2048]{1,0:T(8,128)(2,1)S(1)}, u32[]{:S(2)}, u32[]{:S(2)}) collective-permute-start(bf16[64,2048]{1,0:T(8,128)(2,1)S(1)} %constant_dynamic-update-slice_fusion.4.refs_1_), channel_id=1, source_target_pairs={{0,16},{8,24},{16,0},{24,8},{1,17},{9,25},{17,1},{25,9},{2,18},{10... | collective-permute-start | bytes 786440 | tf_op jit(solution)/shard_map/ppermute | solution.py:253
  24.5 0.0 copy-start
  24.5 4.4 %shard_map.95 = (bf16[128,2048]{1,0:T(8,128)(2,1)}, bf16[128,512]{1,0:T(8,128)(2,1)S(1)}, bf16[128,1152]{1,0:T(8,128)(2,1)}) custom-call(bf16[64,2048]{1,0:T(8,128)(2,1)S(1)} %constant_dynamic-update-slice_fusion.refs_0_, bf16[64,2048]{1,0:T(8,128)(2,1)S(1)} %constant_dynamic-update-slice_fusion.4.refs_1_, bf16[1024,2048]{1,0:T(8,128)(2,1)S(1)} %get-tuple-element.43.refs_2_, ...), custom_call_target="tpu_custom_call" | custom-call | flops 10737418240 | bytes 8912896 | tf_op jit(solution)/shard_map/pallas_call | solution.py:35
  28.9 3.9 %all-to-all-start = ((bf16[8,16,1152]{2,1,0:T(8,128)(2,1)}), bf16[8,16,1152]{2,1,0:T(8,128)(2,1)S(1)}, u32[]{:S(2)}, u32[]{:S(2)}) async-start(bf16[8,16,1152]{2,1,0:T(8,128)(2,1)} %bitcast.16), calls=%async_computation | async-start | bytes 589824 | tf_op jit(solution)/shard_map/all_to_all | solution.py:330
  32.8 0.0 collective-permute-start.7
  32.8 0.5 collective-permute-start.8
  33.3 0.0 collective-permute-done.9.refs_4_
  33.3 0.1 collective-permute-start.10
  33.4 0.0 collective-permute-done.11.refs_6_
  33.4 0.4 collective-permute-start.12
  33.8 8.2 %all-to-all-done = bf16[8,16,1152]{2,1,0:T(8,128)(2,1)S(1)} async-done(((bf16[8,16,1152]{2,1,0:T(8,128)(2,1)}), bf16[8,16,1152]{2,1,0:T(8,128)(2,1)S(1)}, u32[]{:S(2)}, u32[]{:S(2)}) %all-to-all-start) | async-done | bytes 294944 | tf_op jit(solution)/shard_map/all_to_all | solution.py:330
  42.0 0.0 copy-done
  42.0 0.9 %shard_map.96 = (bf16[64,1024]{1,0:T(8,128)(2,1)}, bf16[2,64]{1,0:T(2,128)(2,1)}) custom-call(bf16[128,64]{1,0:T(8,128)(2,1)S(1)} %get-tuple-element.29.place0, bf16[128,64]{1,0:T(8,128)(2,1)S(1)} %get-tuple-element.30.place1, bf16[2,64]{1,0:T(2,128)(2,1)S(1)} %bitcast.11, bf16[128,1152]{1,0:T(8,128)(2,1)S(1)} %bitcast.9), custom_call_target="tpu_custom_call" | custom-call | bytes 327936 | tf_op jit(solution)/shard_map/pallas_call | solution.py:35
  42.9 0.0 collective-permute-done.7.refs_2_
  42.9 0.0 collective-permute-done.8.refs_3_
  42.9 0.0 collective-permute-done.10.refs_5_
  42.9 0.0 collective-permute-done.12.refs_7_
  42.9 8.7 %shard_map.97 = (bf16[256,2048]{1,0:T(8,128)(2,1)}, bf16[512,1024]{1,0:T(8,128)(2,1)}) custom-call(bf16[64,2048]{1,0:T(8,128)(2,1)S(1)} %constant_dynamic-update-slice_fusion.refs_0_, bf16[64,2048]{1,0:T(8,128)(2,1)S(1)} %constant_dynamic-update-slice_fusion.4.refs_1_, bf16[64,2048]{1,0:T(8,128)(2,1)S(1)} %collective-permute-done.7.refs_2_, ...), custom_call_target="tpu_custom_call" | custom-call | flops 2147483648 | bytes 11141120 | tf_op jit(solution)/shard_map/pallas_call | solution.py:35
  (8 shorter events, 0.0 us)
Async XLA Ops:
  2.0 14.2 %collective-permute-start = (bf16[16,2048]{1,0:T(8,128)(2,1)S(1)}, bf16[16,2048]{1,0:T(8,128)(2,1)S(1)}, u32[]{:S(2)}, u32[]{:S(2)}) collective-permute-start(bf16[16,2048]{1,0:T(8,128)(2,1)S(1)} %get-tuple-element.32), channel_id=1, source_target_pairs={{0,7},{1,6},{2,5},{3,4},{4,3},{5,2},{6,1},{7,0},{8,15},{9,14},{10,... | collective-permute-start | bytes 196616 | tf_op jit(solution)/shard_map/ppermute | solution.py:244
  8.1 6.2 %collective-permute-start.1 = (bf16[16,2048]{1,0:T(8,128)(2,1)S(1)}, bf16[16,2048]{1,0:T(8,128)(2,1)S(1)}, u32[]{:S(2)}, u32[]{:S(2)}) collective-permute-start(bf16[16,2048]{1,0:T(8,128)(2,1)S(1)} %get-tuple-element.33), channel_id=1, source_target_pairs={{0,6},{1,7},{2,4},{3,5},{4,2},{5,3},{6,0},{7,1},{8,14},{9,15},{10,... | collective-permute-start | bytes 196616 | tf_op jit(solution)/shard_map/ppermute | solution.py:244
  8.3 4.4 %collective-permute-start.2 = (bf16[16,2048]{1,0:T(8,128)(2,1)S(1)}, bf16[16,2048]{1,0:T(8,128)(2,1)S(1)}, u32[]{:S(2)}, u32[]{:S(2)}) collective-permute-start(bf16[16,2048]{1,0:T(8,128)(2,1)S(1)} %get-tuple-element.34), channel_id=1, source_target_pairs={{0,1},{1,0},{2,3},{3,2},{4,5},{5,4},{6,7},{7,6},{8,9},{9,8},{10,11... | collective-permute-start | bytes 196616 | tf_op jit(solution)/shard_map/ppermute | solution.py:244
  8.7 9.2 %collective-permute-start.3 = (bf16[16,2048]{1,0:T(8,128)(2,1)S(1)}, bf16[16,2048]{1,0:T(8,128)(2,1)S(1)}, u32[]{:S(2)}, u32[]{:S(2)}) collective-permute-start(bf16[16,2048]{1,0:T(8,128)(2,1)S(1)} %get-tuple-element.35), channel_id=1, source_target_pairs={{0,5},{1,4},{2,7},{3,6},{4,1},{5,0},{6,3},{7,2},{8,13},{9,12},{10,... | collective-permute-start | bytes 196616 | tf_op jit(solution)/shard_map/ppermute | solution.py:244
  10.6 8.8 %collective-permute-start.4 = (bf16[16,2048]{1,0:T(8,128)(2,1)S(1)}, bf16[16,2048]{1,0:T(8,128)(2,1)S(1)}, u32[]{:S(2)}, u32[]{:S(2)}) collective-permute-start(bf16[16,2048]{1,0:T(8,128)(2,1)S(1)} %get-tuple-element.36), channel_id=1, source_target_pairs={{0,4},{1,5},{2,6},{3,7},{4,0},{5,1},{6,2},{7,3},{8,12},{9,13},{10,... | collective-permute-start | bytes 196616 | tf_op jit(solution)/shard_map/ppermute | solution.py:244
  12.7 10.1 %collective-permute-start.5 = (bf16[16,2048]{1,0:T(8,128)(2,1)S(1)}, bf16[16,2048]{1,0:T(8,128)(2,1)S(1)}, u32[]{:S(2)}, u32[]{:S(2)}) collective-permute-start(bf16[16,2048]{1,0:T(8,128)(2,1)S(1)} %get-tuple-element.38), channel_id=1, source_target_pairs={{0,3},{1,2},{2,1},{3,0},{4,7},{5,6},{6,5},{7,4},{8,11},{9,10},{10,... | collective-permute-start | bytes 196616 | tf_op jit(solution)/shard_map/ppermute | solution.py:244
  14.2 8.6 %collective-permute-start.6 = (bf16[16,2048]{1,0:T(8,128)(2,1)S(1)}, bf16[16,2048]{1,0:T(8,128)(2,1)S(1)}, u32[]{:S(2)}, u32[]{:S(2)}) collective-permute-start(bf16[16,2048]{1,0:T(8,128)(2,1)S(1)} %get-tuple-element.40), channel_id=1, source_target_pairs={{0,2},{1,3},{2,0},{3,1},{4,6},{5,7},{6,4},{7,5},{8,10},{9,11},{10,... | collective-permute-start | bytes 196616 | tf_op jit(solution)/shard_map/ppermute | solution.py:244
  16.3 17.0 %collective-permute-start.9 = (bf16[64,2048]{1,0:T(8,128)(2,1)S(1)}, bf16[64,2048]{1,0:T(8,128)(2,1)S(1)}, u32[]{:S(2)}, u32[]{:S(2)}) collective-permute-start(bf16[64,2048]{1,0:T(8,128)(2,1)S(1)} %constant_dynamic-update-slice_fusion.refs_0_), channel_id=1, source_target_pairs={{0,16},{8,24},{16,0},{24,8},{1,17},{9,25},{17,1},{25,9},{2,18},{10... | collective-permute-start | bytes 786440 | tf_op jit(solution)/shard_map/ppermute | solution.py:253
  22.9 10.5 %collective-permute-start.11 = (bf16[64,2048]{1,0:T(8,128)(2,1)S(1)}, bf16[64,2048]{1,0:T(8,128)(2,1)S(1)}, u32[]{:S(2)}, u32[]{:S(2)}) collective-permute-start(bf16[64,2048]{1,0:T(8,128)(2,1)S(1)} %constant_dynamic-update-slice_fusion.4.refs_1_), channel_id=1, source_target_pairs={{0,16},{8,24},{16,0},{24,8},{1,17},{9,25},{17,1},{25,9},{2,18},{10... | collective-permute-start | bytes 786440 | tf_op jit(solution)/shard_map/ppermute | solution.py:253
  24.5 17.6 %copy-start = (bf16[64,2]{0,1:T(2,128)(2,1)S(1)}, bf16[64,2]{0,1:T(2,128)(2,1)}, u32[]{:S(2)}) copy-start(bf16[64,2]{0,1:T(2,128)(2,1)} %param.9) | copy-start | bytes 772
  28.9 13.1 %all-to-all-start = ((bf16[8,16,1152]{2,1,0:T(8,128)(2,1)}), bf16[8,16,1152]{2,1,0:T(8,128)(2,1)S(1)}, u32[]{:S(2)}, u32[]{:S(2)}) async-start(bf16[8,16,1152]{2,1,0:T(8,128)(2,1)} %bitcast.16), calls=%async_computation | async-start | bytes 589824 | tf_op jit(solution)/shard_map/all_to_all | solution.py:330
  32.8 10.1 %collective-permute-start.7 = (bf16[64,2048]{1,0:T(8,128)(2,1)S(1)}, bf16[64,2048]{1,0:T(8,128)(2,1)S(1)}, u32[]{:S(2)}, u32[]{:S(2)}) collective-permute-start(bf16[64,2048]{1,0:T(8,128)(2,1)S(1)} %constant_dynamic-update-slice_fusion.refs_0_), channel_id=1, source_target_pairs={{0,8},{8,0},{16,24},{24,16},{1,9},{9,1},{17,25},{25,17},{2,10},{10... | collective-permute-start | bytes 786440 | tf_op jit(solution)/shard_map/ppermute | solution.py:248
  32.8 10.1 %collective-permute-start.8 = (bf16[64,2048]{1,0:T(8,128)(2,1)S(1)}, bf16[64,2048]{1,0:T(8,128)(2,1)S(1)}, u32[]{:S(2)}, u32[]{:S(2)}) collective-permute-start(bf16[64,2048]{1,0:T(8,128)(2,1)S(1)} %constant_dynamic-update-slice_fusion.4.refs_1_), channel_id=1, source_target_pairs={{0,8},{8,0},{16,24},{24,16},{1,9},{9,1},{17,25},{25,17},{2,10},{10... | collective-permute-start | bytes 786440 | tf_op jit(solution)/shard_map/ppermute | solution.py:248
  33.3 9.6 %collective-permute-start.10 = (bf16[64,2048]{1,0:T(8,128)(2,1)S(1)}, bf16[64,2048]{1,0:T(8,128)(2,1)S(1)}, u32[]{:S(2)}, u32[]{:S(2)}) collective-permute-start(bf16[64,2048]{1,0:T(8,128)(2,1)S(1)} %collective-permute-done.9.refs_4_), channel_id=1, source_target_pairs={{0,8},{8,0},{16,24},{24,16},{1,9},{9,1},{17,25},{25,17},{2,10},{10... | collective-permute-start | bytes 786440 | tf_op jit(solution)/shard_map/ppermute | solution.py:248
  33.4 9.5 %collective-permute-start.12 = (bf16[64,2048]{1,0:T(8,128)(2,1)S(1)}, bf16[64,2048]{1,0:T(8,128)(2,1)S(1)}, u32[]{:S(2)}, u32[]{:S(2)}) collective-permute-start(bf16[64,2048]{1,0:T(8,128)(2,1)S(1)} %collective-permute-done.11.refs_6_), channel_id=1, source_target_pairs={{0,8},{8,0},{16,24},{24,16},{1,9},{9,1},{17,25},{25,17},{2,10},{10... | collective-permute-start | bytes 786440 | tf_op jit(solution)/shard_map/ppermute | solution.py:248

commit v6 on v5

--- a/solution.py
+++ b/solution.py
@@ -106,17 +106,6 @@
     return pl.ds(pl.multiple_of(jnp.bitwise_xor(me, k) * capacity, capacity), capacity)
 
 
-def load_kernel(in_hbm, out_hbm, weight_in, weight_out, sems):
-    copies = [
-        pltpu.make_async_copy(source, target, sems.at[i])
-        for i, (source, target) in enumerate(((in_hbm, weight_in), (out_hbm, weight_out)))
-    ]
-    for copy in copies:
-        copy.start()
-    for copy in copies:
-        copy.wait()
-
-
 def combine_kernel(experts, capacity, place0, place1, gates, back, token_grads, gate_grads, rows):
     tok_count, feat_width = token_grads.shape
     me = lax.axis_index("expert")
@@ -140,98 +129,156 @@
     return ref[:, pl.ds(pl.multiple_of(lax.axis_index("dp") * width, width), width)]
 
 
-def own_kernel(tile, order, *refs):
-    row_refs, (weight_in, weight_out, d_pre_hbm, h_cut, back_hbm, *scratch) = refs[:2], refs[2:]
-    hidden, d_pre, back, sems = scratch
-    me = lax.axis_index("expert")
-    feat_width, ffw = weight_in.shape
-    x, s = stack(row_refs, 0, feat_width), stack(row_refs, 1, feat_width)
-    slots_all = x.shape[0]
-    capacity = slots_all // len(order)
-    dgate = jnp.zeros((slots_all, LANES), F32)
-    dx = jnp.zeros((slots_all, feat_width), F32)
-    for at in range(0, ffw, tile):
-        cols = slice(at, at + tile)
+def rows_backward(tiles, x, s, weight_in, weight_out, hidden, d_pre, rows, before, dgate=None):
+    for t, cols in enumerate(tiles):
+        if t == 1:
+            for copy in before:
+                copy.wait()
         act, slope = gelu_and_slope(dot(x, weight_in[:, cols]))
         hidden[:, cols] = act
         d_hidden = dot(s, weight_out[cols, :], (1, 1))
-        part = (d_hidden * slope).astype(BF16)
-        d_pre[:, cols] = part
-        product = d_hidden * act.astype(F32)
-        for lane in range(0, tile, LANES):
-            dgate = dgate + product[:, lane : lane + LANES]
-        dx = dx + dot(part, weight_in[:, cols], (1, 1))
-    d_pre_out = pltpu.make_async_copy(d_pre, d_pre_hbm, sems.at[0])
-    d_pre_out.start()
-    dgate = jnp.broadcast_to(jnp.sum(dgate, axis=1, keepdims=True), (slots_all, LANES))
-    for i, k in enumerate(order):
-        rows, target = slice(i * capacity, (i + 1) * capacity), block_rows(me, k, capacity)
-        back[target, :feat_width] = dx[rows].astype(BF16)
-        back[target, feat_width:] = dgate[rows].astype(BF16)
-    back_out = pltpu.make_async_copy(back, back_hbm, sems.at[1])
-    back_out.start()
-    h_cut[...] = my_part(hidden)
-    d_pre_out.wait()
-    back_out.wait()
-
-
-def grads_kernel(tile, pieces, *refs):
-    row_refs, refs = refs[:pieces], refs[pieces:]
-    d_pre0, h_cut0, in_hbm, out_hbm, grad_in_hbm, grad_out_hbm = refs[:6]
-    rows, weight_in, weight_out, hidden, h_cut, d_pre, grad_in, grad_out, sems, out_sems = refs[6:]
+        d_pre[rows, cols] = (d_hidden * slope).astype(BF16)
+        if dgate is not None:
+            product = d_hidden * act.astype(F32)
+            for lane in range(0, product.shape[1], LANES):
+                dgate = dgate + product[:, lane : lane + LANES]
+    if dgate is not None:
+        return jnp.broadcast_to(jnp.sum(dgate, axis=1, keepdims=True), dgate.shape)
+
+
+def fetch_weights(fetch, tiles, in_hbm, out_hbm, weight_in, weight_out):
+    copies = []
+    for cols in tiles:
+        copies.append(fetch(in_hbm.at[:, cols], weight_in.at[:, cols]))
+        copies.append(fetch(out_hbm.at[cols, :], weight_out.at[cols, :]))
+    return copies
+
+
+def fetcher(sems):
+    count = iter(range(sems.shape[0]))
+
+    def fetch(source, target):
+        copy = pltpu.make_async_copy(source, target, sems.at[next(count)])
+        copy.start()
+        return copy
+
+    return fetch
+
+
+def own_first_kernel(tile, *refs):
+    rows, in_hbm, out_hbm, weight_in, weight_out, d_pre_hbm, h_cut_hbm, back, *scratch = refs
+    hidden, d_pre, h_cut, sems = scratch
     width, ffw = weight_in.shape
     tiles = [slice(at, at + tile) for at in range(0, ffw, tile)]
-    own = d_pre0.shape[0]
+    fetch = fetcher(sems)
+    copies = fetch_weights(fetch, tiles, in_hbm, out_hbm, weight_in, weight_out)
+    for copy in copies[:2]:
+        copy.wait()
+    x, s = rows[:, :width], rows[:, width:]
+    zero = jnp.zeros((x.shape[0], LANES), F32)
+    back[:, width:] = rows_backward(
+        tiles, x, s, weight_in, weight_out, hidden, d_pre, slice(None), copies[2:], zero
+    ).astype(BF16)
+    h_cut[...] = my_part(hidden)
+    outs = [fetch(d_pre, d_pre_hbm), fetch(h_cut, h_cut_hbm)]
+    wide = width // 4
+    for at in range(0, width, wide):
+        cols = slice(at, at + wide)
+        back[:, cols] = dot(d_pre[...], weight_in[cols, :], (1, 1)).astype(BF16)
+    for copy in outs:
+        copy.wait()
+
+
+def own_second_kernel(tile, order, *refs):
+    rows, first_back, weight_in, weight_out, d_pre_hbm, h_cut_hbm, back_hbm, *scratch = refs
+    hidden, d_pre, h_cut, back, sems = scratch
+    me = lax.axis_index("expert")
+    width, ffw = weight_in.shape
+    tiles = [slice(at, at + tile) for at in range(0, ffw, tile)]
+    fetch = fetcher(sems)
+    capacity = 2 * rows.shape[0] // len(order)
+    half = len(order) // 2
+    spans = [slice(i * capacity, (i + 1) * capacity) for i in range(half)]
+    targets = [block_rows(me, k, capacity) for k in order]
+    for span, target in zip(spans, targets[:half]):
+        back[target, :] = first_back[span, :]
+    x, s = rows[:, :width], rows[:, width:]
+    zero = jnp.zeros((x.shape[0], LANES), F32)
+    dgate = rows_backward(
+        tiles, x, s, weight_in, weight_out, hidden, d_pre, slice(None), [], zero
+    )
+    h_cut[...] = my_part(hidden)
+    outs = [fetch(d_pre, d_pre_hbm), fetch(h_cut, h_cut_hbm)]
+    for span, target in zip(spans, targets[half:]):
+        back[target, width:] = dgate[span].astype(BF16)
+    outs.append(fetch(back.at[:, width:], back_hbm.at[:, width:]))
+    wide = width // 4
+    for at in range(0, width, wide):
+        cols = slice(at, at + wide)
+        dx = dot(d_pre[...], weight_in[cols, :], (1, 1)).astype(BF16)
+        for span, target in zip(spans, targets[half:]):
+            back[target, cols] = dx[span]
+        outs.append(fetch(back.at[:, cols], back_hbm.at[:, cols]))
+    for copy in outs:
+        copy.wait()
+
+
+def early_kernel(tile, pieces, *refs):
+    row_refs, refs = refs[:pieces], refs[pieces:]
+    in_hbm, out_hbm, weight_in, weight_out, d_pre, h_cut, rows, hidden, sems = refs
+    width, ffw = weight_in.shape
     piece = row_refs[0].shape[0]
-    todo = []
-
-    def fetch(source, target):
-        todo.append(pltpu.make_async_copy(source, target, sems.at[len(todo)]))
-        todo[-1].start()
-        return todo[-1]
-
-    first = [
-        fetch(ref, rows.at[pl.ds(i * piece, piece)])
-        for i, ref in enumerate(row_refs)
-        if i * piece >= own
-    ]
-    weights = [
-        fetch(*pair)
-        for cols in tiles
-        for pair in (
-            (in_hbm.at[:, cols], weight_in.at[:, cols]),
-            (out_hbm.at[cols, :], weight_out.at[cols, :]),
-        )
-    ]
-    rest = [
-        fetch(ref, rows.at[pl.ds(i * piece, piece)])
-        for i, ref in enumerate(row_refs)
-        if i * piece < own
-    ]
-    rest += [fetch(d_pre0, d_pre.at[:own, :]), fetch(h_cut0, h_cut.at[:own, :])]
-    for copy in first + weights[:2]:
+    tiles = [slice(at, at + tile) for at in range(0, ffw, tile)]
+    fetch = fetcher(sems)
+    copies = [fetch(ref, rows.at[pl.ds(i * piece, piece)]) for i, ref in enumerate(row_refs)]
+    copies += fetch_weights(fetch, tiles, in_hbm, out_hbm, weight_in, weight_out)
+    for copy in copies[: pieces + 2]:
         copy.wait()
-    x, s = rows[own:, :width], rows[own:, width:]
+    x, s = rows[:, :width], rows[:, width:]
+    rest = copies[pieces + 2 :]
+    rows_backward(tiles, x, s, weight_in, weight_out, hidden, d_pre, slice(None), rest)
+    h_cut[...] = my_part(hidden)
+
+
+def grads_kernel(tile, pieces, late, *refs):
+    row_refs, refs = refs[:pieces], refs[pieces:]
+    d_pre_refs, h_cut_refs, refs = refs[:3], refs[3:6], refs[6:]
+    weight_in, weight_out, grad_in_hbm, grad_out_hbm = refs[:4]
+    rows, hidden, h_cut, d_pre, grad_in, grad_out, sems, out_sems = refs[4:]
+    width, ffw = weight_in.shape
+    tiles = [slice(at, at + tile) for at in range(0, ffw, tile)]
+    piece = row_refs[0].shape[0]
+    known = (pieces - late) * piece
+    fetch = fetcher(sems)
+    copies = [
+        fetch(row_refs[i], rows.at[pl.ds(i * piece, piece)])
+        for i in [*range(pieces - late, pieces), *range(pieces - late)]
+    ]
+    at = 0
+    for source, cut_source in zip(d_pre_refs, h_cut_refs):
+        span = pl.ds(at, source.shape[0])
+        copies += [fetch(source, d_pre.at[span]), fetch(cut_source, h_cut.at[span])]
+        at += source.shape[0]
+    for copy in copies[:late]:
+        copy.wait()
+    x, s = rows[known:, :width], rows[known:, width:]
+    rows_backward(
+        tiles, x, s, weight_in, weight_out, hidden, d_pre, slice(known, None), copies[late:]
+    )
     cut = grad_in.shape[0]
     mine = pl.ds(pl.multiple_of(lax.axis_index("dp") * cut, cut), cut)
+    send = fetcher(out_sems)
     outs = []
-    for t, cols in enumerate(tiles):
-        if t == 1:
-            for copy in weights[2:] + rest:
-                copy.wait()
-        act, slope = gelu_and_slope(dot(x, weight_in[:, cols]))
-        hidden[:, cols] = act
-        d_pre[own:, cols] = (dot(s, weight_out[cols, :], (1, 1)) * slope).astype(BF16)
-    for t, cols in enumerate(tiles):
+    for cols in tiles:
         grad_in[:, cols] = dot(rows[:, mine], d_pre[:, cols], (0, 0)).astype(BF16)
-        outs.append(
-            pltpu.make_async_copy(grad_in.at[:, cols], grad_in_hbm.at[:, cols], out_sems.at[t])
-        )
-        outs[-1].start()
-    h_cut[own:, :] = my_part(hidden)
-    grad_out[...] = dot(h_cut[...], rows[:, width:], (0, 0)).astype(BF16)
-    outs.append(pltpu.make_async_copy(grad_out, grad_out_hbm, out_sems.at[len(tiles)]))
-    outs[-1].start()
+        outs.append(send(grad_in.at[:, cols], grad_in_hbm.at[:, cols]))
+    h_cut[known:, :] = my_part(hidden)
+    wide = width // 4
+    for at in range(0, width, wide):
+        cols = slice(at, at + wide)
+        s_cols = slice(width + at, width + at + wide)
+        grad_out[:, cols] = dot(h_cut[...], rows[:, s_cols], (0, 0)).astype(BF16)
+        outs.append(send(grad_out.at[:, cols], grad_out_hbm.at[:, cols]))
     for copy in outs:
         copy.wait()
 
@@ -295,72 +342,95 @@
         permute(blocks[k] if i < 2 else after(blocks[k], got_a[1 - i]), k)
         for i, k in enumerate(order_b)
     ]
-    weight_in, weight_out = call(
-        load_kernel,
-        [pltpu.VMEM((feat_width, ffw), BF16), pltpu.VMEM((ffw, feat_width), BF16)],
-        [after(proj_in[0], got_b[0]), after(proj_out[0], got_b[0])],
-        spaces=[pltpu.HBM] * 2,
-        scratch=[pltpu.SemaphoreType.DMA((2,))],
-    )
-    weights = [
-        pltpu.with_memory_space_constraint(w, pltpu.VMEM) for w in (weight_in, weight_out)
-    ]
     rows_a = jnp.concatenate(got_a, axis=0)
     chips_a = [shift_chips(rows_a, k) for k in range(1, groups // 2)]
     core_a = swap_cores(after(rows_a, got_b[0]))
     rows_b = jnp.concatenate(got_b, axis=0)
     chips_b = [shift_chips(rows_b, k) for k in range(1, groups // 2)]
     core_b = swap_cores(rows_b)
-    d_pre0, h_cut0, back = call(
-        functools.partial(own_kernel, tile, order),
-        [
-            pltpu.HBM((slots_all, ffw), BF16),
-            shape((slots_all, tile)),
-            pltpu.HBM((slots_all, feat_width + LANES), BF16),
+    hbm_weights = [proj_in[0], proj_out[0]]
+    vmem_weights = [pltpu.VMEM((feat_width, ffw), BF16), pltpu.VMEM((ffw, feat_width), BF16)]
+    own = slots_all // 2
+    own_out = [pltpu.HBM((own, ffw), BF16), pltpu.HBM((own, tile), BF16)]
+    own_scratch = [
+        pltpu.VMEM((own, ffw), BF16),
+        pltpu.VMEM((own, ffw), BF16),
+        pltpu.VMEM((own, tile), BF16),
+    ]
+    weight_in, weight_out, d_pre_a, h_cut_a, back_a = call(
+        functools.partial(own_first_kernel, tile),
+        [*vmem_weights, *own_out, shape((own, feat_width + LANES))],
+        [rows_a, *hbm_weights],
+        10 * product,
+        scratch=[*own_scratch, pltpu.SemaphoreType.DMA((2 * groups + 2,))],
+        spaces=[pltpu.VMEM] + [pltpu.HBM] * 2,
+    )
+    weights = [
+        pltpu.with_memory_space_constraint(w, pltpu.VMEM) for w in (weight_in, weight_out)
+    ]
+    d_pre_b, h_cut_b, back = call(
+        functools.partial(own_second_kernel, tile, order),
+        [*own_out, pltpu.HBM((slots_all, feat_width + LANES), BF16)],
+        [rows_b, back_a, *weights],
+        10 * product,
+        scratch=[
+            *own_scratch,
+            pltpu.VMEM((slots_all, feat_width + LANES), BF16),
+            pltpu.SemaphoreType.DMA((7,)),
         ],
-        [rows_a, rows_b, *weights],
-        20 * product,
+    )
+    back = lax.all_to_all(
+        after(back, core_a, core_b).reshape(experts, capacity, feat_width + LANES), "expert", 0, 0, tiled=True
+    ).reshape(slots_all, feat_width + LANES)
+    relayed_a = [swap_cores(after(rows, d_pre_b)) for rows in chips_a]
+    relayed_b = [swap_cores(rows) for rows in chips_b]
+    early = [core_a, core_b, *chips_a]
+    early_rows = sum(piece.shape[0] for piece in early)
+    weight_in, weight_out, d_pre1, h_cut1 = call(
+        functools.partial(early_kernel, tile, len(early)),
+        [*vmem_weights, shape((early_rows, ffw)), shape((early_rows, tile))],
+        [*early, *hbm_weights],
+        product,
         scratch=[
-            pltpu.VMEM((slots_all, ffw), BF16),
-            pltpu.VMEM((slots_all, ffw), BF16),
-            pltpu.VMEM((slots_all, feat_width + LANES), BF16),
-            pltpu.SemaphoreType.DMA((2,)),
+            pltpu.VMEM((early_rows, 2 * feat_width), BF16),
+            pltpu.VMEM((early_rows, ffw), BF16),
+            pltpu.SemaphoreType.DMA((len(early) + 2 * groups,)),
         ],
-    )
-    back = lax.all_to_all(
-        back.reshape(experts, capacity, feat_width + LANES), "expert", 0, 0, tiled=True
-    ).reshape(slots_all, feat_width + LANES)
-    relayed_a = [swap_cores(after(rows, d_pre0)) for rows in chips_a]
-    relayed_b = [swap_cores(rows) for rows in chips_b]
-    pieces = [rows_a, rows_b, core_a, core_b, *chips_a, *relayed_a, *chips_b, *relayed_b]
+        spaces=[pl.ANY] * len(early) + [pltpu.HBM] * 2,
+    )
+    late = [*relayed_a, *chips_b, *relayed_b]
+    pieces = [rows_a, rows_b, *early, *late]
     rows_all = groups * slots_all
+    weights = [
+        pltpu.with_memory_space_constraint(w, pltpu.VMEM) for w in (weight_in, weight_out)
+    ]
     grad_in, grad_out = call(
-        functools.partial(grads_kernel, tile, len(pieces)),
+        functools.partial(grads_kernel, tile, len(pieces), len(late)),
         [
             pltpu.HBM((feat_width // groups, ffw), BF16),
             pltpu.HBM((ffw // groups, feat_width), BF16),
         ],
-        [*pieces, d_pre0, h_cut0, proj_in[0], proj_out[0]],
+        [*pieces, d_pre_a, d_pre_b, d_pre1, h_cut_a, h_cut_b, h_cut1, *weights],
         4 * product,
         limit=32,
         scratch=[
             pltpu.VMEM((rows_all, 2 * feat_width), BF16),
-            pltpu.VMEM((feat_width, ffw), BF16),
-            pltpu.VMEM((ffw, feat_width), BF16),
-            pltpu.VMEM((rows_all - slots_all, ffw), BF16),
+            pltpu.VMEM((rows_all - slots_all - early_rows, ffw), BF16),
             pltpu.VMEM((rows_all, tile), BF16),
             pltpu.VMEM((rows_all, ffw), BF16),
             pltpu.VMEM((feat_width // groups, ffw), BF16),
             pltpu.VMEM((ffw // groups, feat_width), BF16),
-            pltpu.SemaphoreType.DMA((len(pieces) + 2 * groups + 2,)),
-            pltpu.SemaphoreType.DMA((groups + 1,)),
+            pltpu.SemaphoreType.DMA((len(pieces) + 6,)),
+            pltpu.SemaphoreType.DMA((groups + 4,)),
         ],
-        spaces=[pl.ANY] * len(pieces) + [pltpu.HBM, pl.ANY] + [pltpu.HBM] * 2,
+        spaces=[pl.ANY] * len(pieces)
+        + [pltpu.HBM, pltpu.HBM, pl.ANY] * 2
+        + [pltpu.VMEM] * 2,
     )
     token_grads, gate_grads = call(
         functools.partial(combine_kernel, experts, capacity),
         [shape((tok_count, feat_width)), shape((2, tok_count))],
-        [*places, gates.T, back],
+        [*places, gates.T, after(back, grad_in)],
         scratch=[pltpu.VMEM((slots_all, feat_width + LANES), BF16)],
     )
     return (token_grads, gate_grads.T, grad_in[None], grad_out[None])

time: 51.9 us -> 50.1 us (0.965)
  waiting for transfers between devices: 9.87 us -> 1.03 us
  Pallas kernels: 18.9 us -> 24.2 us
  starting transfers between devices: 22.1 us -> 23.8 us
    all_to_all x1, waiting for transfers between devices: 8.19 us -> 0.01 us  [local(): lax.all_to_all(after(back, core_a, core_b).reshape(experts, capacity, fea...]
    pallas_call x5 -> x6, Pallas kernels: 18.9 us -> 24.2 us  [call(): pl.pallas_call(kernel, out_shape=out_shape, in_specs=[pl.BlockSpec(memory...]
    ppermute x7, starting transfers between devices: 14 us -> 15.6 us  [permute(): lax.ppermute(block, 'expert', [(i, i ^ k) for i in range(lax.axis_size('e...]
    all_to_all x1, starting transfers between devices: 3.92 us -> 5.25 us  [local(): lax.all_to_all(after(back, core_a, core_b).reshape(experts, capacity, fea...]
    ppermute x2, starting transfers between devices: 3.16 us -> 2.16 us  [shift_chips(): lax.ppermute(rows, 'dp', [(i, (i + 2 * k) % groups) for i in range(groups)])]
    ppermute x7, waiting for transfers between devices: 1.66 us -> 1.01 us  [permute(): lax.ppermute(block, 'expert', [(i, i ^ k) for i in range(lax.axis_size('e...]
  transfers between devices with their start and end apart: 14 -> 14, of which waited for: 3 -> 2; matrix products, arithmetic and copies ran while one was open for 0% -> 0% of each run, Pallas kernels for 17% -> 44%
where the time goes in v6:
time: 50.1 us; the launch traced here: 49.9 us
  Pallas kernels  24.2 us (48%)
  starting transfers between devices  23.8 us (48%)
  waiting for transfers between devices  1.03 us (2%)
  between operations  0.82 us (2%)
    pallas_call x6, Pallas kernels, call(): pl.pallas_call(kernel, out_shape=out_shape, in_specs=[pl.BlockSpec(memory...  24.2 us
    ppermute x7, starting transfers between devices, permute(): lax.ppermute(block, 'expert', [(i, i ^ k) for i in range(lax.axis_size('e...  15.6 us
    all_to_all x1, starting transfers between devices, local(): lax.all_to_all(after(back, core_a, core_b).reshape(experts, capacity, fea...  5.25 us
    ppermute x2, starting transfers between devices, shift_chips(): lax.ppermute(rows, 'dp', [(i, (i + 2 * k) % groups) for i in range(groups)])  2.16 us
    ppermute x7, waiting for transfers between devices, permute(): lax.ppermute(block, 'expert', [(i, i ^ k) for i in range(lax.axis_size('e...  1.01 us
  transfers between devices with their start and end apart: 14, of which 2 were waited for; matrix products, arithmetic and copies ran while one was open for 0% of the time, Pallas kernels for 44%

profile of v6, /device:TPU:0, one launch (start us, length us, event | category | flops | bytes accessed | tf_op | source)
XLA Modules:
  0.0 49.9 jit_solution(17537563628614288669)
XLA Ops:
  0.6 1.4 %shard_map.93 = (bf16[16,2048]{1,0:T(8,128)(2,1)S(1)}, bf16[16,2048]{1,0:T(8,128)(2,1)S(1)}, bf16[16,2048]{1,0:T(8,128)(2,1)S(1)}, bf16[16,2048]{1,0:T(8,128)(2,...) custom-call(s32[2,64]{1,0:T(2,128)} %bitcast.17, ...), custom_call_target="tpu_custom_call" | custom-call | bytes 262912 | tf_op jit(solution)/shard_map/pallas_call | solution.py:35
  2.0 5.0 %collective-permute-start = (bf16[16,2048]{1,0:T(8,128)(2,1)S(1)}, bf16[16,2048]{1,0:T(8,128)(2,1)S(1)}, u32[]{:S(2)}, u32[]{:S(2)}) collective-permute-start(bf16[16,2048]{1,0:T(8,128)(2,1)S(1)} %get-tuple-element.38), channel_id=1, source_target_pairs={{0,5},{1,4},{2,7},{3,6},{4,1},{5,0},{6,3},{7,2},{8,13},{9,12},{10,... | collective-permute-start | bytes 196616 | tf_op jit(solution)/shard_map/ppermute | solution.py:291
  7.1 0.3 collective-permute-start.1
  7.4 0.3 collective-permute-start.2
  7.7 3.8 %collective-permute-start.4 = (bf16[16,2048]{1,0:T(8,128)(2,1)S(1)}, bf16[16,2048]{1,0:T(8,128)(2,1)S(1)}, u32[]{:S(2)}, u32[]{:S(2)}) collective-permute-start(bf16[16,2048]{1,0:T(8,128)(2,1)S(1)} %get-tuple-element.44), channel_id=1, source_target_pairs={{0,6},{1,7},{2,4},{3,5},{4,2},{5,3},{6,0},{7,1},{8,14},{9,15},{10,... | collective-permute-start | bytes 196616 | tf_op jit(solution)/shard_map/ppermute | solution.py:291
  11.5 1.2 %collective-permute-start.6 = (bf16[16,2048]{1,0:T(8,128)(2,1)S(1)}, bf16[16,2048]{1,0:T(8,128)(2,1)S(1)}, u32[]{:S(2)}, u32[]{:S(2)}) collective-permute-start(bf16[16,2048]{1,0:T(8,128)(2,1)S(1)} %get-tuple-element.47), channel_id=1, source_target_pairs={{0,7},{1,6},{2,5},{3,4},{4,3},{5,2},{6,1},{7,0},{8,15},{9,14},{10,... | collective-permute-start | bytes 196616 | tf_op jit(solution)/shard_map/ppermute | solution.py:291
  12.7 0.0 collective-permute-done.2
  12.7 0.5 %collective-permute-start.3 = (bf16[16,2048]{1,0:T(8,128)(2,1)S(1)}, bf16[16,2048]{1,0:T(8,128)(2,1)S(1)}, u32[]{:S(2)}, u32[]{:S(2)}) collective-permute-start(bf16[16,2048]{1,0:T(8,128)(2,1)S(1)} %get-tuple-element.42), channel_id=1, source_target_pairs={{0,3},{1,2},{2,1},{3,0},{4,7},{5,6},{6,5},{7,4},{8,11},{9,10},{10,... | collective-permute-start | bytes 196616 | tf_op jit(solution)/shard_map/ppermute | solution.py:291
  13.2 0.8 %collective-permute-done.4 = bf16[16,2048]{1,0:T(8,128)(2,1)S(1)} collective-permute-done((bf16[16,2048]{1,0:T(8,128)(2,1)S(1)}, bf16[16,2048]{1,0:T(8,128)(2,1)S(1)}, u32[]{:S(2)}, u32[]{:S(2)}) %collective-permute-start.4) | collective-permute-done | bytes 65568 | tf_op jit(solution)/shard_map/ppermute | solution.py:291
  14.1 4.4 %collective-permute-start.5 = (bf16[16,2048]{1,0:T(8,128)(2,1)S(1)}, bf16[16,2048]{1,0:T(8,128)(2,1)S(1)}, u32[]{:S(2)}, u32[]{:S(2)}) collective-permute-start(bf16[16,2048]{1,0:T(8,128)(2,1)S(1)} %get-tuple-element.45), channel_id=1, source_target_pairs={{0,2},{1,3},{2,0},{3,1},{4,6},{5,7},{6,4},{7,5},{8,10},{9,11},{10,... | collective-permute-start | bytes 196616 | tf_op jit(solution)/shard_map/ppermute | solution.py:291
  18.4 0.2 collective-permute-done.6
  18.6 1.6 %collective-permute-start.9 = (bf16[64,2048]{1,0:T(8,128)(2,1)S(1)}, bf16[64,2048]{1,0:T(8,128)(2,1)S(1)}, u32[]{:S(2)}, u32[]{:S(2)}) collective-permute-start(bf16[64,2048]{1,0:T(8,128)(2,1)S(1)} %constant_dynamic-update-slice_fusion.4.refs_0_), channel_id=1, source_target_pairs={{0,16},{8,24},{16,0},{24,8},{1,17},{9,25},{17,1},{25,9},{2,18},{10... | collective-permute-start | bytes 786440 | tf_op jit(solution)/shard_map/ppermute | solution.py:300
  20.2 0.0 collective-permute-done
  20.2 0.0 collective-permute-start.7
  20.2 7.0 %shard_map.94 = (bf16[1024,2048]{1,0:T(8,128)(2,1)S(1)}, bf16[2048,1024]{1,0:T(8,128)(2,1)S(1)}, bf16[64,2048]{1,0:T(8,128)(2,1)}, bf16[64,512]{1,0:T(8,128)(2,1)}, bf16[64,1152]{1,0:T(8,128)(2,1)S(1)}) custom-call(bf16[64,2048]{1,0:T(8,128)(2,1)S(1)} %constant_dynamic-update-slice_fusion.4.refs_0_, bf16[1024,2048]{1,0:T(8,128)(2,1)} %bitcast.12, ...), custom_call_target="tpu_custom_call" | custom-call | flops 5368709120 | bytes 8650752 | tf_op jit(solution)/shard_map/pallas_call | solution.py:35
  27.2 0.0 collective-permute-done.1
  27.3 0.0 collective-permute-done.3
  27.3 0.0 collective-permute-done.5
  27.3 0.6 %collective-permute-start.11 = (bf16[64,2048]{1,0:T(8,128)(2,1)S(1)}, bf16[64,2048]{1,0:T(8,128)(2,1)S(1)}, u32[]{:S(2)}, u32[]{:S(2)}) collective-permute-start(bf16[64,2048]{1,0:T(8,128)(2,1)S(1)} %constant_dynamic-update-slice_fusion.refs_0_.refs_1_), channel_id=1, source_target_pairs={{0,16},{8,24},{16,0},{24,8},{1,17},{9,25},{17,1},{25,9},{2,18},{10... | collective-permute-start | bytes 786440 | tf_op jit(solution)/shard_map/ppermute | solution.py:300
  27.9 0.2 collective-permute-start.8
  28.1 4.2 %shard_map.95 = (bf16[64,2048]{1,0:T(8,128)(2,1)}, bf16[64,512]{1,0:T(8,128)(2,1)}, bf16[128,1152]{1,0:T(8,128)(2,1)}) custom-call(bf16[64,2048]{1,0:T(8,128)(2,1)S(1)} %constant_dynamic-update-slice_fusion.refs_0_.refs_1_, bf16[64,1152]{1,0:T(8,128)(2,1)S(1)} %get-tuple-element.48.refs_1_, bf16[1024,2048]{1,0:T(8,128)(2,1)S(1)} %get-tuple-element.49.refs_2_, ...), custom_call_target="tpu_custom_call" | custom-call | flops 5368709120 | bytes 8798208 | tf_op jit(solution)/shard_map/pallas_call | solution.py:35
  32.3 0.0 collective-permute-done.7.refs_0_.refs_2_
  32.3 0.0 collective-permute-done.8.refs_1_.refs_3_
  32.3 5.3 %all-to-all-start = ((bf16[8,16,1152]{2,1,0:T(8,128)(2,1)}), bf16[8,16,1152]{2,1,0:T(8,128)(2,1)S(1)}, u32[]{:S(2)}, u32[]{:S(2)}) async-start(bf16[8,16,1152]{2,1,0:T(8,128)(2,1)} %bitcast.16), calls=%async_computation | async-start | bytes 589824 | tf_op jit(solution)/shard_map/all_to_all | solution.py:382
  37.6 0.0 collective-permute-done.9.refs_2_.refs_4_
  37.6 0.1 collective-permute-start.10
  37.6 0.0 collective-permute-done.11.refs_6_
  37.6 0.5 collective-permute-start.12
  38.1 5.5 %shard_map.96 = (bf16[1024,2048]{1,0:T(8,128)(2,1)S(1)}, bf16[2048,1024]{1,0:T(8,128)(2,1)S(1)}, bf16[192,2048]{1,0:T(8,128)(2,1)S(1)}, bf16[192,512]{1,0:T(8,128)(2,1)S(1)}) custom-call(bf16[64,2048]{1,0:T(8,128)(2,1)S(1)} %collective-permute-done.7.refs_0_.refs_2_, bf16[64,2048]{1,0:T(8,128)(2,1)S(1)} %collective-permute-done.8.refs_1_.refs_3_, ...), custom_call_target="tpu_custom_call" | custom-call | flops 536870912 | bytes 9175040 | tf_op jit(solution)/shard_map/pallas_call | solution.py:35
  43.6 0.0 collective-permute-done.10.refs_5_
  43.6 0.0 collective-permute-done.12.refs_7_
  43.6 0.0 copy-start
  43.6 5.3 %shard_map.97 = (bf16[256,2048]{1,0:T(8,128)(2,1)}, bf16[512,1024]{1,0:T(8,128)(2,1)}) custom-call(bf16[64,2048]{1,0:T(8,128)(2,1)S(1)} %constant_dynamic-update-slice_fusion.4.refs_0_, bf16[64,2048]{1,0:T(8,128)(2,1)S(1)} %constant_dynamic-update-slice_fusion.refs_0_.refs_1_, bf16[64,2048]{1,0:T(8,128)(2,1)S(1)} %collective-permute-done.7.refs_0_.refs_2_, ...), custom_call_target="tpu_custom_call" | custom-call | flops 2147483648 | bytes 12124160 | tf_op jit(solution)/shard_map/pallas_call | solution.py:35
  49.0 0.0 all-to-all-done
  49.0 0.0 copy-done
  49.0 0.9 %shard_map.98 = (bf16[64,1024]{1,0:T(8,128)(2,1)}, bf16[2,64]{1,0:T(2,128)(2,1)}) custom-call(bf16[128,64]{1,0:T(8,128)(2,1)S(1)} %get-tuple-element.36.place0, bf16[128,64]{1,0:T(8,128)(2,1)S(1)} %get-tuple-element.37.place1, bf16[2,64]{1,0:T(2,128)(2,1)S(1)} %bitcast.11, bf16[128,1152]{1,0:T(8,128)(2,1)S(1)} %bitcast.9), custom_call_target="tpu_custom_call" | custom-call | bytes 327936 | tf_op jit(solution)/shard_map/pallas_call | solution.py:35
  (8 shorter events, 0.0 us)
Async XLA Ops:
  2.0 18.2 %collective-permute-start = (bf16[16,2048]{1,0:T(8,128)(2,1)S(1)}, bf16[16,2048]{1,0:T(8,128)(2,1)S(1)}, u32[]{:S(2)}, u32[]{:S(2)}) collective-permute-start(bf16[16,2048]{1,0:T(8,128)(2,1)S(1)} %get-tuple-element.38), channel_id=1, source_target_pairs={{0,5},{1,4},{2,7},{3,6},{4,1},{5,0},{6,3},{7,2},{8,13},{9,12},{10,... | collective-permute-start | bytes 196616 | tf_op jit(solution)/shard_map/ppermute | solution.py:291
  7.1 20.2 %collective-permute-start.1 = (bf16[16,2048]{1,0:T(8,128)(2,1)S(1)}, bf16[16,2048]{1,0:T(8,128)(2,1)S(1)}, u32[]{:S(2)}, u32[]{:S(2)}) collective-permute-start(bf16[16,2048]{1,0:T(8,128)(2,1)S(1)} %get-tuple-element.39), channel_id=1, source_target_pairs={{0,4},{1,5},{2,6},{3,7},{4,0},{5,1},{6,2},{7,3},{8,12},{9,13},{10,... | collective-permute-start | bytes 196616 | tf_op jit(solution)/shard_map/ppermute | solution.py:291
  7.4 5.3 %collective-permute-start.2 = (bf16[16,2048]{1,0:T(8,128)(2,1)S(1)}, bf16[16,2048]{1,0:T(8,128)(2,1)S(1)}, u32[]{:S(2)}, u32[]{:S(2)}) collective-permute-start(bf16[16,2048]{1,0:T(8,128)(2,1)S(1)} %get-tuple-element.41), channel_id=1, source_target_pairs={{0,1},{1,0},{2,3},{3,2},{4,5},{5,4},{6,7},{7,6},{8,9},{9,8},{10,11... | collective-permute-start | bytes 196616 | tf_op jit(solution)/shard_map/ppermute | solution.py:291
  7.7 6.3 %collective-permute-start.4 = (bf16[16,2048]{1,0:T(8,128)(2,1)S(1)}, bf16[16,2048]{1,0:T(8,128)(2,1)S(1)}, u32[]{:S(2)}, u32[]{:S(2)}) collective-permute-start(bf16[16,2048]{1,0:T(8,128)(2,1)S(1)} %get-tuple-element.44), channel_id=1, source_target_pairs={{0,6},{1,7},{2,4},{3,5},{4,2},{5,3},{6,0},{7,1},{8,14},{9,15},{10,... | collective-permute-start | bytes 196616 | tf_op jit(solution)/shard_map/ppermute | solution.py:291
  11.5 7.1 %collective-permute-start.6 = (bf16[16,2048]{1,0:T(8,128)(2,1)S(1)}, bf16[16,2048]{1,0:T(8,128)(2,1)S(1)}, u32[]{:S(2)}, u32[]{:S(2)}) collective-permute-start(bf16[16,2048]{1,0:T(8,128)(2,1)S(1)} %get-tuple-element.47), channel_id=1, source_target_pairs={{0,7},{1,6},{2,5},{3,4},{4,3},{5,2},{6,1},{7,0},{8,15},{9,14},{10,... | collective-permute-start | bytes 196616 | tf_op jit(solution)/shard_map/ppermute | solution.py:291
  12.7 14.6 %collective-permute-start.3 = (bf16[16,2048]{1,0:T(8,128)(2,1)S(1)}, bf16[16,2048]{1,0:T(8,128)(2,1)S(1)}, u32[]{:S(2)}, u32[]{:S(2)}) collective-permute-start(bf16[16,2048]{1,0:T(8,128)(2,1)S(1)} %get-tuple-element.42), channel_id=1, source_target_pairs={{0,3},{1,2},{2,1},{3,0},{4,7},{5,6},{6,5},{7,4},{8,11},{9,10},{10,... | collective-permute-start | bytes 196616 | tf_op jit(solution)/shard_map/ppermute | solution.py:291
  14.1 13.2 %collective-permute-start.5 = (bf16[16,2048]{1,0:T(8,128)(2,1)S(1)}, bf16[16,2048]{1,0:T(8,128)(2,1)S(1)}, u32[]{:S(2)}, u32[]{:S(2)}) collective-permute-start(bf16[16,2048]{1,0:T(8,128)(2,1)S(1)} %get-tuple-element.45), channel_id=1, source_target_pairs={{0,2},{1,3},{2,0},{3,1},{4,6},{5,7},{6,4},{7,5},{8,10},{9,11},{10,... | collective-permute-start | bytes 196616 | tf_op jit(solution)/shard_map/ppermute | solution.py:291
  18.6 18.9 %collective-permute-start.9 = (bf16[64,2048]{1,0:T(8,128)(2,1)S(1)}, bf16[64,2048]{1,0:T(8,128)(2,1)S(1)}, u32[]{:S(2)}, u32[]{:S(2)}) collective-permute-start(bf16[64,2048]{1,0:T(8,128)(2,1)S(1)} %constant_dynamic-update-slice_fusion.4.refs_0_), channel_id=1, source_target_pairs={{0,16},{8,24},{16,0},{24,8},{1,17},{9,25},{17,1},{25,9},{2,18},{10... | collective-permute-start | bytes 786440 | tf_op jit(solution)/shard_map/ppermute | solution.py:300
  20.2 12.1 %collective-permute-start.7 = (bf16[64,2048]{1,0:T(8,128)(2,1)S(1)}, bf16[64,2048]{1,0:T(8,128)(2,1)S(1)}, u32[]{:S(2)}, u32[]{:S(2)}) collective-permute-start(bf16[64,2048]{1,0:T(8,128)(2,1)S(1)} %constant_dynamic-update-slice_fusion.4.refs_0_), channel_id=1, source_target_pairs={{0,8},{8,0},{16,24},{24,16},{1,9},{9,1},{17,25},{25,17},{2,10},{10... | collective-permute-start | bytes 786440 | tf_op jit(solution)/shard_map/ppermute | solution.py:295
  27.3 10.3 %collective-permute-start.11 = (bf16[64,2048]{1,0:T(8,128)(2,1)S(1)}, bf16[64,2048]{1,0:T(8,128)(2,1)S(1)}, u32[]{:S(2)}, u32[]{:S(2)}) collective-permute-start(bf16[64,2048]{1,0:T(8,128)(2,1)S(1)} %constant_dynamic-update-slice_fusion.refs_0_.refs_1_), channel_id=1, source_target_pairs={{0,16},{8,24},{16,0},{24,8},{1,17},{9,25},{17,1},{25,9},{2,18},{10... | collective-permute-start | bytes 786440 | tf_op jit(solution)/shard_map/ppermute | solution.py:300
  27.9 4.4 %collective-permute-start.8 = (bf16[64,2048]{1,0:T(8,128)(2,1)S(1)}, bf16[64,2048]{1,0:T(8,128)(2,1)S(1)}, u32[]{:S(2)}, u32[]{:S(2)}) collective-permute-start(bf16[64,2048]{1,0:T(8,128)(2,1)S(1)} %constant_dynamic-update-slice_fusion.refs_0_.refs_1_), channel_id=1, source_target_pairs={{0,8},{8,0},{16,24},{24,16},{1,9},{9,1},{17,25},{25,17},{2,10},{10... | collective-permute-start | bytes 786440 | tf_op jit(solution)/shard_map/ppermute | solution.py:295
  32.3 16.7 %all-to-all-start = ((bf16[8,16,1152]{2,1,0:T(8,128)(2,1)}), bf16[8,16,1152]{2,1,0:T(8,128)(2,1)S(1)}, u32[]{:S(2)}, u32[]{:S(2)}) async-start(bf16[8,16,1152]{2,1,0:T(8,128)(2,1)} %bitcast.16), calls=%async_computation | async-start | bytes 589824 | tf_op jit(solution)/shard_map/all_to_all | solution.py:382
  37.6 6.1 %collective-permute-start.10 = (bf16[64,2048]{1,0:T(8,128)(2,1)S(1)}, bf16[64,2048]{1,0:T(8,128)(2,1)S(1)}, u32[]{:S(2)}, u32[]{:S(2)}) collective-permute-start(bf16[64,2048]{1,0:T(8,128)(2,1)S(1)} %collective-permute-done.9.refs_2_.refs_4_), channel_id=1, source_target_pairs={{0,8},{8,0},{16,24},{24,16},{1,9},{9,1},{17,25},{25,17},{2,10},{10... | collective-permute-start | bytes 786440 | tf_op jit(solution)/shard_map/ppermute | solution.py:295
  37.6 6.0 %collective-permute-start.12 = (bf16[64,2048]{1,0:T(8,128)(2,1)S(1)}, bf16[64,2048]{1,0:T(8,128)(2,1)S(1)}, u32[]{:S(2)}, u32[]{:S(2)}) collective-permute-start(bf16[64,2048]{1,0:T(8,128)(2,1)S(1)} %collective-permute-done.11.refs_6_), channel_id=1, source_target_pairs={{0,8},{8,0},{16,24},{24,16},{1,9},{9,1},{17,25},{25,17},{2,10},{10... | collective-permute-start | bytes 786440 | tf_op jit(solution)/shard_map/ppermute | solution.py:295
  43.6 5.3 %copy-start = (bf16[64,2]{0,1:T(2,128)(2,1)S(1)}, bf16[64,2]{0,1:T(2,128)(2,1)}, u32[]{:S(2)}) copy-start(bf16[64,2]{0,1:T(2,128)(2,1)} %param.9) | copy-start | bytes 772

commit v7 on v5

--- a/solution.py
+++ b/solution.py
@@ -106,17 +106,6 @@
     return pl.ds(pl.multiple_of(jnp.bitwise_xor(me, k) * capacity, capacity), capacity)
 
 
-def load_kernel(in_hbm, out_hbm, weight_in, weight_out, sems):
-    copies = [
-        pltpu.make_async_copy(source, target, sems.at[i])
-        for i, (source, target) in enumerate(((in_hbm, weight_in), (out_hbm, weight_out)))
-    ]
-    for copy in copies:
-        copy.start()
-    for copy in copies:
-        copy.wait()
-
-
 def combine_kernel(experts, capacity, place0, place1, gates, back, token_grads, gate_grads, rows):
     tok_count, feat_width = token_grads.shape
     me = lax.axis_index("expert")
@@ -140,98 +129,118 @@
     return ref[:, pl.ds(pl.multiple_of(lax.axis_index("dp") * width, width), width)]
 
 
+def fetcher(sems):
+    count = iter(range(sems.shape[0]))
+
+    def fetch(source, target):
+        copy = pltpu.make_async_copy(source, target, sems.at[next(count)])
+        copy.start()
+        return copy
+
+    return fetch
+
+
 def own_kernel(tile, order, *refs):
-    row_refs, (weight_in, weight_out, d_pre_hbm, h_cut, back_hbm, *scratch) = refs[:2], refs[2:]
-    hidden, d_pre, back, sems = scratch
+    row_refs, refs = refs[:2], refs[2:]
+    in_hbm, out_hbm, d_pre_hbm, h_cut_hbm, back_hbm, *scratch = refs
+    weight_in, weight_out, hidden, d_pre, h_cut, back, sems = scratch
     me = lax.axis_index("expert")
-    feat_width, ffw = weight_in.shape
-    x, s = stack(row_refs, 0, feat_width), stack(row_refs, 1, feat_width)
+    width, ffw = weight_in.shape
+    tiles = [slice(at, at + tile) for at in range(0, ffw, tile)]
+    fetch = fetcher(sems)
+    copies = [
+        (
+            fetch(in_hbm.at[:, cols], weight_in.at[:, cols]),
+            fetch(out_hbm.at[cols, :], weight_out.at[cols, :]),
+        )
+        for cols in tiles
+    ]
+    x, s = stack(row_refs, 0, width), stack(row_refs, 1, width)
     slots_all = x.shape[0]
     capacity = slots_all // len(order)
     dgate = jnp.zeros((slots_all, LANES), F32)
-    dx = jnp.zeros((slots_all, feat_width), F32)
-    for at in range(0, ffw, tile):
-        cols = slice(at, at + tile)
+    for cols, (copy_in, copy_out) in zip(tiles, copies):
+        copy_in.wait()
         act, slope = gelu_and_slope(dot(x, weight_in[:, cols]))
         hidden[:, cols] = act
+        copy_out.wait()
         d_hidden = dot(s, weight_out[cols, :], (1, 1))
-        part = (d_hidden * slope).astype(BF16)
-        d_pre[:, cols] = part
+        d_pre[:, cols] = (d_hidden * slope).astype(BF16)
         product = d_hidden * act.astype(F32)
         for lane in range(0, tile, LANES):
             dgate = dgate + product[:, lane : lane + LANES]
-        dx = dx + dot(part, weight_in[:, cols], (1, 1))
-    d_pre_out = pltpu.make_async_copy(d_pre, d_pre_hbm, sems.at[0])
-    d_pre_out.start()
+    h_cut[...] = my_part(hidden)
     dgate = jnp.broadcast_to(jnp.sum(dgate, axis=1, keepdims=True), (slots_all, LANES))
-    for i, k in enumerate(order):
-        rows, target = slice(i * capacity, (i + 1) * capacity), block_rows(me, k, capacity)
-        back[target, :feat_width] = dx[rows].astype(BF16)
-        back[target, feat_width:] = dgate[rows].astype(BF16)
-    back_out = pltpu.make_async_copy(back, back_hbm, sems.at[1])
-    back_out.start()
-    h_cut[...] = my_part(hidden)
-    d_pre_out.wait()
-    back_out.wait()
+    places = [
+        (slice(i * capacity, (i + 1) * capacity), block_rows(me, k, capacity))
+        for i, k in enumerate(order)
+    ]
+    for rows, target in places:
+        back[target, width:] = dgate[rows].astype(BF16)
+    outs = [
+        fetch(d_pre, d_pre_hbm),
+        fetch(h_cut, h_cut_hbm),
+        fetch(back.at[:, width:], back_hbm.at[:, width:]),
+    ]
+    wide = width // 4
+    for at in range(0, width, wide):
+        cols = slice(at, at + wide)
+        dx = dot(d_pre[...], weight_in[cols, :], (1, 1)).astype(BF16)
+        for rows, target in places:
+            back[target, cols] = dx[rows]
+        outs.append(fetch(back.at[:, cols], back_hbm.at[:, cols]))
+    for copy in outs:
+        copy.wait()
 
 
 def grads_kernel(tile, pieces, *refs):
     row_refs, refs = refs[:pieces], refs[pieces:]
-    d_pre0, h_cut0, in_hbm, out_hbm, grad_in_hbm, grad_out_hbm = refs[:6]
-    rows, weight_in, weight_out, hidden, h_cut, d_pre, grad_in, grad_out, sems, out_sems = refs[6:]
+    d_pre_own, h_cut_own, in_hbm, out_hbm, grad_in_hbm, grad_out_hbm, *scratch = refs
+    rows, weight_in, weight_out, hidden, h_cut, d_pre, grad_in, grad_out, sems, out_sems = scratch
     width, ffw = weight_in.shape
     tiles = [slice(at, at + tile) for at in range(0, ffw, tile)]
-    own = d_pre0.shape[0]
-    piece = row_refs[0].shape[0]
-    todo = []
-
-    def fetch(source, target):
-        todo.append(pltpu.make_async_copy(source, target, sems.at[len(todo)]))
-        todo[-1].start()
-        return todo[-1]
-
-    first = [
-        fetch(ref, rows.at[pl.ds(i * piece, piece)])
-        for i, ref in enumerate(row_refs)
-        if i * piece >= own
-    ]
-    weights = [
-        fetch(*pair)
-        for cols in tiles
-        for pair in (
-            (in_hbm.at[:, cols], weight_in.at[:, cols]),
-            (out_hbm.at[cols, :], weight_out.at[cols, :]),
+    own, piece = d_pre_own.shape[0], row_refs[0].shape[0]
+    fetch, send = fetcher(sems), fetcher(out_sems)
+
+    def fetch_rows(which):
+        return [fetch(row_refs[i], rows.at[pl.ds(i * piece, piece)]) for i in which]
+
+    def fetch_weights(cols):
+        return (
+            fetch(in_hbm.at[:, cols], weight_in.at[:, cols]),
+            fetch(out_hbm.at[cols, :], weight_out.at[cols, :]),
         )
-    ]
-    rest = [
-        fetch(ref, rows.at[pl.ds(i * piece, piece)])
-        for i, ref in enumerate(row_refs)
-        if i * piece < own
-    ]
-    rest += [fetch(d_pre0, d_pre.at[:own, :]), fetch(h_cut0, h_cut.at[:own, :])]
-    for copy in first + weights[:2]:
+
+    first = fetch_rows(range(own // piece, pieces))
+    weights = [fetch_weights(tiles[0])]
+    rest = fetch_rows(range(own // piece))
+    rest.append(fetch(d_pre_own, d_pre.at[pl.ds(0, own)]))
+    rest.append(fetch(h_cut_own, h_cut.at[pl.ds(0, own)]))
+    weights += [fetch_weights(cols) for cols in tiles[1:]]
+    for copy in first:
         copy.wait()
     x, s = rows[own:, :width], rows[own:, width:]
     cut = grad_in.shape[0]
     mine = pl.ds(pl.multiple_of(lax.axis_index("dp") * cut, cut), cut)
     outs = []
-    for t, cols in enumerate(tiles):
-        if t == 1:
-            for copy in weights[2:] + rest:
-                copy.wait()
+    for t, (cols, (copy_in, copy_out)) in enumerate(zip(tiles, weights)):
+        copy_in.wait()
         act, slope = gelu_and_slope(dot(x, weight_in[:, cols]))
         hidden[:, cols] = act
+        copy_out.wait()
         d_pre[own:, cols] = (dot(s, weight_out[cols, :], (1, 1)) * slope).astype(BF16)
-    for t, cols in enumerate(tiles):
+        if t == 0:
+            for copy in rest:
+                copy.wait()
         grad_in[:, cols] = dot(rows[:, mine], d_pre[:, cols], (0, 0)).astype(BF16)
-        outs.append(
-            pltpu.make_async_copy(grad_in.at[:, cols], grad_in_hbm.at[:, cols], out_sems.at[t])
-        )
-        outs[-1].start()
+        outs.append(send(grad_in.at[:, cols], grad_in_hbm.at[:, cols]))
     h_cut[own:, :] = my_part(hidden)
-    grad_out[...] = dot(h_cut[...], rows[:, width:], (0, 0)).astype(BF16)
-    outs.append(pltpu.make_async_copy(grad_out, grad_out_hbm, out_sems.at[len(tiles)]))
-    outs[-1].start()
+    wide = width // 4
+    for at in range(0, width, wide):
+        cols = slice(at, at + wide)
+        s_cols = slice(width + at, width + at + wide)
+        grad_out[:, cols] = dot(h_cut[...], rows[:, s_cols], (0, 0)).astype(BF16)
+        outs.append(send(grad_out.at[:, cols], grad_out_hbm.at[:, cols]))
     for copy in outs:
         copy.wait()
 
@@ -295,42 +304,41 @@
         permute(blocks[k] if i < 2 else after(blocks[k], got_a[1 - i]), k)
         for i, k in enumerate(order_b)
     ]
-    weight_in, weight_out = call(
-        load_kernel,
-        [pltpu.VMEM((feat_width, ffw), BF16), pltpu.VMEM((ffw, feat_width), BF16)],
-        [after(proj_in[0], got_b[0]), after(proj_out[0], got_b[0])],
-        spaces=[pltpu.HBM] * 2,
-        scratch=[pltpu.SemaphoreType.DMA((2,))],
-    )
-    weights = [
-        pltpu.with_memory_space_constraint(w, pltpu.VMEM) for w in (weight_in, weight_out)
-    ]
     rows_a = jnp.concatenate(got_a, axis=0)
     chips_a = [shift_chips(rows_a, k) for k in range(1, groups // 2)]
     core_a = swap_cores(after(rows_a, got_b[0]))
     rows_b = jnp.concatenate(got_b, axis=0)
     chips_b = [shift_chips(rows_b, k) for k in range(1, groups // 2)]
     core_b = swap_cores(rows_b)
-    d_pre0, h_cut0, back = call(
+    weights = [proj_in[0], proj_out[0]]
+    weight_space = [pltpu.VMEM((feat_width, ffw), BF16), pltpu.VMEM((ffw, feat_width), BF16)]
+    d_pre, h_cut, back = call(
         functools.partial(own_kernel, tile, order),
         [
             pltpu.HBM((slots_all, ffw), BF16),
-            shape((slots_all, tile)),
+            pltpu.HBM((slots_all, tile), BF16),
             pltpu.HBM((slots_all, feat_width + LANES), BF16),
         ],
         [rows_a, rows_b, *weights],
         20 * product,
         scratch=[
+            *weight_space,
             pltpu.VMEM((slots_all, ffw), BF16),
             pltpu.VMEM((slots_all, ffw), BF16),
+            pltpu.VMEM((slots_all, tile), BF16),
             pltpu.VMEM((slots_all, feat_width + LANES), BF16),
-            pltpu.SemaphoreType.DMA((2,)),
-        ],
+            pltpu.SemaphoreType.DMA((2 * groups + 7,)),
+        ],
+        spaces=[pltpu.VMEM] * 2 + [pltpu.HBM] * 2,
     )
     back = lax.all_to_all(
-        back.reshape(experts, capacity, feat_width + LANES), "expert", 0, 0, tiled=True
+        after(back, core_a, core_b).reshape(experts, capacity, feat_width + LANES),
+        "expert",
+        0,
+        0,
+        tiled=True,
     ).reshape(slots_all, feat_width + LANES)
-    relayed_a = [swap_cores(after(rows, d_pre0)) for rows in chips_a]
+    relayed_a = [swap_cores(after(rows, d_pre)) for rows in chips_a]
     relayed_b = [swap_cores(rows) for rows in chips_b]
     pieces = [rows_a, rows_b, core_a, core_b, *chips_a, *relayed_a, *chips_b, *relayed_b]
     rows_all = groups * slots_all
@@ -340,27 +348,26 @@
             pltpu.HBM((feat_width // groups, ffw), BF16),
             pltpu.HBM((ffw // groups, feat_width), BF16),
         ],
-        [*pieces, d_pre0, h_cut0, proj_in[0], proj_out[0]],
+        [*pieces, d_pre, h_cut, *weights],
         4 * product,
         limit=32,
         scratch=[
             pltpu.VMEM((rows_all, 2 * feat_width), BF16),
-            pltpu.VMEM((feat_width, ffw), BF16),
-            pltpu.VMEM((ffw, feat_width), BF16),
+            *weight_space,
             pltpu.VMEM((rows_all - slots_all, ffw), BF16),
             pltpu.VMEM((rows_all, tile), BF16),
             pltpu.VMEM((rows_all, ffw), BF16),
             pltpu.VMEM((feat_width // groups, ffw), BF16),
             pltpu.VMEM((ffw // groups, feat_width), BF16),
             pltpu.SemaphoreType.DMA((len(pieces) + 2 * groups + 2,)),
-            pltpu.SemaphoreType.DMA((groups + 1,)),
-        ],
-        spaces=[pl.ANY] * len(pieces) + [pltpu.HBM, pl.ANY] + [pltpu.HBM] * 2,
+            pltpu.SemaphoreType.DMA((groups + 4,)),
+        ],
+        spaces=[pl.ANY] * len(pieces) + [pltpu.HBM] * 4,
     )
     token_grads, gate_grads = call(
         functools.partial(combine_kernel, experts, capacity),
         [shape((tok_count, feat_width)), shape((2, tok_count))],
-        [*places, gates.T, back],
+        [*places, gates.T, after(back, grad_in)],
         scratch=[pltpu.VMEM((slots_all, feat_width + LANES), BF16)],
     )
     return (token_grads, gate_grads.T, grad_in[None], grad_out[None])

time: 51.9 us -> 47.8 us (0.921)
  waiting for transfers between devices: 9.87 us -> 6.41 us
    all_to_all x1, waiting for transfers between devices: 8.19 us -> 0.01 us  [local(): lax.all_to_all(after(back, core_a, core_b).reshape(experts, capacity, fea...]
    ppermute x7, waiting for transfers between devices: 1.66 us -> 5 us  [permute(): lax.ppermute(block, 'expert', [(i, i ^ k) for i in range(lax.axis_size('e...]
    ppermute x4, waiting for transfers between devices: 0.01 us -> 1.4 us  [swap_cores(): lax.ppermute(rows, 'dp', [(i, i ^ 1) for i in range(lax.axis_size('dp'))])]
    ppermute x7, starting transfers between devices: 14 us -> 13.1 us  [permute(): lax.ppermute(block, 'expert', [(i, i ^ k) for i in range(lax.axis_size('e...]
    all_to_all x1, starting transfers between devices: 3.92 us -> 4.8 us  [local(): lax.all_to_all(after(back, core_a, core_b).reshape(experts, capacity, fea...]
    pallas_call x5 -> x4, Pallas kernels: 18.9 us -> 18.8 us  [call(): pl.pallas_call(kernel, out_shape=out_shape, in_specs=[pl.BlockSpec(memory...]
  transfers between devices with their start and end apart: 14 -> 14, of which waited for: 3 -> 5; matrix products, arithmetic and copies ran while one was open for 0% -> 0% of each run, Pallas kernels for 17% -> 35%
where the time goes in v7:
time: 47.8 us; the launch traced here: 47.6 us
  starting transfers between devices  21.6 us (45%)
  Pallas kernels  18.8 us (39%)
  waiting for transfers between devices  6.41 us (13%)
  between operations  0.74 us (2%)
    pallas_call x4, Pallas kernels, call(): pl.pallas_call(kernel, out_shape=out_shape, in_specs=[pl.BlockSpec(memory...  18.8 us
    ppermute x7, starting transfers between devices, permute(): lax.ppermute(block, 'expert', [(i, i ^ k) for i in range(lax.axis_size('e...  13.1 us
    ppermute x7, waiting for transfers between devices, permute(): lax.ppermute(block, 'expert', [(i, i ^ k) for i in range(lax.axis_size('e...  5 us
    all_to_all x1, starting transfers between devices, local(): lax.all_to_all(after(back, core_a, core_b).reshape(experts, capacity, fea...  4.8 us
    ppermute x2, starting transfers between devices, shift_chips(): lax.ppermute(rows, 'dp', [(i, (i + 2 * k) % groups) for i in range(groups)])  3.17 us
    ppermute x4, waiting for transfers between devices, swap_cores(): lax.ppermute(rows, 'dp', [(i, i ^ 1) for i in range(lax.axis_size('dp'))])  1.4 us
  transfers between devices with their start and end apart: 14, of which 5 were waited for; matrix products, arithmetic and copies ran while one was open for 0% of the time, Pallas kernels for 35%

profile of v7, /device:TPU:0, one launch (start us, length us, event | category | flops | bytes accessed | tf_op | source)
XLA Modules:
  0.0 47.6 jit_solution(12753652626881420924)
XLA Ops:
  0.6 1.4 %shard_map.93 = (bf16[16,2048]{1,0:T(8,128)(2,1)S(1)}, bf16[16,2048]{1,0:T(8,128)(2,1)S(1)}, bf16[16,2048]{1,0:T(8,128)(2,1)S(1)}, bf16[16,2048]{1,0:T(8,128)(2,...) custom-call(s32[2,64]{1,0:T(2,128)} %bitcast.17, ...), custom_call_target="tpu_custom_call" | custom-call | bytes 262912 | tf_op jit(solution)/shard_map/pallas_call | solution.py:35
  2.0 6.0 %collective-permute-start = (bf16[16,2048]{1,0:T(8,128)(2,1)S(1)}, bf16[16,2048]{1,0:T(8,128)(2,1)S(1)}, u32[]{:S(2)}, u32[]{:S(2)}) collective-permute-start(bf16[16,2048]{1,0:T(8,128)(2,1)S(1)} %get-tuple-element.30), channel_id=1, source_target_pairs={{0,7},{1,6},{2,5},{3,4},{4,3},{5,2},{6,1},{7,0},{8,15},{9,14},{10,... | collective-permute-start | bytes 196616 | tf_op jit(solution)/shard_map/ppermute | solution.py:253
  8.1 0.2 collective-permute-start.1
  8.3 0.4 collective-permute-start.2
  8.7 1.8 %collective-permute-start.3 = (bf16[16,2048]{1,0:T(8,128)(2,1)S(1)}, bf16[16,2048]{1,0:T(8,128)(2,1)S(1)}, u32[]{:S(2)}, u32[]{:S(2)}) collective-permute-start(bf16[16,2048]{1,0:T(8,128)(2,1)S(1)} %get-tuple-element.33), channel_id=1, source_target_pairs={{0,5},{1,4},{2,7},{3,6},{4,1},{5,0},{6,3},{7,2},{8,13},{9,12},{10,... | collective-permute-start | bytes 196616 | tf_op jit(solution)/shard_map/ppermute | solution.py:253
  10.6 2.1 %collective-permute-start.4 = (bf16[16,2048]{1,0:T(8,128)(2,1)S(1)}, bf16[16,2048]{1,0:T(8,128)(2,1)S(1)}, u32[]{:S(2)}, u32[]{:S(2)}) collective-permute-start(bf16[16,2048]{1,0:T(8,128)(2,1)S(1)} %get-tuple-element.34), channel_id=1, source_target_pairs={{0,4},{1,5},{2,6},{3,7},{4,0},{5,1},{6,2},{7,3},{8,12},{9,13},{10,... | collective-permute-start | bytes 196616 | tf_op jit(solution)/shard_map/ppermute | solution.py:253
  12.7 1.5 %collective-permute-done.1 = bf16[16,2048]{1,0:T(8,128)(2,1)S(1)} collective-permute-done((bf16[16,2048]{1,0:T(8,128)(2,1)S(1)}, bf16[16,2048]{1,0:T(8,128)(2,1)S(1)}, u32[]{:S(2)}, u32[]{:S(2)}) %collective-permute-start.1) | collective-permute-done | bytes 65568 | tf_op jit(solution)/shard_map/ppermute | solution.py:253
  14.2 2.4 %collective-permute-start.6 = (bf16[16,2048]{1,0:T(8,128)(2,1)S(1)}, bf16[16,2048]{1,0:T(8,128)(2,1)S(1)}, u32[]{:S(2)}, u32[]{:S(2)}) collective-permute-start(bf16[16,2048]{1,0:T(8,128)(2,1)S(1)} %get-tuple-element.38), channel_id=1, source_target_pairs={{0,2},{1,3},{2,0},{3,1},{4,6},{5,7},{6,4},{7,5},{8,10},{9,11},{10,... | collective-permute-start | bytes 196616 | tf_op jit(solution)/shard_map/ppermute | solution.py:253
  16.6 0.0 collective-permute-done.2
  16.6 0.0 collective-permute-start.5
  16.7 0.0 collective-permute-done
  16.7 1.6 %collective-permute-start.9 = (bf16[64,2048]{1,0:T(8,128)(2,1)S(1)}, bf16[64,2048]{1,0:T(8,128)(2,1)S(1)}, u32[]{:S(2)}, u32[]{:S(2)}) collective-permute-start(bf16[64,2048]{1,0:T(8,128)(2,1)S(1)} %constant_dynamic-update-slice_fusion.refs_0_), channel_id=1, source_target_pairs={{0,16},{8,24},{16,0},{24,8},{1,17},{9,25},{17,1},{25,9},{2,18},{10... | collective-permute-start | bytes 786440 | tf_op jit(solution)/shard_map/ppermute | solution.py:262
  18.3 0.0 collective-permute-done.3
  18.3 0.0 collective-permute-start.7
  18.3 1.1 %collective-permute-done.4 = bf16[16,2048]{1,0:T(8,128)(2,1)S(1)} collective-permute-done((bf16[16,2048]{1,0:T(8,128)(2,1)S(1)}, bf16[16,2048]{1,0:T(8,128)(2,1)S(1)}, u32[]{:S(2)}, u32[]{:S(2)}) %collective-permute-start.4) | collective-permute-done | bytes 65568 | tf_op jit(solution)/shard_map/ppermute | solution.py:253
  19.4 2.4 %collective-permute-done.5 = bf16[16,2048]{1,0:T(8,128)(2,1)S(1)} collective-permute-done((bf16[16,2048]{1,0:T(8,128)(2,1)S(1)}, bf16[16,2048]{1,0:T(8,128)(2,1)S(1)}, u32[]{:S(2)}, u32[]{:S(2)}) %collective-permute-start.5) | collective-permute-done | bytes 65568 | tf_op jit(solution)/shard_map/ppermute | solution.py:253
  21.8 0.0 collective-permute-done.6
  21.8 1.6 %collective-permute-start.11 = (bf16[64,2048]{1,0:T(8,128)(2,1)S(1)}, bf16[64,2048]{1,0:T(8,128)(2,1)S(1)}, u32[]{:S(2)}, u32[]{:S(2)}) collective-permute-start(bf16[64,2048]{1,0:T(8,128)(2,1)S(1)} %constant_dynamic-update-slice_fusion.4.refs_1_), channel_id=1, source_target_pairs={{0,16},{8,24},{16,0},{24,8},{1,17},{9,25},{17,1},{25,9},{2,18},{10... | collective-permute-start | bytes 786440 | tf_op jit(solution)/shard_map/ppermute | solution.py:262
  23.4 0.0 collective-permute-start.8
  23.4 6.9 %shard_map.94 = (bf16[128,2048]{1,0:T(8,128)(2,1)}, bf16[128,512]{1,0:T(8,128)(2,1)}, bf16[128,1152]{1,0:T(8,128)(2,1)}) custom-call(bf16[64,2048]{1,0:T(8,128)(2,1)S(1)} %constant_dynamic-update-slice_fusion.refs_0_, bf16[64,2048]{1,0:T(8,128)(2,1)S(1)} %constant_dynamic-update-slice_fusion.4.refs_1_, bf16[1024,2048]{1,0:T(8,128)(2,1)} %bitcast.12, ...), custom_call_target="tpu_custom_call" | custom-call | flops 10737418240 | bytes 8912896 | tf_op jit(solution)/shard_map/pallas_call | solution.py:35
  30.3 0.0 collective-permute-done.7.refs_2_
  30.3 0.0 collective-permute-done.8.refs_3_
  30.3 4.8 %all-to-all-start = ((bf16[8,16,1152]{2,1,0:T(8,128)(2,1)}), bf16[8,16,1152]{2,1,0:T(8,128)(2,1)S(1)}, u32[]{:S(2)}, u32[]{:S(2)}) async-start(bf16[8,16,1152]{2,1,0:T(8,128)(2,1)} %bitcast.16), calls=%async_computation | async-start | bytes 589824 | tf_op jit(solution)/shard_map/all_to_all | solution.py:334
  35.1 0.0 collective-permute-done.9.refs_4_
  35.1 0.3 collective-permute-start.10
  35.4 0.0 collective-permute-done.11.refs_6_
  35.4 0.3 collective-permute-start.12
  35.7 1.0 %collective-permute-done.10.refs_5_ = bf16[64,2048]{1,0:T(8,128)(2,1)S(1)} collective-permute-done((bf16[64,2048]{1,0:T(8,128)(2,1)S(1)}, bf16[64,2048]{1,0:T(8,128)(2,1)S(1)}, u32[]{:S(2)}, u32[]{:S(2)}) %collective-permute-start.10) | collective-permute-done | bytes 262176 | tf_op jit(solution)/shard_map/ppermute | solution.py:257
  36.7 0.4 collective-permute-done.12.refs_7_
  37.1 0.0 copy-start
  37.1 9.6 %shard_map.95 = (bf16[256,2048]{1,0:T(8,128)(2,1)}, bf16[512,1024]{1,0:T(8,128)(2,1)}) custom-call(bf16[64,2048]{1,0:T(8,128)(2,1)S(1)} %constant_dynamic-update-slice_fusion.refs_0_, bf16[64,2048]{1,0:T(8,128)(2,1)S(1)} %constant_dynamic-update-slice_fusion.4.refs_1_, bf16[64,2048]{1,0:T(8,128)(2,1)S(1)} %collective-permute-done.7.refs_2_, ...), custom_call_target="tpu_custom_call" | custom-call | flops 2147483648 | bytes 11141120 | tf_op jit(solution)/shard_map/pallas_call | solution.py:35
  46.7 0.0 all-to-all-done
  46.7 0.0 copy-done
  46.7 0.9 %shard_map.96 = (bf16[64,1024]{1,0:T(8,128)(2,1)}, bf16[2,64]{1,0:T(2,128)(2,1)}) custom-call(bf16[128,64]{1,0:T(8,128)(2,1)S(1)} %get-tuple-element.27.place0, bf16[128,64]{1,0:T(8,128)(2,1)S(1)} %get-tuple-element.28.place1, bf16[2,64]{1,0:T(2,128)(2,1)S(1)} %bitcast.11, bf16[128,1152]{1,0:T(8,128)(2,1)S(1)} %bitcast.9), custom_call_target="tpu_custom_call" | custom-call | bytes 327936 | tf_op jit(solution)/shard_map/pallas_call | solution.py:35
  (8 shorter events, 0.0 us)
Async XLA Ops:
  2.0 14.6 %collective-permute-start = (bf16[16,2048]{1,0:T(8,128)(2,1)S(1)}, bf16[16,2048]{1,0:T(8,128)(2,1)S(1)}, u32[]{:S(2)}, u32[]{:S(2)}) collective-permute-start(bf16[16,2048]{1,0:T(8,128)(2,1)S(1)} %get-tuple-element.30), channel_id=1, source_target_pairs={{0,7},{1,6},{2,5},{3,4},{4,3},{5,2},{6,1},{7,0},{8,15},{9,14},{10,... | collective-permute-start | bytes 196616 | tf_op jit(solution)/shard_map/ppermute | solution.py:253
  8.1 6.1 %collective-permute-start.1 = (bf16[16,2048]{1,0:T(8,128)(2,1)S(1)}, bf16[16,2048]{1,0:T(8,128)(2,1)S(1)}, u32[]{:S(2)}, u32[]{:S(2)}) collective-permute-start(bf16[16,2048]{1,0:T(8,128)(2,1)S(1)} %get-tuple-element.31), channel_id=1, source_target_pairs={{0,6},{1,7},{2,4},{3,5},{4,2},{5,3},{6,0},{7,1},{8,14},{9,15},{10,... | collective-permute-start | bytes 196616 | tf_op jit(solution)/shard_map/ppermute | solution.py:253
  8.3 8.3 %collective-permute-start.2 = (bf16[16,2048]{1,0:T(8,128)(2,1)S(1)}, bf16[16,2048]{1,0:T(8,128)(2,1)S(1)}, u32[]{:S(2)}, u32[]{:S(2)}) collective-permute-start(bf16[16,2048]{1,0:T(8,128)(2,1)S(1)} %get-tuple-element.32), channel_id=1, source_target_pairs={{0,1},{1,0},{2,3},{3,2},{4,5},{5,4},{6,7},{7,6},{8,9},{9,8},{10,11... | collective-permute-start | bytes 196616 | tf_op jit(solution)/shard_map/ppermute | solution.py:253
  8.7 9.6 %collective-permute-start.3 = (bf16[16,2048]{1,0:T(8,128)(2,1)S(1)}, bf16[16,2048]{1,0:T(8,128)(2,1)S(1)}, u32[]{:S(2)}, u32[]{:S(2)}) collective-permute-start(bf16[16,2048]{1,0:T(8,128)(2,1)S(1)} %get-tuple-element.33), channel_id=1, source_target_pairs={{0,5},{1,4},{2,7},{3,6},{4,1},{5,0},{6,3},{7,2},{8,13},{9,12},{10,... | collective-permute-start | bytes 196616 | tf_op jit(solution)/shard_map/ppermute | solution.py:253
  10.6 8.8 %collective-permute-start.4 = (bf16[16,2048]{1,0:T(8,128)(2,1)S(1)}, bf16[16,2048]{1,0:T(8,128)(2,1)S(1)}, u32[]{:S(2)}, u32[]{:S(2)}) collective-permute-start(bf16[16,2048]{1,0:T(8,128)(2,1)S(1)} %get-tuple-element.34), channel_id=1, source_target_pairs={{0,4},{1,5},{2,6},{3,7},{4,0},{5,1},{6,2},{7,3},{8,12},{9,13},{10,... | collective-permute-start | bytes 196616 | tf_op jit(solution)/shard_map/ppermute | solution.py:253
  14.2 7.5 %collective-permute-start.6 = (bf16[16,2048]{1,0:T(8,128)(2,1)S(1)}, bf16[16,2048]{1,0:T(8,128)(2,1)S(1)}, u32[]{:S(2)}, u32[]{:S(2)}) collective-permute-start(bf16[16,2048]{1,0:T(8,128)(2,1)S(1)} %get-tuple-element.38), channel_id=1, source_target_pairs={{0,2},{1,3},{2,0},{3,1},{4,6},{5,7},{6,4},{7,5},{8,10},{9,11},{10,... | collective-permute-start | bytes 196616 | tf_op jit(solution)/shard_map/ppermute | solution.py:253
  16.6 5.2 %collective-permute-start.5 = (bf16[16,2048]{1,0:T(8,128)(2,1)S(1)}, bf16[16,2048]{1,0:T(8,128)(2,1)S(1)}, u32[]{:S(2)}, u32[]{:S(2)}) collective-permute-start(bf16[16,2048]{1,0:T(8,128)(2,1)S(1)} %get-tuple-element.36), channel_id=1, source_target_pairs={{0,3},{1,2},{2,1},{3,0},{4,7},{5,6},{6,5},{7,4},{8,11},{9,10},{10,... | collective-permute-start | bytes 196616 | tf_op jit(solution)/shard_map/ppermute | solution.py:253
  16.7 18.4 %collective-permute-start.9 = (bf16[64,2048]{1,0:T(8,128)(2,1)S(1)}, bf16[64,2048]{1,0:T(8,128)(2,1)S(1)}, u32[]{:S(2)}, u32[]{:S(2)}) collective-permute-start(bf16[64,2048]{1,0:T(8,128)(2,1)S(1)} %constant_dynamic-update-slice_fusion.refs_0_), channel_id=1, source_target_pairs={{0,16},{8,24},{16,0},{24,8},{1,17},{9,25},{17,1},{25,9},{2,18},{10... | collective-permute-start | bytes 786440 | tf_op jit(solution)/shard_map/ppermute | solution.py:262
  18.3 12.0 %collective-permute-start.7 = (bf16[64,2048]{1,0:T(8,128)(2,1)S(1)}, bf16[64,2048]{1,0:T(8,128)(2,1)S(1)}, u32[]{:S(2)}, u32[]{:S(2)}) collective-permute-start(bf16[64,2048]{1,0:T(8,128)(2,1)S(1)} %constant_dynamic-update-slice_fusion.refs_0_), channel_id=1, source_target_pairs={{0,8},{8,0},{16,24},{24,16},{1,9},{9,1},{17,25},{25,17},{2,10},{10... | collective-permute-start | bytes 786440 | tf_op jit(solution)/shard_map/ppermute | solution.py:257
  21.8 13.6 %collective-permute-start.11 = (bf16[64,2048]{1,0:T(8,128)(2,1)S(1)}, bf16[64,2048]{1,0:T(8,128)(2,1)S(1)}, u32[]{:S(2)}, u32[]{:S(2)}) collective-permute-start(bf16[64,2048]{1,0:T(8,128)(2,1)S(1)} %constant_dynamic-update-slice_fusion.4.refs_1_), channel_id=1, source_target_pairs={{0,16},{8,24},{16,0},{24,8},{1,17},{9,25},{17,1},{25,9},{2,18},{10... | collective-permute-start | bytes 786440 | tf_op jit(solution)/shard_map/ppermute | solution.py:262
  23.4 6.9 %collective-permute-start.8 = (bf16[64,2048]{1,0:T(8,128)(2,1)S(1)}, bf16[64,2048]{1,0:T(8,128)(2,1)S(1)}, u32[]{:S(2)}, u32[]{:S(2)}) collective-permute-start(bf16[64,2048]{1,0:T(8,128)(2,1)S(1)} %constant_dynamic-update-slice_fusion.4.refs_1_), channel_id=1, source_target_pairs={{0,8},{8,0},{16,24},{24,16},{1,9},{9,1},{17,25},{25,17},{2,10},{10... | collective-permute-start | bytes 786440 | tf_op jit(solution)/shard_map/ppermute | solution.py:257
  30.3 16.4 %all-to-all-start = ((bf16[8,16,1152]{2,1,0:T(8,128)(2,1)}), bf16[8,16,1152]{2,1,0:T(8,128)(2,1)S(1)}, u32[]{:S(2)}, u32[]{:S(2)}) async-start(bf16[8,16,1152]{2,1,0:T(8,128)(2,1)} %bitcast.16), calls=%async_computation | async-start | bytes 589824 | tf_op jit(solution)/shard_map/all_to_all | solution.py:334
  35.1 1.6 %collective-permute-start.10 = (bf16[64,2048]{1,0:T(8,128)(2,1)S(1)}, bf16[64,2048]{1,0:T(8,128)(2,1)S(1)}, u32[]{:S(2)}, u32[]{:S(2)}) collective-permute-start(bf16[64,2048]{1,0:T(8,128)(2,1)S(1)} %collective-permute-done.9.refs_4_), channel_id=1, source_target_pairs={{0,8},{8,0},{16,24},{24,16},{1,9},{9,1},{17,25},{25,17},{2,10},{10... | collective-permute-start | bytes 786440 | tf_op jit(solution)/shard_map/ppermute | solution.py:257
  35.4 1.7 %collective-permute-start.12 = (bf16[64,2048]{1,0:T(8,128)(2,1)S(1)}, bf16[64,2048]{1,0:T(8,128)(2,1)S(1)}, u32[]{:S(2)}, u32[]{:S(2)}) collective-permute-start(bf16[64,2048]{1,0:T(8,128)(2,1)S(1)} %collective-permute-done.11.refs_6_), channel_id=1, source_target_pairs={{0,8},{8,0},{16,24},{24,16},{1,9},{9,1},{17,25},{25,17},{2,10},{10... | collective-permute-start | bytes 786440 | tf_op jit(solution)/shard_map/ppermute | solution.py:257
  37.1 9.6 %copy-start = (bf16[64,2]{0,1:T(2,128)(2,1)S(1)}, bf16[64,2]{0,1:T(2,128)(2,1)}, u32[]{:S(2)}) copy-start(bf16[64,2]{0,1:T(2,128)(2,1)} %param.9) | copy-start | bytes 772

commit v8 on v7

--- a/solution.py
+++ b/solution.py
@@ -19,10 +19,33 @@
     )
 
 
-def gelu_and_slope(pre_act):
-    cdf = 0.5 * (1.0 + lax.erf(pre_act * 0.7071067811865476))
-    pdf = jnp.exp(-0.5 * pre_act * pre_act) * 0.3989422804014327
-    return (pre_act * cdf).astype(BF16), cdf + pre_act * pdf
+ERFCX = (
+    0.253879726412498,
+    0.2540954353994894,
+    0.22517936671423447,
+    0.19823402024047995,
+    0.02224511740159976,
+    0.22829329587490593,
+    -0.2514442500538998,
+    0.06951765914158435,
+)
+
+
+def gelu_and_slope(pre_act, invert=lambda v: 1.0 / v):
+    gauss = jnp.exp(-0.5 * pre_act * pre_act)
+    t = invert(1.0 + (0.45 * 0.7071067811865476) * jnp.abs(pre_act))
+    poly = 0.5 * ERFCX[-1]
+    for c in ERFCX[-2::-1]:
+        poly = poly * t + 0.5 * c
+    tail = gauss * t * poly
+    cdf = jnp.where(pre_act < 0.0, tail, 1.0 - tail)
+    return (pre_act * cdf).astype(BF16), cdf + pre_act * (gauss * 0.3989422804014327)
+
+
+def activate(pre_act):
+    return gelu_and_slope(
+        pre_act, functools.partial(pltpu.reciprocal, approx=False, full_range=False)
+    )
 
 
 def call(kernel, out_shape, args, flops=0, limit=24, scratch=(), spaces=None):
@@ -142,28 +165,19 @@
 
 def own_kernel(tile, order, *refs):
     row_refs, refs = refs[:2], refs[2:]
-    in_hbm, out_hbm, d_pre_hbm, h_cut_hbm, back_hbm, *scratch = refs
-    weight_in, weight_out, hidden, d_pre, h_cut, back, sems = scratch
+    weight_in, weight_out, d_pre_hbm, h_cut_hbm, back_hbm, *scratch = refs
+    hidden, d_pre, h_cut, back, sems = scratch
     me = lax.axis_index("expert")
     width, ffw = weight_in.shape
     tiles = [slice(at, at + tile) for at in range(0, ffw, tile)]
     fetch = fetcher(sems)
-    copies = [
-        (
-            fetch(in_hbm.at[:, cols], weight_in.at[:, cols]),
-            fetch(out_hbm.at[cols, :], weight_out.at[cols, :]),
-        )
-        for cols in tiles
-    ]
     x, s = stack(row_refs, 0, width), stack(row_refs, 1, width)
     slots_all = x.shape[0]
     capacity = slots_all // len(order)
     dgate = jnp.zeros((slots_all, LANES), F32)
-    for cols, (copy_in, copy_out) in zip(tiles, copies):
-        copy_in.wait()
-        act, slope = gelu_and_slope(dot(x, weight_in[:, cols]))
+    for cols in tiles:
+        act, slope = activate(dot(x, weight_in[:, cols]))
         hidden[:, cols] = act
-        copy_out.wait()
         d_hidden = dot(s, weight_out[cols, :], (1, 1))
         d_pre[:, cols] = (d_hidden * slope).astype(BF16)
         product = d_hidden * act.astype(F32)
@@ -223,15 +237,17 @@
     cut = grad_in.shape[0]
     mine = pl.ds(pl.multiple_of(lax.axis_index("dp") * cut, cut), cut)
     outs = []
-    for t, (cols, (copy_in, copy_out)) in enumerate(zip(tiles, weights)):
-        copy_in.wait()
-        act, slope = gelu_and_slope(dot(x, weight_in[:, cols]))
+    for t, cols in enumerate(tiles):
+        if t == 1:
+            for copy in [copy for pair in weights[1:] for copy in pair] + rest:
+                copy.wait()
+        if t == 0:
+            for copy in weights[0]:
+                copy.wait()
+        act, slope = activate(dot(x, weight_in[:, cols]))
         hidden[:, cols] = act
-        copy_out.wait()
         d_pre[own:, cols] = (dot(s, weight_out[cols, :], (1, 1)) * slope).astype(BF16)
-        if t == 0:
-            for copy in rest:
-                copy.wait()
+    for cols in tiles:
         grad_in[:, cols] = dot(rows[:, mine], d_pre[:, cols], (0, 0)).astype(BF16)
         outs.append(send(grad_in.at[:, cols], grad_in_hbm.at[:, cols]))
     h_cut[own:, :] = my_part(hidden)
@@ -286,6 +302,7 @@
         functools.partial(route_kernel, experts, capacity),
         [shape((capacity, 2 * feat_width))] * experts + [place] * 2,
         [routes.T, gates.T, tokens, cotangent],
+        30 * product,
         spaces=[pltpu.HBM] * 4,
         scratch=[
             pltpu.VMEM((2, tok_count), jnp.int32),
@@ -297,11 +314,13 @@
     )
     blocks, places = routed[:experts], routed[experts:]
     rest = list(range(experts - 1, 1, -1))
+    if len(rest) > 4:
+        rest.insert(2, rest.pop(-2))
     order = [0, *rest[:2], 1, *rest[2:]]
     order_a, order_b = order[:half], order[half:]
     got_a = [blocks[0]] + [permute(blocks[k], k) for k in order_a[1:]]
     got_b = [
-        permute(blocks[k] if i < 2 else after(blocks[k], got_a[1 - i]), k)
+        permute(blocks[k] if i < 2 else after(blocks[k], got_a[-1]), k)
         for i, k in enumerate(order_b)
     ]
     rows_a = jnp.concatenate(got_a, axis=0)
@@ -319,17 +338,19 @@
             pltpu.HBM((slots_all, tile), BF16),
             pltpu.HBM((slots_all, feat_width + LANES), BF16),
         ],
-        [rows_a, rows_b, *weights],
+        [
+            rows_a,
+            rows_b,
+            *[pltpu.with_memory_space_constraint(w, pltpu.VMEM) for w in weights],
+        ],
         20 * product,
         scratch=[
-            *weight_space,
             pltpu.VMEM((slots_all, ffw), BF16),
             pltpu.VMEM((slots_all, ffw), BF16),
             pltpu.VMEM((slots_all, tile), BF16),
             pltpu.VMEM((slots_all, feat_width + LANES), BF16),
-            pltpu.SemaphoreType.DMA((2 * groups + 7,)),
-        ],
-        spaces=[pltpu.VMEM] * 2 + [pltpu.HBM] * 2,
+            pltpu.SemaphoreType.DMA((7,)),
+        ],
     )
     back = lax.all_to_all(
         after(back, core_a, core_b).reshape(experts, capacity, feat_width + LANES),

time: 47.8 us -> 44.6 us (0.933)
  waiting for transfers between devices: 6.41 us -> 1.96 us
  starting transfers between devices: 21.6 us -> 24.2 us
  Pallas kernels: 18.8 us -> 17.4 us
    ppermute x7, waiting for transfers between devices: 5 us -> 0.55 us  [permute(): lax.ppermute(block, 'expert', [(i, i ^ k) for i in range(lax.axis_size('e...]
    ppermute x7, starting transfers between devices: 13.1 us -> 16.7 us  [permute(): lax.ppermute(block, 'expert', [(i, i ^ k) for i in range(lax.axis_size('e...]
    pallas_call x4, Pallas kernels: 18.8 us -> 17.4 us  [call(): pl.pallas_call(kernel, out_shape=out_shape, in_specs=[pl.BlockSpec(memory...]
    all_to_all x1, starting transfers between devices: 4.8 us -> 3.71 us  [local(): lax.all_to_all(after(back, core_a, core_b).reshape(experts, capacity, fea...]
  transfers between devices with their start and end apart: 14 -> 14, of which waited for: 5 -> 3; matrix products, arithmetic and copies ran while one was open for 0% -> 0% of each run, Pallas kernels for 35% -> 34%
where the time goes in v8:
time: 44.6 us; the launch traced here: 44.4 us
  starting transfers between devices  24.2 us (54%)
  Pallas kernels  17.4 us (39%)
  waiting for transfers between devices  1.96 us (4%)
  between operations  0.78 us (2%)
    pallas_call x4, Pallas kernels, call(): pl.pallas_call(kernel, out_shape=out_shape, in_specs=[pl.BlockSpec(memory...  17.4 us
    ppermute x7, starting transfers between devices, permute(): lax.ppermute(block, 'expert', [(i, i ^ k) for i in range(lax.axis_size('e...  16.7 us
    all_to_all x1, starting transfers between devices, local(): lax.all_to_all(after(back, core_a, core_b).reshape(experts, capacity, fea...  3.71 us
    ppermute x2, starting transfers between devices, shift_chips(): lax.ppermute(rows, 'dp', [(i, (i + 2 * k) % groups) for i in range(groups)])  3.13 us
    ppermute x4, waiting for transfers between devices, swap_cores(): lax.ppermute(rows, 'dp', [(i, i ^ 1) for i in range(lax.axis_size('dp'))])  1.4 us
  transfers between devices with their start and end apart: 14, of which 3 were waited for; matrix products, arithmetic and copies ran while one was open for 0% of the time, Pallas kernels for 34%

profile of v8, /device:TPU:0, one launch (start us, length us, event | category | flops | bytes accessed | tf_op | source)
XLA Modules:
  0.0 44.4 jit_solution(11505426578265717618)
XLA Ops:
  0.6 0.0 copy-start
  0.6 0.0 copy-start.1
  0.7 1.6 %shard_map.93 = (bf16[16,2048]{1,0:T(8,128)(2,1)S(1)}, bf16[16,2048]{1,0:T(8,128)(2,1)S(1)}, bf16[16,2048]{1,0:T(8,128)(2,1)S(1)}, bf16[16,2048]{1,0:T(8,128)(2,...) custom-call(s32[2,64]{1,0:T(2,128)} %bitcast.19, ...), custom_call_target="tpu_custom_call" | custom-call | flops 16106127360 | bytes 262912 | tf_op jit(solution)/shard_map/pallas_call | solution.py:58
  2.2 6.0 %collective-permute-start = (bf16[16,2048]{1,0:T(8,128)(2,1)S(1)}, bf16[16,2048]{1,0:T(8,128)(2,1)S(1)}, u32[]{:S(2)}, u32[]{:S(2)}) collective-permute-start(bf16[16,2048]{1,0:T(8,128)(2,1)S(1)} %get-tuple-element.30), channel_id=1, source_target_pairs={{0,7},{1,6},{2,5},{3,4},{4,3},{5,2},{6,1},{7,0},{8,15},{9,14},{10,... | collective-permute-start | bytes 196616 | tf_op jit(solution)/shard_map/ppermute | solution.py:269
  8.3 0.2 collective-permute-start.1
  8.5 0.4 collective-permute-start.2
  8.9 0.8 %collective-permute-start.3 = (bf16[16,2048]{1,0:T(8,128)(2,1)S(1)}, bf16[16,2048]{1,0:T(8,128)(2,1)S(1)}, u32[]{:S(2)}, u32[]{:S(2)}) collective-permute-start(bf16[16,2048]{1,0:T(8,128)(2,1)S(1)} %get-tuple-element.33), channel_id=1, source_target_pairs={{0,3},{1,2},{2,1},{3,0},{4,7},{5,6},{6,5},{7,4},{8,11},{9,10},{10,... | collective-permute-start | bytes 196616 | tf_op jit(solution)/shard_map/ppermute | solution.py:269
  9.7 4.4 %collective-permute-start.4 = (bf16[16,2048]{1,0:T(8,128)(2,1)S(1)}, bf16[16,2048]{1,0:T(8,128)(2,1)S(1)}, u32[]{:S(2)}, u32[]{:S(2)}) collective-permute-start(bf16[16,2048]{1,0:T(8,128)(2,1)S(1)} %get-tuple-element.34), channel_id=1, source_target_pairs={{0,5},{1,4},{2,7},{3,6},{4,1},{5,0},{6,3},{7,2},{8,13},{9,12},{10,... | collective-permute-start | bytes 196616 | tf_op jit(solution)/shard_map/ppermute | solution.py:269
  14.1 0.0 collective-permute-done.2
  14.1 0.1 collective-permute-start.5
  14.2 0.0 collective-permute-done
  14.2 4.8 %collective-permute-start.6 = (bf16[16,2048]{1,0:T(8,128)(2,1)S(1)}, bf16[16,2048]{1,0:T(8,128)(2,1)S(1)}, u32[]{:S(2)}, u32[]{:S(2)}) collective-permute-start(bf16[16,2048]{1,0:T(8,128)(2,1)S(1)} %get-tuple-element.38), channel_id=1, source_target_pairs={{0,2},{1,3},{2,0},{3,1},{4,6},{5,7},{6,4},{7,5},{8,10},{9,11},{10,... | collective-permute-start | bytes 196616 | tf_op jit(solution)/shard_map/ppermute | solution.py:269
  19.0 0.0 collective-permute-done.1
  19.0 1.6 %collective-permute-start.9 = (bf16[64,2048]{1,0:T(8,128)(2,1)S(1)}, bf16[64,2048]{1,0:T(8,128)(2,1)S(1)}, u32[]{:S(2)}, u32[]{:S(2)}) collective-permute-start(bf16[64,2048]{1,0:T(8,128)(2,1)S(1)} %constant_dynamic-update-slice_fusion.refs_0_), channel_id=1, source_target_pairs={{0,16},{8,24},{16,0},{24,8},{1,17},{9,25},{17,1},{25,9},{2,18},{10... | collective-permute-start | bytes 786440 | tf_op jit(solution)/shard_map/ppermute | solution.py:278
  20.6 0.0 collective-permute-done.3
  20.6 0.0 collective-permute-start.7
  20.6 0.0 collective-permute-done.4
  20.7 0.0 collective-permute-done.5
  20.7 0.5 %collective-permute-done.6 = bf16[16,2048]{1,0:T(8,128)(2,1)S(1)} collective-permute-done((bf16[16,2048]{1,0:T(8,128)(2,1)S(1)}, bf16[16,2048]{1,0:T(8,128)(2,1)S(1)}, u32[]{:S(2)}, u32[]{:S(2)}) %collective-permute-start.6) | collective-permute-done | bytes 65568 | tf_op jit(solution)/shard_map/ppermute | solution.py:269
  21.2 1.5 %collective-permute-start.11 = (bf16[64,2048]{1,0:T(8,128)(2,1)S(1)}, bf16[64,2048]{1,0:T(8,128)(2,1)S(1)}, u32[]{:S(2)}, u32[]{:S(2)}) collective-permute-start(bf16[64,2048]{1,0:T(8,128)(2,1)S(1)} %constant_dynamic-update-slice_fusion.4.refs_1_), channel_id=1, source_target_pairs={{0,16},{8,24},{16,0},{24,8},{1,17},{9,25},{17,1},{25,9},{2,18},{10... | collective-permute-start | bytes 786440 | tf_op jit(solution)/shard_map/ppermute | solution.py:278
  22.8 0.0 collective-permute-start.8
  22.8 0.0 copy-done
  22.8 0.0 copy-done.1
  22.8 4.8 %shard_map.94 = (bf16[128,2048]{1,0:T(8,128)(2,1)}, bf16[128,512]{1,0:T(8,128)(2,1)}, bf16[128,1152]{1,0:T(8,128)(2,1)}) custom-call(bf16[64,2048]{1,0:T(8,128)(2,1)S(1)} %constant_dynamic-update-slice_fusion.refs_0_, bf16[64,2048]{1,0:T(8,128)(2,1)S(1)} %constant_dynamic-update-slice_fusion.4.refs_1_, bf16[1024,2048]{1,0:T(8,128)(2,1)S(1)} %bitcast.10, ...), custom_call_target="tpu_custom_call" | custom-call | flops 10737418240 | bytes 8912896 | tf_op jit(solution)/shard_map/pallas_call | solution.py:58
  27.5 0.0 collective-permute-done.7.refs_2_
  27.6 0.0 collective-permute-done.8.refs_3_
  27.6 3.7 %all-to-all-start = ((bf16[8,16,1152]{2,1,0:T(8,128)(2,1)}), bf16[8,16,1152]{2,1,0:T(8,128)(2,1)S(1)}, u32[]{:S(2)}, u32[]{:S(2)}) async-start(bf16[8,16,1152]{2,1,0:T(8,128)(2,1)} %bitcast.16), calls=%async_computation | async-start | bytes 589824 | tf_op jit(solution)/shard_map/all_to_all | solution.py:355
  31.3 0.0 collective-permute-done.9.refs_4_
  31.3 0.3 collective-permute-start.10
  31.6 0.0 collective-permute-done.11.refs_6_
  31.6 0.3 collective-permute-start.12
  31.9 1.0 %collective-permute-done.10.refs_5_ = bf16[64,2048]{1,0:T(8,128)(2,1)S(1)} collective-permute-done((bf16[64,2048]{1,0:T(8,128)(2,1)S(1)}, bf16[64,2048]{1,0:T(8,128)(2,1)S(1)}, u32[]{:S(2)}, u32[]{:S(2)}) %collective-permute-start.10) | collective-permute-done | bytes 262176 | tf_op jit(solution)/shard_map/ppermute | solution.py:273
  32.9 0.4 collective-permute-done.12.refs_7_
  33.3 0.0 copy-start.2
  33.3 10.2 %shard_map.95 = (bf16[256,2048]{1,0:T(8,128)(2,1)}, bf16[512,1024]{1,0:T(8,128)(2,1)}) custom-call(bf16[64,2048]{1,0:T(8,128)(2,1)S(1)} %constant_dynamic-update-slice_fusion.refs_0_, bf16[64,2048]{1,0:T(8,128)(2,1)S(1)} %constant_dynamic-update-slice_fusion.4.refs_1_, bf16[64,2048]{1,0:T(8,128)(2,1)S(1)} %collective-permute-done.7.refs_2_, ...), custom_call_target="tpu_custom_call" | custom-call | flops 2147483648 | bytes 11141120 | tf_op jit(solution)/shard_map/pallas_call | solution.py:58
  43.5 0.0 all-to-all-done
  43.5 0.0 copy-done.2
  43.5 0.9 %shard_map.96 = (bf16[64,1024]{1,0:T(8,128)(2,1)}, bf16[2,64]{1,0:T(2,128)(2,1)}) custom-call(bf16[128,64]{1,0:T(8,128)(2,1)S(1)} %get-tuple-element.27.place0, bf16[128,64]{1,0:T(8,128)(2,1)S(1)} %get-tuple-element.28.place1, bf16[2,64]{1,0:T(2,128)(2,1)S(1)} %bitcast.15, bf16[128,1152]{1,0:T(8,128)(2,1)S(1)} %bitcast.13), custom_call_target="tpu_custom_call" | custom-call | bytes 327936 | tf_op jit(solution)/shard_map/pallas_call | solution.py:58
  (8 shorter events, 0.0 us)
Async XLA Ops:
  0.6 22.1 %copy-start = (bf16[1,1024,2048]{2,1,0:T(8,128)(2,1)S(1)}, bf16[1,1024,2048]{2,1,0:T(8,128)(2,1)}, u32[]{:S(2)}) copy-start(bf16[1,1024,2048]{2,1,0:T(8,128)(2,1)} %param.10) | copy-start | bytes 12582916
  0.6 22.1 %copy-start.1 = (bf16[1,2048,1024]{2,1,0:T(8,128)(2,1)S(1)}, bf16[1,2048,1024]{2,1,0:T(8,128)(2,1)}, u32[]{:S(2)}) copy-start(bf16[1,2048,1024]{2,1,0:T(8,128)(2,1)} %param.11) | copy-start | bytes 12582916
  2.2 12.0 %collective-permute-start = (bf16[16,2048]{1,0:T(8,128)(2,1)S(1)}, bf16[16,2048]{1,0:T(8,128)(2,1)S(1)}, u32[]{:S(2)}, u32[]{:S(2)}) collective-permute-start(bf16[16,2048]{1,0:T(8,128)(2,1)S(1)} %get-tuple-element.30), channel_id=1, source_target_pairs={{0,7},{1,6},{2,5},{3,4},{4,3},{5,2},{6,1},{7,0},{8,15},{9,14},{10,... | collective-permute-start | bytes 196616 | tf_op jit(solution)/shard_map/ppermute | solution.py:269
  8.3 10.7 %collective-permute-start.1 = (bf16[16,2048]{1,0:T(8,128)(2,1)S(1)}, bf16[16,2048]{1,0:T(8,128)(2,1)S(1)}, u32[]{:S(2)}, u32[]{:S(2)}) collective-permute-start(bf16[16,2048]{1,0:T(8,128)(2,1)S(1)} %get-tuple-element.31), channel_id=1, source_target_pairs={{0,6},{1,7},{2,4},{3,5},{4,2},{5,3},{6,0},{7,1},{8,14},{9,15},{10,... | collective-permute-start | bytes 196616 | tf_op jit(solution)/shard_map/ppermute | solution.py:269
  8.5 5.6 %collective-permute-start.2 = (bf16[16,2048]{1,0:T(8,128)(2,1)S(1)}, bf16[16,2048]{1,0:T(8,128)(2,1)S(1)}, u32[]{:S(2)}, u32[]{:S(2)}) collective-permute-start(bf16[16,2048]{1,0:T(8,128)(2,1)S(1)} %get-tuple-element.32), channel_id=1, source_target_pairs={{0,1},{1,0},{2,3},{3,2},{4,5},{5,4},{6,7},{7,6},{8,9},{9,8},{10,11... | collective-permute-start | bytes 196616 | tf_op jit(solution)/shard_map/ppermute | solution.py:269
  8.9 11.7 %collective-permute-start.3 = (bf16[16,2048]{1,0:T(8,128)(2,1)S(1)}, bf16[16,2048]{1,0:T(8,128)(2,1)S(1)}, u32[]{:S(2)}, u32[]{:S(2)}) collective-permute-start(bf16[16,2048]{1,0:T(8,128)(2,1)S(1)} %get-tuple-element.33), channel_id=1, source_target_pairs={{0,3},{1,2},{2,1},{3,0},{4,7},{5,6},{6,5},{7,4},{8,11},{9,10},{10,... | collective-permute-start | bytes 196616 | tf_op jit(solution)/shard_map/ppermute | solution.py:269
  9.7 10.9 %collective-permute-start.4 = (bf16[16,2048]{1,0:T(8,128)(2,1)S(1)}, bf16[16,2048]{1,0:T(8,128)(2,1)S(1)}, u32[]{:S(2)}, u32[]{:S(2)}) collective-permute-start(bf16[16,2048]{1,0:T(8,128)(2,1)S(1)} %get-tuple-element.34), channel_id=1, source_target_pairs={{0,5},{1,4},{2,7},{3,6},{4,1},{5,0},{6,3},{7,2},{8,13},{9,12},{10,... | collective-permute-start | bytes 196616 | tf_op jit(solution)/shard_map/ppermute | solution.py:269
  14.1 6.6 %collective-permute-start.5 = (bf16[16,2048]{1,0:T(8,128)(2,1)S(1)}, bf16[16,2048]{1,0:T(8,128)(2,1)S(1)}, u32[]{:S(2)}, u32[]{:S(2)}) collective-permute-start(bf16[16,2048]{1,0:T(8,128)(2,1)S(1)} %get-tuple-element.36), channel_id=1, source_target_pairs={{0,4},{1,5},{2,6},{3,7},{4,0},{5,1},{6,2},{7,3},{8,12},{9,13},{10,... | collective-permute-start | bytes 196616 | tf_op jit(solution)/shard_map/ppermute | solution.py:269
  14.2 7.0 %collective-permute-start.6 = (bf16[16,2048]{1,0:T(8,128)(2,1)S(1)}, bf16[16,2048]{1,0:T(8,128)(2,1)S(1)}, u32[]{:S(2)}, u32[]{:S(2)}) collective-permute-start(bf16[16,2048]{1,0:T(8,128)(2,1)S(1)} %get-tuple-element.38), channel_id=1, source_target_pairs={{0,2},{1,3},{2,0},{3,1},{4,6},{5,7},{6,4},{7,5},{8,10},{9,11},{10,... | collective-permute-start | bytes 196616 | tf_op jit(solution)/shard_map/ppermute | solution.py:269
  19.0 12.3 %collective-permute-start.9 = (bf16[64,2048]{1,0:T(8,128)(2,1)S(1)}, bf16[64,2048]{1,0:T(8,128)(2,1)S(1)}, u32[]{:S(2)}, u32[]{:S(2)}) collective-permute-start(bf16[64,2048]{1,0:T(8,128)(2,1)S(1)} %constant_dynamic-update-slice_fusion.refs_0_), channel_id=1, source_target_pairs={{0,16},{8,24},{16,0},{24,8},{1,17},{9,25},{17,1},{25,9},{2,18},{10... | collective-permute-start | bytes 786440 | tf_op jit(solution)/shard_map/ppermute | solution.py:278
  20.6 6.9 %collective-permute-start.7 = (bf16[64,2048]{1,0:T(8,128)(2,1)S(1)}, bf16[64,2048]{1,0:T(8,128)(2,1)S(1)}, u32[]{:S(2)}, u32[]{:S(2)}) collective-permute-start(bf16[64,2048]{1,0:T(8,128)(2,1)S(1)} %constant_dynamic-update-slice_fusion.refs_0_), channel_id=1, source_target_pairs={{0,8},{8,0},{16,24},{24,16},{1,9},{9,1},{17,25},{25,17},{2,10},{10... | collective-permute-start | bytes 786440 | tf_op jit(solution)/shard_map/ppermute | solution.py:273
  21.2 10.4 %collective-permute-start.11 = (bf16[64,2048]{1,0:T(8,128)(2,1)S(1)}, bf16[64,2048]{1,0:T(8,128)(2,1)S(1)}, u32[]{:S(2)}, u32[]{:S(2)}) collective-permute-start(bf16[64,2048]{1,0:T(8,128)(2,1)S(1)} %constant_dynamic-update-slice_fusion.4.refs_1_), channel_id=1, source_target_pairs={{0,16},{8,24},{16,0},{24,8},{1,17},{9,25},{17,1},{25,9},{2,18},{10... | collective-permute-start | bytes 786440 | tf_op jit(solution)/shard_map/ppermute | solution.py:278
  22.8 4.8 %collective-permute-start.8 = (bf16[64,2048]{1,0:T(8,128)(2,1)S(1)}, bf16[64,2048]{1,0:T(8,128)(2,1)S(1)}, u32[]{:S(2)}, u32[]{:S(2)}) collective-permute-start(bf16[64,2048]{1,0:T(8,128)(2,1)S(1)} %constant_dynamic-update-slice_fusion.4.refs_1_), channel_id=1, source_target_pairs={{0,8},{8,0},{16,24},{24,16},{1,9},{9,1},{17,25},{25,17},{2,10},{10... | collective-permute-start | bytes 786440 | tf_op jit(solution)/shard_map/ppermute | solution.py:273
  27.6 15.9 %all-to-all-start = ((bf16[8,16,1152]{2,1,0:T(8,128)(2,1)}), bf16[8,16,1152]{2,1,0:T(8,128)(2,1)S(1)}, u32[]{:S(2)}, u32[]{:S(2)}) async-start(bf16[8,16,1152]{2,1,0:T(8,128)(2,1)} %bitcast.16), calls=%async_computation | async-start | bytes 589824 | tf_op jit(solution)/shard_map/all_to_all | solution.py:355
  31.3 1.6 %collective-permute-start.10 = (bf16[64,2048]{1,0:T(8,128)(2,1)S(1)}, bf16[64,2048]{1,0:T(8,128)(2,1)S(1)}, u32[]{:S(2)}, u32[]{:S(2)}) collective-permute-start(bf16[64,2048]{1,0:T(8,128)(2,1)S(1)} %collective-permute-done.9.refs_4_), channel_id=1, source_target_pairs={{0,8},{8,0},{16,24},{24,16},{1,9},{9,1},{17,25},{25,17},{2,10},{10... | collective-permute-start | bytes 786440 | tf_op jit(solution)/shard_map/ppermute | solution.py:273
  31.6 1.7 %collective-permute-start.12 = (bf16[64,2048]{1,0:T(8,128)(2,1)S(1)}, bf16[64,2048]{1,0:T(8,128)(2,1)S(1)}, u32[]{:S(2)}, u32[]{:S(2)}) collective-permute-start(bf16[64,2048]{1,0:T(8,128)(2,1)S(1)} %collective-permute-done.11.refs_6_), channel_id=1, source_target_pairs={{0,8},{8,0},{16,24},{24,16},{1,9},{9,1},{17,25},{25,17},{2,10},{10... | collective-permute-start | bytes 786440 | tf_op jit(solution)/shard_map/ppermute | solution.py:273
  33.3 10.2 %copy-start.2 = (bf16[64,2]{0,1:T(2,128)(2,1)S(1)}, bf16[64,2]{0,1:T(2,128)(2,1)}, u32[]{:S(2)}) copy-start(bf16[64,2]{0,1:T(2,128)(2,1)} %param.9) | copy-start | bytes 772

commit v9 on v8

--- a/solution.py
+++ b/solution.py
@@ -19,33 +19,10 @@
     )
 
 
-ERFCX = (
-    0.253879726412498,
-    0.2540954353994894,
-    0.22517936671423447,
-    0.19823402024047995,
-    0.02224511740159976,
-    0.22829329587490593,
-    -0.2514442500538998,
-    0.06951765914158435,
-)
-
-
-def gelu_and_slope(pre_act, invert=lambda v: 1.0 / v):
-    gauss = jnp.exp(-0.5 * pre_act * pre_act)
-    t = invert(1.0 + (0.45 * 0.7071067811865476) * jnp.abs(pre_act))
-    poly = 0.5 * ERFCX[-1]
-    for c in ERFCX[-2::-1]:
-        poly = poly * t + 0.5 * c
-    tail = gauss * t * poly
-    cdf = jnp.where(pre_act < 0.0, tail, 1.0 - tail)
-    return (pre_act * cdf).astype(BF16), cdf + pre_act * (gauss * 0.3989422804014327)
-
-
 def activate(pre_act):
-    return gelu_and_slope(
-        pre_act, functools.partial(pltpu.reciprocal, approx=False, full_range=False)
-    )
+    cdf = 0.5 * (1.0 + lax.erf(pre_act * 0.7071067811865476))
+    pdf = jnp.exp(-0.5 * pre_act * pre_act) * 0.3989422804014327
+    return (pre_act * cdf).astype(BF16), cdf + pre_act * pdf
 
 
 def call(kernel, out_shape, args, flops=0, limit=24, scratch=(), spaces=None):
@@ -207,50 +184,68 @@
         copy.wait()
 
 
-def grads_kernel(tile, pieces, *refs):
+def early_kernel(tile, pieces, *refs):
     row_refs, refs = refs[:pieces], refs[pieces:]
-    d_pre_own, h_cut_own, in_hbm, out_hbm, grad_in_hbm, grad_out_hbm, *scratch = refs
-    rows, weight_in, weight_out, hidden, h_cut, d_pre, grad_in, grad_out, sems, out_sems = scratch
+    in_hbm, out_hbm, weight_in, weight_out, d_pre, h_cut, rows, hidden, sems = refs
     width, ffw = weight_in.shape
+    piece = row_refs[0].shape[0]
     tiles = [slice(at, at + tile) for at in range(0, ffw, tile)]
-    own, piece = d_pre_own.shape[0], row_refs[0].shape[0]
-    fetch, send = fetcher(sems), fetcher(out_sems)
-
-    def fetch_rows(which):
-        return [fetch(row_refs[i], rows.at[pl.ds(i * piece, piece)]) for i in which]
-
-    def fetch_weights(cols):
-        return (
+    fetch = fetcher(sems)
+    first = [fetch(ref, rows.at[pl.ds(i * piece, piece)]) for i, ref in enumerate(row_refs)]
+    weights = [
+        (
             fetch(in_hbm.at[:, cols], weight_in.at[:, cols]),
             fetch(out_hbm.at[cols, :], weight_out.at[cols, :]),
         )
-
-    first = fetch_rows(range(own // piece, pieces))
-    weights = [fetch_weights(tiles[0])]
-    rest = fetch_rows(range(own // piece))
-    rest.append(fetch(d_pre_own, d_pre.at[pl.ds(0, own)]))
-    rest.append(fetch(h_cut_own, h_cut.at[pl.ds(0, own)]))
-    weights += [fetch_weights(cols) for cols in tiles[1:]]
+        for cols in tiles
+    ]
     for copy in first:
         copy.wait()
-    x, s = rows[own:, :width], rows[own:, width:]
+    x, s = rows[:, :width], rows[:, width:]
+    for cols, (copy_in, copy_out) in zip(tiles, weights):
+        copy_in.wait()
+        copy_out.wait()
+        act, slope = activate(dot(x, weight_in[:, cols]))
+        hidden[:, cols] = act
+        d_pre[:, cols] = (dot(s, weight_out[cols, :], (1, 1)) * slope).astype(BF16)
+    h_cut[...] = my_part(hidden)
+
+
+def grads_kernel(tile, pieces, late, *refs):
+    row_refs, refs = refs[:pieces], refs[pieces:]
+    d_pre_refs, h_cut_refs, refs = refs[:2], refs[2:4], refs[4:]
+    weight_in, weight_out, grad_in_hbm, grad_out_hbm, *scratch = refs
+    rows, hidden, h_cut, d_pre, grad_in, grad_out, sems, out_sems = scratch
+    width, ffw = weight_in.shape
+    tiles = [slice(at, at + tile) for at in range(0, ffw, tile)]
+    piece = row_refs[0].shape[0]
+    known = (pieces - late) * piece
+    fetch, send = fetcher(sems), fetcher(out_sems)
+    copies = [
+        fetch(row_refs[i], rows.at[pl.ds(i * piece, piece)])
+        for i in [*range(pieces - late, pieces), *range(pieces - late)]
+    ]
+    at = 0
+    for source, cut_source in zip(d_pre_refs, h_cut_refs):
+        span = pl.ds(at, source.shape[0])
+        copies += [fetch(source, d_pre.at[span]), fetch(cut_source, h_cut.at[span])]
+        at += source.shape[0]
+    for copy in copies[:late]:
+        copy.wait()
+    x, s = rows[known:, :width], rows[known:, width:]
+    for cols in tiles:
+        act, slope = activate(dot(x, weight_in[:, cols]))
+        hidden[:, cols] = act
+        d_pre[known:, cols] = (dot(s, weight_out[cols, :], (1, 1)) * slope).astype(BF16)
+    for copy in copies[late:]:
+        copy.wait()
     cut = grad_in.shape[0]
     mine = pl.ds(pl.multiple_of(lax.axis_index("dp") * cut, cut), cut)
     outs = []
-    for t, cols in enumerate(tiles):
-        if t == 1:
-            for copy in [copy for pair in weights[1:] for copy in pair] + rest:
-                copy.wait()
-        if t == 0:
-            for copy in weights[0]:
-                copy.wait()
-        act, slope = activate(dot(x, weight_in[:, cols]))
-        hidden[:, cols] = act
-        d_pre[own:, cols] = (dot(s, weight_out[cols, :], (1, 1)) * slope).astype(BF16)
     for cols in tiles:
         grad_in[:, cols] = dot(rows[:, mine], d_pre[:, cols], (0, 0)).astype(BF16)
         outs.append(send(grad_in.at[:, cols], grad_in_hbm.at[:, cols]))
-    h_cut[own:, :] = my_part(hidden)
+    h_cut[known:, :] = my_part(hidden)
     wide = width // 4
     for at in range(0, width, wide):
         cols = slice(at, at + wide)
@@ -361,29 +356,53 @@
     ).reshape(slots_all, feat_width + LANES)
     relayed_a = [swap_cores(after(rows, d_pre)) for rows in chips_a]
     relayed_b = [swap_cores(rows) for rows in chips_b]
-    pieces = [rows_a, rows_b, core_a, core_b, *chips_a, *relayed_a, *chips_b, *relayed_b]
+    early = [core_a, core_b, *chips_a]
+    late = [*relayed_a, *chips_b, *relayed_b]
+    early_rows = sum(piece.shape[0] for piece in early)
+    late_rows = sum(piece.shape[0] for piece in late)
+    weight_in, weight_out, d_pre_early, h_cut_early = call(
+        functools.partial(early_kernel, tile, len(early)),
+        [*weight_space, shape((early_rows, ffw)), shape((early_rows, tile))],
+        [*early, *weights],
+        2 * product,
+        scratch=[
+            pltpu.VMEM((early_rows, 2 * feat_width), BF16),
+            pltpu.VMEM((early_rows, ffw), BF16),
+            pltpu.SemaphoreType.DMA((len(early) + 2 * groups,)),
+        ],
+        spaces=[pl.ANY] * len(early) + [pltpu.HBM] * 2,
+    )
+    pieces = [rows_a, rows_b, *early, *late]
     rows_all = groups * slots_all
     grad_in, grad_out = call(
-        functools.partial(grads_kernel, tile, len(pieces)),
+        functools.partial(grads_kernel, tile, len(pieces), len(late)),
         [
             pltpu.HBM((feat_width // groups, ffw), BF16),
             pltpu.HBM((ffw // groups, feat_width), BF16),
         ],
-        [*pieces, d_pre, h_cut, *weights],
+        [
+            *pieces,
+            *[d_pre, d_pre_early, h_cut, h_cut_early],
+            *[
+                pltpu.with_memory_space_constraint(w, pltpu.VMEM)
+                for w in (weight_in, weight_out)
+            ],
+        ],
         4 * product,
         limit=32,
         scratch=[
             pltpu.VMEM((rows_all, 2 * feat_width), BF16),
-            *weight_space,
-            pltpu.VMEM((rows_all - slots_all, ffw), BF16),
+            pltpu.VMEM((late_rows, ffw), BF16),
             pltpu.VMEM((rows_all, tile), BF16),
             pltpu.VMEM((rows_all, ffw), BF16),
             pltpu.VMEM((feat_width // groups, ffw), BF16),
             pltpu.VMEM((ffw // groups, feat_width), BF16),
-            pltpu.SemaphoreType.DMA((len(pieces) + 2 * groups + 2,)),
+            pltpu.SemaphoreType.DMA((len(pieces) + 4,)),
             pltpu.SemaphoreType.DMA((groups + 4,)),
         ],
-        spaces=[pl.ANY] * len(pieces) + [pltpu.HBM] * 4,
+        spaces=[pl.ANY] * len(pieces)
+        + [pltpu.HBM, pl.ANY] * 2
+        + [pltpu.VMEM] * 2,
     )
     token_grads, gate_grads = call(
         functools.partial(combine_kernel, experts, capacity),
@@ -420,7 +439,7 @@
 
     x = swap_blocks(dot(either, tokens))
     s = swap_blocks(dot(placing, jnp.concatenate(scaled, axis=0)))
-    hidden0, slope0 = gelu_and_slope(dot(x, weight_in))
+    hidden0, slope0 = activate(dot(x, weight_in))
     d_hidden0 = dot(s, weight_out, (1, 1))
     d_pre0 = (d_hidden0 * slope0).astype(BF16)
     dgate = jnp.sum(hidden0.astype(F32) * d_hidden0, axis=1, keepdims=True)
@@ -430,7 +449,7 @@
     )
     x_all = jnp.concatenate([x, *gather_groups(x)], axis=0)
     s_all = jnp.concatenate([s, *gather_groups(s)], axis=0)
-    hidden1, slope1 = gelu_and_slope(dot(x_all[slots_all:], weight_in))
+    hidden1, slope1 = activate(dot(x_all[slots_all:], weight_in))
     d_pre1 = (dot(s_all[slots_all:], weight_out, (1, 1)) * slope1).astype(BF16)
     hidden = jnp.concatenate([hidden0, hidden1], axis=0)
     d_pre = jnp.concatenate([d_pre0, d_pre1], axis=0)

time: 44.6 us -> 42.5 us (0.953)
  waiting for transfers between devices: 1.96 us -> 0.57 us
  Pallas kernels: 17.4 us -> 16.7 us
    ppermute x4, waiting for transfers between devices: 1.4 us -> 0.01 us  [swap_cores(): lax.ppermute(rows, 'dp', [(i, i ^ 1) for i in range(lax.axis_size('dp'))])]
    pallas_call x4 -> x5, Pallas kernels: 17.4 us -> 16.7 us  [call(): pl.pallas_call(kernel, out_shape=out_shape, in_specs=[pl.BlockSpec(memory...]
  transfers between devices with their start and end apart: 14 -> 14, of which waited for: 3 -> 1; matrix products, arithmetic and copies ran while one was open for 0% -> 0% of each run, Pallas kernels for 34% -> 34%
where the time goes in v9:
time: 42.5 us; the launch traced here: 42.3 us
  starting transfers between devices  24.2 us (57%)
  Pallas kernels  16.7 us (39%)
  between operations  0.81 us (2%)
  waiting for transfers between devices  0.57 us (1%)
    ppermute x7, starting transfers between devices, permute(): lax.ppermute(block, 'expert', [(i, i ^ k) for i in range(lax.axis_size('e...  16.7 us
    pallas_call x5, Pallas kernels, call(): pl.pallas_call(kernel, out_shape=out_shape, in_specs=[pl.BlockSpec(memory...  16.7 us
    all_to_all x1, starting transfers between devices, local(): lax.all_to_all(after(back, core_a, core_b).reshape(experts, capacity, fea...  3.72 us
    ppermute x2, starting transfers between devices, shift_chips(): lax.ppermute(rows, 'dp', [(i, (i + 2 * k) % groups) for i in range(groups)])  3.13 us
  transfers between devices with their start and end apart: 14, of which 1 were waited for; matrix products, arithmetic and copies ran while one was open for 0% of the time, Pallas kernels for 34%

profile of v9, /device:TPU:0, one launch (start us, length us, event | category | flops | bytes accessed | tf_op | source)
XLA Modules:
  0.0 42.3 jit_solution(17400910231917971614)
XLA Ops:
  0.6 0.0 copy-start
  0.6 0.0 copy-start.1
  0.7 1.6 %shard_map.93 = (bf16[16,2048]{1,0:T(8,128)(2,1)S(1)}, bf16[16,2048]{1,0:T(8,128)(2,1)S(1)}, bf16[16,2048]{1,0:T(8,128)(2,1)S(1)}, bf16[16,2048]{1,0:T(8,128)(2,...) custom-call(s32[2,64]{1,0:T(2,128)} %bitcast.19, ...), custom_call_target="tpu_custom_call" | custom-call | flops 16106127360 | bytes 262912 | tf_op jit(solution)/shard_map/pallas_call | solution.py:35
  2.2 6.0 %collective-permute-start = (bf16[16,2048]{1,0:T(8,128)(2,1)S(1)}, bf16[16,2048]{1,0:T(8,128)(2,1)S(1)}, u32[]{:S(2)}, u32[]{:S(2)}) collective-permute-start(bf16[16,2048]{1,0:T(8,128)(2,1)S(1)} %get-tuple-element.34), channel_id=1, source_target_pairs={{0,7},{1,6},{2,5},{3,4},{4,3},{5,2},{6,1},{7,0},{8,15},{9,14},{10,... | collective-permute-start | bytes 196616 | tf_op jit(solution)/shard_map/ppermute | solution.py:264
  8.3 0.2 collective-permute-start.1
  8.5 0.4 collective-permute-start.2
  8.9 0.8 %collective-permute-start.3 = (bf16[16,2048]{1,0:T(8,128)(2,1)S(1)}, bf16[16,2048]{1,0:T(8,128)(2,1)S(1)}, u32[]{:S(2)}, u32[]{:S(2)}) collective-permute-start(bf16[16,2048]{1,0:T(8,128)(2,1)S(1)} %get-tuple-element.37), channel_id=1, source_target_pairs={{0,3},{1,2},{2,1},{3,0},{4,7},{5,6},{6,5},{7,4},{8,11},{9,10},{10,... | collective-permute-start | bytes 196616 | tf_op jit(solution)/shard_map/ppermute | solution.py:264
  9.7 4.4 %collective-permute-start.4 = (bf16[16,2048]{1,0:T(8,128)(2,1)S(1)}, bf16[16,2048]{1,0:T(8,128)(2,1)S(1)}, u32[]{:S(2)}, u32[]{:S(2)}) collective-permute-start(bf16[16,2048]{1,0:T(8,128)(2,1)S(1)} %get-tuple-element.38), channel_id=1, source_target_pairs={{0,5},{1,4},{2,7},{3,6},{4,1},{5,0},{6,3},{7,2},{8,13},{9,12},{10,... | collective-permute-start | bytes 196616 | tf_op jit(solution)/shard_map/ppermute | solution.py:264
  14.1 0.0 collective-permute-done.2
  14.1 0.1 collective-permute-start.5
  14.2 0.0 collective-permute-done
  14.2 4.8 %collective-permute-start.6 = (bf16[16,2048]{1,0:T(8,128)(2,1)S(1)}, bf16[16,2048]{1,0:T(8,128)(2,1)S(1)}, u32[]{:S(2)}, u32[]{:S(2)}) collective-permute-start(bf16[16,2048]{1,0:T(8,128)(2,1)S(1)} %get-tuple-element.42), channel_id=1, source_target_pairs={{0,2},{1,3},{2,0},{3,1},{4,6},{5,7},{6,4},{7,5},{8,10},{9,11},{10,... | collective-permute-start | bytes 196616 | tf_op jit(solution)/shard_map/ppermute | solution.py:264
  19.0 0.0 collective-permute-done.1
  19.0 1.6 %collective-permute-start.9 = (bf16[64,2048]{1,0:T(8,128)(2,1)S(1)}, bf16[64,2048]{1,0:T(8,128)(2,1)S(1)}, u32[]{:S(2)}, u32[]{:S(2)}) collective-permute-start(bf16[64,2048]{1,0:T(8,128)(2,1)S(1)} %constant_dynamic-update-slice_fusion.refs_0_), channel_id=1, source_target_pairs={{0,16},{8,24},{16,0},{24,8},{1,17},{9,25},{17,1},{25,9},{2,18},{10... | collective-permute-start | bytes 786440 | tf_op jit(solution)/shard_map/ppermute | solution.py:273
  20.6 0.0 collective-permute-done.3
  20.6 0.0 collective-permute-start.7
  20.6 0.0 collective-permute-done.4
  20.7 0.0 collective-permute-done.5
  20.7 0.5 %collective-permute-done.6 = bf16[16,2048]{1,0:T(8,128)(2,1)S(1)} collective-permute-done((bf16[16,2048]{1,0:T(8,128)(2,1)S(1)}, bf16[16,2048]{1,0:T(8,128)(2,1)S(1)}, u32[]{:S(2)}, u32[]{:S(2)}) %collective-permute-start.6) | collective-permute-done | bytes 65568 | tf_op jit(solution)/shard_map/ppermute | solution.py:264
  21.2 1.5 %collective-permute-start.11 = (bf16[64,2048]{1,0:T(8,128)(2,1)S(1)}, bf16[64,2048]{1,0:T(8,128)(2,1)S(1)}, u32[]{:S(2)}, u32[]{:S(2)}) collective-permute-start(bf16[64,2048]{1,0:T(8,128)(2,1)S(1)} %constant_dynamic-update-slice_fusion.4.refs_1_), channel_id=1, source_target_pairs={{0,16},{8,24},{16,0},{24,8},{1,17},{9,25},{17,1},{25,9},{2,18},{10... | collective-permute-start | bytes 786440 | tf_op jit(solution)/shard_map/ppermute | solution.py:273
  22.8 0.0 collective-permute-start.8
  22.8 0.0 copy-done
  22.8 0.0 copy-done.1
  22.8 4.3 %shard_map.94 = (bf16[128,2048]{1,0:T(8,128)(2,1)}, bf16[128,512]{1,0:T(8,128)(2,1)}, bf16[128,1152]{1,0:T(8,128)(2,1)}) custom-call(bf16[64,2048]{1,0:T(8,128)(2,1)S(1)} %constant_dynamic-update-slice_fusion.refs_0_, bf16[64,2048]{1,0:T(8,128)(2,1)S(1)} %constant_dynamic-update-slice_fusion.4.refs_1_, bf16[1024,2048]{1,0:T(8,128)(2,1)S(1)} %bitcast.10, ...), custom_call_target="tpu_custom_call" | custom-call | flops 10737418240 | bytes 8912896 | tf_op jit(solution)/shard_map/pallas_call | solution.py:35
  27.1 0.0 collective-permute-done.7.refs_0_.refs_2_
  27.1 0.0 collective-permute-done.8.refs_1_.refs_3_
  27.1 3.7 %all-to-all-start = ((bf16[8,16,1152]{2,1,0:T(8,128)(2,1)}), bf16[8,16,1152]{2,1,0:T(8,128)(2,1)S(1)}, u32[]{:S(2)}, u32[]{:S(2)}) async-start(bf16[8,16,1152]{2,1,0:T(8,128)(2,1)} %bitcast.16), calls=%async_computation | async-start | bytes 589824 | tf_op jit(solution)/shard_map/all_to_all | solution.py:350
  30.8 0.0 collective-permute-done.9.refs_2_.refs_4_
  30.8 0.3 collective-permute-start.10
  31.1 0.0 collective-permute-done.11.refs_6_
  31.1 0.3 collective-permute-start.12
  31.4 4.7 %shard_map.95 = (bf16[1024,2048]{1,0:T(8,128)(2,1)S(1)}, bf16[2048,1024]{1,0:T(8,128)(2,1)S(1)}, bf16[192,2048]{1,0:T(8,128)(2,1)S(1)}, bf16[192,512]{1,0:T(8,128)(2,1)S(1)}) custom-call(bf16[64,2048]{1,0:T(8,128)(2,1)S(1)} %collective-permute-done.7.refs_0_.refs_2_, bf16[64,2048]{1,0:T(8,128)(2,1)S(1)} %collective-permute-done.8.refs_1_.refs_3_, ...), custom_call_target="tpu_custom_call" | custom-call | flops 1073741824 | bytes 9175040 | tf_op jit(solution)/shard_map/pallas_call | solution.py:35
  36.1 0.0 collective-permute-done.10.refs_5_
  36.1 0.0 collective-permute-done.12.refs_7_
  36.1 0.0 copy-start.2
  36.2 5.2 %shard_map.96 = (bf16[256,2048]{1,0:T(8,128)(2,1)}, bf16[512,1024]{1,0:T(8,128)(2,1)}) custom-call(bf16[64,2048]{1,0:T(8,128)(2,1)S(1)} %constant_dynamic-update-slice_fusion.refs_0_, bf16[64,2048]{1,0:T(8,128)(2,1)S(1)} %constant_dynamic-update-slice_fusion.4.refs_1_, bf16[64,2048]{1,0:T(8,128)(2,1)S(1)} %collective-permute-done.7.refs_0_.refs_2_, ...), custom_call_target="tpu_custom_call" | custom-call | flops 2147483648 | bytes 12124160 | tf_op jit(solution)/shard_map/pallas_call | solution.py:35
  41.4 0.0 all-to-all-done
  41.4 0.0 copy-done.2
  41.4 0.9 %shard_map.97 = (bf16[64,1024]{1,0:T(8,128)(2,1)}, bf16[2,64]{1,0:T(2,128)(2,1)}) custom-call(bf16[128,64]{1,0:T(8,128)(2,1)S(1)} %get-tuple-element.31.place0, bf16[128,64]{1,0:T(8,128)(2,1)S(1)} %get-tuple-element.32.place1, bf16[2,64]{1,0:T(2,128)(2,1)S(1)} %bitcast.15, bf16[128,1152]{1,0:T(8,128)(2,1)S(1)} %bitcast.13), custom_call_target="tpu_custom_call" | custom-call | bytes 327936 | tf_op jit(solution)/shard_map/pallas_call | solution.py:35
  (8 shorter events, 0.0 us)
Async XLA Ops:
  0.6 22.1 %copy-start = (bf16[1,1024,2048]{2,1,0:T(8,128)(2,1)S(1)}, bf16[1,1024,2048]{2,1,0:T(8,128)(2,1)}, u32[]{:S(2)}) copy-start(bf16[1,1024,2048]{2,1,0:T(8,128)(2,1)} %param.10) | copy-start | bytes 12582916
  0.6 22.1 %copy-start.1 = (bf16[1,2048,1024]{2,1,0:T(8,128)(2,1)S(1)}, bf16[1,2048,1024]{2,1,0:T(8,128)(2,1)}, u32[]{:S(2)}) copy-start(bf16[1,2048,1024]{2,1,0:T(8,128)(2,1)} %param.11) | copy-start | bytes 12582916
  2.2 12.0 %collective-permute-start = (bf16[16,2048]{1,0:T(8,128)(2,1)S(1)}, bf16[16,2048]{1,0:T(8,128)(2,1)S(1)}, u32[]{:S(2)}, u32[]{:S(2)}) collective-permute-start(bf16[16,2048]{1,0:T(8,128)(2,1)S(1)} %get-tuple-element.34), channel_id=1, source_target_pairs={{0,7},{1,6},{2,5},{3,4},{4,3},{5,2},{6,1},{7,0},{8,15},{9,14},{10,... | collective-permute-start | bytes 196616 | tf_op jit(solution)/shard_map/ppermute | solution.py:264
  8.3 10.7 %collective-permute-start.1 = (bf16[16,2048]{1,0:T(8,128)(2,1)S(1)}, bf16[16,2048]{1,0:T(8,128)(2,1)S(1)}, u32[]{:S(2)}, u32[]{:S(2)}) collective-permute-start(bf16[16,2048]{1,0:T(8,128)(2,1)S(1)} %get-tuple-element.35), channel_id=1, source_target_pairs={{0,6},{1,7},{2,4},{3,5},{4,2},{5,3},{6,0},{7,1},{8,14},{9,15},{10,... | collective-permute-start | bytes 196616 | tf_op jit(solution)/shard_map/ppermute | solution.py:264
  8.5 5.6 %collective-permute-start.2 = (bf16[16,2048]{1,0:T(8,128)(2,1)S(1)}, bf16[16,2048]{1,0:T(8,128)(2,1)S(1)}, u32[]{:S(2)}, u32[]{:S(2)}) collective-permute-start(bf16[16,2048]{1,0:T(8,128)(2,1)S(1)} %get-tuple-element.36), channel_id=1, source_target_pairs={{0,1},{1,0},{2,3},{3,2},{4,5},{5,4},{6,7},{7,6},{8,9},{9,8},{10,11... | collective-permute-start | bytes 196616 | tf_op jit(solution)/shard_map/ppermute | solution.py:264
  8.9 11.7 %collective-permute-start.3 = (bf16[16,2048]{1,0:T(8,128)(2,1)S(1)}, bf16[16,2048]{1,0:T(8,128)(2,1)S(1)}, u32[]{:S(2)}, u32[]{:S(2)}) collective-permute-start(bf16[16,2048]{1,0:T(8,128)(2,1)S(1)} %get-tuple-element.37), channel_id=1, source_target_pairs={{0,3},{1,2},{2,1},{3,0},{4,7},{5,6},{6,5},{7,4},{8,11},{9,10},{10,... | collective-permute-start | bytes 196616 | tf_op jit(solution)/shard_map/ppermute | solution.py:264
  9.7 10.9 %collective-permute-start.4 = (bf16[16,2048]{1,0:T(8,128)(2,1)S(1)}, bf16[16,2048]{1,0:T(8,128)(2,1)S(1)}, u32[]{:S(2)}, u32[]{:S(2)}) collective-permute-start(bf16[16,2048]{1,0:T(8,128)(2,1)S(1)} %get-tuple-element.38), channel_id=1, source_target_pairs={{0,5},{1,4},{2,7},{3,6},{4,1},{5,0},{6,3},{7,2},{8,13},{9,12},{10,... | collective-permute-start | bytes 196616 | tf_op jit(solution)/shard_map/ppermute | solution.py:264
  14.1 6.6 %collective-permute-start.5 = (bf16[16,2048]{1,0:T(8,128)(2,1)S(1)}, bf16[16,2048]{1,0:T(8,128)(2,1)S(1)}, u32[]{:S(2)}, u32[]{:S(2)}) collective-permute-start(bf16[16,2048]{1,0:T(8,128)(2,1)S(1)} %get-tuple-element.40), channel_id=1, source_target_pairs={{0,4},{1,5},{2,6},{3,7},{4,0},{5,1},{6,2},{7,3},{8,12},{9,13},{10,... | collective-permute-start | bytes 196616 | tf_op jit(solution)/shard_map/ppermute | solution.py:264
  14.2 7.0 %collective-permute-start.6 = (bf16[16,2048]{1,0:T(8,128)(2,1)S(1)}, bf16[16,2048]{1,0:T(8,128)(2,1)S(1)}, u32[]{:S(2)}, u32[]{:S(2)}) collective-permute-start(bf16[16,2048]{1,0:T(8,128)(2,1)S(1)} %get-tuple-element.42), channel_id=1, source_target_pairs={{0,2},{1,3},{2,0},{3,1},{4,6},{5,7},{6,4},{7,5},{8,10},{9,11},{10,... | collective-permute-start | bytes 196616 | tf_op jit(solution)/shard_map/ppermute | solution.py:264
  19.0 11.8 %collective-permute-start.9 = (bf16[64,2048]{1,0:T(8,128)(2,1)S(1)}, bf16[64,2048]{1,0:T(8,128)(2,1)S(1)}, u32[]{:S(2)}, u32[]{:S(2)}) collective-permute-start(bf16[64,2048]{1,0:T(8,128)(2,1)S(1)} %constant_dynamic-update-slice_fusion.refs_0_), channel_id=1, source_target_pairs={{0,16},{8,24},{16,0},{24,8},{1,17},{9,25},{17,1},{25,9},{2,18},{10... | collective-permute-start | bytes 786440 | tf_op jit(solution)/shard_map/ppermute | solution.py:273
  20.6 6.5 %collective-permute-start.7 = (bf16[64,2048]{1,0:T(8,128)(2,1)S(1)}, bf16[64,2048]{1,0:T(8,128)(2,1)S(1)}, u32[]{:S(2)}, u32[]{:S(2)}) collective-permute-start(bf16[64,2048]{1,0:T(8,128)(2,1)S(1)} %constant_dynamic-update-slice_fusion.refs_0_), channel_id=1, source_target_pairs={{0,8},{8,0},{16,24},{24,16},{1,9},{9,1},{17,25},{25,17},{2,10},{10... | collective-permute-start | bytes 786440 | tf_op jit(solution)/shard_map/ppermute | solution.py:268
  21.2 9.9 %collective-permute-start.11 = (bf16[64,2048]{1,0:T(8,128)(2,1)S(1)}, bf16[64,2048]{1,0:T(8,128)(2,1)S(1)}, u32[]{:S(2)}, u32[]{:S(2)}) collective-permute-start(bf16[64,2048]{1,0:T(8,128)(2,1)S(1)} %constant_dynamic-update-slice_fusion.4.refs_1_), channel_id=1, source_target_pairs={{0,16},{8,24},{16,0},{24,8},{1,17},{9,25},{17,1},{25,9},{2,18},{10... | collective-permute-start | bytes 786440 | tf_op jit(solution)/shard_map/ppermute | solution.py:273
  22.8 4.3 %collective-permute-start.8 = (bf16[64,2048]{1,0:T(8,128)(2,1)S(1)}, bf16[64,2048]{1,0:T(8,128)(2,1)S(1)}, u32[]{:S(2)}, u32[]{:S(2)}) collective-permute-start(bf16[64,2048]{1,0:T(8,128)(2,1)S(1)} %constant_dynamic-update-slice_fusion.4.refs_1_), channel_id=1, source_target_pairs={{0,8},{8,0},{16,24},{24,16},{1,9},{9,1},{17,25},{25,17},{2,10},{10... | collective-permute-start | bytes 786440 | tf_op jit(solution)/shard_map/ppermute | solution.py:268
  27.1 14.3 %all-to-all-start = ((bf16[8,16,1152]{2,1,0:T(8,128)(2,1)}), bf16[8,16,1152]{2,1,0:T(8,128)(2,1)S(1)}, u32[]{:S(2)}, u32[]{:S(2)}) async-start(bf16[8,16,1152]{2,1,0:T(8,128)(2,1)} %bitcast.16), calls=%async_computation | async-start | bytes 589824 | tf_op jit(solution)/shard_map/all_to_all | solution.py:350
  30.8 5.3 %collective-permute-start.10 = (bf16[64,2048]{1,0:T(8,128)(2,1)S(1)}, bf16[64,2048]{1,0:T(8,128)(2,1)S(1)}, u32[]{:S(2)}, u32[]{:S(2)}) collective-permute-start(bf16[64,2048]{1,0:T(8,128)(2,1)S(1)} %collective-permute-done.9.refs_2_.refs_4_), channel_id=1, source_target_pairs={{0,8},{8,0},{16,24},{24,16},{1,9},{9,1},{17,25},{25,17},{2,10},{10... | collective-permute-start | bytes 786440 | tf_op jit(solution)/shard_map/ppermute | solution.py:268
  31.1 5.0 %collective-permute-start.12 = (bf16[64,2048]{1,0:T(8,128)(2,1)S(1)}, bf16[64,2048]{1,0:T(8,128)(2,1)S(1)}, u32[]{:S(2)}, u32[]{:S(2)}) collective-permute-start(bf16[64,2048]{1,0:T(8,128)(2,1)S(1)} %collective-permute-done.11.refs_6_), channel_id=1, source_target_pairs={{0,8},{8,0},{16,24},{24,16},{1,9},{9,1},{17,25},{25,17},{2,10},{10... | collective-permute-start | bytes 786440 | tf_op jit(solution)/shard_map/ppermute | solution.py:268
  36.1 5.3 %copy-start.2 = (bf16[64,2]{0,1:T(2,128)(2,1)S(1)}, bf16[64,2]{0,1:T(2,128)(2,1)}, u32[]{:S(2)}) copy-start(bf16[64,2]{0,1:T(2,128)(2,1)} %param.9) | copy-start | bytes 772

commit v10 on v9

--- a/solution.py
+++ b/solution.py
@@ -230,28 +230,25 @@
         span = pl.ds(at, source.shape[0])
         copies += [fetch(source, d_pre.at[span]), fetch(cut_source, h_cut.at[span])]
         at += source.shape[0]
-    for copy in copies[:late]:
-        copy.wait()
-    x, s = rows[known:, :width], rows[known:, width:]
+    x, s = stack(row_refs[-late:], 0, width), stack(row_refs[-late:], 1, width)
     for cols in tiles:
         act, slope = activate(dot(x, weight_in[:, cols]))
         hidden[:, cols] = act
         d_pre[known:, cols] = (dot(s, weight_out[cols, :], (1, 1)) * slope).astype(BF16)
-    for copy in copies[late:]:
+    for copy in copies:
         copy.wait()
     cut = grad_in.shape[0]
     mine = pl.ds(pl.multiple_of(lax.axis_index("dp") * cut, cut), cut)
     outs = []
-    for cols in tiles:
+    for at in range(0, ffw, ffw // 2):
+        cols = slice(at, at + ffw // 2)
         grad_in[:, cols] = dot(rows[:, mine], d_pre[:, cols], (0, 0)).astype(BF16)
         outs.append(send(grad_in.at[:, cols], grad_in_hbm.at[:, cols]))
     h_cut[known:, :] = my_part(hidden)
-    wide = width // 4
-    for at in range(0, width, wide):
-        cols = slice(at, at + wide)
-        s_cols = slice(width + at, width + at + wide)
-        grad_out[:, cols] = dot(h_cut[...], rows[:, s_cols], (0, 0)).astype(BF16)
-        outs.append(send(grad_out.at[:, cols], grad_out_hbm.at[:, cols]))
+    for at in range(0, tile, tile // 2):
+        part = slice(at, at + tile // 2)
+        grad_out[part, :] = dot(h_cut[:, part], rows[:, width:], (0, 0)).astype(BF16)
+        outs.append(send(grad_out.at[part, :], grad_out_hbm.at[part, :]))
     for copy in outs:
         copy.wait()
 
@@ -309,8 +306,6 @@
     )
     blocks, places = routed[:experts], routed[experts:]
     rest = list(range(experts - 1, 1, -1))
-    if len(rest) > 4:
-        rest.insert(2, rest.pop(-2))
     order = [0, *rest[:2], 1, *rest[2:]]
     order_a, order_b = order[:half], order[half:]
     got_a = [blocks[0]] + [permute(blocks[k], k) for k in order_a[1:]]
@@ -398,9 +393,10 @@
             pltpu.VMEM((feat_width // groups, ffw), BF16),
             pltpu.VMEM((ffw // groups, feat_width), BF16),
             pltpu.SemaphoreType.DMA((len(pieces) + 4,)),
-            pltpu.SemaphoreType.DMA((groups + 4,)),
-        ],
-        spaces=[pl.ANY] * len(pieces)
+            pltpu.SemaphoreType.DMA((4,)),
+        ],
+        spaces=[pl.ANY] * (len(pieces) - len(late))
+        + [pltpu.VMEM] * len(late)
         + [pltpu.HBM, pl.ANY] * 2
         + [pltpu.VMEM] * 2,
     )

time: 42.5 us -> 42.7 us (level)
  waiting for transfers between devices: 0.57 us -> 3.54 us
  starting transfers between devices: 24.2 us -> 21.5 us
    ppermute x7, starting transfers between devices: 16.7 us -> 12.6 us  [permute(): lax.ppermute(block, 'expert', [(i, i ^ k) for i in range(lax.axis_size('e...]
    ppermute x7, waiting for transfers between devices: 0.55 us -> 3.52 us  [permute(): lax.ppermute(block, 'expert', [(i, i ^ k) for i in range(lax.axis_size('e...]
    all_to_all x1, starting transfers between devices: 3.72 us -> 5.13 us  [local(): lax.all_to_all(after(back, core_a, core_b).reshape(experts, capacity, fea...]
  transfers between devices with their start and end apart: 14 -> 14, of which waited for: 1 -> 4; matrix products, arithmetic and copies ran while one was open for 0% -> 0% of each run, Pallas kernels for 34% -> 33%
where the time goes in v10:
time: 42.7 us; the launch traced here: 42.5 us
  starting transfers between devices  21.5 us (50%)
  Pallas kernels  16.6 us (39%)
  waiting for transfers between devices  3.54 us (8%)
  between operations  0.78 us (2%)
    pallas_call x5, Pallas kernels, call(): pl.pallas_call(kernel, out_shape=out_shape, in_specs=[pl.BlockSpec(memory...  16.6 us
    ppermute x7, starting transfers between devices, permute(): lax.ppermute(block, 'expert', [(i, i ^ k) for i in range(lax.axis_size('e...  12.6 us
    all_to_all x1, starting transfers between devices, local(): lax.all_to_all(after(back, core_a, core_b).reshape(experts, capacity, fea...  5.13 us
    ppermute x7, waiting for transfers between devices, permute(): lax.ppermute(block, 'expert', [(i, i ^ k) for i in range(lax.axis_size('e...  3.52 us
    ppermute x2, starting transfers between devices, shift_chips(): lax.ppermute(rows, 'dp', [(i, (i + 2 * k) % groups) for i in range(groups)])  3.22 us
  transfers between devices with their start and end apart: 14, of which 4 were waited for; matrix products, arithmetic and copies ran while one was open for 0% of the time, Pallas kernels for 33%

profile of v10, /device:TPU:0, one launch (start us, length us, event | category | flops | bytes accessed | tf_op | source)
XLA Modules:
  0.0 42.5 jit_solution(2192819235297940125)
XLA Ops:
  0.6 0.0 copy-start
  0.6 0.0 copy-start.1
  0.7 1.6 %shard_map.93 = (bf16[16,2048]{1,0:T(8,128)(2,1)S(1)}, bf16[16,2048]{1,0:T(8,128)(2,1)S(1)}, bf16[16,2048]{1,0:T(8,128)(2,1)S(1)}, bf16[16,2048]{1,0:T(8,128)(2,...) custom-call(s32[2,64]{1,0:T(2,128)} %bitcast.19, ...), custom_call_target="tpu_custom_call" | custom-call | flops 16106127360 | bytes 262912 | tf_op jit(solution)/shard_map/pallas_call | solution.py:35
  2.2 6.0 %collective-permute-start = (bf16[16,2048]{1,0:T(8,128)(2,1)S(1)}, bf16[16,2048]{1,0:T(8,128)(2,1)S(1)}, u32[]{:S(2)}, u32[]{:S(2)}) collective-permute-start(bf16[16,2048]{1,0:T(8,128)(2,1)S(1)} %get-tuple-element.34), channel_id=1, source_target_pairs={{0,7},{1,6},{2,5},{3,4},{4,3},{5,2},{6,1},{7,0},{8,15},{9,14},{10,... | collective-permute-start | bytes 196616 | tf_op jit(solution)/shard_map/ppermute | solution.py:261
  8.3 0.2 collective-permute-start.1
  8.5 0.4 collective-permute-start.2
  8.9 1.8 %collective-permute-start.3 = (bf16[16,2048]{1,0:T(8,128)(2,1)S(1)}, bf16[16,2048]{1,0:T(8,128)(2,1)S(1)}, u32[]{:S(2)}, u32[]{:S(2)}) collective-permute-start(bf16[16,2048]{1,0:T(8,128)(2,1)S(1)} %get-tuple-element.37), channel_id=1, source_target_pairs={{0,5},{1,4},{2,7},{3,6},{4,1},{5,0},{6,3},{7,2},{8,13},{9,12},{10,... | collective-permute-start | bytes 196616 | tf_op jit(solution)/shard_map/ppermute | solution.py:261
  10.7 2.1 %collective-permute-start.4 = (bf16[16,2048]{1,0:T(8,128)(2,1)S(1)}, bf16[16,2048]{1,0:T(8,128)(2,1)S(1)}, u32[]{:S(2)}, u32[]{:S(2)}) collective-permute-start(bf16[16,2048]{1,0:T(8,128)(2,1)S(1)} %get-tuple-element.38), channel_id=1, source_target_pairs={{0,4},{1,5},{2,6},{3,7},{4,0},{5,1},{6,2},{7,3},{8,12},{9,13},{10,... | collective-permute-start | bytes 196616 | tf_op jit(solution)/shard_map/ppermute | solution.py:261
  12.9 0.0 collective-permute-done.2
  12.9 1.3 %collective-permute-start.5 = (bf16[16,2048]{1,0:T(8,128)(2,1)S(1)}, bf16[16,2048]{1,0:T(8,128)(2,1)S(1)}, u32[]{:S(2)}, u32[]{:S(2)}) collective-permute-start(bf16[16,2048]{1,0:T(8,128)(2,1)S(1)} %get-tuple-element.40), channel_id=1, source_target_pairs={{0,3},{1,2},{2,1},{3,0},{4,7},{5,6},{6,5},{7,4},{8,11},{9,10},{10,... | collective-permute-start | bytes 196616 | tf_op jit(solution)/shard_map/ppermute | solution.py:261
  14.2 0.0 collective-permute-done
  14.2 0.6 %collective-permute-start.6 = (bf16[16,2048]{1,0:T(8,128)(2,1)S(1)}, bf16[16,2048]{1,0:T(8,128)(2,1)S(1)}, u32[]{:S(2)}, u32[]{:S(2)}) collective-permute-start(bf16[16,2048]{1,0:T(8,128)(2,1)S(1)} %get-tuple-element.42), channel_id=1, source_target_pairs={{0,2},{1,3},{2,0},{3,1},{4,6},{5,7},{6,4},{7,5},{8,10},{9,11},{10,... | collective-permute-start | bytes 196616 | tf_op jit(solution)/shard_map/ppermute | solution.py:261
  14.8 0.0 collective-permute-done.1
  14.9 1.7 %collective-permute-start.9 = (bf16[64,2048]{1,0:T(8,128)(2,1)S(1)}, bf16[64,2048]{1,0:T(8,128)(2,1)S(1)}, u32[]{:S(2)}, u32[]{:S(2)}) collective-permute-start(bf16[64,2048]{1,0:T(8,128)(2,1)S(1)} %constant_dynamic-update-slice_fusion.refs_0_), channel_id=1, source_target_pairs={{0,16},{8,24},{16,0},{24,8},{1,17},{9,25},{17,1},{25,9},{2,18},{10... | collective-permute-start | bytes 786440 | tf_op jit(solution)/shard_map/ppermute | solution.py:270
  16.6 1.1 %collective-permute-done.3 = bf16[16,2048]{1,0:T(8,128)(2,1)S(1)} collective-permute-done((bf16[16,2048]{1,0:T(8,128)(2,1)S(1)}, bf16[16,2048]{1,0:T(8,128)(2,1)S(1)}, u32[]{:S(2)}, u32[]{:S(2)}) %collective-permute-start.3) | collective-permute-done | bytes 65568 | tf_op jit(solution)/shard_map/ppermute | solution.py:261
  17.7 0.0 collective-permute-start.7
  17.7 1.8 %collective-permute-done.4 = bf16[16,2048]{1,0:T(8,128)(2,1)S(1)} collective-permute-done((bf16[16,2048]{1,0:T(8,128)(2,1)S(1)}, bf16[16,2048]{1,0:T(8,128)(2,1)S(1)}, u32[]{:S(2)}, u32[]{:S(2)}) %collective-permute-start.4) | collective-permute-done | bytes 65568 | tf_op jit(solution)/shard_map/ppermute | solution.py:261
  19.5 0.3 collective-permute-done.5
  19.8 0.3 collective-permute-done.6
  20.1 1.5 %collective-permute-start.11 = (bf16[64,2048]{1,0:T(8,128)(2,1)S(1)}, bf16[64,2048]{1,0:T(8,128)(2,1)S(1)}, u32[]{:S(2)}, u32[]{:S(2)}) collective-permute-start(bf16[64,2048]{1,0:T(8,128)(2,1)S(1)} %constant_dynamic-update-slice_fusion.4.refs_1_), channel_id=1, source_target_pairs={{0,16},{8,24},{16,0},{24,8},{1,17},{9,25},{17,1},{25,9},{2,18},{10... | collective-permute-start | bytes 786440 | tf_op jit(solution)/shard_map/ppermute | solution.py:270
  21.6 0.0 collective-permute-start.8
  21.6 0.0 copy-done
  21.6 0.0 copy-done.1
  21.6 4.3 %shard_map.94 = (bf16[128,2048]{1,0:T(8,128)(2,1)}, bf16[128,512]{1,0:T(8,128)(2,1)}, bf16[128,1152]{1,0:T(8,128)(2,1)}) custom-call(bf16[64,2048]{1,0:T(8,128)(2,1)S(1)} %constant_dynamic-update-slice_fusion.refs_0_, bf16[64,2048]{1,0:T(8,128)(2,1)S(1)} %constant_dynamic-update-slice_fusion.4.refs_1_, bf16[1024,2048]{1,0:T(8,128)(2,1)S(1)} %bitcast.10, ...), custom_call_target="tpu_custom_call" | custom-call | flops 10737418240 | bytes 8912896 | tf_op jit(solution)/shard_map/pallas_call | solution.py:35
  25.9 0.0 collective-permute-done.7.refs_0_.refs_2_
  25.9 0.0 collective-permute-done.8.refs_1_.refs_3_
  26.0 5.1 %all-to-all-start = ((bf16[8,16,1152]{2,1,0:T(8,128)(2,1)}), bf16[8,16,1152]{2,1,0:T(8,128)(2,1)S(1)}, u32[]{:S(2)}, u32[]{:S(2)}) async-start(bf16[8,16,1152]{2,1,0:T(8,128)(2,1)} %bitcast.16), calls=%async_computation | async-start | bytes 589824 | tf_op jit(solution)/shard_map/all_to_all | solution.py:345
  31.1 0.0 collective-permute-done.9.refs_2_.refs_4_
  31.1 0.3 collective-permute-start.10
  31.4 0.0 collective-permute-done.11.refs_6_
  31.4 0.3 collective-permute-start.12
  31.7 4.7 %shard_map.95 = (bf16[1024,2048]{1,0:T(8,128)(2,1)S(1)}, bf16[2048,1024]{1,0:T(8,128)(2,1)S(1)}, bf16[192,2048]{1,0:T(8,128)(2,1)S(1)}, bf16[192,512]{1,0:T(8,128)(2,1)S(1)}) custom-call(bf16[64,2048]{1,0:T(8,128)(2,1)S(1)} %collective-permute-done.7.refs_0_.refs_2_, bf16[64,2048]{1,0:T(8,128)(2,1)S(1)} %collective-permute-done.8.refs_1_.refs_3_, ...), custom_call_target="tpu_custom_call" | custom-call | flops 1073741824 | bytes 9175040 | tf_op jit(solution)/shard_map/pallas_call | solution.py:35
  36.4 0.0 collective-permute-done.10.refs_5_
  36.4 0.0 collective-permute-done.12.refs_7_
  36.4 0.0 copy-start.2
  36.4 5.1 %shard_map.96 = (bf16[256,2048]{1,0:T(8,128)(2,1)}, bf16[512,1024]{1,0:T(8,128)(2,1)}) custom-call(bf16[64,2048]{1,0:T(8,128)(2,1)S(1)} %constant_dynamic-update-slice_fusion.refs_0_, bf16[64,2048]{1,0:T(8,128)(2,1)S(1)} %constant_dynamic-update-slice_fusion.4.refs_1_, bf16[64,2048]{1,0:T(8,128)(2,1)S(1)} %collective-permute-done.7.refs_0_.refs_2_, ...), custom_call_target="tpu_custom_call" | custom-call | flops 2147483648 | bytes 12124160 | tf_op jit(solution)/shard_map/pallas_call | solution.py:35
  41.6 0.0 all-to-all-done
  41.6 0.0 copy-done.2
  41.6 0.9 %shard_map.97 = (bf16[64,1024]{1,0:T(8,128)(2,1)}, bf16[2,64]{1,0:T(2,128)(2,1)}) custom-call(bf16[128,64]{1,0:T(8,128)(2,1)S(1)} %get-tuple-element.31.place0, bf16[128,64]{1,0:T(8,128)(2,1)S(1)} %get-tuple-element.32.place1, bf16[2,64]{1,0:T(2,128)(2,1)S(1)} %bitcast.15, bf16[128,1152]{1,0:T(8,128)(2,1)S(1)} %bitcast.13), custom_call_target="tpu_custom_call" | custom-call | bytes 327936 | tf_op jit(solution)/shard_map/pallas_call | solution.py:35
  (8 shorter events, 0.0 us)
Async XLA Ops:
  0.6 21.0 %copy-start = (bf16[1,1024,2048]{2,1,0:T(8,128)(2,1)S(1)}, bf16[1,1024,2048]{2,1,0:T(8,128)(2,1)}, u32[]{:S(2)}) copy-start(bf16[1,1024,2048]{2,1,0:T(8,128)(2,1)} %param.10) | copy-start | bytes 12582916
  0.6 21.0 %copy-start.1 = (bf16[1,2048,1024]{2,1,0:T(8,128)(2,1)S(1)}, bf16[1,2048,1024]{2,1,0:T(8,128)(2,1)}, u32[]{:S(2)}) copy-start(bf16[1,2048,1024]{2,1,0:T(8,128)(2,1)} %param.11) | copy-start | bytes 12582916
  2.2 12.0 %collective-permute-start = (bf16[16,2048]{1,0:T(8,128)(2,1)S(1)}, bf16[16,2048]{1,0:T(8,128)(2,1)S(1)}, u32[]{:S(2)}, u32[]{:S(2)}) collective-permute-start(bf16[16,2048]{1,0:T(8,128)(2,1)S(1)} %get-tuple-element.34), channel_id=1, source_target_pairs={{0,7},{1,6},{2,5},{3,4},{4,3},{5,2},{6,1},{7,0},{8,15},{9,14},{10,... | collective-permute-start | bytes 196616 | tf_op jit(solution)/shard_map/ppermute | solution.py:261
  8.3 6.6 %collective-permute-start.1 = (bf16[16,2048]{1,0:T(8,128)(2,1)S(1)}, bf16[16,2048]{1,0:T(8,128)(2,1)S(1)}, u32[]{:S(2)}, u32[]{:S(2)}) collective-permute-start(bf16[16,2048]{1,0:T(8,128)(2,1)S(1)} %get-tuple-element.35), channel_id=1, source_target_pairs={{0,6},{1,7},{2,4},{3,5},{4,2},{5,3},{6,0},{7,1},{8,14},{9,15},{10,... | collective-permute-start | bytes 196616 | tf_op jit(solution)/shard_map/ppermute | solution.py:261
  8.5 4.4 %collective-permute-start.2 = (bf16[16,2048]{1,0:T(8,128)(2,1)S(1)}, bf16[16,2048]{1,0:T(8,128)(2,1)S(1)}, u32[]{:S(2)}, u32[]{:S(2)}) collective-permute-start(bf16[16,2048]{1,0:T(8,128)(2,1)S(1)} %get-tuple-element.36), channel_id=1, source_target_pairs={{0,1},{1,0},{2,3},{3,2},{4,5},{5,4},{6,7},{7,6},{8,9},{9,8},{10,11... | collective-permute-start | bytes 196616 | tf_op jit(solution)/shard_map/ppermute | solution.py:261
  8.9 8.8 %collective-permute-start.3 = (bf16[16,2048]{1,0:T(8,128)(2,1)S(1)}, bf16[16,2048]{1,0:T(8,128)(2,1)S(1)}, u32[]{:S(2)}, u32[]{:S(2)}) collective-permute-start(bf16[16,2048]{1,0:T(8,128)(2,1)S(1)} %get-tuple-element.37), channel_id=1, source_target_pairs={{0,5},{1,4},{2,7},{3,6},{4,1},{5,0},{6,3},{7,2},{8,13},{9,12},{10,... | collective-permute-start | bytes 196616 | tf_op jit(solution)/shard_map/ppermute | solution.py:261
  10.7 8.8 %collective-permute-start.4 = (bf16[16,2048]{1,0:T(8,128)(2,1)S(1)}, bf16[16,2048]{1,0:T(8,128)(2,1)S(1)}, u32[]{:S(2)}, u32[]{:S(2)}) collective-permute-start(bf16[16,2048]{1,0:T(8,128)(2,1)S(1)} %get-tuple-element.38), channel_id=1, source_target_pairs={{0,4},{1,5},{2,6},{3,7},{4,0},{5,1},{6,2},{7,3},{8,12},{9,13},{10,... | collective-permute-start | bytes 196616 | tf_op jit(solution)/shard_map/ppermute | solution.py:261
  12.9 6.9 %collective-permute-start.5 = (bf16[16,2048]{1,0:T(8,128)(2,1)S(1)}, bf16[16,2048]{1,0:T(8,128)(2,1)S(1)}, u32[]{:S(2)}, u32[]{:S(2)}) collective-permute-start(bf16[16,2048]{1,0:T(8,128)(2,1)S(1)} %get-tuple-element.40), channel_id=1, source_target_pairs={{0,3},{1,2},{2,1},{3,0},{4,7},{5,6},{6,5},{7,4},{8,11},{9,10},{10,... | collective-permute-start | bytes 196616 | tf_op jit(solution)/shard_map/ppermute | solution.py:261
  14.2 5.9 %collective-permute-start.6 = (bf16[16,2048]{1,0:T(8,128)(2,1)S(1)}, bf16[16,2048]{1,0:T(8,128)(2,1)S(1)}, u32[]{:S(2)}, u32[]{:S(2)}) collective-permute-start(bf16[16,2048]{1,0:T(8,128)(2,1)S(1)} %get-tuple-element.42), channel_id=1, source_target_pairs={{0,2},{1,3},{2,0},{3,1},{4,6},{5,7},{6,4},{7,5},{8,10},{9,11},{10,... | collective-permute-start | bytes 196616 | tf_op jit(solution)/shard_map/ppermute | solution.py:261
  14.9 16.2 %collective-permute-start.9 = (bf16[64,2048]{1,0:T(8,128)(2,1)S(1)}, bf16[64,2048]{1,0:T(8,128)(2,1)S(1)}, u32[]{:S(2)}, u32[]{:S(2)}) collective-permute-start(bf16[64,2048]{1,0:T(8,128)(2,1)S(1)} %constant_dynamic-update-slice_fusion.refs_0_), channel_id=1, source_target_pairs={{0,16},{8,24},{16,0},{24,8},{1,17},{9,25},{17,1},{25,9},{2,18},{10... | collective-permute-start | bytes 786440 | tf_op jit(solution)/shard_map/ppermute | solution.py:270
  17.7 8.2 %collective-permute-start.7 = (bf16[64,2048]{1,0:T(8,128)(2,1)S(1)}, bf16[64,2048]{1,0:T(8,128)(2,1)S(1)}, u32[]{:S(2)}, u32[]{:S(2)}) collective-permute-start(bf16[64,2048]{1,0:T(8,128)(2,1)S(1)} %constant_dynamic-update-slice_fusion.refs_0_), channel_id=1, source_target_pairs={{0,8},{8,0},{16,24},{24,16},{1,9},{9,1},{17,25},{25,17},{2,10},{10... | collective-permute-start | bytes 786440 | tf_op jit(solution)/shard_map/ppermute | solution.py:265
  20.1 11.3 %collective-permute-start.11 = (bf16[64,2048]{1,0:T(8,128)(2,1)S(1)}, bf16[64,2048]{1,0:T(8,128)(2,1)S(1)}, u32[]{:S(2)}, u32[]{:S(2)}) collective-permute-start(bf16[64,2048]{1,0:T(8,128)(2,1)S(1)} %constant_dynamic-update-slice_fusion.4.refs_1_), channel_id=1, source_target_pairs={{0,16},{8,24},{16,0},{24,8},{1,17},{9,25},{17,1},{25,9},{2,18},{10... | collective-permute-start | bytes 786440 | tf_op jit(solution)/shard_map/ppermute | solution.py:270
  21.6 4.3 %collective-permute-start.8 = (bf16[64,2048]{1,0:T(8,128)(2,1)S(1)}, bf16[64,2048]{1,0:T(8,128)(2,1)S(1)}, u32[]{:S(2)}, u32[]{:S(2)}) collective-permute-start(bf16[64,2048]{1,0:T(8,128)(2,1)S(1)} %constant_dynamic-update-slice_fusion.4.refs_1_), channel_id=1, source_target_pairs={{0,8},{8,0},{16,24},{24,16},{1,9},{9,1},{17,25},{25,17},{2,10},{10... | collective-permute-start | bytes 786440 | tf_op jit(solution)/shard_map/ppermute | solution.py:265
  26.0 15.6 %all-to-all-start = ((bf16[8,16,1152]{2,1,0:T(8,128)(2,1)}), bf16[8,16,1152]{2,1,0:T(8,128)(2,1)S(1)}, u32[]{:S(2)}, u32[]{:S(2)}) async-start(bf16[8,16,1152]{2,1,0:T(8,128)(2,1)} %bitcast.16), calls=%async_computation | async-start | bytes 589824 | tf_op jit(solution)/shard_map/all_to_all | solution.py:345
  31.1 5.3 %collective-permute-start.10 = (bf16[64,2048]{1,0:T(8,128)(2,1)S(1)}, bf16[64,2048]{1,0:T(8,128)(2,1)S(1)}, u32[]{:S(2)}, u32[]{:S(2)}) collective-permute-start(bf16[64,2048]{1,0:T(8,128)(2,1)S(1)} %collective-permute-done.9.refs_2_.refs_4_), channel_id=1, source_target_pairs={{0,8},{8,0},{16,24},{24,16},{1,9},{9,1},{17,25},{25,17},{2,10},{10... | collective-permute-start | bytes 786440 | tf_op jit(solution)/shard_map/ppermute | solution.py:265
  31.4 5.0 %collective-permute-start.12 = (bf16[64,2048]{1,0:T(8,128)(2,1)S(1)}, bf16[64,2048]{1,0:T(8,128)(2,1)S(1)}, u32[]{:S(2)}, u32[]{:S(2)}) collective-permute-start(bf16[64,2048]{1,0:T(8,128)(2,1)S(1)} %collective-permute-done.11.refs_6_), channel_id=1, source_target_pairs={{0,8},{8,0},{16,24},{24,16},{1,9},{9,1},{17,25},{25,17},{2,10},{10... | collective-permute-start | bytes 786440 | tf_op jit(solution)/shard_map/ppermute | solution.py:265
  36.4 5.2 %copy-start.2 = (bf16[64,2]{0,1:T(2,128)(2,1)S(1)}, bf16[64,2]{0,1:T(2,128)(2,1)}, u32[]{:S(2)}) copy-start(bf16[64,2]{0,1:T(2,128)(2,1)} %param.9) | copy-start | bytes 772

commit v11 on v10

--- a/solution.py
+++ b/solution.py
@@ -142,12 +142,13 @@
 
 def own_kernel(tile, order, *refs):
     row_refs, refs = refs[:2], refs[2:]
-    weight_in, weight_out, d_pre_hbm, h_cut_hbm, back_hbm, *scratch = refs
+    weight_in, weight_out, d_pre_hbm, h_cut_hbm, back_hbm, kept, *scratch = refs
     hidden, d_pre, h_cut, back, sems = scratch
     me = lax.axis_index("expert")
     width, ffw = weight_in.shape
     tiles = [slice(at, at + tile) for at in range(0, ffw, tile)]
     fetch = fetcher(sems)
+    keep = fetch(weight_in.at[:, tiles[0]], kept)
     x, s = stack(row_refs, 0, width), stack(row_refs, 1, width)
     slots_all = x.shape[0]
     capacity = slots_all // len(order)
@@ -169,6 +170,7 @@
     for rows, target in places:
         back[target, width:] = dgate[rows].astype(BF16)
     outs = [
+        keep,
         fetch(d_pre, d_pre_hbm),
         fetch(h_cut, h_cut_hbm),
         fetch(back.at[:, width:], back_hbm.at[:, width:]),
@@ -186,29 +188,26 @@
 
 def early_kernel(tile, pieces, *refs):
     row_refs, refs = refs[:pieces], refs[pieces:]
-    in_hbm, out_hbm, weight_in, weight_out, d_pre, h_cut, rows, hidden, sems = refs
+    kept, in_hbm, out_hbm, weight_in, weight_out, d_pre, h_cut, hidden, sems = refs
     width, ffw = weight_in.shape
-    piece = row_refs[0].shape[0]
     tiles = [slice(at, at + tile) for at in range(0, ffw, tile)]
     fetch = fetcher(sems)
-    first = [fetch(ref, rows.at[pl.ds(i * piece, piece)]) for i, ref in enumerate(row_refs)]
-    weights = [
-        (
-            fetch(in_hbm.at[:, cols], weight_in.at[:, cols]),
-            fetch(out_hbm.at[cols, :], weight_out.at[cols, :]),
-        )
-        for cols in tiles
-    ]
-    for copy in first:
-        copy.wait()
-    x, s = rows[:, :width], rows[:, width:]
-    for cols, (copy_in, copy_out) in zip(tiles, weights):
-        copy_in.wait()
-        copy_out.wait()
-        act, slope = activate(dot(x, weight_in[:, cols]))
+    copies_out = [fetch(out_hbm.at[tiles[0], :], weight_out.at[tiles[0], :])]
+    copies_in = []
+    for cols in tiles[1:]:
+        copies_in.append(fetch(in_hbm.at[:, cols], weight_in.at[:, cols]))
+        copies_out.append(fetch(out_hbm.at[cols, :], weight_out.at[cols, :]))
+    whole = fetch(kept, weight_in.at[:, tiles[0]])
+    x, s = stack(row_refs, 0, width), stack(row_refs, 1, width)
+    for t, cols in enumerate(tiles):
+        if t:
+            copies_in[t - 1].wait()
+        act, slope = activate(dot(x, weight_in[:, cols] if t else kept[...]))
         hidden[:, cols] = act
+        copies_out[t].wait()
         d_pre[:, cols] = (dot(s, weight_out[cols, :], (1, 1)) * slope).astype(BF16)
     h_cut[...] = my_part(hidden)
+    whole.wait()
 
 
 def grads_kernel(tile, pieces, late, *refs):
@@ -321,12 +320,13 @@
     core_b = swap_cores(rows_b)
     weights = [proj_in[0], proj_out[0]]
     weight_space = [pltpu.VMEM((feat_width, ffw), BF16), pltpu.VMEM((ffw, feat_width), BF16)]
-    d_pre, h_cut, back = call(
+    d_pre, h_cut, back, kept = call(
         functools.partial(own_kernel, tile, order),
         [
             pltpu.HBM((slots_all, ffw), BF16),
             pltpu.HBM((slots_all, tile), BF16),
             pltpu.HBM((slots_all, feat_width + LANES), BF16),
+            pltpu.VMEM((feat_width, tile), BF16),
         ],
         [
             rows_a,
@@ -339,7 +339,7 @@
             pltpu.VMEM((slots_all, ffw), BF16),
             pltpu.VMEM((slots_all, tile), BF16),
             pltpu.VMEM((slots_all, feat_width + LANES), BF16),
-            pltpu.SemaphoreType.DMA((7,)),
+            pltpu.SemaphoreType.DMA((8,)),
         ],
     )
     back = lax.all_to_all(
@@ -358,14 +358,13 @@
     weight_in, weight_out, d_pre_early, h_cut_early = call(
         functools.partial(early_kernel, tile, len(early)),
         [*weight_space, shape((early_rows, ffw)), shape((early_rows, tile))],
-        [*early, *weights],
+        [*early, pltpu.with_memory_space_constraint(kept, pltpu.VMEM), *weights],
         2 * product,
         scratch=[
-            pltpu.VMEM((early_rows, 2 * feat_width), BF16),
             pltpu.VMEM((early_rows, ffw), BF16),
-            pltpu.SemaphoreType.DMA((len(early) + 2 * groups,)),
-        ],
-        spaces=[pl.ANY] * len(early) + [pltpu.HBM] * 2,
+            pltpu.SemaphoreType.DMA((2 * groups,)),
+        ],
+        spaces=[pltpu.VMEM] * (len(early) + 1) + [pltpu.HBM] * 2,
     )
     pieces = [rows_a, rows_b, *early, *late]
     rows_all = groups * slots_all

time: 42.7 us -> 42.9 us (level)
  transfers between devices with their start and end apart: 14 -> 14, of which waited for: 4 -> 4; matrix products, arithmetic and copies ran while one was open for 0% -> 0% of each run, Pallas kernels for 33% -> 34%
where the time goes in v11:
time: 42.9 us; the launch traced here: 42.7 us
  starting transfers between devices  21.5 us (50%)
  Pallas kernels  16.8 us (39%)
  waiting for transfers between devices  3.54 us (8%)
  between operations  0.78 us (2%)
    pallas_call x5, Pallas kernels, call(): pl.pallas_call(kernel, out_shape=out_shape, in_specs=[pl.BlockSpec(memory...  16.8 us
    ppermute x7, starting transfers between devices, permute(): lax.ppermute(block, 'expert', [(i, i ^ k) for i in range(lax.axis_size('e...  12.6 us
    all_to_all x1, starting transfers between devices, local(): lax.all_to_all(after(back, core_a, core_b).reshape(experts, capacity, fea...  5.14 us
    ppermute x7, waiting for transfers between devices, permute(): lax.ppermute(block, 'expert', [(i, i ^ k) for i in range(lax.axis_size('e...  3.52 us
    ppermute x2, starting transfers between devices, shift_chips(): lax.ppermute(rows, 'dp', [(i, (i + 2 * k) % groups) for i in range(groups)])  3.22 us
  transfers between devices with their start and end apart: 14, of which 4 were waited for; matrix products, arithmetic and copies ran while one was open for 0% of the time, Pallas kernels for 34%

profile of v11, /device:TPU:0, one launch (start us, length us, event | category | flops | bytes accessed | tf_op | source)
XLA Modules:
  0.0 42.7 jit_solution(8609782313319460889)
XLA Ops:
  0.6 0.0 copy-start
  0.6 0.0 copy-start.1
  0.7 1.6 %shard_map.93 = (bf16[16,2048]{1,0:T(8,128)(2,1)S(1)}, bf16[16,2048]{1,0:T(8,128)(2,1)S(1)}, bf16[16,2048]{1,0:T(8,128)(2,1)S(1)}, bf16[16,2048]{1,0:T(8,128)(2,...) custom-call(s32[2,64]{1,0:T(2,128)} %bitcast.19, ...), custom_call_target="tpu_custom_call" | custom-call | flops 16106127360 | bytes 262912 | tf_op jit(solution)/shard_map/pallas_call | solution.py:35
  2.2 6.0 %collective-permute-start = (bf16[16,2048]{1,0:T(8,128)(2,1)S(1)}, bf16[16,2048]{1,0:T(8,128)(2,1)S(1)}, u32[]{:S(2)}, u32[]{:S(2)}) collective-permute-start(bf16[16,2048]{1,0:T(8,128)(2,1)S(1)} %get-tuple-element.35), channel_id=1, source_target_pairs={{0,7},{1,6},{2,5},{3,4},{4,3},{5,2},{6,1},{7,0},{8,15},{9,14},{10,... | collective-permute-start | bytes 196616 | tf_op jit(solution)/shard_map/ppermute | solution.py:260
  8.3 0.2 collective-permute-start.1
  8.5 0.4 collective-permute-start.2
  8.9 1.8 %collective-permute-start.3 = (bf16[16,2048]{1,0:T(8,128)(2,1)S(1)}, bf16[16,2048]{1,0:T(8,128)(2,1)S(1)}, u32[]{:S(2)}, u32[]{:S(2)}) collective-permute-start(bf16[16,2048]{1,0:T(8,128)(2,1)S(1)} %get-tuple-element.38), channel_id=1, source_target_pairs={{0,5},{1,4},{2,7},{3,6},{4,1},{5,0},{6,3},{7,2},{8,13},{9,12},{10,... | collective-permute-start | bytes 196616 | tf_op jit(solution)/shard_map/ppermute | solution.py:260
  10.7 2.1 %collective-permute-start.4 = (bf16[16,2048]{1,0:T(8,128)(2,1)S(1)}, bf16[16,2048]{1,0:T(8,128)(2,1)S(1)}, u32[]{:S(2)}, u32[]{:S(2)}) collective-permute-start(bf16[16,2048]{1,0:T(8,128)(2,1)S(1)} %get-tuple-element.39), channel_id=1, source_target_pairs={{0,4},{1,5},{2,6},{3,7},{4,0},{5,1},{6,2},{7,3},{8,12},{9,13},{10,... | collective-permute-start | bytes 196616 | tf_op jit(solution)/shard_map/ppermute | solution.py:260
  12.9 0.0 collective-permute-done.2
  12.9 1.3 %collective-permute-start.5 = (bf16[16,2048]{1,0:T(8,128)(2,1)S(1)}, bf16[16,2048]{1,0:T(8,128)(2,1)S(1)}, u32[]{:S(2)}, u32[]{:S(2)}) collective-permute-start(bf16[16,2048]{1,0:T(8,128)(2,1)S(1)} %get-tuple-element.41), channel_id=1, source_target_pairs={{0,3},{1,2},{2,1},{3,0},{4,7},{5,6},{6,5},{7,4},{8,11},{9,10},{10,... | collective-permute-start | bytes 196616 | tf_op jit(solution)/shard_map/ppermute | solution.py:260
  14.2 0.0 collective-permute-done
  14.2 0.6 %collective-permute-start.6 = (bf16[16,2048]{1,0:T(8,128)(2,1)S(1)}, bf16[16,2048]{1,0:T(8,128)(2,1)S(1)}, u32[]{:S(2)}, u32[]{:S(2)}) collective-permute-start(bf16[16,2048]{1,0:T(8,128)(2,1)S(1)} %get-tuple-element.43), channel_id=1, source_target_pairs={{0,2},{1,3},{2,0},{3,1},{4,6},{5,7},{6,4},{7,5},{8,10},{9,11},{10,... | collective-permute-start | bytes 196616 | tf_op jit(solution)/shard_map/ppermute | solution.py:260
  14.8 0.0 collective-permute-done.1
  14.9 1.7 %collective-permute-start.9 = (bf16[64,2048]{1,0:T(8,128)(2,1)S(1)}, bf16[64,2048]{1,0:T(8,128)(2,1)S(1)}, u32[]{:S(2)}, u32[]{:S(2)}) collective-permute-start(bf16[64,2048]{1,0:T(8,128)(2,1)S(1)} %constant_dynamic-update-slice_fusion.refs_0_), channel_id=1, source_target_pairs={{0,16},{8,24},{16,0},{24,8},{1,17},{9,25},{17,1},{25,9},{2,18},{10... | collective-permute-start | bytes 786440 | tf_op jit(solution)/shard_map/ppermute | solution.py:269
  16.6 1.1 %collective-permute-done.3 = bf16[16,2048]{1,0:T(8,128)(2,1)S(1)} collective-permute-done((bf16[16,2048]{1,0:T(8,128)(2,1)S(1)}, bf16[16,2048]{1,0:T(8,128)(2,1)S(1)}, u32[]{:S(2)}, u32[]{:S(2)}) %collective-permute-start.3) | collective-permute-done | bytes 65568 | tf_op jit(solution)/shard_map/ppermute | solution.py:260
  17.7 0.0 collective-permute-start.7
  17.7 1.8 %collective-permute-done.4 = bf16[16,2048]{1,0:T(8,128)(2,1)S(1)} collective-permute-done((bf16[16,2048]{1,0:T(8,128)(2,1)S(1)}, bf16[16,2048]{1,0:T(8,128)(2,1)S(1)}, u32[]{:S(2)}, u32[]{:S(2)}) %collective-permute-start.4) | collective-permute-done | bytes 65568 | tf_op jit(solution)/shard_map/ppermute | solution.py:260
  19.5 0.3 collective-permute-done.5
  19.8 0.3 collective-permute-done.6
  20.1 1.5 %collective-permute-start.11 = (bf16[64,2048]{1,0:T(8,128)(2,1)S(1)}, bf16[64,2048]{1,0:T(8,128)(2,1)S(1)}, u32[]{:S(2)}, u32[]{:S(2)}) collective-permute-start(bf16[64,2048]{1,0:T(8,128)(2,1)S(1)} %constant_dynamic-update-slice_fusion.4.refs_1_), channel_id=1, source_target_pairs={{0,16},{8,24},{16,0},{24,8},{1,17},{9,25},{17,1},{25,9},{2,18},{10... | collective-permute-start | bytes 786440 | tf_op jit(solution)/shard_map/ppermute | solution.py:269
  21.6 0.0 collective-permute-start.8
  21.6 0.0 copy-done
  21.6 0.0 copy-done.1
  21.6 4.5 %shard_map.94 = (bf16[128,2048]{1,0:T(8,128)(2,1)}, bf16[128,512]{1,0:T(8,128)(2,1)}, bf16[128,1152]{1,0:T(8,128)(2,1)}, bf16[1024,512]{1,0:T(8,128)(2,1)S(1)}) custom-call(bf16[64,2048]{1,0:T(8,128)(2,1)S(1)} %constant_dynamic-update-slice_fusion.refs_0_, bf16[64,2048]{1,0:T(8,128)(2,1)S(1)} %constant_dynamic-update-slice_fusion.4.refs_1_, ...), custom_call_target="tpu_custom_call" | custom-call | flops 10737418240 | bytes 8912896 | tf_op jit(solution)/shard_map/pallas_call | solution.py:35
  26.1 0.0 collective-permute-done.7.refs_0_.refs_2_
  26.1 0.0 collective-permute-done.8.refs_1_.refs_3_
  26.1 5.1 %all-to-all-start = ((bf16[8,16,1152]{2,1,0:T(8,128)(2,1)}), bf16[8,16,1152]{2,1,0:T(8,128)(2,1)S(1)}, u32[]{:S(2)}, u32[]{:S(2)}) async-start(bf16[8,16,1152]{2,1,0:T(8,128)(2,1)} %bitcast.16), calls=%async_computation | async-start | bytes 589824 | tf_op jit(solution)/shard_map/all_to_all | solution.py:345
  31.3 0.0 collective-permute-done.9.refs_2_.refs_4_
  31.3 0.3 collective-permute-start.10
  31.6 0.0 collective-permute-done.11.refs_6_
  31.6 0.3 collective-permute-start.12
  31.9 4.8 %shard_map.95 = (bf16[1024,2048]{1,0:T(8,128)(2,1)S(1)}, bf16[2048,1024]{1,0:T(8,128)(2,1)S(1)}, bf16[192,2048]{1,0:T(8,128)(2,1)S(1)}, bf16[192,512]{1,0:T(8,128)(2,1)S(1)}) custom-call(bf16[64,2048]{1,0:T(8,128)(2,1)S(1)} %collective-permute-done.7.refs_0_.refs_2_, bf16[64,2048]{1,0:T(8,128)(2,1)S(1)} %collective-permute-done.8.refs_1_.refs_3_, ...), custom_call_target="tpu_custom_call" | custom-call | flops 1073741824 | bytes 10223616 | tf_op jit(solution)/shard_map/pallas_call | solution.py:35
  36.7 0.0 collective-permute-done.10.refs_5_
  36.7 0.0 collective-permute-done.12.refs_7_
  36.7 0.0 copy-start.2
  36.7 5.1 %shard_map.96 = (bf16[256,2048]{1,0:T(8,128)(2,1)}, bf16[512,1024]{1,0:T(8,128)(2,1)}) custom-call(bf16[64,2048]{1,0:T(8,128)(2,1)S(1)} %constant_dynamic-update-slice_fusion.refs_0_, bf16[64,2048]{1,0:T(8,128)(2,1)S(1)} %constant_dynamic-update-slice_fusion.4.refs_1_, bf16[64,2048]{1,0:T(8,128)(2,1)S(1)} %collective-permute-done.7.refs_0_.refs_2_, ...), custom_call_target="tpu_custom_call" | custom-call | flops 2147483648 | bytes 12124160 | tf_op jit(solution)/shard_map/pallas_call | solution.py:35
  41.8 0.0 all-to-all-done
  41.8 0.0 copy-done.2
  41.8 0.9 %shard_map.97 = (bf16[64,1024]{1,0:T(8,128)(2,1)}, bf16[2,64]{1,0:T(2,128)(2,1)}) custom-call(bf16[128,64]{1,0:T(8,128)(2,1)S(1)} %get-tuple-element.32.place0, bf16[128,64]{1,0:T(8,128)(2,1)S(1)} %get-tuple-element.33.place1, bf16[2,64]{1,0:T(2,128)(2,1)S(1)} %bitcast.15, bf16[128,1152]{1,0:T(8,128)(2,1)S(1)} %bitcast.13), custom_call_target="tpu_custom_call" | custom-call | bytes 327936 | tf_op jit(solution)/shard_map/pallas_call | solution.py:35
  (8 shorter events, 0.0 us)
Async XLA Ops:
  0.6 21.0 %copy-start = (bf16[1,1024,2048]{2,1,0:T(8,128)(2,1)S(1)}, bf16[1,1024,2048]{2,1,0:T(8,128)(2,1)}, u32[]{:S(2)}) copy-start(bf16[1,1024,2048]{2,1,0:T(8,128)(2,1)} %param.10) | copy-start | bytes 12582916
  0.6 21.0 %copy-start.1 = (bf16[1,2048,1024]{2,1,0:T(8,128)(2,1)S(1)}, bf16[1,2048,1024]{2,1,0:T(8,128)(2,1)}, u32[]{:S(2)}) copy-start(bf16[1,2048,1024]{2,1,0:T(8,128)(2,1)} %param.11) | copy-start | bytes 12582916
  2.2 12.0 %collective-permute-start = (bf16[16,2048]{1,0:T(8,128)(2,1)S(1)}, bf16[16,2048]{1,0:T(8,128)(2,1)S(1)}, u32[]{:S(2)}, u32[]{:S(2)}) collective-permute-start(bf16[16,2048]{1,0:T(8,128)(2,1)S(1)} %get-tuple-element.35), channel_id=1, source_target_pairs={{0,7},{1,6},{2,5},{3,4},{4,3},{5,2},{6,1},{7,0},{8,15},{9,14},{10,... | collective-permute-start | bytes 196616 | tf_op jit(solution)/shard_map/ppermute | solution.py:260
  8.3 6.6 %collective-permute-start.1 = (bf16[16,2048]{1,0:T(8,128)(2,1)S(1)}, bf16[16,2048]{1,0:T(8,128)(2,1)S(1)}, u32[]{:S(2)}, u32[]{:S(2)}) collective-permute-start(bf16[16,2048]{1,0:T(8,128)(2,1)S(1)} %get-tuple-element.36), channel_id=1, source_target_pairs={{0,6},{1,7},{2,4},{3,5},{4,2},{5,3},{6,0},{7,1},{8,14},{9,15},{10,... | collective-permute-start | bytes 196616 | tf_op jit(solution)/shard_map/ppermute | solution.py:260
  8.5 4.4 %collective-permute-start.2 = (bf16[16,2048]{1,0:T(8,128)(2,1)S(1)}, bf16[16,2048]{1,0:T(8,128)(2,1)S(1)}, u32[]{:S(2)}, u32[]{:S(2)}) collective-permute-start(bf16[16,2048]{1,0:T(8,128)(2,1)S(1)} %get-tuple-element.37), channel_id=1, source_target_pairs={{0,1},{1,0},{2,3},{3,2},{4,5},{5,4},{6,7},{7,6},{8,9},{9,8},{10,11... | collective-permute-start | bytes 196616 | tf_op jit(solution)/shard_map/ppermute | solution.py:260
  8.9 8.8 %collective-permute-start.3 = (bf16[16,2048]{1,0:T(8,128)(2,1)S(1)}, bf16[16,2048]{1,0:T(8,128)(2,1)S(1)}, u32[]{:S(2)}, u32[]{:S(2)}) collective-permute-start(bf16[16,2048]{1,0:T(8,128)(2,1)S(1)} %get-tuple-element.38), channel_id=1, source_target_pairs={{0,5},{1,4},{2,7},{3,6},{4,1},{5,0},{6,3},{7,2},{8,13},{9,12},{10,... | collective-permute-start | bytes 196616 | tf_op jit(solution)/shard_map/ppermute | solution.py:260
  10.7 8.8 %collective-permute-start.4 = (bf16[16,2048]{1,0:T(8,128)(2,1)S(1)}, bf16[16,2048]{1,0:T(8,128)(2,1)S(1)}, u32[]{:S(2)}, u32[]{:S(2)}) collective-permute-start(bf16[16,2048]{1,0:T(8,128)(2,1)S(1)} %get-tuple-element.39), channel_id=1, source_target_pairs={{0,4},{1,5},{2,6},{3,7},{4,0},{5,1},{6,2},{7,3},{8,12},{9,13},{10,... | collective-permute-start | bytes 196616 | tf_op jit(solution)/shard_map/ppermute | solution.py:260
  12.9 6.9 %collective-permute-start.5 = (bf16[16,2048]{1,0:T(8,128)(2,1)S(1)}, bf16[16,2048]{1,0:T(8,128)(2,1)S(1)}, u32[]{:S(2)}, u32[]{:S(2)}) collective-permute-start(bf16[16,2048]{1,0:T(8,128)(2,1)S(1)} %get-tuple-element.41), channel_id=1, source_target_pairs={{0,3},{1,2},{2,1},{3,0},{4,7},{5,6},{6,5},{7,4},{8,11},{9,10},{10,... | collective-permute-start | bytes 196616 | tf_op jit(solution)/shard_map/ppermute | solution.py:260
  14.2 5.9 %collective-permute-start.6 = (bf16[16,2048]{1,0:T(8,128)(2,1)S(1)}, bf16[16,2048]{1,0:T(8,128)(2,1)S(1)}, u32[]{:S(2)}, u32[]{:S(2)}) collective-permute-start(bf16[16,2048]{1,0:T(8,128)(2,1)S(1)} %get-tuple-element.43), channel_id=1, source_target_pairs={{0,2},{1,3},{2,0},{3,1},{4,6},{5,7},{6,4},{7,5},{8,10},{9,11},{10,... | collective-permute-start | bytes 196616 | tf_op jit(solution)/shard_map/ppermute | solution.py:260
  14.9 16.4 %collective-permute-start.9 = (bf16[64,2048]{1,0:T(8,128)(2,1)S(1)}, bf16[64,2048]{1,0:T(8,128)(2,1)S(1)}, u32[]{:S(2)}, u32[]{:S(2)}) collective-permute-start(bf16[64,2048]{1,0:T(8,128)(2,1)S(1)} %constant_dynamic-update-slice_fusion.refs_0_), channel_id=1, source_target_pairs={{0,16},{8,24},{16,0},{24,8},{1,17},{9,25},{17,1},{25,9},{2,18},{10... | collective-permute-start | bytes 786440 | tf_op jit(solution)/shard_map/ppermute | solution.py:269
  17.7 8.4 %collective-permute-start.7 = (bf16[64,2048]{1,0:T(8,128)(2,1)S(1)}, bf16[64,2048]{1,0:T(8,128)(2,1)S(1)}, u32[]{:S(2)}, u32[]{:S(2)}) collective-permute-start(bf16[64,2048]{1,0:T(8,128)(2,1)S(1)} %constant_dynamic-update-slice_fusion.refs_0_), channel_id=1, source_target_pairs={{0,8},{8,0},{16,24},{24,16},{1,9},{9,1},{17,25},{25,17},{2,10},{10... | collective-permute-start | bytes 786440 | tf_op jit(solution)/shard_map/ppermute | solution.py:264
  20.1 11.4 %collective-permute-start.11 = (bf16[64,2048]{1,0:T(8,128)(2,1)S(1)}, bf16[64,2048]{1,0:T(8,128)(2,1)S(1)}, u32[]{:S(2)}, u32[]{:S(2)}) collective-permute-start(bf16[64,2048]{1,0:T(8,128)(2,1)S(1)} %constant_dynamic-update-slice_fusion.4.refs_1_), channel_id=1, source_target_pairs={{0,16},{8,24},{16,0},{24,8},{1,17},{9,25},{17,1},{25,9},{2,18},{10... | collective-permute-start | bytes 786440 | tf_op jit(solution)/shard_map/ppermute | solution.py:269
  21.6 4.5 %collective-permute-start.8 = (bf16[64,2048]{1,0:T(8,128)(2,1)S(1)}, bf16[64,2048]{1,0:T(8,128)(2,1)S(1)}, u32[]{:S(2)}, u32[]{:S(2)}) collective-permute-start(bf16[64,2048]{1,0:T(8,128)(2,1)S(1)} %constant_dynamic-update-slice_fusion.4.refs_1_), channel_id=1, source_target_pairs={{0,8},{8,0},{16,24},{24,16},{1,9},{9,1},{17,25},{25,17},{2,10},{10... | collective-permute-start | bytes 786440 | tf_op jit(solution)/shard_map/ppermute | solution.py:264
  26.1 15.7 %all-to-all-start = ((bf16[8,16,1152]{2,1,0:T(8,128)(2,1)}), bf16[8,16,1152]{2,1,0:T(8,128)(2,1)S(1)}, u32[]{:S(2)}, u32[]{:S(2)}) async-start(bf16[8,16,1152]{2,1,0:T(8,128)(2,1)} %bitcast.16), calls=%async_computation | async-start | bytes 589824 | tf_op jit(solution)/shard_map/all_to_all | solution.py:345
  31.3 5.4 %collective-permute-start.10 = (bf16[64,2048]{1,0:T(8,128)(2,1)S(1)}, bf16[64,2048]{1,0:T(8,128)(2,1)S(1)}, u32[]{:S(2)}, u32[]{:S(2)}) collective-permute-start(bf16[64,2048]{1,0:T(8,128)(2,1)S(1)} %collective-permute-done.9.refs_2_.refs_4_), channel_id=1, source_target_pairs={{0,8},{8,0},{16,24},{24,16},{1,9},{9,1},{17,25},{25,17},{2,10},{10... | collective-permute-start | bytes 786440 | tf_op jit(solution)/shard_map/ppermute | solution.py:264
  31.6 5.1 %collective-permute-start.12 = (bf16[64,2048]{1,0:T(8,128)(2,1)S(1)}, bf16[64,2048]{1,0:T(8,128)(2,1)S(1)}, u32[]{:S(2)}, u32[]{:S(2)}) collective-permute-start(bf16[64,2048]{1,0:T(8,128)(2,1)S(1)} %collective-permute-done.11.refs_6_), channel_id=1, source_target_pairs={{0,8},{8,0},{16,24},{24,16},{1,9},{9,1},{17,25},{25,17},{2,10},{10... | collective-permute-start | bytes 786440 | tf_op jit(solution)/shard_map/ppermute | solution.py:264
  36.7 5.2 %copy-start.2 = (bf16[64,2]{0,1:T(2,128)(2,1)S(1)}, bf16[64,2]{0,1:T(2,128)(2,1)}, u32[]{:S(2)}) copy-start(bf16[64,2]{0,1:T(2,128)(2,1)} %param.9) | copy-start | bytes 772

commit v12 on v10

--- a/solution.py
+++ b/solution.py
@@ -140,6 +140,19 @@
     return fetch
 
 
+def backward_tiles(tiles, x, s, weight_in, weight_out, arrived=lambda t: None):
+    arrived(0)
+    ahead = dot(x, weight_in[:, tiles[0]])
+    for t, cols in enumerate(tiles):
+        pre_act = ahead
+        if t + 1 < len(tiles):
+            arrived(t + 1)
+            ahead = dot(x, weight_in[:, tiles[t + 1]])
+        d_hidden = dot(s, weight_out[cols, :], (1, 1))
+        act, slope = activate(pre_act)
+        yield cols, act, d_hidden, (d_hidden * slope).astype(BF16)
+
+
 def own_kernel(tile, order, *refs):
     row_refs, refs = refs[:2], refs[2:]
     weight_in, weight_out, d_pre_hbm, h_cut_hbm, back_hbm, *scratch = refs
@@ -152,11 +165,9 @@
     slots_all = x.shape[0]
     capacity = slots_all // len(order)
     dgate = jnp.zeros((slots_all, LANES), F32)
-    for cols in tiles:
-        act, slope = activate(dot(x, weight_in[:, cols]))
+    for cols, act, d_hidden, part in backward_tiles(tiles, x, s, weight_in, weight_out):
         hidden[:, cols] = act
-        d_hidden = dot(s, weight_out[cols, :], (1, 1))
-        d_pre[:, cols] = (d_hidden * slope).astype(BF16)
+        d_pre[:, cols] = part
         product = d_hidden * act.astype(F32)
         for lane in range(0, tile, LANES):
             dgate = dgate + product[:, lane : lane + LANES]
@@ -186,28 +197,26 @@
 
 def early_kernel(tile, pieces, *refs):
     row_refs, refs = refs[:pieces], refs[pieces:]
-    in_hbm, out_hbm, weight_in, weight_out, d_pre, h_cut, rows, hidden, sems = refs
+    in_hbm, out_hbm, weight_in, weight_out, d_pre, h_cut, hidden, sems = refs
     width, ffw = weight_in.shape
-    piece = row_refs[0].shape[0]
     tiles = [slice(at, at + tile) for at in range(0, ffw, tile)]
     fetch = fetcher(sems)
-    first = [fetch(ref, rows.at[pl.ds(i * piece, piece)]) for i, ref in enumerate(row_refs)]
-    weights = [
+    copies = [
         (
             fetch(in_hbm.at[:, cols], weight_in.at[:, cols]),
             fetch(out_hbm.at[cols, :], weight_out.at[cols, :]),
         )
         for cols in tiles
     ]
-    for copy in first:
-        copy.wait()
-    x, s = rows[:, :width], rows[:, width:]
-    for cols, (copy_in, copy_out) in zip(tiles, weights):
-        copy_in.wait()
-        copy_out.wait()
-        act, slope = activate(dot(x, weight_in[:, cols]))
+
+    def arrived(t):
+        for copy in copies[t]:
+            copy.wait()
+
+    x, s = stack(row_refs, 0, width), stack(row_refs, 1, width)
+    for cols, act, _, part in backward_tiles(tiles, x, s, weight_in, weight_out, arrived):
         hidden[:, cols] = act
-        d_pre[:, cols] = (dot(s, weight_out[cols, :], (1, 1)) * slope).astype(BF16)
+        d_pre[:, cols] = part
     h_cut[...] = my_part(hidden)
 
 
@@ -231,10 +240,9 @@
         copies += [fetch(source, d_pre.at[span]), fetch(cut_source, h_cut.at[span])]
         at += source.shape[0]
     x, s = stack(row_refs[-late:], 0, width), stack(row_refs[-late:], 1, width)
-    for cols in tiles:
-        act, slope = activate(dot(x, weight_in[:, cols]))
+    for cols, act, _, part in backward_tiles(tiles, x, s, weight_in, weight_out):
         hidden[:, cols] = act
-        d_pre[known:, cols] = (dot(s, weight_out[cols, :], (1, 1)) * slope).astype(BF16)
+        d_pre[known:, cols] = part
     for copy in copies:
         copy.wait()
     cut = grad_in.shape[0]
@@ -361,11 +369,10 @@
         [*early, *weights],
         2 * product,
         scratch=[
-            pltpu.VMEM((early_rows, 2 * feat_width), BF16),
             pltpu.VMEM((early_rows, ffw), BF16),
-            pltpu.SemaphoreType.DMA((len(early) + 2 * groups,)),
-        ],
-        spaces=[pl.ANY] * len(early) + [pltpu.HBM] * 2,
+            pltpu.SemaphoreType.DMA((2 * groups,)),
+        ],
+        spaces=[pltpu.VMEM] * len(early) + [pltpu.HBM] * 2,
     )
     pieces = [rows_a, rows_b, *early, *late]
     rows_all = groups * slots_all

time: 42.7 us -> 42.9 us (level)
  transfers between devices with their start and end apart: 14 -> 14, of which waited for: 4 -> 4; matrix products, arithmetic and copies ran while one was open for 0% -> 0% of each run, Pallas kernels for 33% -> 34%
where the time goes in v12:
time: 42.9 us; the launch traced here: 42.7 us
  starting transfers between devices  21.5 us (50%)
  Pallas kernels  16.8 us (39%)
  waiting for transfers between devices  3.54 us (8%)
  between operations  0.78 us (2%)
    pallas_call x5, Pallas kernels, call(): pl.pallas_call(kernel, out_shape=out_shape, in_specs=[pl.BlockSpec(memory...  16.8 us
    ppermute x7, starting transfers between devices, permute(): lax.ppermute(block, 'expert', [(i, i ^ k) for i in range(lax.axis_size('e...  12.6 us
    all_to_all x1, starting transfers between devices, local(): lax.all_to_all(after(back, core_a, core_b).reshape(experts, capacity, fea...  5.13 us
    ppermute x7, waiting for transfers between devices, permute(): lax.ppermute(block, 'expert', [(i, i ^ k) for i in range(lax.axis_size('e...  3.52 us
    ppermute x2, starting transfers between devices, shift_chips(): lax.ppermute(rows, 'dp', [(i, (i + 2 * k) % groups) for i in range(groups)])  3.22 us
  transfers between devices with their start and end apart: 14, of which 4 were waited for; matrix products, arithmetic and copies ran while one was open for 0% of the time, Pallas kernels for 34%

profile of v12, /device:TPU:0, one launch (start us, length us, event | category | flops | bytes accessed | tf_op | source)
XLA Modules:
  0.0 42.7 jit_solution(5870832297345988574)
XLA Ops:
  0.6 0.0 copy-start
  0.6 0.0 copy-start.1
  0.7 1.6 %shard_map.93 = (bf16[16,2048]{1,0:T(8,128)(2,1)S(1)}, bf16[16,2048]{1,0:T(8,128)(2,1)S(1)}, bf16[16,2048]{1,0:T(8,128)(2,1)S(1)}, bf16[16,2048]{1,0:T(8,128)(2,...) custom-call(s32[2,64]{1,0:T(2,128)} %bitcast.19, ...), custom_call_target="tpu_custom_call" | custom-call | flops 16106127360 | bytes 262912 | tf_op jit(solution)/shard_map/pallas_call | solution.py:35
  2.2 6.0 %collective-permute-start = (bf16[16,2048]{1,0:T(8,128)(2,1)S(1)}, bf16[16,2048]{1,0:T(8,128)(2,1)S(1)}, u32[]{:S(2)}, u32[]{:S(2)}) collective-permute-start(bf16[16,2048]{1,0:T(8,128)(2,1)S(1)} %get-tuple-element.34), channel_id=1, source_target_pairs={{0,7},{1,6},{2,5},{3,4},{4,3},{5,2},{6,1},{7,0},{8,15},{9,14},{10,... | collective-permute-start | bytes 196616 | tf_op jit(solution)/shard_map/ppermute | solution.py:269
  8.3 0.2 collective-permute-start.1
  8.5 0.4 collective-permute-start.2
  8.9 1.8 %collective-permute-start.3 = (bf16[16,2048]{1,0:T(8,128)(2,1)S(1)}, bf16[16,2048]{1,0:T(8,128)(2,1)S(1)}, u32[]{:S(2)}, u32[]{:S(2)}) collective-permute-start(bf16[16,2048]{1,0:T(8,128)(2,1)S(1)} %get-tuple-element.37), channel_id=1, source_target_pairs={{0,5},{1,4},{2,7},{3,6},{4,1},{5,0},{6,3},{7,2},{8,13},{9,12},{10,... | collective-permute-start | bytes 196616 | tf_op jit(solution)/shard_map/ppermute | solution.py:269
  10.7 2.1 %collective-permute-start.4 = (bf16[16,2048]{1,0:T(8,128)(2,1)S(1)}, bf16[16,2048]{1,0:T(8,128)(2,1)S(1)}, u32[]{:S(2)}, u32[]{:S(2)}) collective-permute-start(bf16[16,2048]{1,0:T(8,128)(2,1)S(1)} %get-tuple-element.38), channel_id=1, source_target_pairs={{0,4},{1,5},{2,6},{3,7},{4,0},{5,1},{6,2},{7,3},{8,12},{9,13},{10,... | collective-permute-start | bytes 196616 | tf_op jit(solution)/shard_map/ppermute | solution.py:269
  12.9 0.0 collective-permute-done.2
  12.9 1.3 %collective-permute-start.5 = (bf16[16,2048]{1,0:T(8,128)(2,1)S(1)}, bf16[16,2048]{1,0:T(8,128)(2,1)S(1)}, u32[]{:S(2)}, u32[]{:S(2)}) collective-permute-start(bf16[16,2048]{1,0:T(8,128)(2,1)S(1)} %get-tuple-element.40), channel_id=1, source_target_pairs={{0,3},{1,2},{2,1},{3,0},{4,7},{5,6},{6,5},{7,4},{8,11},{9,10},{10,... | collective-permute-start | bytes 196616 | tf_op jit(solution)/shard_map/ppermute | solution.py:269
  14.2 0.0 collective-permute-done
  14.2 0.6 %collective-permute-start.6 = (bf16[16,2048]{1,0:T(8,128)(2,1)S(1)}, bf16[16,2048]{1,0:T(8,128)(2,1)S(1)}, u32[]{:S(2)}, u32[]{:S(2)}) collective-permute-start(bf16[16,2048]{1,0:T(8,128)(2,1)S(1)} %get-tuple-element.42), channel_id=1, source_target_pairs={{0,2},{1,3},{2,0},{3,1},{4,6},{5,7},{6,4},{7,5},{8,10},{9,11},{10,... | collective-permute-start | bytes 196616 | tf_op jit(solution)/shard_map/ppermute | solution.py:269
  14.8 0.0 collective-permute-done.1
  14.9 1.7 %collective-permute-start.9 = (bf16[64,2048]{1,0:T(8,128)(2,1)S(1)}, bf16[64,2048]{1,0:T(8,128)(2,1)S(1)}, u32[]{:S(2)}, u32[]{:S(2)}) collective-permute-start(bf16[64,2048]{1,0:T(8,128)(2,1)S(1)} %constant_dynamic-update-slice_fusion.refs_0_), channel_id=1, source_target_pairs={{0,16},{8,24},{16,0},{24,8},{1,17},{9,25},{17,1},{25,9},{2,18},{10... | collective-permute-start | bytes 786440 | tf_op jit(solution)/shard_map/ppermute | solution.py:278
  16.6 1.1 %collective-permute-done.3 = bf16[16,2048]{1,0:T(8,128)(2,1)S(1)} collective-permute-done((bf16[16,2048]{1,0:T(8,128)(2,1)S(1)}, bf16[16,2048]{1,0:T(8,128)(2,1)S(1)}, u32[]{:S(2)}, u32[]{:S(2)}) %collective-permute-start.3) | collective-permute-done | bytes 65568 | tf_op jit(solution)/shard_map/ppermute | solution.py:269
  17.7 0.0 collective-permute-start.7
  17.7 1.8 %collective-permute-done.4 = bf16[16,2048]{1,0:T(8,128)(2,1)S(1)} collective-permute-done((bf16[16,2048]{1,0:T(8,128)(2,1)S(1)}, bf16[16,2048]{1,0:T(8,128)(2,1)S(1)}, u32[]{:S(2)}, u32[]{:S(2)}) %collective-permute-start.4) | collective-permute-done | bytes 65568 | tf_op jit(solution)/shard_map/ppermute | solution.py:269
  19.5 0.3 collective-permute-done.5
  19.8 0.3 collective-permute-done.6
  20.1 1.5 %collective-permute-start.11 = (bf16[64,2048]{1,0:T(8,128)(2,1)S(1)}, bf16[64,2048]{1,0:T(8,128)(2,1)S(1)}, u32[]{:S(2)}, u32[]{:S(2)}) collective-permute-start(bf16[64,2048]{1,0:T(8,128)(2,1)S(1)} %constant_dynamic-update-slice_fusion.4.refs_1_), channel_id=1, source_target_pairs={{0,16},{8,24},{16,0},{24,8},{1,17},{9,25},{17,1},{25,9},{2,18},{10... | collective-permute-start | bytes 786440 | tf_op jit(solution)/shard_map/ppermute | solution.py:278
  21.6 0.0 collective-permute-start.8
  21.6 0.0 copy-done
  21.6 0.0 copy-done.1
  21.6 4.3 %shard_map.94 = (bf16[128,2048]{1,0:T(8,128)(2,1)}, bf16[128,512]{1,0:T(8,128)(2,1)}, bf16[128,1152]{1,0:T(8,128)(2,1)}) custom-call(bf16[64,2048]{1,0:T(8,128)(2,1)S(1)} %constant_dynamic-update-slice_fusion.refs_0_, bf16[64,2048]{1,0:T(8,128)(2,1)S(1)} %constant_dynamic-update-slice_fusion.4.refs_1_, bf16[1024,2048]{1,0:T(8,128)(2,1)S(1)} %bitcast.10, ...), custom_call_target="tpu_custom_call" | custom-call | flops 10737418240 | bytes 8912896 | tf_op jit(solution)/shard_map/pallas_call | solution.py:35
  25.9 0.0 collective-permute-done.7.refs_0_.refs_2_
  25.9 0.0 collective-permute-done.8.refs_1_.refs_3_
  25.9 5.1 %all-to-all-start = ((bf16[8,16,1152]{2,1,0:T(8,128)(2,1)}), bf16[8,16,1152]{2,1,0:T(8,128)(2,1)S(1)}, u32[]{:S(2)}, u32[]{:S(2)}) async-start(bf16[8,16,1152]{2,1,0:T(8,128)(2,1)} %bitcast.16), calls=%async_computation | async-start | bytes 589824 | tf_op jit(solution)/shard_map/all_to_all | solution.py:353
  31.1 0.0 collective-permute-done.9.refs_2_.refs_4_
  31.1 0.3 collective-permute-start.10
  31.4 0.0 collective-permute-done.11.refs_6_
  31.4 0.3 collective-permute-start.12
  31.7 4.9 %shard_map.95 = (bf16[1024,2048]{1,0:T(8,128)(2,1)S(1)}, bf16[2048,1024]{1,0:T(8,128)(2,1)S(1)}, bf16[192,2048]{1,0:T(8,128)(2,1)S(1)}, bf16[192,512]{1,0:T(8,128)(2,1)S(1)}) custom-call(bf16[64,2048]{1,0:T(8,128)(2,1)S(1)} %collective-permute-done.7.refs_0_.refs_2_, bf16[64,2048]{1,0:T(8,128)(2,1)S(1)} %collective-permute-done.8.refs_1_.refs_3_, ...), custom_call_target="tpu_custom_call" | custom-call | flops 1073741824 | bytes 9175040 | tf_op jit(solution)/shard_map/pallas_call | solution.py:35
  36.6 0.0 collective-permute-done.10.refs_5_
  36.6 0.0 collective-permute-done.12.refs_7_
  36.6 0.0 copy-start.2
  36.6 5.1 %shard_map.96 = (bf16[256,2048]{1,0:T(8,128)(2,1)}, bf16[512,1024]{1,0:T(8,128)(2,1)}) custom-call(bf16[64,2048]{1,0:T(8,128)(2,1)S(1)} %constant_dynamic-update-slice_fusion.refs_0_, bf16[64,2048]{1,0:T(8,128)(2,1)S(1)} %constant_dynamic-update-slice_fusion.4.refs_1_, bf16[64,2048]{1,0:T(8,128)(2,1)S(1)} %collective-permute-done.7.refs_0_.refs_2_, ...), custom_call_target="tpu_custom_call" | custom-call | flops 2147483648 | bytes 12124160 | tf_op jit(solution)/shard_map/pallas_call | solution.py:35
  41.8 0.0 all-to-all-done
  41.8 0.0 copy-done.2
  41.8 0.9 %shard_map.97 = (bf16[64,1024]{1,0:T(8,128)(2,1)}, bf16[2,64]{1,0:T(2,128)(2,1)}) custom-call(bf16[128,64]{1,0:T(8,128)(2,1)S(1)} %get-tuple-element.31.place0, bf16[128,64]{1,0:T(8,128)(2,1)S(1)} %get-tuple-element.32.place1, bf16[2,64]{1,0:T(2,128)(2,1)S(1)} %bitcast.15, bf16[128,1152]{1,0:T(8,128)(2,1)S(1)} %bitcast.13), custom_call_target="tpu_custom_call" | custom-call | bytes 327936 | tf_op jit(solution)/shard_map/pallas_call | solution.py:35
  (8 shorter events, 0.0 us)
Async XLA Ops:
  0.6 21.0 %copy-start = (bf16[1,1024,2048]{2,1,0:T(8,128)(2,1)S(1)}, bf16[1,1024,2048]{2,1,0:T(8,128)(2,1)}, u32[]{:S(2)}) copy-start(bf16[1,1024,2048]{2,1,0:T(8,128)(2,1)} %param.10) | copy-start | bytes 12582916
  0.6 21.0 %copy-start.1 = (bf16[1,2048,1024]{2,1,0:T(8,128)(2,1)S(1)}, bf16[1,2048,1024]{2,1,0:T(8,128)(2,1)}, u32[]{:S(2)}) copy-start(bf16[1,2048,1024]{2,1,0:T(8,128)(2,1)} %param.11) | copy-start | bytes 12582916
  2.2 12.0 %collective-permute-start = (bf16[16,2048]{1,0:T(8,128)(2,1)S(1)}, bf16[16,2048]{1,0:T(8,128)(2,1)S(1)}, u32[]{:S(2)}, u32[]{:S(2)}) collective-permute-start(bf16[16,2048]{1,0:T(8,128)(2,1)S(1)} %get-tuple-element.34), channel_id=1, source_target_pairs={{0,7},{1,6},{2,5},{3,4},{4,3},{5,2},{6,1},{7,0},{8,15},{9,14},{10,... | collective-permute-start | bytes 196616 | tf_op jit(solution)/shard_map/ppermute | solution.py:269
  8.3 6.6 %collective-permute-start.1 = (bf16[16,2048]{1,0:T(8,128)(2,1)S(1)}, bf16[16,2048]{1,0:T(8,128)(2,1)S(1)}, u32[]{:S(2)}, u32[]{:S(2)}) collective-permute-start(bf16[16,2048]{1,0:T(8,128)(2,1)S(1)} %get-tuple-element.35), channel_id=1, source_target_pairs={{0,6},{1,7},{2,4},{3,5},{4,2},{5,3},{6,0},{7,1},{8,14},{9,15},{10,... | collective-permute-start | bytes 196616 | tf_op jit(solution)/shard_map/ppermute | solution.py:269
  8.5 4.4 %collective-permute-start.2 = (bf16[16,2048]{1,0:T(8,128)(2,1)S(1)}, bf16[16,2048]{1,0:T(8,128)(2,1)S(1)}, u32[]{:S(2)}, u32[]{:S(2)}) collective-permute-start(bf16[16,2048]{1,0:T(8,128)(2,1)S(1)} %get-tuple-element.36), channel_id=1, source_target_pairs={{0,1},{1,0},{2,3},{3,2},{4,5},{5,4},{6,7},{7,6},{8,9},{9,8},{10,11... | collective-permute-start | bytes 196616 | tf_op jit(solution)/shard_map/ppermute | solution.py:269
  8.9 8.8 %collective-permute-start.3 = (bf16[16,2048]{1,0:T(8,128)(2,1)S(1)}, bf16[16,2048]{1,0:T(8,128)(2,1)S(1)}, u32[]{:S(2)}, u32[]{:S(2)}) collective-permute-start(bf16[16,2048]{1,0:T(8,128)(2,1)S(1)} %get-tuple-element.37), channel_id=1, source_target_pairs={{0,5},{1,4},{2,7},{3,6},{4,1},{5,0},{6,3},{7,2},{8,13},{9,12},{10,... | collective-permute-start | bytes 196616 | tf_op jit(solution)/shard_map/ppermute | solution.py:269
  10.7 8.8 %collective-permute-start.4 = (bf16[16,2048]{1,0:T(8,128)(2,1)S(1)}, bf16[16,2048]{1,0:T(8,128)(2,1)S(1)}, u32[]{:S(2)}, u32[]{:S(2)}) collective-permute-start(bf16[16,2048]{1,0:T(8,128)(2,1)S(1)} %get-tuple-element.38), channel_id=1, source_target_pairs={{0,4},{1,5},{2,6},{3,7},{4,0},{5,1},{6,2},{7,3},{8,12},{9,13},{10,... | collective-permute-start | bytes 196616 | tf_op jit(solution)/shard_map/ppermute | solution.py:269
  12.9 6.9 %collective-permute-start.5 = (bf16[16,2048]{1,0:T(8,128)(2,1)S(1)}, bf16[16,2048]{1,0:T(8,128)(2,1)S(1)}, u32[]{:S(2)}, u32[]{:S(2)}) collective-permute-start(bf16[16,2048]{1,0:T(8,128)(2,1)S(1)} %get-tuple-element.40), channel_id=1, source_target_pairs={{0,3},{1,2},{2,1},{3,0},{4,7},{5,6},{6,5},{7,4},{8,11},{9,10},{10,... | collective-permute-start | bytes 196616 | tf_op jit(solution)/shard_map/ppermute | solution.py:269
  14.2 5.9 %collective-permute-start.6 = (bf16[16,2048]{1,0:T(8,128)(2,1)S(1)}, bf16[16,2048]{1,0:T(8,128)(2,1)S(1)}, u32[]{:S(2)}, u32[]{:S(2)}) collective-permute-start(bf16[16,2048]{1,0:T(8,128)(2,1)S(1)} %get-tuple-element.42), channel_id=1, source_target_pairs={{0,2},{1,3},{2,0},{3,1},{4,6},{5,7},{6,4},{7,5},{8,10},{9,11},{10,... | collective-permute-start | bytes 196616 | tf_op jit(solution)/shard_map/ppermute | solution.py:269
  14.9 16.2 %collective-permute-start.9 = (bf16[64,2048]{1,0:T(8,128)(2,1)S(1)}, bf16[64,2048]{1,0:T(8,128)(2,1)S(1)}, u32[]{:S(2)}, u32[]{:S(2)}) collective-permute-start(bf16[64,2048]{1,0:T(8,128)(2,1)S(1)} %constant_dynamic-update-slice_fusion.refs_0_), channel_id=1, source_target_pairs={{0,16},{8,24},{16,0},{24,8},{1,17},{9,25},{17,1},{25,9},{2,18},{10... | collective-permute-start | bytes 786440 | tf_op jit(solution)/shard_map/ppermute | solution.py:278
  17.7 8.2 %collective-permute-start.7 = (bf16[64,2048]{1,0:T(8,128)(2,1)S(1)}, bf16[64,2048]{1,0:T(8,128)(2,1)S(1)}, u32[]{:S(2)}, u32[]{:S(2)}) collective-permute-start(bf16[64,2048]{1,0:T(8,128)(2,1)S(1)} %constant_dynamic-update-slice_fusion.refs_0_), channel_id=1, source_target_pairs={{0,8},{8,0},{16,24},{24,16},{1,9},{9,1},{17,25},{25,17},{2,10},{10... | collective-permute-start | bytes 786440 | tf_op jit(solution)/shard_map/ppermute | solution.py:273
  20.1 11.3 %collective-permute-start.11 = (bf16[64,2048]{1,0:T(8,128)(2,1)S(1)}, bf16[64,2048]{1,0:T(8,128)(2,1)S(1)}, u32[]{:S(2)}, u32[]{:S(2)}) collective-permute-start(bf16[64,2048]{1,0:T(8,128)(2,1)S(1)} %constant_dynamic-update-slice_fusion.4.refs_1_), channel_id=1, source_target_pairs={{0,16},{8,24},{16,0},{24,8},{1,17},{9,25},{17,1},{25,9},{2,18},{10... | collective-permute-start | bytes 786440 | tf_op jit(solution)/shard_map/ppermute | solution.py:278
  21.6 4.3 %collective-permute-start.8 = (bf16[64,2048]{1,0:T(8,128)(2,1)S(1)}, bf16[64,2048]{1,0:T(8,128)(2,1)S(1)}, u32[]{:S(2)}, u32[]{:S(2)}) collective-permute-start(bf16[64,2048]{1,0:T(8,128)(2,1)S(1)} %constant_dynamic-update-slice_fusion.4.refs_1_), channel_id=1, source_target_pairs={{0,8},{8,0},{16,24},{24,16},{1,9},{9,1},{17,25},{25,17},{2,10},{10... | collective-permute-start | bytes 786440 | tf_op jit(solution)/shard_map/ppermute | solution.py:273
  25.9 15.8 %all-to-all-start = ((bf16[8,16,1152]{2,1,0:T(8,128)(2,1)}), bf16[8,16,1152]{2,1,0:T(8,128)(2,1)S(1)}, u32[]{:S(2)}, u32[]{:S(2)}) async-start(bf16[8,16,1152]{2,1,0:T(8,128)(2,1)} %bitcast.16), calls=%async_computation | async-start | bytes 589824 | tf_op jit(solution)/shard_map/all_to_all | solution.py:353
  31.1 5.5 %collective-permute-start.10 = (bf16[64,2048]{1,0:T(8,128)(2,1)S(1)}, bf16[64,2048]{1,0:T(8,128)(2,1)S(1)}, u32[]{:S(2)}, u32[]{:S(2)}) collective-permute-start(bf16[64,2048]{1,0:T(8,128)(2,1)S(1)} %collective-permute-done.9.refs_2_.refs_4_), channel_id=1, source_target_pairs={{0,8},{8,0},{16,24},{24,16},{1,9},{9,1},{17,25},{25,17},{2,10},{10... | collective-permute-start | bytes 786440 | tf_op jit(solution)/shard_map/ppermute | solution.py:273
  31.4 5.2 %collective-permute-start.12 = (bf16[64,2048]{1,0:T(8,128)(2,1)S(1)}, bf16[64,2048]{1,0:T(8,128)(2,1)S(1)}, u32[]{:S(2)}, u32[]{:S(2)}) collective-permute-start(bf16[64,2048]{1,0:T(8,128)(2,1)S(1)} %collective-permute-done.11.refs_6_), channel_id=1, source_target_pairs={{0,8},{8,0},{16,24},{24,16},{1,9},{9,1},{17,25},{25,17},{2,10},{10... | collective-permute-start | bytes 786440 | tf_op jit(solution)/shard_map/ppermute | solution.py:273
  36.6 5.2 %copy-start.2 = (bf16[64,2]{0,1:T(2,128)(2,1)S(1)}, bf16[64,2]{0,1:T(2,128)(2,1)}, u32[]{:S(2)}) copy-start(bf16[64,2]{0,1:T(2,128)(2,1)} %param.9) | copy-start | bytes 772

commit v13 on v10

--- a/solution.py
+++ b/solution.py
@@ -185,13 +185,27 @@
 
 
 def early_kernel(tile, pieces, *refs):
+    row_refs, (weight_in, weight_out, d_pre, h_cut, hidden) = refs[:pieces], refs[pieces:]
+    width, ffw = weight_in.shape
+    x, s = stack(row_refs, 0, width), stack(row_refs, 1, width)
+    for at in range(0, ffw, tile):
+        cols = slice(at, at + tile)
+        act, slope = activate(dot(x, weight_in[:, cols]))
+        hidden[:, cols] = act
+        d_pre[:, cols] = (dot(s, weight_out[cols, :], (1, 1)) * slope).astype(BF16)
+    h_cut[...] = my_part(hidden)
+
+
+def grads_kernel(tile, pieces, late, *refs):
     row_refs, refs = refs[:pieces], refs[pieces:]
-    in_hbm, out_hbm, weight_in, weight_out, d_pre, h_cut, rows, hidden, sems = refs
+    d_pre_refs, h_cut_refs, refs = refs[:2], refs[2:4], refs[4:]
+    in_hbm, out_hbm, grad_in_hbm, grad_out_hbm, weight_in, weight_out, *scratch = refs
+    rows, hidden, h_cut, d_pre, grad_in, grad_out, sems, out_sems = scratch
     width, ffw = weight_in.shape
+    tiles = [slice(at, at + tile) for at in range(0, ffw, tile)]
     piece = row_refs[0].shape[0]
-    tiles = [slice(at, at + tile) for at in range(0, ffw, tile)]
-    fetch = fetcher(sems)
-    first = [fetch(ref, rows.at[pl.ds(i * piece, piece)]) for i, ref in enumerate(row_refs)]
+    known = (pieces - late) * piece
+    fetch, send = fetcher(sems), fetcher(out_sems)
     weights = [
         (
             fetch(in_hbm.at[:, cols], weight_in.at[:, cols]),
@@ -199,28 +213,6 @@
         )
         for cols in tiles
     ]
-    for copy in first:
-        copy.wait()
-    x, s = rows[:, :width], rows[:, width:]
-    for cols, (copy_in, copy_out) in zip(tiles, weights):
-        copy_in.wait()
-        copy_out.wait()
-        act, slope = activate(dot(x, weight_in[:, cols]))
-        hidden[:, cols] = act
-        d_pre[:, cols] = (dot(s, weight_out[cols, :], (1, 1)) * slope).astype(BF16)
-    h_cut[...] = my_part(hidden)
-
-
-def grads_kernel(tile, pieces, late, *refs):
-    row_refs, refs = refs[:pieces], refs[pieces:]
-    d_pre_refs, h_cut_refs, refs = refs[:2], refs[2:4], refs[4:]
-    weight_in, weight_out, grad_in_hbm, grad_out_hbm, *scratch = refs
-    rows, hidden, h_cut, d_pre, grad_in, grad_out, sems, out_sems = scratch
-    width, ffw = weight_in.shape
-    tiles = [slice(at, at + tile) for at in range(0, ffw, tile)]
-    piece = row_refs[0].shape[0]
-    known = (pieces - late) * piece
-    fetch, send = fetcher(sems), fetcher(out_sems)
     copies = [
         fetch(row_refs[i], rows.at[pl.ds(i * piece, piece)])
         for i in [*range(pieces - late, pieces), *range(pieces - late)]
@@ -231,7 +223,9 @@
         copies += [fetch(source, d_pre.at[span]), fetch(cut_source, h_cut.at[span])]
         at += source.shape[0]
     x, s = stack(row_refs[-late:], 0, width), stack(row_refs[-late:], 1, width)
-    for cols in tiles:
+    for cols, pair in zip(tiles, weights):
+        for copy in pair:
+            copy.wait()
         act, slope = activate(dot(x, weight_in[:, cols]))
         hidden[:, cols] = act
         d_pre[known:, cols] = (dot(s, weight_out[cols, :], (1, 1)) * slope).astype(BF16)
@@ -320,7 +314,7 @@
     chips_b = [shift_chips(rows_b, k) for k in range(1, groups // 2)]
     core_b = swap_cores(rows_b)
     weights = [proj_in[0], proj_out[0]]
-    weight_space = [pltpu.VMEM((feat_width, ffw), BF16), pltpu.VMEM((ffw, feat_width), BF16)]
+    near_weights = [pltpu.with_memory_space_constraint(w, pltpu.VMEM) for w in weights]
     d_pre, h_cut, back = call(
         functools.partial(own_kernel, tile, order),
         [
@@ -328,11 +322,7 @@
             pltpu.HBM((slots_all, tile), BF16),
             pltpu.HBM((slots_all, feat_width + LANES), BF16),
         ],
-        [
-            rows_a,
-            rows_b,
-            *[pltpu.with_memory_space_constraint(w, pltpu.VMEM) for w in weights],
-        ],
+        [rows_a, rows_b, *near_weights],
         20 * product,
         scratch=[
             pltpu.VMEM((slots_all, ffw), BF16),
@@ -342,31 +332,26 @@
             pltpu.SemaphoreType.DMA((7,)),
         ],
     )
+    early = [after(rows, d_pre) for rows in [core_a, core_b, *chips_a]]
+    early_rows = sum(piece.shape[0] for piece in early)
+    d_pre_early, h_cut_early = call(
+        functools.partial(early_kernel, tile, len(early)),
+        [shape((early_rows, ffw)), shape((early_rows, tile))],
+        [*early, *near_weights],
+        2 * product,
+        scratch=[pltpu.VMEM((early_rows, ffw), BF16)],
+    )
     back = lax.all_to_all(
-        after(back, core_a, core_b).reshape(experts, capacity, feat_width + LANES),
+        after(back, d_pre_early).reshape(experts, capacity, feat_width + LANES),
         "expert",
         0,
         0,
         tiled=True,
     ).reshape(slots_all, feat_width + LANES)
     relayed_a = [swap_cores(after(rows, d_pre)) for rows in chips_a]
-    relayed_b = [swap_cores(rows) for rows in chips_b]
-    early = [core_a, core_b, *chips_a]
+    relayed_b = [swap_cores(after(rows, d_pre_early)) for rows in chips_b]
     late = [*relayed_a, *chips_b, *relayed_b]
-    early_rows = sum(piece.shape[0] for piece in early)
     late_rows = sum(piece.shape[0] for piece in late)
-    weight_in, weight_out, d_pre_early, h_cut_early = call(
-        functools.partial(early_kernel, tile, len(early)),
-        [*weight_space, shape((early_rows, ffw)), shape((early_rows, tile))],
-        [*early, *weights],
-        2 * product,
-        scratch=[
-            pltpu.VMEM((early_rows, 2 * feat_width), BF16),
-            pltpu.VMEM((early_rows, ffw), BF16),
-            pltpu.SemaphoreType.DMA((len(early) + 2 * groups,)),
-        ],
-        spaces=[pl.ANY] * len(early) + [pltpu.HBM] * 2,
-    )
     pieces = [rows_a, rows_b, *early, *late]
     rows_all = groups * slots_all
     grad_in, grad_out = call(
@@ -375,30 +360,25 @@
             pltpu.HBM((feat_width // groups, ffw), BF16),
             pltpu.HBM((ffw // groups, feat_width), BF16),
         ],
-        [
-            *pieces,
-            *[d_pre, d_pre_early, h_cut, h_cut_early],
-            *[
-                pltpu.with_memory_space_constraint(w, pltpu.VMEM)
-                for w in (weight_in, weight_out)
-            ],
-        ],
+        [*pieces, *[d_pre, d_pre_early, h_cut, h_cut_early], *weights],
         4 * product,
-        limit=32,
+        limit=36,
         scratch=[
+            pltpu.VMEM((feat_width, ffw), BF16),
+            pltpu.VMEM((ffw, feat_width), BF16),
             pltpu.VMEM((rows_all, 2 * feat_width), BF16),
             pltpu.VMEM((late_rows, ffw), BF16),
             pltpu.VMEM((rows_all, tile), BF16),
             pltpu.VMEM((rows_all, ffw), BF16),
             pltpu.VMEM((feat_width // groups, ffw), BF16),
             pltpu.VMEM((ffw // groups, feat_width), BF16),
-            pltpu.SemaphoreType.DMA((len(pieces) + 4,)),
+            pltpu.SemaphoreType.DMA((len(pieces) + 4 + 2 * groups,)),
             pltpu.SemaphoreType.DMA((4,)),
         ],
         spaces=[pl.ANY] * (len(pieces) - len(late))
         + [pltpu.VMEM] * len(late)
         + [pltpu.HBM, pl.ANY] * 2
-        + [pltpu.VMEM] * 2,
+        + [pltpu.HBM] * 2,
     )
     token_grads, gate_grads = call(
         functools.partial(combine_kernel, experts, capacity),

time: 42.7 us -> 44.9 us (1.052)
  waiting for transfers between devices: 3.54 us -> 6.41 us
  Pallas kernels: 16.6 us -> 16 us
    all_to_all x1, waiting for transfers between devices: 0.01 us -> 1.49 us  [local(): lax.all_to_all(after(back, d_pre_early).reshape(experts, capacity, feat_w...]
    ppermute x4, waiting for transfers between devices: 0.01 us -> 1.4 us  [swap_cores(): lax.ppermute(rows, 'dp', [(i, i ^ 1) for i in range(lax.axis_size('dp'))])]
    pallas_call x5, Pallas kernels: 16.6 us -> 16 us  [call(): pl.pallas_call(kernel, out_shape=out_shape, in_specs=[pl.BlockSpec(memory...]
  transfers between devices with their start and end apart: 14 -> 14, of which waited for: 4 -> 7; matrix products, arithmetic and copies ran while one was open for 0% -> 0% of each run, Pallas kernels for 33% -> 30%
where the time goes in v13:
time: 44.9 us; the launch traced here: 44.7 us
  starting transfers between devices  21.5 us (48%)
  Pallas kernels  16 us (36%)
  waiting for transfers between devices  6.41 us (14%)
  between operations  0.75 us (2%)
    pallas_call x5, Pallas kernels, call(): pl.pallas_call(kernel, out_shape=out_shape, in_specs=[pl.BlockSpec(memory...  16 us
    ppermute x7, starting transfers between devices, permute(): lax.ppermute(block, 'expert', [(i, i ^ k) for i in range(lax.axis_size('e...  12.6 us
    all_to_all x1, starting transfers between devices, local(): lax.all_to_all(after(back, d_pre_early).reshape(experts, capacity, feat_w...  5.13 us
    ppermute x7, waiting for transfers between devices, permute(): lax.ppermute(block, 'expert', [(i, i ^ k) for i in range(lax.axis_size('e...  3.52 us
    ppermute x2, starting transfers between devices, shift_chips(): lax.ppermute(rows, 'dp', [(i, (i + 2 * k) % groups) for i in range(groups)])  3.22 us
    all_to_all x1, waiting for transfers between devices, local(): lax.all_to_all(after(back, d_pre_early).reshape(experts, capacity, feat_w...  1.49 us
    ppermute x4, waiting for transfers between devices, swap_cores(): lax.ppermute(rows, 'dp', [(i, i ^ 1) for i in range(lax.axis_size('dp'))])  1.4 us
  transfers between devices with their start and end apart: 14, of which 7 were waited for; matrix products, arithmetic and copies ran while one was open for 0% of the time, Pallas kernels for 30%

profile of v13, /device:TPU:0, one launch (start us, length us, event | category | flops | bytes accessed | tf_op | source)
XLA Modules:
  0.0 44.7 jit_solution(17777533084820536451)
XLA Ops:
  0.6 0.0 copy-start
  0.6 0.0 copy-start.1
  0.7 1.6 %shard_map.93 = (bf16[16,2048]{1,0:T(8,128)(2,1)S(1)}, bf16[16,2048]{1,0:T(8,128)(2,1)S(1)}, bf16[16,2048]{1,0:T(8,128)(2,1)S(1)}, bf16[16,2048]{1,0:T(8,128)(2,...) custom-call(s32[2,64]{1,0:T(2,128)} %bitcast.20, ...), custom_call_target="tpu_custom_call" | custom-call | flops 16106127360 | bytes 262912 | tf_op jit(solution)/shard_map/pallas_call | solution.py:35
  2.2 6.0 %collective-permute-start = (bf16[16,2048]{1,0:T(8,128)(2,1)S(1)}, bf16[16,2048]{1,0:T(8,128)(2,1)S(1)}, u32[]{:S(2)}, u32[]{:S(2)}) collective-permute-start(bf16[16,2048]{1,0:T(8,128)(2,1)S(1)} %get-tuple-element.35), channel_id=1, source_target_pairs={{0,7},{1,6},{2,5},{3,4},{4,3},{5,2},{6,1},{7,0},{8,15},{9,14},{10,... | collective-permute-start | bytes 196616 | tf_op jit(solution)/shard_map/ppermute | solution.py:255
  8.3 0.2 collective-permute-start.1
  8.5 0.4 collective-permute-start.2
  8.9 1.8 %collective-permute-start.3 = (bf16[16,2048]{1,0:T(8,128)(2,1)S(1)}, bf16[16,2048]{1,0:T(8,128)(2,1)S(1)}, u32[]{:S(2)}, u32[]{:S(2)}) collective-permute-start(bf16[16,2048]{1,0:T(8,128)(2,1)S(1)} %get-tuple-element.38), channel_id=1, source_target_pairs={{0,5},{1,4},{2,7},{3,6},{4,1},{5,0},{6,3},{7,2},{8,13},{9,12},{10,... | collective-permute-start | bytes 196616 | tf_op jit(solution)/shard_map/ppermute | solution.py:255
  10.7 2.1 %collective-permute-start.4 = (bf16[16,2048]{1,0:T(8,128)(2,1)S(1)}, bf16[16,2048]{1,0:T(8,128)(2,1)S(1)}, u32[]{:S(2)}, u32[]{:S(2)}) collective-permute-start(bf16[16,2048]{1,0:T(8,128)(2,1)S(1)} %get-tuple-element.39), channel_id=1, source_target_pairs={{0,4},{1,5},{2,6},{3,7},{4,0},{5,1},{6,2},{7,3},{8,12},{9,13},{10,... | collective-permute-start | bytes 196616 | tf_op jit(solution)/shard_map/ppermute | solution.py:255
  12.9 0.0 collective-permute-done.2
  12.9 1.3 %collective-permute-start.5 = (bf16[16,2048]{1,0:T(8,128)(2,1)S(1)}, bf16[16,2048]{1,0:T(8,128)(2,1)S(1)}, u32[]{:S(2)}, u32[]{:S(2)}) collective-permute-start(bf16[16,2048]{1,0:T(8,128)(2,1)S(1)} %get-tuple-element.41), channel_id=1, source_target_pairs={{0,3},{1,2},{2,1},{3,0},{4,7},{5,6},{6,5},{7,4},{8,11},{9,10},{10,... | collective-permute-start | bytes 196616 | tf_op jit(solution)/shard_map/ppermute | solution.py:255
  14.2 0.0 collective-permute-done
  14.2 0.6 %collective-permute-start.6 = (bf16[16,2048]{1,0:T(8,128)(2,1)S(1)}, bf16[16,2048]{1,0:T(8,128)(2,1)S(1)}, u32[]{:S(2)}, u32[]{:S(2)}) collective-permute-start(bf16[16,2048]{1,0:T(8,128)(2,1)S(1)} %get-tuple-element.43), channel_id=1, source_target_pairs={{0,2},{1,3},{2,0},{3,1},{4,6},{5,7},{6,4},{7,5},{8,10},{9,11},{10,... | collective-permute-start | bytes 196616 | tf_op jit(solution)/shard_map/ppermute | solution.py:255
  14.8 0.0 collective-permute-done.1
  14.9 1.7 %collective-permute-start.9 = (bf16[64,2048]{1,0:T(8,128)(2,1)S(1)}, bf16[64,2048]{1,0:T(8,128)(2,1)S(1)}, u32[]{:S(2)}, u32[]{:S(2)}) collective-permute-start(bf16[64,2048]{1,0:T(8,128)(2,1)S(1)} %constant_dynamic-update-slice_fusion.refs_0_), channel_id=1, source_target_pairs={{0,16},{8,24},{16,0},{24,8},{1,17},{9,25},{17,1},{25,9},{2,18},{10... | collective-permute-start | bytes 786440 | tf_op jit(solution)/shard_map/ppermute | solution.py:264
  16.6 1.1 %collective-permute-done.3 = bf16[16,2048]{1,0:T(8,128)(2,1)S(1)} collective-permute-done((bf16[16,2048]{1,0:T(8,128)(2,1)S(1)}, bf16[16,2048]{1,0:T(8,128)(2,1)S(1)}, u32[]{:S(2)}, u32[]{:S(2)}) %collective-permute-start.3) | collective-permute-done | bytes 65568 | tf_op jit(solution)/shard_map/ppermute | solution.py:255
  17.7 0.0 collective-permute-start.7
  17.7 1.8 %collective-permute-done.4 = bf16[16,2048]{1,0:T(8,128)(2,1)S(1)} collective-permute-done((bf16[16,2048]{1,0:T(8,128)(2,1)S(1)}, bf16[16,2048]{1,0:T(8,128)(2,1)S(1)}, u32[]{:S(2)}, u32[]{:S(2)}) %collective-permute-start.4) | collective-permute-done | bytes 65568 | tf_op jit(solution)/shard_map/ppermute | solution.py:255
  19.5 0.3 collective-permute-done.5
  19.8 0.3 collective-permute-done.6
  20.1 1.5 %collective-permute-start.11 = (bf16[64,2048]{1,0:T(8,128)(2,1)S(1)}, bf16[64,2048]{1,0:T(8,128)(2,1)S(1)}, u32[]{:S(2)}, u32[]{:S(2)}) collective-permute-start(bf16[64,2048]{1,0:T(8,128)(2,1)S(1)} %constant_dynamic-update-slice_fusion.4.refs_1_), channel_id=1, source_target_pairs={{0,16},{8,24},{16,0},{24,8},{1,17},{9,25},{17,1},{25,9},{2,18},{10... | collective-permute-start | bytes 786440 | tf_op jit(solution)/shard_map/ppermute | solution.py:264
  21.6 0.0 collective-permute-start.8
  21.6 0.0 copy-done
  21.6 0.0 copy-done.1
  21.6 4.3 %shard_map.94 = (bf16[128,2048]{1,0:T(8,128)(2,1)}, bf16[128,512]{1,0:T(8,128)(2,1)}, bf16[128,1152]{1,0:T(8,128)(2,1)}) custom-call(bf16[64,2048]{1,0:T(8,128)(2,1)S(1)} %constant_dynamic-update-slice_fusion.refs_0_, bf16[64,2048]{1,0:T(8,128)(2,1)S(1)} %constant_dynamic-update-slice_fusion.4.refs_1_, bf16[1024,2048]{1,0:T(8,128)(2,1)S(1)} %bitcast.10, ...), custom_call_target="tpu_custom_call" | custom-call | flops 10737418240 | bytes 8912896 | tf_op jit(solution)/shard_map/pallas_call | solution.py:35
  25.9 0.0 collective-permute-done.9.refs_2_.refs_4_
  25.9 0.0 collective-permute-done.7.refs_0_.refs_2_
  26.0 0.0 collective-permute-done.8.refs_1_.refs_3_
  26.0 2.4 %shard_map.95 = (bf16[192,2048]{1,0:T(8,128)(2,1)S(1)}, bf16[192,512]{1,0:T(8,128)(2,1)S(1)}) custom-call(bf16[64,2048]{1,0:T(8,128)(2,1)S(1)} %collective-permute-done.7.refs_0_.refs_2_, bf16[64,2048]{1,0:T(8,128)(2,1)S(1)} %collective-permute-done.8.refs_1_.refs_3_, bf16[64,2048]{1,0:T(8,128)(2,1)S(1)} %collective-permute-done.9.refs_2_.refs_4_, ...), custom_call_target="tpu_custom_call" | custom-call | flops 1073741824 | bytes 9175040 | tf_op jit(solution)/shard_map/pallas_call | solution.py:35
  28.4 5.1 %all-to-all-start = ((bf16[8,16,1152]{2,1,0:T(8,128)(2,1)}), bf16[8,16,1152]{2,1,0:T(8,128)(2,1)S(1)}, u32[]{:S(2)}, u32[]{:S(2)}) async-start(bf16[8,16,1152]{2,1,0:T(8,128)(2,1)} %bitcast.4), calls=%async_computation | async-start | bytes 589824 | tf_op jit(solution)/shard_map/all_to_all | solution.py:344
  33.5 0.2 collective-permute-start.10
  33.8 0.0 collective-permute-done.11.refs_6_
  33.8 0.3 collective-permute-start.12
  34.1 1.0 %collective-permute-done.10.refs_5_ = bf16[64,2048]{1,0:T(8,128)(2,1)S(1)} collective-permute-done((bf16[64,2048]{1,0:T(8,128)(2,1)S(1)}, bf16[64,2048]{1,0:T(8,128)(2,1)S(1)}, u32[]{:S(2)}, u32[]{:S(2)}) %collective-permute-start.10) | collective-permute-done | bytes 262176 | tf_op jit(solution)/shard_map/ppermute | solution.py:259
  35.1 0.4 collective-permute-done.12.refs_7_
  35.5 0.0 copy-start.2
  35.5 6.8 %shard_map.96 = (bf16[256,2048]{1,0:T(8,128)(2,1)}, bf16[512,1024]{1,0:T(8,128)(2,1)}) custom-call(bf16[64,2048]{1,0:T(8,128)(2,1)S(1)} %constant_dynamic-update-slice_fusion.refs_0_, bf16[64,2048]{1,0:T(8,128)(2,1)S(1)} %constant_dynamic-update-slice_fusion.4.refs_1_, bf16[64,2048]{1,0:T(8,128)(2,1)S(1)} %collective-permute-done.7.refs_0_.refs_2_, ...), custom_call_target="tpu_custom_call" | custom-call | flops 2147483648 | bytes 12124160 | tf_op jit(solution)/shard_map/pallas_call | solution.py:35
  42.3 1.5 %all-to-all-done = bf16[8,16,1152]{2,1,0:T(8,128)(2,1)S(1)} async-done(((bf16[8,16,1152]{2,1,0:T(8,128)(2,1)}), bf16[8,16,1152]{2,1,0:T(8,128)(2,1)S(1)}, u32[]{:S(2)}, u32[]{:S(2)}) %all-to-all-start) | async-done | bytes 294944 | tf_op jit(solution)/shard_map/all_to_all | solution.py:344
  43.8 0.0 copy-done.2
  43.8 0.9 %shard_map.97 = (bf16[64,1024]{1,0:T(8,128)(2,1)}, bf16[2,64]{1,0:T(2,128)(2,1)}) custom-call(bf16[128,64]{1,0:T(8,128)(2,1)S(1)} %get-tuple-element.32.place0, bf16[128,64]{1,0:T(8,128)(2,1)S(1)} %get-tuple-element.33.place1, bf16[2,64]{1,0:T(2,128)(2,1)S(1)} %bitcast.17, bf16[128,1152]{1,0:T(8,128)(2,1)S(1)} %bitcast.15), custom_call_target="tpu_custom_call" | custom-call | bytes 327936 | tf_op jit(solution)/shard_map/pallas_call | solution.py:35
  (8 shorter events, 0.0 us)
Async XLA Ops:
  0.6 21.0 %copy-start = (bf16[1,1024,2048]{2,1,0:T(8,128)(2,1)S(1)}, bf16[1,1024,2048]{2,1,0:T(8,128)(2,1)}, u32[]{:S(2)}) copy-start(bf16[1,1024,2048]{2,1,0:T(8,128)(2,1)} %param.10) | copy-start | bytes 12582916
  0.6 21.0 %copy-start.1 = (bf16[1,2048,1024]{2,1,0:T(8,128)(2,1)S(1)}, bf16[1,2048,1024]{2,1,0:T(8,128)(2,1)}, u32[]{:S(2)}) copy-start(bf16[1,2048,1024]{2,1,0:T(8,128)(2,1)} %param.11) | copy-start | bytes 12582916
  2.2 12.0 %collective-permute-start = (bf16[16,2048]{1,0:T(8,128)(2,1)S(1)}, bf16[16,2048]{1,0:T(8,128)(2,1)S(1)}, u32[]{:S(2)}, u32[]{:S(2)}) collective-permute-start(bf16[16,2048]{1,0:T(8,128)(2,1)S(1)} %get-tuple-element.35), channel_id=1, source_target_pairs={{0,7},{1,6},{2,5},{3,4},{4,3},{5,2},{6,1},{7,0},{8,15},{9,14},{10,... | collective-permute-start | bytes 196616 | tf_op jit(solution)/shard_map/ppermute | solution.py:255
  8.3 6.6 %collective-permute-start.1 = (bf16[16,2048]{1,0:T(8,128)(2,1)S(1)}, bf16[16,2048]{1,0:T(8,128)(2,1)S(1)}, u32[]{:S(2)}, u32[]{:S(2)}) collective-permute-start(bf16[16,2048]{1,0:T(8,128)(2,1)S(1)} %get-tuple-element.36), channel_id=1, source_target_pairs={{0,6},{1,7},{2,4},{3,5},{4,2},{5,3},{6,0},{7,1},{8,14},{9,15},{10,... | collective-permute-start | bytes 196616 | tf_op jit(solution)/shard_map/ppermute | solution.py:255
  8.5 4.4 %collective-permute-start.2 = (bf16[16,2048]{1,0:T(8,128)(2,1)S(1)}, bf16[16,2048]{1,0:T(8,128)(2,1)S(1)}, u32[]{:S(2)}, u32[]{:S(2)}) collective-permute-start(bf16[16,2048]{1,0:T(8,128)(2,1)S(1)} %get-tuple-element.37), channel_id=1, source_target_pairs={{0,1},{1,0},{2,3},{3,2},{4,5},{5,4},{6,7},{7,6},{8,9},{9,8},{10,11... | collective-permute-start | bytes 196616 | tf_op jit(solution)/shard_map/ppermute | solution.py:255
  8.9 8.8 %collective-permute-start.3 = (bf16[16,2048]{1,0:T(8,128)(2,1)S(1)}, bf16[16,2048]{1,0:T(8,128)(2,1)S(1)}, u32[]{:S(2)}, u32[]{:S(2)}) collective-permute-start(bf16[16,2048]{1,0:T(8,128)(2,1)S(1)} %get-tuple-element.38), channel_id=1, source_target_pairs={{0,5},{1,4},{2,7},{3,6},{4,1},{5,0},{6,3},{7,2},{8,13},{9,12},{10,... | collective-permute-start | bytes 196616 | tf_op jit(solution)/shard_map/ppermute | solution.py:255
  10.7 8.8 %collective-permute-start.4 = (bf16[16,2048]{1,0:T(8,128)(2,1)S(1)}, bf16[16,2048]{1,0:T(8,128)(2,1)S(1)}, u32[]{:S(2)}, u32[]{:S(2)}) collective-permute-start(bf16[16,2048]{1,0:T(8,128)(2,1)S(1)} %get-tuple-element.39), channel_id=1, source_target_pairs={{0,4},{1,5},{2,6},{3,7},{4,0},{5,1},{6,2},{7,3},{8,12},{9,13},{10,... | collective-permute-start | bytes 196616 | tf_op jit(solution)/shard_map/ppermute | solution.py:255
  12.9 6.9 %collective-permute-start.5 = (bf16[16,2048]{1,0:T(8,128)(2,1)S(1)}, bf16[16,2048]{1,0:T(8,128)(2,1)S(1)}, u32[]{:S(2)}, u32[]{:S(2)}) collective-permute-start(bf16[16,2048]{1,0:T(8,128)(2,1)S(1)} %get-tuple-element.41), channel_id=1, source_target_pairs={{0,3},{1,2},{2,1},{3,0},{4,7},{5,6},{6,5},{7,4},{8,11},{9,10},{10,... | collective-permute-start | bytes 196616 | tf_op jit(solution)/shard_map/ppermute | solution.py:255
  14.2 5.9 %collective-permute-start.6 = (bf16[16,2048]{1,0:T(8,128)(2,1)S(1)}, bf16[16,2048]{1,0:T(8,128)(2,1)S(1)}, u32[]{:S(2)}, u32[]{:S(2)}) collective-permute-start(bf16[16,2048]{1,0:T(8,128)(2,1)S(1)} %get-tuple-element.43), channel_id=1, source_target_pairs={{0,2},{1,3},{2,0},{3,1},{4,6},{5,7},{6,4},{7,5},{8,10},{9,11},{10,... | collective-permute-start | bytes 196616 | tf_op jit(solution)/shard_map/ppermute | solution.py:255
  14.9 11.1 %collective-permute-start.9 = (bf16[64,2048]{1,0:T(8,128)(2,1)S(1)}, bf16[64,2048]{1,0:T(8,128)(2,1)S(1)}, u32[]{:S(2)}, u32[]{:S(2)}) collective-permute-start(bf16[64,2048]{1,0:T(8,128)(2,1)S(1)} %constant_dynamic-update-slice_fusion.refs_0_), channel_id=1, source_target_pairs={{0,16},{8,24},{16,0},{24,8},{1,17},{9,25},{17,1},{25,9},{2,18},{10... | collective-permute-start | bytes 786440 | tf_op jit(solution)/shard_map/ppermute | solution.py:264
  17.7 8.3 %collective-permute-start.7 = (bf16[64,2048]{1,0:T(8,128)(2,1)S(1)}, bf16[64,2048]{1,0:T(8,128)(2,1)S(1)}, u32[]{:S(2)}, u32[]{:S(2)}) collective-permute-start(bf16[64,2048]{1,0:T(8,128)(2,1)S(1)} %constant_dynamic-update-slice_fusion.refs_0_), channel_id=1, source_target_pairs={{0,8},{8,0},{16,24},{24,16},{1,9},{9,1},{17,25},{25,17},{2,10},{10... | collective-permute-start | bytes 786440 | tf_op jit(solution)/shard_map/ppermute | solution.py:259
  20.1 13.7 %collective-permute-start.11 = (bf16[64,2048]{1,0:T(8,128)(2,1)S(1)}, bf16[64,2048]{1,0:T(8,128)(2,1)S(1)}, u32[]{:S(2)}, u32[]{:S(2)}) collective-permute-start(bf16[64,2048]{1,0:T(8,128)(2,1)S(1)} %constant_dynamic-update-slice_fusion.4.refs_1_), channel_id=1, source_target_pairs={{0,16},{8,24},{16,0},{24,8},{1,17},{9,25},{17,1},{25,9},{2,18},{10... | collective-permute-start | bytes 786440 | tf_op jit(solution)/shard_map/ppermute | solution.py:264
  21.6 4.3 %collective-permute-start.8 = (bf16[64,2048]{1,0:T(8,128)(2,1)S(1)}, bf16[64,2048]{1,0:T(8,128)(2,1)S(1)}, u32[]{:S(2)}, u32[]{:S(2)}) collective-permute-start(bf16[64,2048]{1,0:T(8,128)(2,1)S(1)} %constant_dynamic-update-slice_fusion.4.refs_1_), channel_id=1, source_target_pairs={{0,8},{8,0},{16,24},{24,16},{1,9},{9,1},{17,25},{25,17},{2,10},{10... | collective-permute-start | bytes 786440 | tf_op jit(solution)/shard_map/ppermute | solution.py:259
  28.4 15.4 %all-to-all-start = ((bf16[8,16,1152]{2,1,0:T(8,128)(2,1)}), bf16[8,16,1152]{2,1,0:T(8,128)(2,1)S(1)}, u32[]{:S(2)}, u32[]{:S(2)}) async-start(bf16[8,16,1152]{2,1,0:T(8,128)(2,1)} %bitcast.4), calls=%async_computation | async-start | bytes 589824 | tf_op jit(solution)/shard_map/all_to_all | solution.py:344
  33.5 1.5 %collective-permute-start.10 = (bf16[64,2048]{1,0:T(8,128)(2,1)S(1)}, bf16[64,2048]{1,0:T(8,128)(2,1)S(1)}, u32[]{:S(2)}, u32[]{:S(2)}) collective-permute-start(bf16[64,2048]{1,0:T(8,128)(2,1)S(1)} %collective-permute-done.9.refs_2_.refs_4_), channel_id=1, source_target_pairs={{0,8},{8,0},{16,24},{24,16},{1,9},{9,1},{17,25},{25,17},{2,10},{10... | collective-permute-start | bytes 786440 | tf_op jit(solution)/shard_map/ppermute | solution.py:259
  33.8 1.7 %collective-permute-start.12 = (bf16[64,2048]{1,0:T(8,128)(2,1)S(1)}, bf16[64,2048]{1,0:T(8,128)(2,1)S(1)}, u32[]{:S(2)}, u32[]{:S(2)}) collective-permute-start(bf16[64,2048]{1,0:T(8,128)(2,1)S(1)} %collective-permute-done.11.refs_6_), channel_id=1, source_target_pairs={{0,8},{8,0},{16,24},{24,16},{1,9},{9,1},{17,25},{25,17},{2,10},{10... | collective-permute-start | bytes 786440 | tf_op jit(solution)/shard_map/ppermute | solution.py:259
  35.5 8.3 %copy-start.2 = (bf16[64,2]{0,1:T(2,128)(2,1)S(1)}, bf16[64,2]{0,1:T(2,128)(2,1)}, u32[]{:S(2)}) copy-start(bf16[64,2]{0,1:T(2,128)(2,1)} %param.9) | copy-start | bytes 772

commit v14 on v10

--- a/solution.py
+++ b/solution.py
@@ -245,8 +245,9 @@
         grad_in[:, cols] = dot(rows[:, mine], d_pre[:, cols], (0, 0)).astype(BF16)
         outs.append(send(grad_in.at[:, cols], grad_in_hbm.at[:, cols]))
     h_cut[known:, :] = my_part(hidden)
-    for at in range(0, tile, tile // 2):
-        part = slice(at, at + tile // 2)
+    wide = h_cut.shape[1] // 2
+    for at in (0, wide):
+        part = slice(at, at + wide)
         grad_out[part, :] = dot(h_cut[:, part], rows[:, width:], (0, 0)).astype(BF16)
         outs.append(send(grad_out.at[part, :], grad_out_hbm.at[part, :]))
     for copy in outs:
@@ -306,6 +307,8 @@
     )
     blocks, places = routed[:experts], routed[experts:]
     rest = list(range(experts - 1, 1, -1))
+    if len(rest) > 4:
+        rest.insert(2, rest.pop(-2))
     order = [0, *rest[:2], 1, *rest[2:]]
     order_a, order_b = order[:half], order[half:]
     got_a = [blocks[0]] + [permute(blocks[k], k) for k in order_a[1:]]
@@ -322,7 +325,7 @@
     weights = [proj_in[0], proj_out[0]]
     weight_space = [pltpu.VMEM((feat_width, ffw), BF16), pltpu.VMEM((ffw, feat_width), BF16)]
     d_pre, h_cut, back = call(
-        functools.partial(own_kernel, tile, order),
+        functools.partial(own_kernel, tile // 2, order),
         [
             pltpu.HBM((slots_all, ffw), BF16),
             pltpu.HBM((slots_all, tile), BF16),
@@ -370,7 +373,7 @@
     pieces = [rows_a, rows_b, *early, *late]
     rows_all = groups * slots_all
     grad_in, grad_out = call(
-        functools.partial(grads_kernel, tile, len(pieces), len(late)),
+        functools.partial(grads_kernel, tile // 2, len(pieces), len(late)),
         [
             pltpu.HBM((feat_width // groups, ffw), BF16),
             pltpu.HBM((ffw // groups, feat_width), BF16),

time: 42.7 us -> 42.5 us (level)
  waiting for transfers between devices: 3.54 us -> 0.61 us
  starting transfers between devices: 21.5 us -> 24.1 us
    ppermute x7, starting transfers between devices: 12.6 us -> 16.7 us  [permute(): lax.ppermute(block, 'expert', [(i, i ^ k) for i in range(lax.axis_size('e...]
    ppermute x7, waiting for transfers between devices: 3.52 us -> 0.55 us  [permute(): lax.ppermute(block, 'expert', [(i, i ^ k) for i in range(lax.axis_size('e...]
    all_to_all x1, starting transfers between devices: 5.13 us -> 3.73 us  [local(): lax.all_to_all(after(back, core_a, core_b).reshape(experts, capacity, fea...]
  transfers between devices with their start and end apart: 14 -> 14, of which waited for: 4 -> 1; matrix products, arithmetic and copies ran while one was open for 0% -> 0% of each run, Pallas kernels for 33% -> 34%
where the time goes in v14:
time: 42.5 us; the launch traced here: 42.2 us
  starting transfers between devices  24.1 us (57%)
  Pallas kernels  16.6 us (39%)
  between operations  0.81 us (2%)
  waiting for transfers between devices  0.61 us (1%)
    ppermute x7, starting transfers between devices, permute(): lax.ppermute(block, 'expert', [(i, i ^ k) for i in range(lax.axis_size('e...  16.7 us
    pallas_call x5, Pallas kernels, call(): pl.pallas_call(kernel, out_shape=out_shape, in_specs=[pl.BlockSpec(memory...  16.6 us
    all_to_all x1, starting transfers between devices, local(): lax.all_to_all(after(back, core_a, core_b).reshape(experts, capacity, fea...  3.73 us
    ppermute x2, starting transfers between devices, shift_chips(): lax.ppermute(rows, 'dp', [(i, (i + 2 * k) % groups) for i in range(groups)])  3.13 us
  transfers between devices with their start and end apart: 14, of which 1 were waited for; matrix products, arithmetic and copies ran while one was open for 0% of the time, Pallas kernels for 34%

profile of v14, /device:TPU:0, one launch (start us, length us, event | category | flops | bytes accessed | tf_op | source)
XLA Modules:
  0.0 42.2 jit_solution(12034361232961430112)
XLA Ops:
  0.6 0.0 copy-start
  0.6 0.0 copy-start.1
  0.7 1.6 %shard_map.93 = (bf16[16,2048]{1,0:T(8,128)(2,1)S(1)}, bf16[16,2048]{1,0:T(8,128)(2,1)S(1)}, bf16[16,2048]{1,0:T(8,128)(2,1)S(1)}, bf16[16,2048]{1,0:T(8,128)(2,...) custom-call(s32[2,64]{1,0:T(2,128)} %bitcast.19, ...), custom_call_target="tpu_custom_call" | custom-call | flops 16106127360 | bytes 262912 | tf_op jit(solution)/shard_map/pallas_call | solution.py:35
  2.2 6.0 %collective-permute-start = (bf16[16,2048]{1,0:T(8,128)(2,1)S(1)}, bf16[16,2048]{1,0:T(8,128)(2,1)S(1)}, u32[]{:S(2)}, u32[]{:S(2)}) collective-permute-start(bf16[16,2048]{1,0:T(8,128)(2,1)S(1)} %get-tuple-element.34), channel_id=1, source_target_pairs={{0,7},{1,6},{2,5},{3,4},{4,3},{5,2},{6,1},{7,0},{8,15},{9,14},{10,... | collective-permute-start | bytes 196616 | tf_op jit(solution)/shard_map/ppermute | solution.py:262
  8.3 0.2 collective-permute-start.1
  8.5 0.4 collective-permute-start.2
  8.9 0.8 %collective-permute-start.3 = (bf16[16,2048]{1,0:T(8,128)(2,1)S(1)}, bf16[16,2048]{1,0:T(8,128)(2,1)S(1)}, u32[]{:S(2)}, u32[]{:S(2)}) collective-permute-start(bf16[16,2048]{1,0:T(8,128)(2,1)S(1)} %get-tuple-element.37), channel_id=1, source_target_pairs={{0,3},{1,2},{2,1},{3,0},{4,7},{5,6},{6,5},{7,4},{8,11},{9,10},{10,... | collective-permute-start | bytes 196616 | tf_op jit(solution)/shard_map/ppermute | solution.py:262
  9.7 4.4 %collective-permute-start.4 = (bf16[16,2048]{1,0:T(8,128)(2,1)S(1)}, bf16[16,2048]{1,0:T(8,128)(2,1)S(1)}, u32[]{:S(2)}, u32[]{:S(2)}) collective-permute-start(bf16[16,2048]{1,0:T(8,128)(2,1)S(1)} %get-tuple-element.38), channel_id=1, source_target_pairs={{0,5},{1,4},{2,7},{3,6},{4,1},{5,0},{6,3},{7,2},{8,13},{9,12},{10,... | collective-permute-start | bytes 196616 | tf_op jit(solution)/shard_map/ppermute | solution.py:262
  14.1 0.0 collective-permute-done.2
  14.1 0.1 collective-permute-start.5
  14.2 0.0 collective-permute-done
  14.2 4.8 %collective-permute-start.6 = (bf16[16,2048]{1,0:T(8,128)(2,1)S(1)}, bf16[16,2048]{1,0:T(8,128)(2,1)S(1)}, u32[]{:S(2)}, u32[]{:S(2)}) collective-permute-start(bf16[16,2048]{1,0:T(8,128)(2,1)S(1)} %get-tuple-element.42), channel_id=1, source_target_pairs={{0,2},{1,3},{2,0},{3,1},{4,6},{5,7},{6,4},{7,5},{8,10},{9,11},{10,... | collective-permute-start | bytes 196616 | tf_op jit(solution)/shard_map/ppermute | solution.py:262
  19.0 0.0 collective-permute-done.1
  19.0 1.6 %collective-permute-start.9 = (bf16[64,2048]{1,0:T(8,128)(2,1)S(1)}, bf16[64,2048]{1,0:T(8,128)(2,1)S(1)}, u32[]{:S(2)}, u32[]{:S(2)}) collective-permute-start(bf16[64,2048]{1,0:T(8,128)(2,1)S(1)} %constant_dynamic-update-slice_fusion.refs_0_), channel_id=1, source_target_pairs={{0,16},{8,24},{16,0},{24,8},{1,17},{9,25},{17,1},{25,9},{2,18},{10... | collective-permute-start | bytes 786440 | tf_op jit(solution)/shard_map/ppermute | solution.py:271
  20.6 0.0 collective-permute-done.3
  20.6 0.0 collective-permute-start.7
  20.6 0.0 collective-permute-done.4
  20.7 0.0 collective-permute-done.5
  20.7 0.5 %collective-permute-done.6 = bf16[16,2048]{1,0:T(8,128)(2,1)S(1)} collective-permute-done((bf16[16,2048]{1,0:T(8,128)(2,1)S(1)}, bf16[16,2048]{1,0:T(8,128)(2,1)S(1)}, u32[]{:S(2)}, u32[]{:S(2)}) %collective-permute-start.6) | collective-permute-done | bytes 65568 | tf_op jit(solution)/shard_map/ppermute | solution.py:262
  21.2 1.5 %collective-permute-start.11 = (bf16[64,2048]{1,0:T(8,128)(2,1)S(1)}, bf16[64,2048]{1,0:T(8,128)(2,1)S(1)}, u32[]{:S(2)}, u32[]{:S(2)}) collective-permute-start(bf16[64,2048]{1,0:T(8,128)(2,1)S(1)} %constant_dynamic-update-slice_fusion.4.refs_1_), channel_id=1, source_target_pairs={{0,16},{8,24},{16,0},{24,8},{1,17},{9,25},{17,1},{25,9},{2,18},{10... | collective-permute-start | bytes 786440 | tf_op jit(solution)/shard_map/ppermute | solution.py:271
  22.8 0.0 collective-permute-start.8
  22.8 0.0 copy-done
  22.8 0.0 copy-done.1
  22.8 4.2 %shard_map.94 = (bf16[128,2048]{1,0:T(8,128)(2,1)}, bf16[128,512]{1,0:T(8,128)(2,1)}, bf16[128,1152]{1,0:T(8,128)(2,1)}) custom-call(bf16[64,2048]{1,0:T(8,128)(2,1)S(1)} %constant_dynamic-update-slice_fusion.refs_0_, bf16[64,2048]{1,0:T(8,128)(2,1)S(1)} %constant_dynamic-update-slice_fusion.4.refs_1_, bf16[1024,2048]{1,0:T(8,128)(2,1)S(1)} %bitcast.10, ...), custom_call_target="tpu_custom_call" | custom-call | flops 10737418240 | bytes 8912896 | tf_op jit(solution)/shard_map/pallas_call | solution.py:35
  27.0 0.0 collective-permute-done.7.refs_0_.refs_2_
  27.0 0.0 collective-permute-done.8.refs_1_.refs_3_
  27.0 3.7 %all-to-all-start = ((bf16[8,16,1152]{2,1,0:T(8,128)(2,1)}), bf16[8,16,1152]{2,1,0:T(8,128)(2,1)S(1)}, u32[]{:S(2)}, u32[]{:S(2)}) async-start(bf16[8,16,1152]{2,1,0:T(8,128)(2,1)} %bitcast.16), calls=%async_computation | async-start | bytes 589824 | tf_op jit(solution)/shard_map/all_to_all | solution.py:348
  30.7 0.0 collective-permute-done.9.refs_2_.refs_4_
  30.7 0.3 collective-permute-start.10
  31.0 0.0 collective-permute-done.11.refs_6_
  31.1 0.2 collective-permute-start.12
  31.3 4.7 %shard_map.95 = (bf16[1024,2048]{1,0:T(8,128)(2,1)S(1)}, bf16[2048,1024]{1,0:T(8,128)(2,1)S(1)}, bf16[192,2048]{1,0:T(8,128)(2,1)S(1)}, bf16[192,512]{1,0:T(8,128)(2,1)S(1)}) custom-call(bf16[64,2048]{1,0:T(8,128)(2,1)S(1)} %collective-permute-done.7.refs_0_.refs_2_, bf16[64,2048]{1,0:T(8,128)(2,1)S(1)} %collective-permute-done.8.refs_1_.refs_3_, ...), custom_call_target="tpu_custom_call" | custom-call | flops 1073741824 | bytes 9175040 | tf_op jit(solution)/shard_map/pallas_call | solution.py:35
  36.0 0.0 collective-permute-done.10.refs_5_
  36.1 0.0 collective-permute-done.12.refs_7_
  36.1 0.0 copy-start.2
  36.1 5.2 %shard_map.96 = (bf16[256,2048]{1,0:T(8,128)(2,1)}, bf16[512,1024]{1,0:T(8,128)(2,1)}) custom-call(bf16[64,2048]{1,0:T(8,128)(2,1)S(1)} %constant_dynamic-update-slice_fusion.refs_0_, bf16[64,2048]{1,0:T(8,128)(2,1)S(1)} %constant_dynamic-update-slice_fusion.4.refs_1_, bf16[64,2048]{1,0:T(8,128)(2,1)S(1)} %collective-permute-done.7.refs_0_.refs_2_, ...), custom_call_target="tpu_custom_call" | custom-call | flops 2147483648 | bytes 12124160 | tf_op jit(solution)/shard_map/pallas_call | solution.py:35
  41.3 0.0 all-to-all-done
  41.3 0.0 copy-done.2
  41.3 0.9 %shard_map.97 = (bf16[64,1024]{1,0:T(8,128)(2,1)}, bf16[2,64]{1,0:T(2,128)(2,1)}) custom-call(bf16[128,64]{1,0:T(8,128)(2,1)S(1)} %get-tuple-element.31.place0, bf16[128,64]{1,0:T(8,128)(2,1)S(1)} %get-tuple-element.32.place1, bf16[2,64]{1,0:T(2,128)(2,1)S(1)} %bitcast.15, bf16[128,1152]{1,0:T(8,128)(2,1)S(1)} %bitcast.13), custom_call_target="tpu_custom_call" | custom-call | bytes 327936 | tf_op jit(solution)/shard_map/pallas_call | solution.py:35
  (8 shorter events, 0.0 us)
Async XLA Ops:
  0.6 22.1 %copy-start = (bf16[1,1024,2048]{2,1,0:T(8,128)(2,1)S(1)}, bf16[1,1024,2048]{2,1,0:T(8,128)(2,1)}, u32[]{:S(2)}) copy-start(bf16[1,1024,2048]{2,1,0:T(8,128)(2,1)} %param.10) | copy-start | bytes 12582916
  0.6 22.1 %copy-start.1 = (bf16[1,2048,1024]{2,1,0:T(8,128)(2,1)S(1)}, bf16[1,2048,1024]{2,1,0:T(8,128)(2,1)}, u32[]{:S(2)}) copy-start(bf16[1,2048,1024]{2,1,0:T(8,128)(2,1)} %param.11) | copy-start | bytes 12582916
  2.2 12.0 %collective-permute-start = (bf16[16,2048]{1,0:T(8,128)(2,1)S(1)}, bf16[16,2048]{1,0:T(8,128)(2,1)S(1)}, u32[]{:S(2)}, u32[]{:S(2)}) collective-permute-start(bf16[16,2048]{1,0:T(8,128)(2,1)S(1)} %get-tuple-element.34), channel_id=1, source_target_pairs={{0,7},{1,6},{2,5},{3,4},{4,3},{5,2},{6,1},{7,0},{8,15},{9,14},{10,... | collective-permute-start | bytes 196616 | tf_op jit(solution)/shard_map/ppermute | solution.py:262
  8.3 10.7 %collective-permute-start.1 = (bf16[16,2048]{1,0:T(8,128)(2,1)S(1)}, bf16[16,2048]{1,0:T(8,128)(2,1)S(1)}, u32[]{:S(2)}, u32[]{:S(2)}) collective-permute-start(bf16[16,2048]{1,0:T(8,128)(2,1)S(1)} %get-tuple-element.35), channel_id=1, source_target_pairs={{0,6},{1,7},{2,4},{3,5},{4,2},{5,3},{6,0},{7,1},{8,14},{9,15},{10,... | collective-permute-start | bytes 196616 | tf_op jit(solution)/shard_map/ppermute | solution.py:262
  8.5 5.6 %collective-permute-start.2 = (bf16[16,2048]{1,0:T(8,128)(2,1)S(1)}, bf16[16,2048]{1,0:T(8,128)(2,1)S(1)}, u32[]{:S(2)}, u32[]{:S(2)}) collective-permute-start(bf16[16,2048]{1,0:T(8,128)(2,1)S(1)} %get-tuple-element.36), channel_id=1, source_target_pairs={{0,1},{1,0},{2,3},{3,2},{4,5},{5,4},{6,7},{7,6},{8,9},{9,8},{10,11... | collective-permute-start | bytes 196616 | tf_op jit(solution)/shard_map/ppermute | solution.py:262
  8.9 11.7 %collective-permute-start.3 = (bf16[16,2048]{1,0:T(8,128)(2,1)S(1)}, bf16[16,2048]{1,0:T(8,128)(2,1)S(1)}, u32[]{:S(2)}, u32[]{:S(2)}) collective-permute-start(bf16[16,2048]{1,0:T(8,128)(2,1)S(1)} %get-tuple-element.37), channel_id=1, source_target_pairs={{0,3},{1,2},{2,1},{3,0},{4,7},{5,6},{6,5},{7,4},{8,11},{9,10},{10,... | collective-permute-start | bytes 196616 | tf_op jit(solution)/shard_map/ppermute | solution.py:262
  9.7 10.9 %collective-permute-start.4 = (bf16[16,2048]{1,0:T(8,128)(2,1)S(1)}, bf16[16,2048]{1,0:T(8,128)(2,1)S(1)}, u32[]{:S(2)}, u32[]{:S(2)}) collective-permute-start(bf16[16,2048]{1,0:T(8,128)(2,1)S(1)} %get-tuple-element.38), channel_id=1, source_target_pairs={{0,5},{1,4},{2,7},{3,6},{4,1},{5,0},{6,3},{7,2},{8,13},{9,12},{10,... | collective-permute-start | bytes 196616 | tf_op jit(solution)/shard_map/ppermute | solution.py:262
  14.1 6.6 %collective-permute-start.5 = (bf16[16,2048]{1,0:T(8,128)(2,1)S(1)}, bf16[16,2048]{1,0:T(8,128)(2,1)S(1)}, u32[]{:S(2)}, u32[]{:S(2)}) collective-permute-start(bf16[16,2048]{1,0:T(8,128)(2,1)S(1)} %get-tuple-element.40), channel_id=1, source_target_pairs={{0,4},{1,5},{2,6},{3,7},{4,0},{5,1},{6,2},{7,3},{8,12},{9,13},{10,... | collective-permute-start | bytes 196616 | tf_op jit(solution)/shard_map/ppermute | solution.py:262
  14.2 7.0 %collective-permute-start.6 = (bf16[16,2048]{1,0:T(8,128)(2,1)S(1)}, bf16[16,2048]{1,0:T(8,128)(2,1)S(1)}, u32[]{:S(2)}, u32[]{:S(2)}) collective-permute-start(bf16[16,2048]{1,0:T(8,128)(2,1)S(1)} %get-tuple-element.42), channel_id=1, source_target_pairs={{0,2},{1,3},{2,0},{3,1},{4,6},{5,7},{6,4},{7,5},{8,10},{9,11},{10,... | collective-permute-start | bytes 196616 | tf_op jit(solution)/shard_map/ppermute | solution.py:262
  19.0 11.7 %collective-permute-start.9 = (bf16[64,2048]{1,0:T(8,128)(2,1)S(1)}, bf16[64,2048]{1,0:T(8,128)(2,1)S(1)}, u32[]{:S(2)}, u32[]{:S(2)}) collective-permute-start(bf16[64,2048]{1,0:T(8,128)(2,1)S(1)} %constant_dynamic-update-slice_fusion.refs_0_), channel_id=1, source_target_pairs={{0,16},{8,24},{16,0},{24,8},{1,17},{9,25},{17,1},{25,9},{2,18},{10... | collective-permute-start | bytes 786440 | tf_op jit(solution)/shard_map/ppermute | solution.py:271
  20.6 6.4 %collective-permute-start.7 = (bf16[64,2048]{1,0:T(8,128)(2,1)S(1)}, bf16[64,2048]{1,0:T(8,128)(2,1)S(1)}, u32[]{:S(2)}, u32[]{:S(2)}) collective-permute-start(bf16[64,2048]{1,0:T(8,128)(2,1)S(1)} %constant_dynamic-update-slice_fusion.refs_0_), channel_id=1, source_target_pairs={{0,8},{8,0},{16,24},{24,16},{1,9},{9,1},{17,25},{25,17},{2,10},{10... | collective-permute-start | bytes 786440 | tf_op jit(solution)/shard_map/ppermute | solution.py:266
  21.2 9.8 %collective-permute-start.11 = (bf16[64,2048]{1,0:T(8,128)(2,1)S(1)}, bf16[64,2048]{1,0:T(8,128)(2,1)S(1)}, u32[]{:S(2)}, u32[]{:S(2)}) collective-permute-start(bf16[64,2048]{1,0:T(8,128)(2,1)S(1)} %constant_dynamic-update-slice_fusion.4.refs_1_), channel_id=1, source_target_pairs={{0,16},{8,24},{16,0},{24,8},{1,17},{9,25},{17,1},{25,9},{2,18},{10... | collective-permute-start | bytes 786440 | tf_op jit(solution)/shard_map/ppermute | solution.py:271
  22.8 4.2 %collective-permute-start.8 = (bf16[64,2048]{1,0:T(8,128)(2,1)S(1)}, bf16[64,2048]{1,0:T(8,128)(2,1)S(1)}, u32[]{:S(2)}, u32[]{:S(2)}) collective-permute-start(bf16[64,2048]{1,0:T(8,128)(2,1)S(1)} %constant_dynamic-update-slice_fusion.4.refs_1_), channel_id=1, source_target_pairs={{0,8},{8,0},{16,24},{24,16},{1,9},{9,1},{17,25},{25,17},{2,10},{10... | collective-permute-start | bytes 786440 | tf_op jit(solution)/shard_map/ppermute | solution.py:266
  27.0 14.3 %all-to-all-start = ((bf16[8,16,1152]{2,1,0:T(8,128)(2,1)}), bf16[8,16,1152]{2,1,0:T(8,128)(2,1)S(1)}, u32[]{:S(2)}, u32[]{:S(2)}) async-start(bf16[8,16,1152]{2,1,0:T(8,128)(2,1)} %bitcast.16), calls=%async_computation | async-start | bytes 589824 | tf_op jit(solution)/shard_map/all_to_all | solution.py:348
  30.7 5.3 %collective-permute-start.10 = (bf16[64,2048]{1,0:T(8,128)(2,1)S(1)}, bf16[64,2048]{1,0:T(8,128)(2,1)S(1)}, u32[]{:S(2)}, u32[]{:S(2)}) collective-permute-start(bf16[64,2048]{1,0:T(8,128)(2,1)S(1)} %collective-permute-done.9.refs_2_.refs_4_), channel_id=1, source_target_pairs={{0,8},{8,0},{16,24},{24,16},{1,9},{9,1},{17,25},{25,17},{2,10},{10... | collective-permute-start | bytes 786440 | tf_op jit(solution)/shard_map/ppermute | solution.py:266
  31.1 5.0 %collective-permute-start.12 = (bf16[64,2048]{1,0:T(8,128)(2,1)S(1)}, bf16[64,2048]{1,0:T(8,128)(2,1)S(1)}, u32[]{:S(2)}, u32[]{:S(2)}) collective-permute-start(bf16[64,2048]{1,0:T(8,128)(2,1)S(1)} %collective-permute-done.11.refs_6_), channel_id=1, source_target_pairs={{0,8},{8,0},{16,24},{24,16},{1,9},{9,1},{17,25},{25,17},{2,10},{10... | collective-permute-start | bytes 786440 | tf_op jit(solution)/shard_map/ppermute | solution.py:266
  36.1 5.3 %copy-start.2 = (bf16[64,2]{0,1:T(2,128)(2,1)S(1)}, bf16[64,2]{0,1:T(2,128)(2,1)}, u32[]{:S(2)}) copy-start(bf16[64,2]{0,1:T(2,128)(2,1)} %param.9) | copy-start | bytes 772

commit v15 on v14

--- a/solution.py
+++ b/solution.py
@@ -50,15 +50,14 @@
     return jax.ShapeDtypeStruct(dims, dtype)
 
 
-def route_kernel(experts, capacity, routes_hbm, gates_hbm, tokens_hbm, cotangent_hbm, *refs):
+def route_kernel(experts, capacity, routes_hbm, gates, tokens_hbm, cotangent_hbm, *refs):
     blocks, place_refs, scratch = refs[:experts], refs[experts : experts + 2], refs[experts + 2 :]
-    routes, gates, tokens, cotangent, sems = scratch
+    routes, tokens, cotangent, sems = scratch
     copies = [
         pltpu.make_async_copy(source, target, sems.at[i])
         for i, (source, target) in enumerate(
             (
                 (routes_hbm, routes),
-                (gates_hbm, gates),
                 (tokens_hbm, tokens),
                 (cotangent_hbm, cotangent),
             )
@@ -78,8 +77,8 @@
     slot_id = lax.broadcasted_iota(jnp.int32, (slots_all, tok_count), 0)
     taken = jnp.zeros((rows, 1), F32)
     places, gated = [], jnp.zeros((slots_all, tok_count), F32)
+    gate_rows = gates[...].astype(F32)
     copies[0].wait()
-    copies[1].wait()
     for choice in range(2):
         chosen = routes[choice : choice + 1, :]
         one_hot = (expert_id == chosen).astype(F32)
@@ -92,10 +91,10 @@
         place = (slot_id == target).astype(F32)
         place_refs[choice][...] = place.astype(BF16)
         places.append(place)
-        gated = gated + place * gates[choice : choice + 1, :].astype(F32)
+        gated = gated + place * gate_rows[choice : choice + 1, :]
+    copies[1].wait()
+    x = dot((places[0] + places[1]).astype(BF16), tokens[...]).astype(BF16)
     copies[2].wait()
-    x = dot((places[0] + places[1]).astype(BF16), tokens[...]).astype(BF16)
-    copies[3].wait()
     s = dot(gated.astype(BF16), cotangent[...]).astype(BF16)
     for k in range(experts):
         blocks[k][:, :feat_width] = x[k * capacity : (k + 1) * capacity]
@@ -296,10 +295,9 @@
         [shape((capacity, 2 * feat_width))] * experts + [place] * 2,
         [routes.T, gates.T, tokens, cotangent],
         30 * product,
-        spaces=[pltpu.HBM] * 4,
+        spaces=[pltpu.HBM, pltpu.VMEM, pltpu.HBM, pltpu.HBM],
         scratch=[
             pltpu.VMEM((2, tok_count), jnp.int32),
-            pltpu.VMEM((2, tok_count), BF16),
             pltpu.VMEM((tok_count, feat_width), BF16),
             pltpu.VMEM((tok_count, feat_width), BF16),
             pltpu.SemaphoreType.DMA((4,)),

time: 42.5 us -> 43.2 us (1.016)
  local copies, waits for them, and re-layouts: 0.07 us -> 0.71 us
    unnamed x12 -> x14, local copies, waits for them, and re-layouts: 0.06 us -> 0.7 us
  transfers between devices with their start and end apart: 14 -> 14, of which waited for: 1 -> 1; matrix products, arithmetic and copies ran while one was open for 0% -> 0% of each run, Pallas kernels for 34% -> 33%
where the time goes in v15:
time: 43.2 us; the launch traced here: 42.9 us
  starting transfers between devices  24.2 us (56%)
  Pallas kernels  16.7 us (39%)
  between operations  0.8 us (2%)
  local copies, waits for them, and re-layouts  0.71 us (2%)
  waiting for transfers between devices  0.59 us (1%)
    ppermute x7, starting transfers between devices, permute(): lax.ppermute(block, 'expert', [(i, i ^ k) for i in range(lax.axis_size('e...  16.7 us
    pallas_call x5, Pallas kernels, call(): pl.pallas_call(kernel, out_shape=out_shape, in_specs=[pl.BlockSpec(memory...  16.7 us
    all_to_all x1, starting transfers between devices, local(): lax.all_to_all(after(back, core_a, core_b).reshape(experts, capacity, fea...  3.74 us
    ppermute x2, starting transfers between devices, shift_chips(): lax.ppermute(rows, 'dp', [(i, (i + 2 * k) % groups) for i in range(groups)])  3.1 us
  transfers between devices with their start and end apart: 14, of which 1 were waited for; matrix products, arithmetic and copies ran while one was open for 0% of the time, Pallas kernels for 33%

profile of v15, /device:TPU:0, one launch (start us, length us, event | category | flops | bytes accessed | tf_op | source)
XLA Modules:
  0.0 42.9 jit_solution(6531744888781105291)
XLA Ops:
  0.6 0.0 copy-start.2
  0.6 0.6 %copy-done.2 = bf16[64,2]{0,1:T(2,128)(2,1)S(1)} copy-done((bf16[64,2]{0,1:T(2,128)(2,1)S(1)}, bf16[64,2]{0,1:T(2,128)(2,1)}, u32[]{:S(2)}) %copy-start.2) | copy-done | bytes 280
  1.3 0.0 copy-start
  1.3 0.0 copy-start.1
  1.3 1.5 %shard_map.93 = (bf16[16,2048]{1,0:T(8,128)(2,1)S(1)}, bf16[16,2048]{1,0:T(8,128)(2,1)S(1)}, bf16[16,2048]{1,0:T(8,128)(2,1)S(1)}, bf16[16,2048]{1,0:T(8,128)(2,...) custom-call(s32[2,64]{1,0:T(2,128)} %bitcast.19, ...), custom_call_target="tpu_custom_call" | custom-call | flops 16106127360 | bytes 262912 | tf_op jit(solution)/shard_map/pallas_call | solution.py:35
  2.8 6.1 %collective-permute-start = (bf16[16,2048]{1,0:T(8,128)(2,1)S(1)}, bf16[16,2048]{1,0:T(8,128)(2,1)S(1)}, u32[]{:S(2)}, u32[]{:S(2)}) collective-permute-start(bf16[16,2048]{1,0:T(8,128)(2,1)S(1)} %get-tuple-element.34), channel_id=1, source_target_pairs={{0,7},{1,6},{2,5},{3,4},{4,3},{5,2},{6,1},{7,0},{8,15},{9,14},{10,... | collective-permute-start | bytes 196616 | tf_op jit(solution)/shard_map/ppermute | solution.py:261
  8.9 0.2 collective-permute-start.1
  9.1 0.4 %collective-permute-start.2 = (bf16[16,2048]{1,0:T(8,128)(2,1)S(1)}, bf16[16,2048]{1,0:T(8,128)(2,1)S(1)}, u32[]{:S(2)}, u32[]{:S(2)}) collective-permute-start(bf16[16,2048]{1,0:T(8,128)(2,1)S(1)} %get-tuple-element.36), channel_id=1, source_target_pairs={{0,1},{1,0},{2,3},{3,2},{4,5},{5,4},{6,7},{7,6},{8,9},{9,8},{10,11... | collective-permute-start | bytes 196616 | tf_op jit(solution)/shard_map/ppermute | solution.py:261
  9.5 0.8 %collective-permute-start.3 = (bf16[16,2048]{1,0:T(8,128)(2,1)S(1)}, bf16[16,2048]{1,0:T(8,128)(2,1)S(1)}, u32[]{:S(2)}, u32[]{:S(2)}) collective-permute-start(bf16[16,2048]{1,0:T(8,128)(2,1)S(1)} %get-tuple-element.37), channel_id=1, source_target_pairs={{0,3},{1,2},{2,1},{3,0},{4,7},{5,6},{6,5},{7,4},{8,11},{9,10},{10,... | collective-permute-start | bytes 196616 | tf_op jit(solution)/shard_map/ppermute | solution.py:261
  10.3 4.4 %collective-permute-start.4 = (bf16[16,2048]{1,0:T(8,128)(2,1)S(1)}, bf16[16,2048]{1,0:T(8,128)(2,1)S(1)}, u32[]{:S(2)}, u32[]{:S(2)}) collective-permute-start(bf16[16,2048]{1,0:T(8,128)(2,1)S(1)} %get-tuple-element.38), channel_id=1, source_target_pairs={{0,5},{1,4},{2,7},{3,6},{4,1},{5,0},{6,3},{7,2},{8,13},{9,12},{10,... | collective-permute-start | bytes 196616 | tf_op jit(solution)/shard_map/ppermute | solution.py:261
  14.7 0.0 collective-permute-done.2
  14.7 0.1 collective-permute-start.5
  14.8 0.0 collective-permute-done
  14.8 4.8 %collective-permute-start.6 = (bf16[16,2048]{1,0:T(8,128)(2,1)S(1)}, bf16[16,2048]{1,0:T(8,128)(2,1)S(1)}, u32[]{:S(2)}, u32[]{:S(2)}) collective-permute-start(bf16[16,2048]{1,0:T(8,128)(2,1)S(1)} %get-tuple-element.42), channel_id=1, source_target_pairs={{0,2},{1,3},{2,0},{3,1},{4,6},{5,7},{6,4},{7,5},{8,10},{9,11},{10,... | collective-permute-start | bytes 196616 | tf_op jit(solution)/shard_map/ppermute | solution.py:261
  19.6 0.0 collective-permute-done.1
  19.6 1.6 %collective-permute-start.9 = (bf16[64,2048]{1,0:T(8,128)(2,1)S(1)}, bf16[64,2048]{1,0:T(8,128)(2,1)S(1)}, u32[]{:S(2)}, u32[]{:S(2)}) collective-permute-start(bf16[64,2048]{1,0:T(8,128)(2,1)S(1)} %constant_dynamic-update-slice_fusion.refs_0_), channel_id=1, source_target_pairs={{0,16},{8,24},{16,0},{24,8},{1,17},{9,25},{17,1},{25,9},{2,18},{10... | collective-permute-start | bytes 786440 | tf_op jit(solution)/shard_map/ppermute | solution.py:270
  21.2 0.0 collective-permute-done.3
  21.2 0.0 collective-permute-start.7
  21.2 0.0 collective-permute-done.4
  21.3 0.0 collective-permute-done.5
  21.3 0.6 %collective-permute-done.6 = bf16[16,2048]{1,0:T(8,128)(2,1)S(1)} collective-permute-done((bf16[16,2048]{1,0:T(8,128)(2,1)S(1)}, bf16[16,2048]{1,0:T(8,128)(2,1)S(1)}, u32[]{:S(2)}, u32[]{:S(2)}) %collective-permute-start.6) | collective-permute-done | bytes 65568 | tf_op jit(solution)/shard_map/ppermute | solution.py:261
  21.8 1.5 %collective-permute-start.11 = (bf16[64,2048]{1,0:T(8,128)(2,1)S(1)}, bf16[64,2048]{1,0:T(8,128)(2,1)S(1)}, u32[]{:S(2)}, u32[]{:S(2)}) collective-permute-start(bf16[64,2048]{1,0:T(8,128)(2,1)S(1)} %constant_dynamic-update-slice_fusion.4.refs_1_), channel_id=1, source_target_pairs={{0,16},{8,24},{16,0},{24,8},{1,17},{9,25},{17,1},{25,9},{2,18},{10... | collective-permute-start | bytes 786440 | tf_op jit(solution)/shard_map/ppermute | solution.py:270
  23.4 0.0 collective-permute-start.8
  23.4 0.0 copy-done
  23.4 0.0 copy-done.1
  23.4 4.3 %shard_map.94 = (bf16[128,2048]{1,0:T(8,128)(2,1)}, bf16[128,512]{1,0:T(8,128)(2,1)}, bf16[128,1152]{1,0:T(8,128)(2,1)}) custom-call(bf16[64,2048]{1,0:T(8,128)(2,1)S(1)} %constant_dynamic-update-slice_fusion.refs_0_, bf16[64,2048]{1,0:T(8,128)(2,1)S(1)} %constant_dynamic-update-slice_fusion.4.refs_1_, bf16[1024,2048]{1,0:T(8,128)(2,1)S(1)} %bitcast.10, ...), custom_call_target="tpu_custom_call" | custom-call | flops 10737418240 | bytes 8912896 | tf_op jit(solution)/shard_map/pallas_call | solution.py:35
  27.7 0.0 collective-permute-done.7.refs_0_.refs_2_
  27.7 0.0 collective-permute-done.8.refs_1_.refs_3_
  27.7 3.7 %all-to-all-start = ((bf16[8,16,1152]{2,1,0:T(8,128)(2,1)}), bf16[8,16,1152]{2,1,0:T(8,128)(2,1)S(1)}, u32[]{:S(2)}, u32[]{:S(2)}) async-start(bf16[8,16,1152]{2,1,0:T(8,128)(2,1)} %bitcast.16), calls=%async_computation | async-start | bytes 589824 | tf_op jit(solution)/shard_map/all_to_all | solution.py:346
  31.4 0.0 collective-permute-done.9.refs_2_.refs_4_
  31.4 0.3 collective-permute-start.10
  31.7 0.0 collective-permute-done.11.refs_6_
  31.7 0.3 collective-permute-start.12
  32.0 4.7 %shard_map.95 = (bf16[1024,2048]{1,0:T(8,128)(2,1)S(1)}, bf16[2048,1024]{1,0:T(8,128)(2,1)S(1)}, bf16[192,2048]{1,0:T(8,128)(2,1)S(1)}, bf16[192,512]{1,0:T(8,128)(2,1)S(1)}) custom-call(bf16[64,2048]{1,0:T(8,128)(2,1)S(1)} %collective-permute-done.7.refs_0_.refs_2_, bf16[64,2048]{1,0:T(8,128)(2,1)S(1)} %collective-permute-done.8.refs_1_.refs_3_, ...), custom_call_target="tpu_custom_call" | custom-call | flops 1073741824 | bytes 9175040 | tf_op jit(solution)/shard_map/pallas_call | solution.py:35
  36.7 0.0 collective-permute-done.10.refs_5_
  36.7 0.0 collective-permute-done.12.refs_7_
  36.8 0.0 copy-start.3
  36.8 5.3 %shard_map.96 = (bf16[256,2048]{1,0:T(8,128)(2,1)}, bf16[512,1024]{1,0:T(8,128)(2,1)}) custom-call(bf16[64,2048]{1,0:T(8,128)(2,1)S(1)} %constant_dynamic-update-slice_fusion.refs_0_, bf16[64,2048]{1,0:T(8,128)(2,1)S(1)} %constant_dynamic-update-slice_fusion.4.refs_1_, bf16[64,2048]{1,0:T(8,128)(2,1)S(1)} %collective-permute-done.7.refs_0_.refs_2_, ...), custom_call_target="tpu_custom_call" | custom-call | flops 2147483648 | bytes 12124160 | tf_op jit(solution)/shard_map/pallas_call | solution.py:35
  42.0 0.0 all-to-all-done
  42.0 0.0 copy-done.3
  42.1 0.9 %shard_map.97 = (bf16[64,1024]{1,0:T(8,128)(2,1)}, bf16[2,64]{1,0:T(2,128)(2,1)}) custom-call(bf16[128,64]{1,0:T(8,128)(2,1)S(1)} %get-tuple-element.31.place0, bf16[128,64]{1,0:T(8,128)(2,1)S(1)} %get-tuple-element.32.place1, bf16[2,64]{1,0:T(2,128)(2,1)S(1)} %bitcast.15, bf16[128,1152]{1,0:T(8,128)(2,1)S(1)} %bitcast.13), custom_call_target="tpu_custom_call" | custom-call | bytes 327936 | tf_op jit(solution)/shard_map/pallas_call | solution.py:35
  (8 shorter events, 0.0 us)
Async XLA Ops:
  0.6 0.7 %copy-start.2 = (bf16[64,2]{0,1:T(2,128)(2,1)S(1)}, bf16[64,2]{0,1:T(2,128)(2,1)}, u32[]{:S(2)}) copy-start(bf16[64,2]{0,1:T(2,128)(2,1)} %param.9) | copy-start | bytes 772
  1.3 22.1 %copy-start = (bf16[1,1024,2048]{2,1,0:T(8,128)(2,1)S(1)}, bf16[1,1024,2048]{2,1,0:T(8,128)(2,1)}, u32[]{:S(2)}) copy-start(bf16[1,1024,2048]{2,1,0:T(8,128)(2,1)} %param.10) | copy-start | bytes 12582916
  1.3 22.1 %copy-start.1 = (bf16[1,2048,1024]{2,1,0:T(8,128)(2,1)S(1)}, bf16[1,2048,1024]{2,1,0:T(8,128)(2,1)}, u32[]{:S(2)}) copy-start(bf16[1,2048,1024]{2,1,0:T(8,128)(2,1)} %param.11) | copy-start | bytes 12582916
  2.8 12.0 %collective-permute-start = (bf16[16,2048]{1,0:T(8,128)(2,1)S(1)}, bf16[16,2048]{1,0:T(8,128)(2,1)S(1)}, u32[]{:S(2)}, u32[]{:S(2)}) collective-permute-start(bf16[16,2048]{1,0:T(8,128)(2,1)S(1)} %get-tuple-element.34), channel_id=1, source_target_pairs={{0,7},{1,6},{2,5},{3,4},{4,3},{5,2},{6,1},{7,0},{8,15},{9,14},{10,... | collective-permute-start | bytes 196616 | tf_op jit(solution)/shard_map/ppermute | solution.py:261
  8.9 10.7 %collective-permute-start.1 = (bf16[16,2048]{1,0:T(8,128)(2,1)S(1)}, bf16[16,2048]{1,0:T(8,128)(2,1)S(1)}, u32[]{:S(2)}, u32[]{:S(2)}) collective-permute-start(bf16[16,2048]{1,0:T(8,128)(2,1)S(1)} %get-tuple-element.35), channel_id=1, source_target_pairs={{0,6},{1,7},{2,4},{3,5},{4,2},{5,3},{6,0},{7,1},{8,14},{9,15},{10,... | collective-permute-start | bytes 196616 | tf_op jit(solution)/shard_map/ppermute | solution.py:261
  9.1 5.6 %collective-permute-start.2 = (bf16[16,2048]{1,0:T(8,128)(2,1)S(1)}, bf16[16,2048]{1,0:T(8,128)(2,1)S(1)}, u32[]{:S(2)}, u32[]{:S(2)}) collective-permute-start(bf16[16,2048]{1,0:T(8,128)(2,1)S(1)} %get-tuple-element.36), channel_id=1, source_target_pairs={{0,1},{1,0},{2,3},{3,2},{4,5},{5,4},{6,7},{7,6},{8,9},{9,8},{10,11... | collective-permute-start | bytes 196616 | tf_op jit(solution)/shard_map/ppermute | solution.py:261
  9.5 11.7 %collective-permute-start.3 = (bf16[16,2048]{1,0:T(8,128)(2,1)S(1)}, bf16[16,2048]{1,0:T(8,128)(2,1)S(1)}, u32[]{:S(2)}, u32[]{:S(2)}) collective-permute-start(bf16[16,2048]{1,0:T(8,128)(2,1)S(1)} %get-tuple-element.37), channel_id=1, source_target_pairs={{0,3},{1,2},{2,1},{3,0},{4,7},{5,6},{6,5},{7,4},{8,11},{9,10},{10,... | collective-permute-start | bytes 196616 | tf_op jit(solution)/shard_map/ppermute | solution.py:261
  10.3 10.9 %collective-permute-start.4 = (bf16[16,2048]{1,0:T(8,128)(2,1)S(1)}, bf16[16,2048]{1,0:T(8,128)(2,1)S(1)}, u32[]{:S(2)}, u32[]{:S(2)}) collective-permute-start(bf16[16,2048]{1,0:T(8,128)(2,1)S(1)} %get-tuple-element.38), channel_id=1, source_target_pairs={{0,5},{1,4},{2,7},{3,6},{4,1},{5,0},{6,3},{7,2},{8,13},{9,12},{10,... | collective-permute-start | bytes 196616 | tf_op jit(solution)/shard_map/ppermute | solution.py:261
  14.7 6.5 %collective-permute-start.5 = (bf16[16,2048]{1,0:T(8,128)(2,1)S(1)}, bf16[16,2048]{1,0:T(8,128)(2,1)S(1)}, u32[]{:S(2)}, u32[]{:S(2)}) collective-permute-start(bf16[16,2048]{1,0:T(8,128)(2,1)S(1)} %get-tuple-element.40), channel_id=1, source_target_pairs={{0,4},{1,5},{2,6},{3,7},{4,0},{5,1},{6,2},{7,3},{8,12},{9,13},{10,... | collective-permute-start | bytes 196616 | tf_op jit(solution)/shard_map/ppermute | solution.py:261
  14.8 7.0 %collective-permute-start.6 = (bf16[16,2048]{1,0:T(8,128)(2,1)S(1)}, bf16[16,2048]{1,0:T(8,128)(2,1)S(1)}, u32[]{:S(2)}, u32[]{:S(2)}) collective-permute-start(bf16[16,2048]{1,0:T(8,128)(2,1)S(1)} %get-tuple-element.42), channel_id=1, source_target_pairs={{0,2},{1,3},{2,0},{3,1},{4,6},{5,7},{6,4},{7,5},{8,10},{9,11},{10,... | collective-permute-start | bytes 196616 | tf_op jit(solution)/shard_map/ppermute | solution.py:261
  19.6 11.8 %collective-permute-start.9 = (bf16[64,2048]{1,0:T(8,128)(2,1)S(1)}, bf16[64,2048]{1,0:T(8,128)(2,1)S(1)}, u32[]{:S(2)}, u32[]{:S(2)}) collective-permute-start(bf16[64,2048]{1,0:T(8,128)(2,1)S(1)} %constant_dynamic-update-slice_fusion.refs_0_), channel_id=1, source_target_pairs={{0,16},{8,24},{16,0},{24,8},{1,17},{9,25},{17,1},{25,9},{2,18},{10... | collective-permute-start | bytes 786440 | tf_op jit(solution)/shard_map/ppermute | solution.py:270
  21.2 6.4 %collective-permute-start.7 = (bf16[64,2048]{1,0:T(8,128)(2,1)S(1)}, bf16[64,2048]{1,0:T(8,128)(2,1)S(1)}, u32[]{:S(2)}, u32[]{:S(2)}) collective-permute-start(bf16[64,2048]{1,0:T(8,128)(2,1)S(1)} %constant_dynamic-update-slice_fusion.refs_0_), channel_id=1, source_target_pairs={{0,8},{8,0},{16,24},{24,16},{1,9},{9,1},{17,25},{25,17},{2,10},{10... | collective-permute-start | bytes 786440 | tf_op jit(solution)/shard_map/ppermute | solution.py:265
  21.8 9.9 %collective-permute-start.11 = (bf16[64,2048]{1,0:T(8,128)(2,1)S(1)}, bf16[64,2048]{1,0:T(8,128)(2,1)S(1)}, u32[]{:S(2)}, u32[]{:S(2)}) collective-permute-start(bf16[64,2048]{1,0:T(8,128)(2,1)S(1)} %constant_dynamic-update-slice_fusion.4.refs_1_), channel_id=1, source_target_pairs={{0,16},{8,24},{16,0},{24,8},{1,17},{9,25},{17,1},{25,9},{2,18},{10... | collective-permute-start | bytes 786440 | tf_op jit(solution)/shard_map/ppermute | solution.py:270
  23.4 4.3 %collective-permute-start.8 = (bf16[64,2048]{1,0:T(8,128)(2,1)S(1)}, bf16[64,2048]{1,0:T(8,128)(2,1)S(1)}, u32[]{:S(2)}, u32[]{:S(2)}) collective-permute-start(bf16[64,2048]{1,0:T(8,128)(2,1)S(1)} %constant_dynamic-update-slice_fusion.4.refs_1_), channel_id=1, source_target_pairs={{0,8},{8,0},{16,24},{24,16},{1,9},{9,1},{17,25},{25,17},{2,10},{10... | collective-permute-start | bytes 786440 | tf_op jit(solution)/shard_map/ppermute | solution.py:265
  27.7 14.4 %all-to-all-start = ((bf16[8,16,1152]{2,1,0:T(8,128)(2,1)}), bf16[8,16,1152]{2,1,0:T(8,128)(2,1)S(1)}, u32[]{:S(2)}, u32[]{:S(2)}) async-start(bf16[8,16,1152]{2,1,0:T(8,128)(2,1)} %bitcast.16), calls=%async_computation | async-start | bytes 589824 | tf_op jit(solution)/shard_map/all_to_all | solution.py:346
  31.4 5.3 %collective-permute-start.10 = (bf16[64,2048]{1,0:T(8,128)(2,1)S(1)}, bf16[64,2048]{1,0:T(8,128)(2,1)S(1)}, u32[]{:S(2)}, u32[]{:S(2)}) collective-permute-start(bf16[64,2048]{1,0:T(8,128)(2,1)S(1)} %collective-permute-done.9.refs_2_.refs_4_), channel_id=1, source_target_pairs={{0,8},{8,0},{16,24},{24,16},{1,9},{9,1},{17,25},{25,17},{2,10},{10... | collective-permute-start | bytes 786440 | tf_op jit(solution)/shard_map/ppermute | solution.py:265
  31.7 5.0 %collective-permute-start.12 = (bf16[64,2048]{1,0:T(8,128)(2,1)S(1)}, bf16[64,2048]{1,0:T(8,128)(2,1)S(1)}, u32[]{:S(2)}, u32[]{:S(2)}) collective-permute-start(bf16[64,2048]{1,0:T(8,128)(2,1)S(1)} %collective-permute-done.11.refs_6_), channel_id=1, source_target_pairs={{0,8},{8,0},{16,24},{24,16},{1,9},{9,1},{17,25},{25,17},{2,10},{10... | collective-permute-start | bytes 786440 | tf_op jit(solution)/shard_map/ppermute | solution.py:265
  36.8 5.3 %copy-start.3 = (bf16[64,2]{0,1:T(2,128)(2,1)S(1)}, bf16[64,2]{0,1:T(2,128)(2,1)}, u32[]{:S(2)}) copy-start(bf16[64,2]{0,1:T(2,128)(2,1)} %param.9) | copy-start | bytes 772

commit v16 on v14

--- a/solution.py
+++ b/solution.py
@@ -308,7 +308,7 @@
     blocks, places = routed[:experts], routed[experts:]
     rest = list(range(experts - 1, 1, -1))
     if len(rest) > 4:
-        rest.insert(2, rest.pop(-2))
+        rest.insert(2, rest.pop())
     order = [0, *rest[:2], 1, *rest[2:]]
     order_a, order_b = order[:half], order[half:]
     got_a = [blocks[0]] + [permute(blocks[k], k) for k in order_a[1:]]

time: 42.5 us -> 41.6 us (0.979)
  starting transfers between devices: 24.1 us -> 22.2 us
  waiting for transfers between devices: 0.61 us -> 1.7 us
    ppermute x7, starting transfers between devices: 16.7 us -> 14.8 us  [permute(): lax.ppermute(block, 'expert', [(i, i ^ k) for i in range(lax.axis_size('e...]
    ppermute x7, waiting for transfers between devices: 0.55 us -> 1.69 us  [permute(): lax.ppermute(block, 'expert', [(i, i ^ k) for i in range(lax.axis_size('e...]
  transfers between devices with their start and end apart: 14 -> 14, of which waited for: 1 -> 2; matrix products, arithmetic and copies ran while one was open for 0% -> 0% of each run, Pallas kernels for 34% -> 34%
where the time goes in v16:
time: 41.6 us; the launch traced here: 41.4 us
  starting transfers between devices  22.2 us (53%)
  Pallas kernels  16.6 us (40%)
  waiting for transfers between devices  1.7 us (4%)
  between operations  0.81 us (2%)
    pallas_call x5, Pallas kernels, call(): pl.pallas_call(kernel, out_shape=out_shape, in_specs=[pl.BlockSpec(memory...  16.6 us
    ppermute x7, starting transfers between devices, permute(): lax.ppermute(block, 'expert', [(i, i ^ k) for i in range(lax.axis_size('e...  14.8 us
    all_to_all x1, starting transfers between devices, local(): lax.all_to_all(after(back, core_a, core_b).reshape(experts, capacity, fea...  3.7 us
    ppermute x2, starting transfers between devices, shift_chips(): lax.ppermute(rows, 'dp', [(i, (i + 2 * k) % groups) for i in range(groups)])  3.11 us
    ppermute x7, waiting for transfers between devices, permute(): lax.ppermute(block, 'expert', [(i, i ^ k) for i in range(lax.axis_size('e...  1.69 us
  transfers between devices with their start and end apart: 14, of which 2 were waited for; matrix products, arithmetic and copies ran while one was open for 0% of the time, Pallas kernels for 34%

profile of v16, /device:TPU:0, one launch (start us, length us, event | category | flops | bytes accessed | tf_op | source)
XLA Modules:
  0.0 41.4 jit_solution(18421476049691820453)
XLA Ops:
  0.6 0.0 copy-start
  0.6 0.0 copy-start.1
  0.7 1.6 %shard_map.93 = (bf16[16,2048]{1,0:T(8,128)(2,1)S(1)}, bf16[16,2048]{1,0:T(8,128)(2,1)S(1)}, bf16[16,2048]{1,0:T(8,128)(2,1)S(1)}, bf16[16,2048]{1,0:T(8,128)(2,...) custom-call(s32[2,64]{1,0:T(2,128)} %bitcast.19, ...), custom_call_target="tpu_custom_call" | custom-call | flops 16106127360 | bytes 262912 | tf_op jit(solution)/shard_map/pallas_call | solution.py:35
  2.2 6.0 %collective-permute-start = (bf16[16,2048]{1,0:T(8,128)(2,1)S(1)}, bf16[16,2048]{1,0:T(8,128)(2,1)S(1)}, u32[]{:S(2)}, u32[]{:S(2)}) collective-permute-start(bf16[16,2048]{1,0:T(8,128)(2,1)S(1)} %get-tuple-element.34), channel_id=1, source_target_pairs={{0,7},{1,6},{2,5},{3,4},{4,3},{5,2},{6,1},{7,0},{8,15},{9,14},{10,... | collective-permute-start | bytes 196616 | tf_op jit(solution)/shard_map/ppermute | solution.py:262
  8.3 0.2 collective-permute-start.1
  8.5 0.4 collective-permute-start.2
  8.9 0.0 collective-permute-start.3
  8.9 5.2 %collective-permute-start.4 = (bf16[16,2048]{1,0:T(8,128)(2,1)S(1)}, bf16[16,2048]{1,0:T(8,128)(2,1)S(1)}, u32[]{:S(2)}, u32[]{:S(2)}) collective-permute-start(bf16[16,2048]{1,0:T(8,128)(2,1)S(1)} %get-tuple-element.38), channel_id=1, source_target_pairs={{0,5},{1,4},{2,7},{3,6},{4,1},{5,0},{6,3},{7,2},{8,13},{9,12},{10,... | collective-permute-start | bytes 196616 | tf_op jit(solution)/shard_map/ppermute | solution.py:262
  14.1 0.0 collective-permute-done.2
  14.1 0.1 collective-permute-start.5
  14.2 0.0 collective-permute-done
  14.2 2.8 %collective-permute-start.6 = (bf16[16,2048]{1,0:T(8,128)(2,1)S(1)}, bf16[16,2048]{1,0:T(8,128)(2,1)S(1)}, u32[]{:S(2)}, u32[]{:S(2)}) collective-permute-start(bf16[16,2048]{1,0:T(8,128)(2,1)S(1)} %get-tuple-element.42), channel_id=1, source_target_pairs={{0,3},{1,2},{2,1},{3,0},{4,7},{5,6},{6,5},{7,4},{8,11},{9,10},{10,... | collective-permute-start | bytes 196616 | tf_op jit(solution)/shard_map/ppermute | solution.py:262
  17.1 0.0 collective-permute-done.1
  17.1 1.6 %collective-permute-start.9 = (bf16[64,2048]{1,0:T(8,128)(2,1)S(1)}, bf16[64,2048]{1,0:T(8,128)(2,1)S(1)}, u32[]{:S(2)}, u32[]{:S(2)}) collective-permute-start(bf16[64,2048]{1,0:T(8,128)(2,1)S(1)} %constant_dynamic-update-slice_fusion.refs_0_), channel_id=1, source_target_pairs={{0,16},{8,24},{16,0},{24,8},{1,17},{9,25},{17,1},{25,9},{2,18},{10... | collective-permute-start | bytes 786440 | tf_op jit(solution)/shard_map/ppermute | solution.py:271
  18.7 0.0 collective-permute-done.3
  18.7 0.0 collective-permute-start.7
  18.7 0.0 collective-permute-done.4
  18.7 1.4 %collective-permute-done.5 = bf16[16,2048]{1,0:T(8,128)(2,1)S(1)} collective-permute-done((bf16[16,2048]{1,0:T(8,128)(2,1)S(1)}, bf16[16,2048]{1,0:T(8,128)(2,1)S(1)}, u32[]{:S(2)}, u32[]{:S(2)}) %collective-permute-start.5) | collective-permute-done | bytes 65568 | tf_op jit(solution)/shard_map/ppermute | solution.py:262
  20.1 0.3 collective-permute-done.6
  20.4 1.5 %collective-permute-start.11 = (bf16[64,2048]{1,0:T(8,128)(2,1)S(1)}, bf16[64,2048]{1,0:T(8,128)(2,1)S(1)}, u32[]{:S(2)}, u32[]{:S(2)}) collective-permute-start(bf16[64,2048]{1,0:T(8,128)(2,1)S(1)} %constant_dynamic-update-slice_fusion.4.refs_1_), channel_id=1, source_target_pairs={{0,16},{8,24},{16,0},{24,8},{1,17},{9,25},{17,1},{25,9},{2,18},{10... | collective-permute-start | bytes 786440 | tf_op jit(solution)/shard_map/ppermute | solution.py:271
  21.9 0.0 collective-permute-start.8
  21.9 0.0 copy-done
  21.9 0.0 copy-done.1
  21.9 4.2 %shard_map.94 = (bf16[128,2048]{1,0:T(8,128)(2,1)}, bf16[128,512]{1,0:T(8,128)(2,1)}, bf16[128,1152]{1,0:T(8,128)(2,1)}) custom-call(bf16[64,2048]{1,0:T(8,128)(2,1)S(1)} %constant_dynamic-update-slice_fusion.refs_0_, bf16[64,2048]{1,0:T(8,128)(2,1)S(1)} %constant_dynamic-update-slice_fusion.4.refs_1_, bf16[1024,2048]{1,0:T(8,128)(2,1)S(1)} %bitcast.10, ...), custom_call_target="tpu_custom_call" | custom-call | flops 10737418240 | bytes 8912896 | tf_op jit(solution)/shard_map/pallas_call | solution.py:35
  26.2 0.0 collective-permute-done.7.refs_0_.refs_2_
  26.2 0.0 collective-permute-done.8.refs_1_.refs_3_
  26.2 3.7 %all-to-all-start = ((bf16[8,16,1152]{2,1,0:T(8,128)(2,1)}), bf16[8,16,1152]{2,1,0:T(8,128)(2,1)S(1)}, u32[]{:S(2)}, u32[]{:S(2)}) async-start(bf16[8,16,1152]{2,1,0:T(8,128)(2,1)} %bitcast.16), calls=%async_computation | async-start | bytes 589824 | tf_op jit(solution)/shard_map/all_to_all | solution.py:348
  29.9 0.0 collective-permute-done.9.refs_2_.refs_4_
  29.9 0.3 collective-permute-start.10
  30.2 0.0 collective-permute-done.11.refs_6_
  30.2 0.3 collective-permute-start.12
  30.5 4.7 %shard_map.95 = (bf16[1024,2048]{1,0:T(8,128)(2,1)S(1)}, bf16[2048,1024]{1,0:T(8,128)(2,1)S(1)}, bf16[192,2048]{1,0:T(8,128)(2,1)S(1)}, bf16[192,512]{1,0:T(8,128)(2,1)S(1)}) custom-call(bf16[64,2048]{1,0:T(8,128)(2,1)S(1)} %collective-permute-done.7.refs_0_.refs_2_, bf16[64,2048]{1,0:T(8,128)(2,1)S(1)} %collective-permute-done.8.refs_1_.refs_3_, ...), custom_call_target="tpu_custom_call" | custom-call | flops 1073741824 | bytes 9175040 | tf_op jit(solution)/shard_map/pallas_call | solution.py:35
  35.2 0.0 collective-permute-done.10.refs_5_
  35.2 0.0 collective-permute-done.12.refs_7_
  35.2 0.0 copy-start.2
  35.2 5.2 %shard_map.96 = (bf16[256,2048]{1,0:T(8,128)(2,1)}, bf16[512,1024]{1,0:T(8,128)(2,1)}) custom-call(bf16[64,2048]{1,0:T(8,128)(2,1)S(1)} %constant_dynamic-update-slice_fusion.refs_0_, bf16[64,2048]{1,0:T(8,128)(2,1)S(1)} %constant_dynamic-update-slice_fusion.4.refs_1_, bf16[64,2048]{1,0:T(8,128)(2,1)S(1)} %collective-permute-done.7.refs_0_.refs_2_, ...), custom_call_target="tpu_custom_call" | custom-call | flops 2147483648 | bytes 12124160 | tf_op jit(solution)/shard_map/pallas_call | solution.py:35
  40.5 0.0 all-to-all-done
  40.5 0.0 copy-done.2
  40.5 0.9 %shard_map.97 = (bf16[64,1024]{1,0:T(8,128)(2,1)}, bf16[2,64]{1,0:T(2,128)(2,1)}) custom-call(bf16[128,64]{1,0:T(8,128)(2,1)S(1)} %get-tuple-element.31.place0, bf16[128,64]{1,0:T(8,128)(2,1)S(1)} %get-tuple-element.32.place1, bf16[2,64]{1,0:T(2,128)(2,1)S(1)} %bitcast.15, bf16[128,1152]{1,0:T(8,128)(2,1)S(1)} %bitcast.13), custom_call_target="tpu_custom_call" | custom-call | bytes 327936 | tf_op jit(solution)/shard_map/pallas_call | solution.py:35
  (8 shorter events, 0.0 us)
Async XLA Ops:
  0.6 21.3 %copy-start = (bf16[1,1024,2048]{2,1,0:T(8,128)(2,1)S(1)}, bf16[1,1024,2048]{2,1,0:T(8,128)(2,1)}, u32[]{:S(2)}) copy-start(bf16[1,1024,2048]{2,1,0:T(8,128)(2,1)} %param.10) | copy-start | bytes 12582916
  0.6 21.3 %copy-start.1 = (bf16[1,2048,1024]{2,1,0:T(8,128)(2,1)S(1)}, bf16[1,2048,1024]{2,1,0:T(8,128)(2,1)}, u32[]{:S(2)}) copy-start(bf16[1,2048,1024]{2,1,0:T(8,128)(2,1)} %param.11) | copy-start | bytes 12582916
  2.2 12.0 %collective-permute-start = (bf16[16,2048]{1,0:T(8,128)(2,1)S(1)}, bf16[16,2048]{1,0:T(8,128)(2,1)S(1)}, u32[]{:S(2)}, u32[]{:S(2)}) collective-permute-start(bf16[16,2048]{1,0:T(8,128)(2,1)S(1)} %get-tuple-element.34), channel_id=1, source_target_pairs={{0,7},{1,6},{2,5},{3,4},{4,3},{5,2},{6,1},{7,0},{8,15},{9,14},{10,... | collective-permute-start | bytes 196616 | tf_op jit(solution)/shard_map/ppermute | solution.py:262
  8.3 8.8 %collective-permute-start.1 = (bf16[16,2048]{1,0:T(8,128)(2,1)S(1)}, bf16[16,2048]{1,0:T(8,128)(2,1)S(1)}, u32[]{:S(2)}, u32[]{:S(2)}) collective-permute-start(bf16[16,2048]{1,0:T(8,128)(2,1)S(1)} %get-tuple-element.35), channel_id=1, source_target_pairs={{0,6},{1,7},{2,4},{3,5},{4,2},{5,3},{6,0},{7,1},{8,14},{9,15},{10,... | collective-permute-start | bytes 196616 | tf_op jit(solution)/shard_map/ppermute | solution.py:262
  8.5 5.6 %collective-permute-start.2 = (bf16[16,2048]{1,0:T(8,128)(2,1)S(1)}, bf16[16,2048]{1,0:T(8,128)(2,1)S(1)}, u32[]{:S(2)}, u32[]{:S(2)}) collective-permute-start(bf16[16,2048]{1,0:T(8,128)(2,1)S(1)} %get-tuple-element.36), channel_id=1, source_target_pairs={{0,1},{1,0},{2,3},{3,2},{4,5},{5,4},{6,7},{7,6},{8,9},{9,8},{10,11... | collective-permute-start | bytes 196616 | tf_op jit(solution)/shard_map/ppermute | solution.py:262
  8.9 9.8 %collective-permute-start.3 = (bf16[16,2048]{1,0:T(8,128)(2,1)S(1)}, bf16[16,2048]{1,0:T(8,128)(2,1)S(1)}, u32[]{:S(2)}, u32[]{:S(2)}) collective-permute-start(bf16[16,2048]{1,0:T(8,128)(2,1)S(1)} %get-tuple-element.37), channel_id=1, source_target_pairs={{0,2},{1,3},{2,0},{3,1},{4,6},{5,7},{6,4},{7,5},{8,10},{9,11},{10,... | collective-permute-start | bytes 196616 | tf_op jit(solution)/shard_map/ppermute | solution.py:262
  8.9 9.8 %collective-permute-start.4 = (bf16[16,2048]{1,0:T(8,128)(2,1)S(1)}, bf16[16,2048]{1,0:T(8,128)(2,1)S(1)}, u32[]{:S(2)}, u32[]{:S(2)}) collective-permute-start(bf16[16,2048]{1,0:T(8,128)(2,1)S(1)} %get-tuple-element.38), channel_id=1, source_target_pairs={{0,5},{1,4},{2,7},{3,6},{4,1},{5,0},{6,3},{7,2},{8,13},{9,12},{10,... | collective-permute-start | bytes 196616 | tf_op jit(solution)/shard_map/ppermute | solution.py:262
  14.1 6.0 %collective-permute-start.5 = (bf16[16,2048]{1,0:T(8,128)(2,1)S(1)}, bf16[16,2048]{1,0:T(8,128)(2,1)S(1)}, u32[]{:S(2)}, u32[]{:S(2)}) collective-permute-start(bf16[16,2048]{1,0:T(8,128)(2,1)S(1)} %get-tuple-element.40), channel_id=1, source_target_pairs={{0,4},{1,5},{2,6},{3,7},{4,0},{5,1},{6,2},{7,3},{8,12},{9,13},{10,... | collective-permute-start | bytes 196616 | tf_op jit(solution)/shard_map/ppermute | solution.py:262
  14.2 6.2 %collective-permute-start.6 = (bf16[16,2048]{1,0:T(8,128)(2,1)S(1)}, bf16[16,2048]{1,0:T(8,128)(2,1)S(1)}, u32[]{:S(2)}, u32[]{:S(2)}) collective-permute-start(bf16[16,2048]{1,0:T(8,128)(2,1)S(1)} %get-tuple-element.42), channel_id=1, source_target_pairs={{0,3},{1,2},{2,1},{3,0},{4,7},{5,6},{6,5},{7,4},{8,11},{9,10},{10,... | collective-permute-start | bytes 196616 | tf_op jit(solution)/shard_map/ppermute | solution.py:262
  17.1 12.8 %collective-permute-start.9 = (bf16[64,2048]{1,0:T(8,128)(2,1)S(1)}, bf16[64,2048]{1,0:T(8,128)(2,1)S(1)}, u32[]{:S(2)}, u32[]{:S(2)}) collective-permute-start(bf16[64,2048]{1,0:T(8,128)(2,1)S(1)} %constant_dynamic-update-slice_fusion.refs_0_), channel_id=1, source_target_pairs={{0,16},{8,24},{16,0},{24,8},{1,17},{9,25},{17,1},{25,9},{2,18},{10... | collective-permute-start | bytes 786440 | tf_op jit(solution)/shard_map/ppermute | solution.py:271
  18.7 7.5 %collective-permute-start.7 = (bf16[64,2048]{1,0:T(8,128)(2,1)S(1)}, bf16[64,2048]{1,0:T(8,128)(2,1)S(1)}, u32[]{:S(2)}, u32[]{:S(2)}) collective-permute-start(bf16[64,2048]{1,0:T(8,128)(2,1)S(1)} %constant_dynamic-update-slice_fusion.refs_0_), channel_id=1, source_target_pairs={{0,8},{8,0},{16,24},{24,16},{1,9},{9,1},{17,25},{25,17},{2,10},{10... | collective-permute-start | bytes 786440 | tf_op jit(solution)/shard_map/ppermute | solution.py:266
  20.4 9.8 %collective-permute-start.11 = (bf16[64,2048]{1,0:T(8,128)(2,1)S(1)}, bf16[64,2048]{1,0:T(8,128)(2,1)S(1)}, u32[]{:S(2)}, u32[]{:S(2)}) collective-permute-start(bf16[64,2048]{1,0:T(8,128)(2,1)S(1)} %constant_dynamic-update-slice_fusion.4.refs_1_), channel_id=1, source_target_pairs={{0,16},{8,24},{16,0},{24,8},{1,17},{9,25},{17,1},{25,9},{2,18},{10... | collective-permute-start | bytes 786440 | tf_op jit(solution)/shard_map/ppermute | solution.py:271
  21.9 4.2 %collective-permute-start.8 = (bf16[64,2048]{1,0:T(8,128)(2,1)S(1)}, bf16[64,2048]{1,0:T(8,128)(2,1)S(1)}, u32[]{:S(2)}, u32[]{:S(2)}) collective-permute-start(bf16[64,2048]{1,0:T(8,128)(2,1)S(1)} %constant_dynamic-update-slice_fusion.4.refs_1_), channel_id=1, source_target_pairs={{0,8},{8,0},{16,24},{24,16},{1,9},{9,1},{17,25},{25,17},{2,10},{10... | collective-permute-start | bytes 786440 | tf_op jit(solution)/shard_map/ppermute | solution.py:266
  26.2 14.3 %all-to-all-start = ((bf16[8,16,1152]{2,1,0:T(8,128)(2,1)}), bf16[8,16,1152]{2,1,0:T(8,128)(2,1)S(1)}, u32[]{:S(2)}, u32[]{:S(2)}) async-start(bf16[8,16,1152]{2,1,0:T(8,128)(2,1)} %bitcast.16), calls=%async_computation | async-start | bytes 589824 | tf_op jit(solution)/shard_map/all_to_all | solution.py:348
  29.9 5.3 %collective-permute-start.10 = (bf16[64,2048]{1,0:T(8,128)(2,1)S(1)}, bf16[64,2048]{1,0:T(8,128)(2,1)S(1)}, u32[]{:S(2)}, u32[]{:S(2)}) collective-permute-start(bf16[64,2048]{1,0:T(8,128)(2,1)S(1)} %collective-permute-done.9.refs_2_.refs_4_), channel_id=1, source_target_pairs={{0,8},{8,0},{16,24},{24,16},{1,9},{9,1},{17,25},{25,17},{2,10},{10... | collective-permute-start | bytes 786440 | tf_op jit(solution)/shard_map/ppermute | solution.py:266
  30.2 5.0 %collective-permute-start.12 = (bf16[64,2048]{1,0:T(8,128)(2,1)S(1)}, bf16[64,2048]{1,0:T(8,128)(2,1)S(1)}, u32[]{:S(2)}, u32[]{:S(2)}) collective-permute-start(bf16[64,2048]{1,0:T(8,128)(2,1)S(1)} %collective-permute-done.11.refs_6_), channel_id=1, source_target_pairs={{0,8},{8,0},{16,24},{24,16},{1,9},{9,1},{17,25},{25,17},{2,10},{10... | collective-permute-start | bytes 786440 | tf_op jit(solution)/shard_map/ppermute | solution.py:266
  35.2 5.3 %copy-start.2 = (bf16[64,2]{0,1:T(2,128)(2,1)S(1)}, bf16[64,2]{0,1:T(2,128)(2,1)}, u32[]{:S(2)}) copy-start(bf16[64,2]{0,1:T(2,128)(2,1)} %param.9) | copy-start | bytes 772
